TPU v7x, 32 devices: a whole 2x2x4 slice. The times are simulated.
32 devices in a mesh: section: 2 (over x), dp: 4 (over z), tensor: 4 (over y, core).
Axes of the slice: x: 2, y: 2, z: 4, core: 2. Of those that a mesh axis runs over, the one named last changes fastest.
Arguments:
- boundary: float32 [2, 8, 1024, 1024], P('section', 'dp', 'tensor'), may hold values from -6 to 6
- w_qkv: bfloat16 [2, 1024, 3, 1024], P('section', 'dp', None, 'tensor'), may hold values from -0.1875 to 0.1875
- w_out: bfloat16 [2, 1024, 1024], P('section', 'tensor', 'dp'), may hold values from -1.5 to 1.5
- w_gate_up: bfloat16 [2, 1024, 2, 2752], P('section', 'dp', None, 'tensor'), may hold values from -0.1875 to 0.1875
- w_down: bfloat16 [2, 2752, 1024], P('section', 'tensor', 'dp'), may hold values from -0.109375 to 0.109375
- norm_gains: bfloat16 [2, 2, 1024], P('section', None, 'dp'), may hold values from 0.099609375 to 1.8984375
- variate_bias: bfloat16 [2, 16, 2], P('section', 'tensor'), may hold values from -1 to 1
- segment_ids: int32 [8, 1024], P('dp'), may hold values from 0 to 8, as said below
- variate_ids: int32 [8, 1024], P('dp'), may hold values from 0 to 3
- time_ids: int32 [8, 1024], P('dp'), may hold values from 0 to 1023
- padding_mask: int32 [8, 1024], P('dp'), may hold values from 0 to 1, as said below
Outputs:
- boundary_out: float32 [2, 8, 1024, 1024], P('section', 'dp', 'tensor')
- grad_qkv: float32 [2, 1024, 3, 1024], P('section', 'dp', None, 'tensor')
- grad_out: float32 [2, 1024, 1024], P('section', 'tensor', 'dp')
- grad_gate_up: float32 [2, 1024, 2, 2752], P('section', 'dp', None, 'tensor')
- grad_down: float32 [2, 2752, 1024], P('section', 'tensor', 'dp')
- grad_gains: float32 [2, 2, 1024], P('section', None, ('dp', 'tensor'))
- grad_bias: float32 [2, 16, 2], P('section', 'tensor')
Inputs may be any that keep to these rules, and one draw needn't show every extreme that they name: `segment_ids`: along each sequence the ids never fall. `padding_mask`: in each sequence the 1s form a prefix of 512 positions or more; in each group of 2 consecutive sequences one sequence has no 0.
All inputs are finite; a program needn't handle non-finite values.
Results may differ from a plain program's by a relative error of at most 0.028.
Values may be sent and summed in bfloat16 or wider, within the bound.
No kernel may reach another device: no remote copies, remote signals or barrier semaphores. Data moves between devices by JAX's collectives and lax.ppermute only.
A program may use at most 256 MiB of HBM per device.

v0:
```python
import math

import jax
import jax.numpy as jnp
from jax import lax
from jax.sharding import PartitionSpec as P

EPS = 1e-05
NEG = -1e30


def from_behind(value, axis, steps):
    count = lax.axis_size(axis)
    initial, last = (max(0, -steps), min(count, count - steps))
    return lax.ppermute(value, axis, [(source, source + steps) for source in range(initial, last)])


def rms_parts(x):
    scale_row = lax.rsqrt(jnp.mean(x * x, axis=-1, keepdims=True) + EPS)
    return (x * scale_row, scale_row)


def rms_back(grad_norm, normed, scale_row, gain):
    grad_hat = grad_norm * gain
    return scale_row * (grad_hat - normed * jnp.mean(grad_hat * normed, axis=-1, keepdims=True))


def angles(time_row, head_dim):
    half_dim = head_dim // 2
    frequency = jnp.exp(-jnp.log(10000.0) * jnp.arange(half_dim, dtype=jnp.float32) / half_dim)
    phases = time_row.astype(jnp.float32)[:, None] * frequency[None, :]
    return (jnp.cos(phases)[:, None, :], jnp.sin(phases)[:, None, :])


def rotate(t, cos_part, sin_part):
    half_dim = t.shape[-1] // 2
    first_half = t[..., :half_dim]
    second = t[..., half_dim:]
    return jnp.concatenate(
        [first_half * cos_part - second * sin_part, first_half * sin_part + second * cos_part],
        axis=-1,
    )


def masked_scores(
    q_block, k, var_bias, seg_block, var_block, pos_block, segment, variate, valid_keys, positions
):
    head_dim = q_block.shape[-1]
    scores = jnp.einsum("qhd,khd->hqk", q_block, k, preferred_element_type=jnp.float32) * (
        1.0 / math.sqrt(head_dim)
    )
    same_var = var_block[:, None] == variate[None, :]
    scores = scores + jnp.where(
        same_var[None], var_bias[:, 0][:, None, None], var_bias[:, 1][:, None, None]
    )
    allowed = (seg_block[:, None] == segment[None, :]) & (
        (valid_keys[None, :] == 1) | (pos_block[:, None] == positions[None, :])
    )
    return (jnp.where(allowed[None], scores, NEG), same_var)


def block_layout(array, blocks, block_rows):
    return array.reshape((blocks, block_rows) + array.shape[1:])


def attend(q, k, v, var_bias, segment, variate, valid_keys):
    seq_len, head_count, head_dim = q.shape
    block_rows = min(512, seq_len)
    blocks = seq_len // block_rows
    positions = jnp.arange(seq_len, dtype=jnp.int32)

    def attend_block(block_args):
        q_block, seg_block, var_block, pos_block = block_args
        masked, same_var = masked_scores(
            q_block,
            k,
            var_bias,
            seg_block,
            var_block,
            pos_block,
            segment,
            variate,
            valid_keys,
            positions,
        )
        row_max = jnp.max(masked, axis=-1, keepdims=True)
        weights = jnp.exp(masked - row_max)
        total_weight = jnp.sum(weights, axis=-1, keepdims=True)
        probs_low = (weights / total_weight).astype(jnp.bfloat16)
        result = jnp.einsum("hqk,khd->qhd", probs_low, v, preferred_element_type=jnp.float32)
        return (result, (row_max + jnp.log(total_weight))[..., 0])

    block_parts = (
        block_layout(q, blocks, block_rows),
        block_layout(segment, blocks, block_rows),
        block_layout(variate, blocks, block_rows),
        block_layout(positions, blocks, block_rows),
    )
    results, log_sums = lax.map(attend_block, block_parts)
    return (results.reshape(seq_len, head_count * head_dim), log_sums)


def attend_back(q, k, v, grad_att, log_sums, var_bias, segment, variate, valid_keys):
    seq_len, head_count, head_dim = q.shape
    block_rows = min(512, seq_len)
    blocks = seq_len // block_rows
    positions = jnp.arange(seq_len, dtype=jnp.int32)
    scale = 1.0 / math.sqrt(head_dim)

    def back_block(carry, block_args):
        grad_k, grad_v, grad_bias = carry
        q_block, go_block, lse_block, seg_block, var_block, pos_block = block_args
        masked, same_var = masked_scores(
            q_block,
            k,
            var_bias,
            seg_block,
            var_block,
            pos_block,
            segment,
            variate,
            valid_keys,
            positions,
        )
        probability = jnp.exp(masked - lse_block[:, :, None])
        grad_prob = jnp.einsum("qhd,khd->hqk", go_block, v, preferred_element_type=jnp.float32)
        inner = jnp.sum(probability * grad_prob, axis=-1, keepdims=True)
        grad_score = (probability * (grad_prob - inner)).astype(jnp.bfloat16)
        grad_q = (
            jnp.einsum("hqk,khd->qhd", grad_score, k, preferred_element_type=jnp.float32) * scale
        )
        grad_k = (
            grad_k
            + jnp.einsum("hqk,qhd->khd", grad_score, q_block, preferred_element_type=jnp.float32)
            * scale
        )
        grad_v = grad_v + jnp.einsum(
            "hqk,qhd->khd",
            probability.astype(jnp.bfloat16),
            go_block,
            preferred_element_type=jnp.float32,
        )
        score_f = grad_score.astype(jnp.float32)
        same_sum = jnp.sum(jnp.where(same_var[None], score_f, 0.0), axis=(1, 2))
        other_sum = jnp.sum(jnp.where(same_var[None], 0.0, score_f), axis=(1, 2))
        grad_bias = grad_bias + jnp.stack([same_sum, other_sum], axis=-1)
        return ((grad_k, grad_v, grad_bias), grad_q)

    initial = (
        jnp.zeros(k.shape, jnp.float32),
        jnp.zeros(v.shape, jnp.float32),
        jnp.zeros((head_count, 2), jnp.float32),
    )
    block_parts = (
        block_layout(q, blocks, block_rows),
        block_layout(grad_att, blocks, block_rows),
        log_sums,
        block_layout(segment, blocks, block_rows),
        block_layout(variate, blocks, block_rows),
        block_layout(positions, blocks, block_rows),
    )
    (grad_k, grad_v, grad_bias), grad_q = lax.scan(back_block, initial, block_parts)
    return (grad_q.reshape(seq_len, head_count, head_dim), grad_k, grad_v, grad_bias)


def forward(x, weights, var_bias, segment, variate, time_row, valid_keys):
    w_qkv, w_out, w_gate_up, w_down, gain_pair = weights
    gains_f = gain_pair.astype(jnp.float32)
    normed_a, scale_a = rms_parts(x)
    gathered_a = lax.all_gather(
        (normed_a * gains_f[0]).astype(jnp.bfloat16), "tensor", axis=0, tiled=True
    )
    seq_len = gathered_a.shape[0]
    model_width = w_qkv.shape[0]
    local_width = w_qkv.shape[2]
    head_count = var_bias.shape[0]
    head_dim = local_width // head_count
    projected = jnp.dot(
        gathered_a, w_qkv.reshape(model_width, 3 * local_width), preferred_element_type=jnp.float32
    )
    cos_part, sin_part = angles(time_row, head_dim)
    query_normed, query_scale = rms_parts(
        projected[:, :local_width].reshape(seq_len, head_count, head_dim)
    )
    key_normed, key_scale = rms_parts(
        projected[:, local_width : 2 * local_width].reshape(seq_len, head_count, head_dim)
    )
    q = rotate(query_normed, cos_part, sin_part).astype(jnp.bfloat16)
    k = rotate(key_normed, cos_part, sin_part).astype(jnp.bfloat16)
    v = projected[:, 2 * local_width :].reshape(seq_len, head_count, head_dim).astype(jnp.bfloat16)
    attended, log_sums = attend(q, k, v, var_bias, segment, variate, valid_keys)
    attended = attended.astype(jnp.bfloat16)
    h = x + lax.psum_scatter(
        jnp.dot(attended, w_out, preferred_element_type=jnp.float32).astype(jnp.bfloat16),
        "tensor",
        scatter_dimension=0,
        tiled=True,
    ).astype(jnp.float32)
    normed_f, scale_f = rms_parts(h)
    gathered_f = lax.all_gather(
        (normed_f * gains_f[1]).astype(jnp.bfloat16), "tensor", axis=0, tiled=True
    )
    hidden_width = w_gate_up.shape[2]
    gate_up = jnp.dot(
        gathered_f,
        w_gate_up.reshape(model_width, 2 * hidden_width),
        preferred_element_type=jnp.float32,
    )
    hidden = (jax.nn.silu(gate_up[:, :hidden_width]) * gate_up[:, hidden_width:]).astype(
        jnp.bfloat16
    )
    output = h + lax.psum_scatter(
        jnp.dot(hidden, w_down, preferred_element_type=jnp.float32).astype(jnp.bfloat16),
        "tensor",
        scatter_dimension=0,
        tiled=True,
    ).astype(jnp.float32)
    kept_state = {
        "normed_a": normed_a,
        "scale_a": scale_a,
        "gathered_a": gathered_a,
        "q": q,
        "k": k,
        "v": v,
        "query_normed": query_normed,
        "query_scale": query_scale,
        "key_normed": key_normed,
        "key_scale": key_scale,
        "log_sums": log_sums,
        "attended": attended,
        "normed_f": normed_f,
        "scale_f": scale_f,
        "gathered_f": gathered_f,
        "gate_up": gate_up,
        "hidden": hidden,
        "segment": segment,
        "variate": variate,
        "time_row": time_row,
        "valid_keys": valid_keys,
    }
    return (output, kept_state)


def backward(grad_y, kept_state, weights, var_bias):
    w_qkv, w_out, w_gate_up, w_down, gain_pair = weights
    gains_f = gain_pair.astype(jnp.float32)
    model_width = w_qkv.shape[0]
    local_width = w_qkv.shape[2]
    hidden_width = w_gate_up.shape[2]
    hidden = kept_state["hidden"]
    attended = kept_state["attended"]
    q = kept_state["q"]
    seq_len, head_count, head_dim = q.shape
    piece = lax.all_gather(grad_y.astype(jnp.bfloat16), "tensor", axis=0, tiled=True)
    grad_hidden = jnp.dot(piece, w_down.T, preferred_element_type=jnp.float32)
    grad_hidden, grad_wdown = (
        grad_hidden,
        jnp.dot(hidden.T, piece, preferred_element_type=jnp.float32),
    )
    gate = kept_state["gate_up"][:, :hidden_width]
    up_part = kept_state["gate_up"][:, hidden_width:]
    sigma = jax.nn.sigmoid(gate)
    grad_gate = grad_hidden * up_part * sigma * (1.0 + gate * (1.0 - sigma))
    grad_up = grad_hidden * gate * sigma
    grad_gu = jnp.concatenate([grad_gate, grad_up], axis=1).astype(jnp.bfloat16)
    grad_wgu = jnp.dot(kept_state["gathered_f"].T, grad_gu, preferred_element_type=jnp.float32)
    flat_gu = w_gate_up.reshape(model_width, 2 * hidden_width)
    grad_norm_f = lax.psum_scatter(
        jnp.dot(grad_gu, flat_gu.T, preferred_element_type=jnp.float32).astype(jnp.bfloat16),
        "tensor",
        scatter_dimension=0,
        tiled=True,
    ).astype(jnp.float32)
    gain_grad_f = jnp.sum(grad_norm_f * kept_state["normed_f"], axis=0)
    grad_h = grad_y + rms_back(
        grad_norm_f, kept_state["normed_f"], kept_state["scale_f"], gains_f[1]
    )
    piece = lax.all_gather(grad_h.astype(jnp.bfloat16), "tensor", axis=0, tiled=True)
    grad_att = jnp.dot(piece, w_out.T, preferred_element_type=jnp.float32)
    grad_att, grad_wout = (grad_att, jnp.dot(attended.T, piece, preferred_element_type=jnp.float32))
    grad_att = grad_att.astype(jnp.bfloat16).reshape(seq_len, head_count, head_dim)
    grad_q, grad_k, grad_v, grad_bias = attend_back(
        q,
        kept_state["k"],
        kept_state["v"],
        grad_att,
        kept_state["log_sums"],
        var_bias,
        kept_state["segment"],
        kept_state["variate"],
        kept_state["valid_keys"],
    )
    cos_part, sin_part = angles(kept_state["time_row"], head_dim)
    grad_q = rms_back(
        rotate(grad_q, cos_part, -sin_part),
        kept_state["query_normed"],
        kept_state["query_scale"],
        1.0,
    )
    grad_k = rms_back(
        rotate(grad_k, cos_part, -sin_part), kept_state["key_normed"], kept_state["key_scale"], 1.0
    )
    grad_proj = jnp.concatenate(
        [
            grad_q.reshape(seq_len, local_width),
            grad_k.reshape(seq_len, local_width),
            grad_v.reshape(seq_len, local_width),
        ],
        axis=1,
    ).astype(jnp.bfloat16)
    grad_wqkv = jnp.dot(kept_state["gathered_a"].T, grad_proj, preferred_element_type=jnp.float32)
    flat_qkv = w_qkv.reshape(model_width, 3 * local_width)
    grad_norm_a = lax.psum_scatter(
        jnp.dot(grad_proj, flat_qkv.T, preferred_element_type=jnp.float32).astype(jnp.bfloat16),
        "tensor",
        scatter_dimension=0,
        tiled=True,
    ).astype(jnp.float32)
    gain_grad_a = jnp.sum(grad_norm_a * kept_state["normed_a"], axis=0)
    grad_x = grad_h + rms_back(
        grad_norm_a, kept_state["normed_a"], kept_state["scale_a"], gains_f[0]
    )
    return (
        grad_x,
        (grad_wqkv, grad_wout, grad_wgu, grad_wdown),
        jnp.stack([gain_grad_a, gain_grad_f]),
        grad_bias,
    )


def fetch_weights(w_qkv, w_out, w_gate_up, w_down, norm_gains):
    return (
        lax.all_gather(w_qkv[0], "dp", axis=0, tiled=True),
        lax.all_gather(w_out[0], "dp", axis=1, tiled=True),
        lax.all_gather(w_gate_up[0], "dp", axis=0, tiled=True),
        lax.all_gather(w_down[0], "dp", axis=1, tiled=True),
        lax.all_gather(norm_gains[0], "dp", axis=1, tiled=True),
    )


def settle(weight_grads):
    return (
        lax.psum_scatter(
            weight_grads[0].astype(jnp.bfloat16), "dp", scatter_dimension=0, tiled=True
        ).astype(jnp.float32),
        lax.psum_scatter(
            weight_grads[1].astype(jnp.bfloat16), "dp", scatter_dimension=1, tiled=True
        ).astype(jnp.float32),
        lax.psum_scatter(
            weight_grads[2].astype(jnp.bfloat16), "dp", scatter_dimension=0, tiled=True
        ).astype(jnp.float32),
        lax.psum_scatter(
            weight_grads[3].astype(jnp.bfloat16), "dp", scatter_dimension=1, tiled=True
        ).astype(jnp.float32),
    )


def add_tuples(running, extra):
    if running is None:
        return extra
    return tuple((a + b for a, b in zip(running, extra)))


def per_device(
    boundary,
    w_qkv,
    w_out,
    w_gate_up,
    w_down,
    norm_gains,
    variate_bias,
    segment_ids,
    variate_ids,
    time_ids,
    padding_mask,
):
    section_index = lax.axis_index("section")
    is_first = section_index == 0
    local_ends = boundary[0]
    micro = local_ends.shape[0]
    var_bias = variate_bias[0].astype(jnp.float32)
    received_act = jnp.zeros_like(local_ends[0])
    received_grad = jnp.zeros_like(local_ends[0])
    states = []
    outputs = []
    input_grads = []
    grad_sums = None
    gain_total = jnp.zeros((2, w_qkv.shape[1] * lax.axis_size("dp")), jnp.float32)
    bias_total = jnp.zeros(var_bias.shape, jnp.float32)
    for tick in range(micro + 2):
        weights = fetch_weights(w_qkv, w_out, w_gate_up, w_down, norm_gains)
        fwd_index = jnp.clip(jnp.where(is_first, tick, tick - 1), 0, micro - 1).astype(jnp.int32)
        x_in = jnp.where(is_first, local_ends[min(tick, micro - 1)], received_act)
        segment = lax.dynamic_index_in_dim(segment_ids, fwd_index, 0, keepdims=False)
        variate = lax.dynamic_index_in_dim(variate_ids, fwd_index, 0, keepdims=False)
        time_row = lax.dynamic_index_in_dim(time_ids, fwd_index, 0, keepdims=False)
        valid_keys = lax.dynamic_index_in_dim(padding_mask, fwd_index, 0, keepdims=False)
        output, kept_state = forward(
            x_in, weights, var_bias, segment, variate, time_row, valid_keys
        )
        states.append(kept_state)
        outputs.append(output)
        received_act = from_behind(output.astype(jnp.bfloat16), "section", 1).astype(jnp.float32)
        if tick >= 2:
            back_state = jax.tree.map(
                lambda later, earlier: jnp.where(is_first, earlier, later),
                kept_state,
                states[tick - 2],
            )
        else:
            back_state = kept_state
        first_usable = 1.0 if tick >= 2 else 0.0
        second_usable = 1.0 if 1 <= tick <= micro else 0.0
        usable = jnp.where(is_first, first_usable, second_usable)
        cotangent = local_ends[min(max(tick - 1, 0), micro - 1)]
        grad_y = jnp.where(is_first, received_grad, cotangent) * usable
        grad_x, weight_grads, gain_grads, bias_grad = backward(
            grad_y, back_state, weights, var_bias
        )
        input_grads.append(grad_x)
        received_grad = from_behind(grad_x.astype(jnp.bfloat16), "section", -1).astype(jnp.float32)
        grad_sums = add_tuples(grad_sums, weight_grads)
        gain_total = gain_total + gain_grads
        bias_total = bias_total + bias_grad
    grad_sums = settle(grad_sums)
    slots = [jnp.where(is_first, input_grads[slot + 2], outputs[slot + 1]) for slot in range(micro)]
    boundary_out = jnp.stack(slots)[None]
    tensor_index = lax.axis_index("tensor")
    tensor_count = lax.axis_size("tensor")
    head_local = var_bias.shape[0]
    bias_full = lax.dynamic_update_slice(
        jnp.zeros((head_local * tensor_count, 2), jnp.float32),
        bias_total,
        (tensor_index * head_local, jnp.zeros((), jnp.int32)),
    )
    gain_all, bias_all = lax.psum((gain_total, bias_full), ("dp", "tensor"))
    piece_width = gain_all.shape[1] // (lax.axis_size("dp") * tensor_count)
    flat_index = lax.axis_index("dp") * tensor_count + tensor_index
    gain_piece = lax.dynamic_slice_in_dim(gain_all, flat_index * piece_width, piece_width, 1)
    bias_piece = lax.dynamic_slice_in_dim(bias_all, tensor_index * head_local, head_local, 0)
    grad_wqkv, grad_wout, grad_wgu, grad_wdown = grad_sums
    local_width = w_qkv.shape[3]
    hidden_width = w_gate_up.shape[3]
    return (
        boundary_out,
        grad_wqkv.reshape(grad_wqkv.shape[0], 3, local_width)[None],
        grad_wout[None],
        grad_wgu.reshape(grad_wgu.shape[0], 2, hidden_width)[None],
        grad_wdown[None],
        gain_piece[None],
        bias_piece[None],
    )


def solution(mesh):
    placed = (
        P("section", "dp", "tensor", None),
        P("section", "dp", None, "tensor"),
        P("section", "tensor", "dp"),
        P("section", "dp", None, "tensor"),
        P("section", "tensor", "dp"),
        P("section", None, "dp"),
        P("section", "tensor", None),
        P("dp", None),
        P("dp", None),
        P("dp", None),
        P("dp", None),
    )
    return jax.shard_map(
        per_device,
        mesh=mesh,
        in_specs=placed,
        out_specs=(
            P("section", "dp", "tensor", None),
            P("section", "dp", None, "tensor"),
            P("section", "tensor", "dp"),
            P("section", "dp", None, "tensor"),
            P("section", "tensor", "dp"),
            P("section", None, ("dp", "tensor")),
            P("section", "tensor", None),
        ),
        check_vma=False,
    )
```

profile of v0, /device:TPU:0, one launch (start us, length us, event | category | flops | bytes accessed | tf_op | source)
XLA Modules:
  0.0 1686.4 jit_solution(17910268225709034860)
XLA Ops:
  9.4 12.8 all-gather
  27.9 22.0 %all-gather.2 = bf16[1,256,1024]{2,1,0:T(8,128)(2,1)S(1)} all-gather(bf16[1,256,256]{2,1,0:T(8,128)(2,1)S(1)} %copy-done.252), channel_id=4, replica_groups=mesh['section'=2,'dp'=4,'tensor'=4] {'dp'}, dimensions={2}, use_global_device_ids=true | all-gather | bytes 655360 | tf_op jit(solution)/shard_map/all_gather | solution.py:334
  59.1 23.0 %all-gather.25.cloned.1.call-done = bf16[1024,1024]{1,0:T(8,128)(2,1)} async-done(((bf16[256,1024]{1,0:T(8,128)(2,1)}), bf16[1024,1024]{1,0:T(8,128)(2,1)}) %all-gather.25.cloned.1.call-update) | async-done | bytes 2097168 | tf_op jit(solution)/shard_map/all_gather | solution.py:170
  91.0 26.1 %while.120 = (s32[]{:T(128)}, bf16[2,512,4,64]{1,3,2,0:T(8,128)(2,1)S(1)}, f32[2,4,512]{2,1,0:T(4,128)S(1)}, s32[2,512]{1,0:T(2,128)S(1)}, s32[1024]{0:T(1024)S(...) while((s32[]{:T(128)}, ...), condition=%wide.region_6.7_spmd.clone, body=%wide.region_3.6_spmd.clone.sunk | while | flops 577240064 | bytes 31295256 | solution.py:99
  121.8 30.5 %reduce-scatter.20.cloned.1.call-done = bf16[256,1024]{1,0:T(8,128)(2,1)} async-done(((bf16[1024,1024]{1,0:T(8,128)(2,1)}), bf16[256,1024]{1,0:T(8,128)(2,1)}) %reduce-scatter.20.cloned.1.call-update) | async-done | bytes 524304 | tf_op jit(solution)/shard_map/reduce_scatter | solution.py:193
  156.9 55.0 %all-gather.61.cloned.1.call-done = bf16[1,1024,2,688]{1,3,2,0:T(8,128)(2,1)} async-done(((bf16[1,256,2,688]{1,3,2,0:T(8,128)(2,1)}), bf16[1,1024,2,688]{1,3,2,0:T(8,128)(2,1)}) %all-gather.61.cloned.1.call-update) | async-done | bytes 2818064 | tf_op jit(solution)/shard_map/all_gather | solution.py:335
  211.9 22.9 %all-gather.29.cloned.1.call-done = bf16[1024,1024]{1,0:T(8,128)(2,1)} async-done(((bf16[256,1024]{1,0:T(8,128)(2,1)}), bf16[1024,1024]{1,0:T(8,128)(2,1)}) %all-gather.29.cloned.1.call-update) | async-done | bytes 2097168 | tf_op jit(solution)/shard_map/all_gather | solution.py:200
  234.8 8.0 fusion.368
  242.7 28.6 %all-gather.59.cloned.1.call-done = bf16[1,688,1024]{2,1,0:T(8,128)(2,1)} async-done(((bf16[1,688,256]{2,1,0:T(8,128)(2,1)}), bf16[1,688,1024]{2,1,0:T(8,128)(2,1)}) %all-gather.59.cloned.1.call-update) | async-done | bytes 1409040 | tf_op jit(solution)/shard_map/all_gather | solution.py:336
  271.4 23.1 %all-gather.27.cloned.1.call-done = bf16[1024,1024]{1,0:T(8,128)(2,1)} async-done(((bf16[256,1024]{1,0:T(8,128)(2,1)}), bf16[1024,1024]{1,0:T(8,128)(2,1)}) %all-gather.27.cloned.1.call-update) | async-done | bytes 2097168 | tf_op jit(solution)/shard_map/all_gather | solution.py:254
  294.5 8.0 multiply_convert_fusion.11
  306.8 7.5 convolution_convert_fusion.6
  314.3 24.0 %reduce-scatter.26.cloned.1.call-done = bf16[256,1024]{1,0:T(8,128)(2,1)} async-done(((bf16[1024,1024]{1,0:T(8,128)(2,1)}), bf16[256,1024]{1,0:T(8,128)(2,1)}) %reduce-scatter.26.cloned.1.call-update) | async-done | bytes 524304 | tf_op jit(solution)/shard_map/reduce_scatter | solution.py:212
  338.3 34.5 %reduce-scatter.22.cloned.1.call-done = bf16[256,1024]{1,0:T(8,128)(2,1)} async-done(((bf16[1024,1024]{1,0:T(8,128)(2,1)}), bf16[256,1024]{1,0:T(8,128)(2,1)}) %reduce-scatter.22.cloned.1.call-update) | async-done | bytes 524304 | tf_op jit(solution)/shard_map/reduce_scatter | solution.py:268
  378.7 11.1 collective-permute-done.1
  393.7 23.5 %all-gather.33.cloned.1.call-done = bf16[1024,1024]{1,0:T(8,128)(2,1)} async-done(((bf16[256,1024]{1,0:T(8,128)(2,1)}), bf16[1024,1024]{1,0:T(8,128)(2,1)}) %all-gather.33.cloned.1.call-update) | async-done | bytes 2097168 | tf_op jit(solution)/shard_map/all_gather | solution.py:170
  424.2 21.8 %while.121 = (s32[]{:T(128)}, bf16[2,512,4,64]{1,3,2,0:T(8,128)(2,1)S(1)}, f32[2,4,512]{2,1,0:T(4,128)S(1)}, s32[2,512]{1,0:T(2,128)S(1)}, s32[1024]{0:T(1024)S(...) while((s32[]{:T(128)}, ...), condition=%wide.region_27.28_spmd.clone, body=%wide.region_24.27_spmd.clone.sunk | while | flops 577240064 | bytes 31295740 | solution.py:99
  450.5 30.9 %reduce-scatter.28.cloned.1.call-done = bf16[256,1024]{1,0:T(8,128)(2,1)} async-done(((bf16[1024,1024]{1,0:T(8,128)(2,1)}), bf16[256,1024]{1,0:T(8,128)(2,1)}) %reduce-scatter.28.cloned.1.call-update) | async-done | bytes 524304 | tf_op jit(solution)/shard_map/reduce_scatter | solution.py:193
  484.2 21.3 %all-gather.31.cloned.1.call-done = bf16[1024,1024]{1,0:T(8,128)(2,1)} async-done(((bf16[256,1024]{1,0:T(8,128)(2,1)}), bf16[1024,1024]{1,0:T(8,128)(2,1)}) %all-gather.31.cloned.1.call-update) | async-done | bytes 2097168 | tf_op jit(solution)/shard_map/all_gather | solution.py:278
  512.0 17.7 %all-gather.37.cloned.1.call-done = bf16[1024,1024]{1,0:T(8,128)(2,1)} async-done(((bf16[256,1024]{1,0:T(8,128)(2,1)}), bf16[1024,1024]{1,0:T(8,128)(2,1)}) %all-gather.37.cloned.1.call-update) | async-done | bytes 2097168 | tf_op jit(solution)/shard_map/all_gather | solution.py:200
  543.8 74.3 %while.124 = (s32[]{:T(128)}, f32[1024,4,64]{0,2,1:T(8,128)S(1)}, f32[1024,4,64]{0,2,1:T(8,128)}, f32[4,2]{0,1:T(2,128)}, f32[2,512,4,64]{1,0,3,2:T(2,128)}, /*i...) while((s32[]{:T(128)}, f32[1024,4,64]{0,2,1:T(8,128)S(1)}, ...), condition=%wide.region_15.16_spmd.clone, body=%wide.region_11.15_spmd.clone.sunk | while | flops 1379793920 | bytes 150546992 | solution.py:162
  562.5 10.3 dynamic_update_slice.82
  599.7 10.3 dynamic_update_slice.82
  636.3 25.2 %reduce-scatter.24.cloned.1.call-done = bf16[256,1024]{1,0:T(8,128)(2,1)} async-done(((bf16[1024,1024]{1,0:T(8,128)(2,1)}), bf16[256,1024]{1,0:T(8,128)(2,1)}) %reduce-scatter.24.cloned.1.call-update) | async-done | bytes 524304 | tf_op jit(solution)/shard_map/reduce_scatter | solution.py:313
  668.6 14.6 collective-permute-done
  700.0 14.0 all-gather.35.cloned.1.call-done
  714.0 6.2 multiply_convert_fusion.8
  727.7 25.3 %while.122 = (s32[]{:T(128)}, bf16[2,512,4,64]{1,3,2,0:T(8,128)(2,1)}, f32[2,4,512]{2,1,0:T(4,128)S(1)}, s32[2,512]{1,0:T(2,128)S(1)}, s32[1024]{0:T(1024)S(1)},...) while((s32[]{:T(128)}, ...), condition=%wide.region_48.49_spmd.clone, body=%wide.region_45.48_spmd.clone.sunk | while | flops 577240064 | bytes 33391952 | solution.py:99
  760.8 32.3 %reduce-scatter.36.cloned.1.call-done = bf16[256,1024]{1,0:T(8,128)(2,1)} async-done(((bf16[1024,1024]{1,0:T(8,128)(2,1)}), bf16[256,1024]{1,0:T(8,128)(2,1)}) %reduce-scatter.36.cloned.1.call-update) | async-done | bytes 524304 | tf_op jit(solution)/shard_map/reduce_scatter | solution.py:193
  796.5 22.7 %all-gather.39.cloned.1.call-done = bf16[1024,1024]{1,0:T(8,128)(2,1)} async-done(((bf16[256,1024]{1,0:T(8,128)(2,1)}), bf16[1024,1024]{1,0:T(8,128)(2,1)}) %all-gather.39.cloned.1.call-update) | async-done | bytes 2097168 | tf_op jit(solution)/shard_map/all_gather | solution.py:278
  829.2 70.5 %while.125 = (s32[]{:T(128)}, f32[1024,4,64]{0,2,1:T(8,128)S(1)}, f32[1024,4,64]{0,2,1:T(8,128)}, f32[4,2]{0,1:T(2,128)S(1)}, f32[2,512,4,64]{1,0,3,2:T(2,128)},...) while((s32[]{:T(128)}, f32[1024,4,64]{0,2,1:T(8,128)S(1)}, ...), condition=%wide.region_36.37_spmd.clone, body=%wide.region_32.36_spmd.clone.sunk | while | flops 1379793920 | bytes 148449840 | solution.py:162
  846.8 10.4 dynamic_update_slice.83
  881.4 10.4 dynamic_update_slice.83
  914.2 29.2 %reduce-scatter.32.cloned.1.call-done = bf16[256,1024]{1,0:T(8,128)(2,1)} async-done(((bf16[1024,1024]{1,0:T(8,128)(2,1)}), bf16[256,1024]{1,0:T(8,128)(2,1)}) %reduce-scatter.32.cloned.1.call-update) | async-done | bytes 524304 | tf_op jit(solution)/shard_map/reduce_scatter | solution.py:313
  948.4 14.2 collective-permute-done.2
  968.2 9.7 broadcast_select_fusion.1
  983.1 10.0 all-gather.43.cloned.1.call-done
  993.1 6.2 fusion.187
  1005.5 21.5 %reduce-scatter.42.cloned.1.call-done = bf16[256,1024]{1,0:T(8,128)(2,1)} async-done(((bf16[1024,1024]{1,0:T(8,128)(2,1)}), bf16[256,1024]{1,0:T(8,128)(2,1)}) %reduce-scatter.42.cloned.1.call-update) | async-done | bytes 524304 | tf_op jit(solution)/shard_map/reduce_scatter | solution.py:212
  1027.0 34.6 %reduce-scatter.38.cloned.1.call-done = bf16[256,1024]{1,0:T(8,128)(2,1)} async-done(((bf16[1024,1024]{1,0:T(8,128)(2,1)}), bf16[256,1024]{1,0:T(8,128)(2,1)}) %reduce-scatter.38.cloned.1.call-update) | async-done | bytes 524304 | tf_op jit(solution)/shard_map/reduce_scatter | solution.py:268
  1070.9 18.6 %all-gather.47.cloned.1.call-done = bf16[1024,1024]{1,0:T(8,128)(2,1)} async-done(((bf16[256,1024]{1,0:T(8,128)(2,1)}), bf16[1024,1024]{1,0:T(8,128)(2,1)}) %all-gather.47.cloned.1.call-update) | async-done | bytes 2097168 | tf_op jit(solution)/shard_map/all_gather | solution.py:278
  1099.5 70.3 %while.126 = (s32[]{:T(128)}, f32[1024,4,64]{0,2,1:T(8,128)S(1)}, f32[1024,4,64]{0,2,1:T(8,128)}, f32[4,2]{0,1:T(2,128)S(1)}, f32[2,512,4,64]{1,0,3,2:T(2,128)},...) while((s32[]{:T(128)}, f32[1024,4,64]{0,2,1:T(8,128)S(1)}, ...), condition=%wide.region_57.58_spmd.clone, body=%wide.region_53.57_spmd.clone.sunk | while | flops 1379793920 | bytes 148449840 | solution.py:162
  1117.0 10.3 dynamic_update_slice.84
  1151.5 10.3 dynamic_update_slice.84
  1188.0 11.1 collective-permute-done.5
  1199.1 16.1 reduce-scatter.40.cloned.1.call-done
  1220.7 22.6 %all-gather.49.cloned.1.call-done = bf16[1024,1024]{1,0:T(8,128)(2,1)} async-done(((bf16[256,1024]{1,0:T(8,128)(2,1)}), bf16[1024,1024]{1,0:T(8,128)(2,1)}) %all-gather.49.cloned.1.call-update) | async-done | bytes 2097168 | tf_op jit(solution)/shard_map/all_gather | solution.py:170
  1253.4 24.2 %while.123 = (s32[]{:T(128)}, bf16[2,512,4,64]{1,3,2,0:T(8,128)(2,1)S(1)}, f32[2,4,512]{2,1,0:T(4,128)S(1)}, s32[2,512]{1,0:T(2,128)S(1)}, s32[1024]{0:T(1024)S(...) while((s32[]{:T(128)}, ...), condition=%wide.region_69.70_spmd.clone, body=%wide.region_66.69_spmd.clone.sunk | while | flops 577240064 | bytes 31295256 | solution.py:99
  1282.5 31.5 %reduce-scatter.44.cloned.1.call-done = bf16[256,1024]{1,0:T(8,128)(2,1)} async-done(((bf16[1024,1024]{1,0:T(8,128)(2,1)}), bf16[256,1024]{1,0:T(8,128)(2,1)}) %reduce-scatter.44.cloned.1.call-update) | async-done | bytes 524304 | tf_op jit(solution)/shard_map/reduce_scatter | solution.py:193
  1318.7 14.5 collective-permute-done.4
  1340.1 11.6 broadcast_select_fusion
  1351.7 13.3 all-gather.51.cloned.1.call-done
  1365.0 6.2 fusion.183
  1383.6 6.1 fusion.200
  1395.7 13.4 reduce-scatter.46.cloned.1.call-done
  1414.0 8.1 fusion.199
  1426.6 6.2 fusion.189
  1450.3 9.8 add_convert_fusion
  1471.0 65.5 %while.127 = (s32[]{:T(128)}, f32[1024,4,64]{0,2,1:T(8,128)S(1)}, f32[1024,4,64]{0,2,1:T(8,128)S(1)}, f32[4,2]{0,1:T(2,128)S(1)}, f32[2,512,4,64]{1,0,3,2:T(2,12...) while((s32[]{:T(128)}, f32[1024,4,64]{0,2,1:T(8,128)S(1)}, ...), condition=%wide.region_78.79_spmd.clone, body=%wide.region_74.78_spmd.clone.sunk | while | flops 1379793920 | bytes 150547024 | solution.py:162
  1487.4 10.4 dynamic_update_slice.85
  1520.1 10.4 dynamic_update_slice.85
  1571.0 34.2 %reduce-scatter.50.cloned.1.call-done = bf16[256,768]{1,0:T(8,128)(2,1)} async-done(((bf16[1024,768]{1,0:T(8,128)(2,1)}), bf16[256,768]{1,0:T(8,128)(2,1)}) %reduce-scatter.50.cloned.1.call-update) | async-done | bytes 393232 | tf_op jit(solution)/shard_map/reduce_scatter | solution.py:343
  1609.6 29.2 %reduce-scatter.48.cloned.1.call-done = bf16[256,1024]{1,0:T(8,128)(2,1)} async-done(((bf16[1024,1024]{1,0:T(8,128)(2,1)}), bf16[256,1024]{1,0:T(8,128)(2,1)}) %reduce-scatter.48.cloned.1.call-update) | async-done | bytes 524304 | tf_op jit(solution)/shard_map/reduce_scatter | solution.py:313
  1641.4 33.4 %all-reduce = (f32[2,1024]{1,0:T(2,128)S(1)}, f32[16,2]{0,1:T(2,128)S(1)}) all-reduce(f32[2,1024]{1,0:T(2,128)S(1)} %fusion.323, f32[16,2]{0,1:T(2,128)S(1)} %dynamic_update_slice.41), channel_id=1, replica_groups=mesh['section'=2,'dp'=4,'tensor'=4] {'dp','tensor'}, use_global_device_ids=true, to_apply=%region_95.96 | all-reduce | flops 2080 | bytes 16640 | tf_op jit(solution)/shard_map/psum | solution.py:436
  (1250 shorter events, 652.4 us)
Async XLA Ops:
  7.2 51.8 %all-gather.57.cloned.1.call-start = ((), (), s32[]{:S(2)}) async-start(), calls=%async_computation.54 | async-start | bytes 1966080 | tf_op jit(solution)/shard_map/all_gather | solution.py:333
  9.4 72.7 %all-gather.25.cloned.1.call-start = ((), (), s32[]{:S(2)}) async-start(), calls=%async_computation.19 | async-start | bytes 2621440 | tf_op jit(solution)/shard_map/all_gather | solution.py:170
  23.7 367.7 %copy-start.192 = (f32[1,1,1024]{2,1,0:T(1,128)}, f32[1,1,1024]{2,1,0:T(1,128)S(1)}, u32[]{:S(2)}) copy-start(f32[1,1,1024]{2,1,0:T(1,128)S(1)} %get-tuple-element.1707) | copy-start | bytes 12292
  23.7 459.0 %copy-start.135 = (f32[1,1,1024]{2,1,0:T(1,128)}, f32[1,1,1024]{2,1,0:T(1,128)S(1)}, u32[]{:S(2)}) copy-start(f32[1,1,1024]{2,1,0:T(1,128)S(1)} %get-tuple-element.1706) | copy-start | bytes 12292
  24.7 127.6 %reduce-scatter.20.cloned.1.call-start = ((), (), s32[]{:S(2)}) async-start(), calls=%async_computation.20 | async-start | bytes 2621440 | tf_op jit(solution)/shard_map/reduce_scatter | solution.py:193
  50.0 67.8 %copy-start.59 = (bf16[1,256,1024]{2,1,0:T(8,128)(2,1)}, bf16[1,256,1024]{2,1,0:T(8,128)(2,1)S(1)}, u32[]{:S(2)}) copy-start(bf16[1,256,1024]{2,1,0:T(8,128)(2,1)S(1)} %all-gather.2) | copy-start | bytes 1572868
  120.8 91.1 %all-gather.61.cloned.1.call-start = ((), (), s32[]{:S(2)}) async-start(), calls=%async_computation.56 | async-start | bytes 3522560 | tf_op jit(solution)/shard_map/all_gather | solution.py:335
  121.4 113.4 %all-gather.29.cloned.1.call-start = ((), (), s32[]{:S(2)}) async-start(), calls=%async_computation.22 | async-start | bytes 2621440 | tf_op jit(solution)/shard_map/all_gather | solution.py:200
  154.4 88.3 %copy-start.293 = (f32[256]{0:T(256)}, f32[256]{0:T(256)S(1)}, u32[]{:S(2)}) copy-start(f32[256]{0:T(256)S(1)} %get-tuple-element.1500) | copy-start | bytes 3076
  154.4 235.4 %copy-start.23 = (f32[256,1024]{1,0:T(8,128)}, f32[256,1024]{1,0:T(8,128)S(1)}, u32[]{:S(2)}) copy-start(f32[256,1024]{1,0:T(8,128)S(1)} %get-tuple-element.1501) | copy-start | bytes 3145732
  154.4 235.4 %copy-start.274 = (f32[256]{0:T(256)}, f32[256]{0:T(256)S(1)}, u32[]{:S(2)}) copy-start(f32[256]{0:T(256)S(1)} %add_rsqrt_fusion.14) | copy-start | bytes 3076
  155.6 115.8 %all-gather.59.cloned.1.call-start = ((), (), s32[]{:S(2)}) async-start(), calls=%async_computation.55 | async-start | bytes 1761280 | tf_op jit(solution)/shard_map/all_gather | solution.py:336
  156.1 138.3 %all-gather.27.cloned.1.call-start = ((), (), s32[]{:S(2)}) async-start(), calls=%async_computation.21 | async-start | bytes 2621440 | tf_op jit(solution)/shard_map/all_gather | solution.py:254
  156.9 181.4 %reduce-scatter.26.cloned.1.call-start = ((), (), s32[]{:S(2)}) async-start(), calls=%async_computation.26 | async-start | bytes 2621440 | tf_op jit(solution)/shard_map/reduce_scatter | solution.py:212
  306.7 66.1 %reduce-scatter.22.cloned.1.call-start = ((), (), s32[]{:S(2)}) async-start(), calls=%async_computation.23 | async-start | bytes 2621440 | tf_op jit(solution)/shard_map/reduce_scatter | solution.py:268
  314.3 102.9 %all-gather.33.cloned.1.call-start = ((), (), s32[]{:S(2)}) async-start(), calls=%async_computation.27 | async-start | bytes 2621440 | tf_op jit(solution)/shard_map/all_gather | solution.py:170
  375.2 14.5 collective-permute-start.1
  393.4 88.0 %reduce-scatter.28.cloned.1.call-start = ((), (), s32[]{:S(2)}) async-start(), calls=%async_computation.28 | async-start | bytes 2621440 | tf_op jit(solution)/shard_map/reduce_scatter | solution.py:193
  449.9 55.6 %all-gather.31.cloned.1.call-start = ((), (), s32[]{:S(2)}) async-start(), calls=%async_computation.24 | async-start | bytes 2621440 | tf_op jit(solution)/shard_map/all_gather | solution.py:278
  450.5 79.2 %all-gather.37.cloned.1.call-start = ((), (), s32[]{:S(2)}) async-start(), calls=%async_computation.30 | async-start | bytes 2621440 | tf_op jit(solution)/shard_map/all_gather | solution.py:200
  482.7 310.4 %copy-start.10 = (f32[256,1024]{1,0:T(8,128)}, f32[256,1024]{1,0:T(8,128)S(1)}, u32[]{:S(2)}) copy-start(f32[256,1024]{1,0:T(8,128)S(1)} %get-tuple-element.1491) | copy-start | bytes 3145732
  483.9 146.0 %reduce-scatter.34.cloned.1.call-start = ((), (), s32[]{:S(2)}) async-start(), calls=%async_computation.34 | async-start | bytes 2621440 | tf_op jit(solution)/shard_map/reduce_scatter | solution.py:212
  542.0 119.5 %reduce-scatter.24.cloned.1.call-start = ((), (), s32[]{:S(2)}) async-start(), calls=%async_computation.25 | async-start | bytes 2621440 | tf_op jit(solution)/shard_map/reduce_scatter | solution.py:313
  629.9 60.1 %all-gather.41.cloned.1.call-start = ((), (), s32[]{:S(2)}) async-start(), calls=%async_computation.35 | async-start | bytes 2621440 | tf_op jit(solution)/shard_map/all_gather | solution.py:170
  632.1 29.4 %collective-permute-start.3 = (bf16[256,1024]{1,0:T(8,128)(2,1)}, bf16[256,1024]{1,0:T(8,128)(2,1)}, u32[]{:S(2)}, u32[]{:S(2)}) collective-permute-start(bf16[256,1024]{1,0:T(8,128)(2,1)} %fusion.300), channel_id=1, source_target_pairs={{0,16},{1,17},{2,18},{3,19},{4,20},{5,21},{6,22},{7,23},{8,24},{9,... | collective-permute-start | bytes 1572872 | tf_op jit(solution)/shard_map/ppermute | solution.py:15
  667.2 46.8 %all-gather.35.cloned.1.call-start = ((), (), s32[]{:S(2)}) async-start(), calls=%async_computation.29 | async-start | bytes 2621440 | tf_op jit(solution)/shard_map/all_gather | solution.py:254
  667.3 15.9 collective-permute-start
  685.2 73.5 %reduce-scatter.30.cloned.1.call-start = ((), (), s32[]{:S(2)}) async-start(), calls=%async_computation.31 | async-start | bytes 2621440 | tf_op jit(solution)/shard_map/reduce_scatter | solution.py:268
  726.8 66.3 %reduce-scatter.36.cloned.1.call-start = ((), (), s32[]{:S(2)}) async-start(), calls=%async_computation.36 | async-start | bytes 2621440 | tf_op jit(solution)/shard_map/reduce_scatter | solution.py:193
  758.6 60.6 %all-gather.39.cloned.1.call-start = ((), (), s32[]{:S(2)}) async-start(), calls=%async_computation.32 | async-start | bytes 2621440 | tf_op jit(solution)/shard_map/all_gather | solution.py:278
  796.4 146.9 %reduce-scatter.32.cloned.1.call-start = ((), (), s32[]{:S(2)}) async-start(), calls=%async_computation.33 | async-start | bytes 2621440 | tf_op jit(solution)/shard_map/reduce_scatter | solution.py:313
  829.2 73.7 %copy-start.132 = (f32[1024,32]{0,1:T(8,128)S(1)}, f32[1024,32]{0,1:T(8,128)}, u32[]{:S(2)}) copy-start(f32[1024,32]{0,1:T(8,128)} %get-tuple-element.1717) | copy-start | bytes 393220
  829.2 73.7 %copy-start.177 = (f32[1024,32]{0,1:T(8,128)S(1)}, f32[1024,32]{0,1:T(8,128)}, u32[]{:S(2)}) copy-start(f32[1024,32]{0,1:T(8,128)} %get-tuple-element.1718) | copy-start | bytes 393220
  911.8 56.4 %all-gather.45.cloned.1.call-start = ((), (), s32[]{:S(2)}) async-start(), calls=%async_computation.38 | async-start | bytes 2621440 | tf_op jit(solution)/shard_map/all_gather | solution.py:200
  914.1 78.9 %all-gather.43.cloned.1.call-start = ((), (), s32[]{:S(2)}) async-start(), calls=%async_computation.37 | async-start | bytes 2621440 | tf_op jit(solution)/shard_map/all_gather | solution.py:254
  947.1 15.5 collective-permute-start.2
  964.4 62.6 %reduce-scatter.42.cloned.1.call-start = ((), (), s32[]{:S(2)}) async-start(), calls=%async_computation.42 | async-start | bytes 2621440 | tf_op jit(solution)/shard_map/reduce_scatter | solution.py:212
  983.0 78.5 %reduce-scatter.38.cloned.1.call-start = ((), (), s32[]{:S(2)}) async-start(), calls=%async_computation.39 | async-start | bytes 2621440 | tf_op jit(solution)/shard_map/reduce_scatter | solution.py:268
  1000.8 60.8 %copy-start.275 = (f32[256]{0:T(256)S(1)}, f32[256]{0:T(256)}, u32[]{:S(2)}) copy-start(f32[256]{0:T(256)} %copy-done.274) | copy-start | bytes 3076
  1005.5 56.1 %copy-start.24 = (f32[256,1024]{1,0:T(8,128)S(1)}, f32[256,1024]{1,0:T(8,128)}, u32[]{:S(2)}) copy-start(f32[256,1024]{1,0:T(8,128)} %copy-done.23) | copy-start | bytes 3145732
  1005.5 84.1 %all-gather.47.cloned.1.call-start = ((), (), s32[]{:S(2)}) async-start(), calls=%async_computation.40 | async-start | bytes 2621440 | tf_op jit(solution)/shard_map/all_gather | solution.py:278
  1066.8 148.4 %reduce-scatter.40.cloned.1.call-start = ((), (), s32[]{:S(2)}) async-start(), calls=%async_computation.41 | async-start | bytes 2621440 | tf_op jit(solution)/shard_map/reduce_scatter | solution.py:313
  1099.5 73.5 %copy-start.175 = (f32[1024,32]{0,1:T(8,128)S(1)}, f32[1024,32]{0,1:T(8,128)}, u32[]{:S(2)}) copy-start(f32[1024,32]{0,1:T(8,128)} %get-tuple-element.1724) | copy-start | bytes 393220
  1099.5 73.5 %copy-start.176 = (f32[1024,32]{0,1:T(8,128)S(1)}, f32[1024,32]{0,1:T(8,128)}, u32[]{:S(2)}) copy-start(f32[1024,32]{0,1:T(8,128)} %get-tuple-element.1725) | copy-start | bytes 393220
  1183.6 59.8 %all-gather.49.cloned.1.call-start = ((), (), s32[]{:S(2)}) async-start(), calls=%async_computation.43 | async-start | bytes 2621440 | tf_op jit(solution)/shard_map/all_gather | solution.py:170
  1183.7 15.4 collective-permute-start.5
  1220.6 93.4 %reduce-scatter.44.cloned.1.call-start = ((), (), s32[]{:S(2)}) async-start(), calls=%async_computation.44 | async-start | bytes 2621440 | tf_op jit(solution)/shard_map/reduce_scatter | solution.py:193
  1282.5 57.7 %all-gather.53.cloned.1.call-start = ((), (), s32[]{:S(2)}) async-start(), calls=%async_computation.46 | async-start | bytes 2621440 | tf_op jit(solution)/shard_map/all_gather | solution.py:200
  1317.4 47.6 %all-gather.51.cloned.1.call-start = ((), (), s32[]{:S(2)}) async-start(), calls=%async_computation.45 | async-start | bytes 2621440 | tf_op jit(solution)/shard_map/all_gather | solution.py:254
  1317.4 15.8 collective-permute-start.4
  1334.2 74.9 %reduce-scatter.46.cloned.1.call-start = ((), (), s32[]{:S(2)}) async-start(), calls=%async_computation.47 | async-start | bytes 2621440 | tf_op jit(solution)/shard_map/reduce_scatter | solution.py:268
  1377.5 82.7 %all-gather.55.cloned.1.call-start = ((), (), s32[]{:S(2)}) async-start(), calls=%async_computation.48 | async-start | bytes 2621440 | tf_op jit(solution)/shard_map/all_gather | solution.py:278
  1413.8 148.1 %reduce-scatter.56.cloned.1.call-start = ((), (), s32[]{:S(2)}) async-start(), calls=%async_computation.53 | async-start | bytes 1761280 | tf_op jit(solution)/shard_map/reduce_scatter | solution.py:352
  1438.9 124.9 %reduce-scatter.54.cloned.1.call-start = ((), (), s32[]{:S(2)}) async-start(), calls=%async_computation.52 | async-start | bytes 3522560 | tf_op jit(solution)/shard_map/reduce_scatter | solution.py:349
  1460.1 109.2 %reduce-scatter.52.cloned.1.call-start = ((), (), s32[]{:S(2)}) async-start(), calls=%async_computation.51 | async-start | bytes 655360 | tf_op jit(solution)/shard_map/reduce_scatter | solution.py:346
  1547.6 57.5 %reduce-scatter.50.cloned.1.call-start = ((), (), s32[]{:S(2)}) async-start(), calls=%async_computation.50 | async-start | bytes 1966080 | tf_op jit(solution)/shard_map/reduce_scatter | solution.py:343
  1558.5 80.3 %reduce-scatter.48.cloned.1.call-start = ((), (), s32[]{:S(2)}) async-start(), calls=%async_computation.49 | async-start | bytes 2621440 | tf_op jit(solution)/shard_map/reduce_scatter | solution.py:313
  1563.7 75.1 %copy-start.15 = (f32[256,1024]{1,0:T(8,128)S(1)}, f32[256,1024]{1,0:T(8,128)}, u32[]{:S(2)}) copy-start(f32[256,1024]{1,0:T(8,128)} %copy-done.12) | copy-start | bytes 3145732
  1563.7 75.1 %copy-start.18 = (f32[256,1024]{1,0:T(8,128)S(1)}, f32[256,1024]{1,0:T(8,128)}, u32[]{:S(2)}) copy-start(f32[256,1024]{1,0:T(8,128)} %copy-done.16) | copy-start | bytes 3145732
  1563.7 75.1 %copy-start.196 = (f32[1,1,1024]{2,1,0:T(1,128)S(1)}, f32[1,1,1024]{2,1,0:T(1,128)}, u32[]{:S(2)}) copy-start(f32[1,1,1024]{2,1,0:T(1,128)} %copy-done.192) | copy-start | bytes 12292
  1563.7 75.1 %copy-start.281 = (f32[256]{0:T(256)S(1)}, f32[256]{0:T(256)}, u32[]{:S(2)}) copy-start(f32[256]{0:T(256)} %copy-done.279) | copy-start | bytes 3076
  1563.8 75.1 %copy-start.304 = (f32[256]{0:T(256)S(1)}, f32[256]{0:T(256)}, u32[]{:S(2)}) copy-start(f32[256]{0:T(256)} %copy-done.303) | copy-start | bytes 3076
  1607.2 68.8 %copy-start.55 = (f32[256,1024]{1,0:T(8,128)S(1)}, f32[256,1024]{1,0:T(8,128)}, u32[]{:S(2)}) copy-start(f32[256,1024]{1,0:T(8,128)} %get-tuple-element.1483) | copy-start | bytes 3145732
  1607.2 68.8 %copy-start.306 = (f32[256]{0:T(256)S(1)}, f32[256]{0:T(256)}, u32[]{:S(2)}) copy-start(f32[256]{0:T(256)} %get-tuple-element.1708) | copy-start | bytes 3076
  (339 other events, 2173.7 us)
Sparse Core Ops, SparseCore 0:
  10.2 48.8 all-gather.56
  61.2 20.8 all-gather.24
  120.9 31.4 reduce-scatter.19
  153.8 58.0 all-gather.60
  214.0 20.7 all-gather.28
  236.3 35.0 all-gather.58
  273.6 20.8 all-gather.26
  306.9 31.4 reduce-scatter.25
  341.4 31.3 reduce-scatter.21
  393.5 23.5 all-gather.32
  450.0 31.4 reduce-scatter.27
  482.9 22.5 all-gather.30
  507.0 22.5 all-gather.36
  542.1 31.4 reduce-scatter.33
  630.0 31.4 reduce-scatter.23
  667.3 22.5 all-gather.40
  691.4 22.5 all-gather.34
  726.9 31.4 reduce-scatter.29
  761.6 31.4 reduce-scatter.35
  796.6 22.5 all-gather.38
  911.9 31.4 reduce-scatter.31
  945.6 22.5 all-gather.44
  970.4 22.5 all-gather.42
  995.6 31.3 reduce-scatter.41
  1030.1 31.4 reduce-scatter.37
  1066.9 22.5 all-gather.46
  1183.7 31.4 reduce-scatter.39
  1220.8 22.5 all-gather.48
  1282.6 31.4 reduce-scatter.43
  1317.5 22.5 all-gather.52
  1342.4 22.5 all-gather.50
  1377.6 31.4 reduce-scatter.45
  1413.9 22.5 all-gather.54
  1439.4 32.7 reduce-scatter.55
  1474.5 53.9 reduce-scatter.53
  1547.7 21.5 reduce-scatter.51
  1571.6 33.5 reduce-scatter.49
  1608.4 30.3 reduce-scatter.47
where the time goes:
time: 1700 us; the launch traced here: 1690 us
  waiting for transfers between devices  793 us (47%)
  matrix products  397 us (23%)
  local copies, waits for them, and re-layouts  198 us (12%)
  other arithmetic  189 us (11%)
  blocking collectives  68.2 us (4%)
  starting transfers between devices  19.6 us (1%)
  between operations  18.3 us (1%)
    reduce_scatter x4, waiting for transfers between devices, forward(): lax.psum_scatter(jnp.dot(attended, w_out, preferred_element_type=jnp.floa...  125 us
    reduce_scatter x4, waiting for transfers between devices, backward(): lax.psum_scatter(jnp.dot(grad_proj, flat_qkv.T, preferred_element_type=jn...  99.7 us
    dynamic_update_slice x16, local copies, waits for them, and re-layouts, attend(): results, log_sums = lax.map(attend_block, block_parts)  90.3 us
    reduce_scatter x4, waiting for transfers between devices, backward(): lax.psum_scatter(jnp.dot(grad_gu, flat_gu.T, preferred_element_type=jnp.f...  82.5 us
    all_gather x4, waiting for transfers between devices, forward(): lax.all_gather((normed_a * gains_f[0]).astype(jnp.bfloat16), 'tensor', ax...  73.8 us
    dot_general x16, matrix products, masked_scores(): jnp.einsum('qhd,khd->hqk', q_block, k, preferred_element_type=jnp.float32)  65.6 us
    ppermute x6, waiting for transfers between devices, from_behind(): lax.ppermute(value, axis, [(source, source + steps) for source in range(i...  65.5 us
    all_gather x4, waiting for transfers between devices, backward(): lax.all_gather(grad_h.astype(jnp.bfloat16), 'tensor', axis=0, tiled=True)  62.6 us
  transfers between devices with their start and end apart: 44, of which 38 were waited for; matrix products, arithmetic and copies ran while one was open for 22% of the time, Pallas kernels for 0%

commit v1 on v0

v1 whole, which is shorter than its diff:
```python
import functools
import math

import jax
import jax.numpy as jnp
from jax import lax
from jax.experimental import pallas as pl
from jax.experimental.pallas import tpu as pltpu
from jax.sharding import PartitionSpec as P

EPS = 1e-05
BIG = 8192.0
LOG2E = 1.4426950408889634
BF = jnp.bfloat16
F32 = jnp.float32
HD = 64
ZB = 256
VMEM_MB = 56
N_VAR = 4
L_SEG = 8
L_PAD = 24
L_LSE = 25


def dot(a, b):
    return lax.dot_general(a, b, (((1,), (0,)), ((), ())), preferred_element_type=F32)


def dot_nt(a, b):
    return lax.dot_general(a, b, (((1,), (1,)), ((), ())), preferred_element_type=F32)


def dot_tn(a, b):
    return lax.dot_general(a, b, (((0,), (0,)), ((), ())), preferred_element_type=F32)


def params(mb=VMEM_MB):
    return pltpu.CompilerParams(
        dimension_semantics=("arbitrary",), vmem_limit_bytes=mb * 1024 * 1024
    )


def cost(flops, nbytes, trans=0):
    return pl.CostEstimate(flops=int(flops), bytes_accessed=int(nbytes), transcendentals=int(trans))


def sds(shape, dtype):
    return jax.ShapeDtypeStruct(shape, dtype)


def whole(shape):
    zeros = (0,) * len(shape)
    return pl.BlockSpec(shape, lambda *_: zeros)


def head_sum(u):
    hi = u.astype(BF)
    lo = (u - hi.astype(F32)).astype(BF)
    row = lax.broadcasted_iota(jnp.int32, (128, 128), 0) // HD
    col = lax.broadcasted_iota(jnp.int32, (128, 128), 1) // HD
    same = jnp.where(row == col, 1.0, 0.0).astype(BF)
    return dot(hi, same) + dot(lo, same)


def half_swap(u):
    lane = lax.broadcasted_iota(jnp.int32, u.shape, 1) % HD
    return jnp.where(lane < HD // 2, pltpu.roll(u, 128 - HD // 2, 1), pltpu.roll(u, HD // 2, 1))


def row_rms(x):
    return lax.rsqrt(jnp.mean(x * x, axis=-1, keepdims=True) + EPS)


def qkv_kernel(save, x_ref, gain_ref, w_ref, cos_ref, sin_ref, *refs):
    if save:
        n_ref, q_ref, k_ref, v_ref, q0_ref, k0_ref, n_scr = refs
    else:
        q_ref, k_ref, v_ref, n_scr = refs

    @pl.when(pl.program_id(0) == 0)
    def _():
        x = x_ref[...]
        n = (x * row_rms(x) * gain_ref[...]).astype(BF)
        n_scr[...] = n
        if save:
            n_ref[...] = n

    width = q_ref.shape[1]
    blocks = w_ref.shape[0]
    proj = dot_nt(n_scr[:, :ZB], w_ref[0, 0])
    for z in range(1, blocks):
        proj = proj + dot_nt(n_scr[:, z * ZB : (z + 1) * ZB], w_ref[z, 0])
    v_ref[...] = proj[:, 2 * width :].astype(BF)
    cos, sin = cos_ref[...], sin_ref[...]
    for which, out in ((0, q_ref), (1, k_ref)):
        if save:
            kept = q0_ref if which == 0 else k0_ref
            kept[...] = proj[:, which * width : (which + 1) * width].astype(BF)
        for pair in range(width // 128):
            u = proj[:, which * width + pair * 128 : which * width + (pair + 1) * 128]
            un = u * lax.rsqrt(head_sum(u * u) * (1.0 / HD) + EPS)
            out[:, pair * 128 : (pair + 1) * 128] = (un * cos + half_swap(un) * sin).astype(BF)


def qkv_call(save, x, gain, w, cos, sin):
    rows, model = x.shape
    zb, tn, feats, _ = w.shape
    width = feats // 3
    total = tn * width
    col = pl.BlockSpec((rows, width), lambda t: (0, t))
    outs = [sds((rows, total), BF)] * 3
    specs = [col] * 3
    if save:
        outs = [sds((rows, model), BF)] + outs + [sds((rows, total), BF)] * 2
        specs = [whole((rows, model))] + specs + [col] * 2
    return pl.pallas_call(
        functools.partial(qkv_kernel, save),
        grid=(tn,),
        in_specs=[
            whole((rows, model)),
            whole((1, model)),
            pl.BlockSpec((zb, 1, feats, ZB), lambda t: (0, t, 0, 0)),
            whole((rows, 128)),
            whole((rows, 128)),
        ],
        out_specs=specs,
        out_shape=outs,
        scratch_shapes=[pltpu.VMEM((rows, model), BF)],
        compiler_params=params(),
        cost_estimate=cost(2 * rows * model * 3 * total, 2 * w.size + 16 * x.size),
    )(x, gain, w, cos, sin)


def pick(first, h, a, b):
    return jnp.where(first, a, b) if h == 0 else jnp.where(first, b, a)


def attend_kernel(
    scale, q_ref, ko_ref, kx_ref, vo_ref, vx_ref, aq_ref, ak_ref, hs_ref, add_ref, o_ref, l_ref
):
    rows = q_ref.shape[0]
    kb = 256
    first = lax.broadcasted_iota(jnp.int32, (1, 128), 1) < HD
    q = q_ref[...].astype(F32)
    base = aq_ref[...]
    raws = []
    for h in range(2):
        qh = pick(first, h, q, base * hs_ref[0, h : h + 1, :]).astype(BF)
        parts = [None] * (rows // kb)
        for half, (k_ref, v_ref) in enumerate(((ko_ref, vo_ref), (kx_ref, vx_ref))):
            for block in range(rows // kb):
                at = slice(block * kb, (block + 1) * kb)
                kk = slice(half * rows + block * kb, half * rows + (block + 1) * kb)
                kh = pick(first, h, k_ref[at, :].astype(F32), ak_ref[kk, :].astype(F32)).astype(BF)
                vh = pick(first, h, v_ref[at, :].astype(F32), 1.0).astype(BF)
                for qb in range(rows // kb):
                    qs = slice(qb * kb, (qb + 1) * kb)
                    s = dot_nt(qh[qs], kh)
                    if half == 0:
                        s = s + add_ref[qs, at]
                    p = jnp.exp2(s * scale).astype(BF)
                    r = dot(p, vh)
                    parts[qb] = r if parts[qb] is None else parts[qb] + r
        raws.append(jnp.concatenate(parts, axis=0))
    sums = jnp.where(first, raws[1], raws[0])
    l_ref[...] = sums
    o_ref[...] = (jnp.where(first, raws[0], raws[1]) / pltpu.roll(sums, HD, 1)).astype(BF)


def attend_call(scale, q, k_own, k_oth, v_own, v_oth, aug_q, aug_k, head_scale, add_own):
    rows, total = q.shape
    pairs = total // 128
    col = pl.BlockSpec((rows, 128), lambda p: (0, p))
    return pl.pallas_call(
        functools.partial(attend_kernel, scale),
        grid=(pairs,),
        in_specs=[
            col,
            col,
            col,
            col,
            col,
            whole(aug_q.shape),
            whole(aug_k.shape),
            pl.BlockSpec((1, 2, 128), lambda p: (p, 0, 0)),
            whole(add_own.shape),
        ],
        out_specs=[col, col],
        out_shape=[sds((rows, total), BF), sds((rows, total), F32)],
        compiler_params=params(),
        cost_estimate=cost(
            4 * 2 * rows * rows * 2 * total, 20 * rows * total, rows * rows * 2 * pairs * 2
        ),
    )(q, k_own, k_oth, v_own, v_oth, aug_q, aug_k, head_scale, add_own)


def ffn_kernel(save, x_ref, o_ref, wo_ref, gain_ref, wgu_ref, wd_ref, *refs):
    if save:
        y_ref, h_ref, n_ref, g_ref, u_ref, z_ref, n_scr, acc = refs
    else:
        y_ref, n_scr, acc = refs
    blocks = wgu_ref.shape[0]
    hidden = wd_ref.shape[2]
    step = pl.program_id(0)

    @pl.when(step == 0)
    def _():
        tn, width = wo_ref.shape[1], wo_ref.shape[2]
        total = jnp.zeros((x_ref.shape[0], 1), F32)
        for z in range(blocks):
            at = slice(z * ZB, (z + 1) * ZB)
            h = x_ref[:, at]
            for t in range(tn):
                h = h + dot(o_ref[:, t * width : (t + 1) * width], wo_ref[z, t])
            acc[:, at] = h
            total = total + jnp.sum(h * h, axis=-1, keepdims=True)
        h = acc[...]
        n = (h * lax.rsqrt(total * (1.0 / h.shape[1]) + EPS) * gain_ref[...]).astype(BF)
        n_scr[...] = n
        if save:
            h_ref[...] = h
            n_ref[...] = n

    gate = dot_nt(n_scr[:, :ZB], wgu_ref[0, 0, :hidden])
    up = dot_nt(n_scr[:, :ZB], wgu_ref[0, 0, hidden:])
    for z in range(1, blocks):
        n = n_scr[:, z * ZB : (z + 1) * ZB]
        gate = gate + dot_nt(n, wgu_ref[z, 0, :hidden])
        up = up + dot_nt(n, wgu_ref[z, 0, hidden:])
    hid = (gate / (1.0 + jnp.exp(-gate)) * up).astype(BF)
    if save:
        g_ref[0] = gate.astype(BF)
        u_ref[0] = up.astype(BF)
        z_ref[0] = hid
    for z in range(blocks):
        at = slice(z * ZB, (z + 1) * ZB)
        acc[:, at] = acc[:, at] + dot(hid, wd_ref[z, 0])

    @pl.when(step == pl.num_programs(0) - 1)
    def _():
        y_ref[...] = acc[...].astype(y_ref.dtype)


def ffn_call(save, x, o, wo, gain, wgu, wd):
    rows, model = x.shape
    zb, tn, hidden, _ = wd.shape
    big = whole((rows, model))
    outs = [sds((rows, model), F32 if save else BF)]
    specs = [big]
    if save:
        part = pl.BlockSpec((1, rows, hidden), lambda t: (t, 0, 0))
        outs += [sds((rows, model), F32), sds((rows, model), BF)] + [
            sds((tn, rows, hidden), BF)
        ] * 3
        specs += [big, big, part, part, part]
    return pl.pallas_call(
        functools.partial(ffn_kernel, save),
        grid=(tn,),
        in_specs=[
            big,
            whole(o.shape),
            whole(wo.shape),
            whole((1, model)),
            pl.BlockSpec((zb, 1, 2 * hidden, ZB), lambda t: (0, t, 0, 0)),
            pl.BlockSpec((zb, 1, hidden, ZB), lambda t: (0, t, 0, 0)),
        ],
        out_specs=specs,
        out_shape=outs,
        scratch_shapes=[pltpu.VMEM((rows, model), BF), pltpu.VMEM((rows, model), F32)],
        compiler_params=params(),
        cost_estimate=cost(
            2 * rows * model * (3 * tn * hidden + model), 6 * wd.size + 2 * wo.size + 20 * x.size
        ),
    )(x, o, wo, gain, wgu, wd)


def ffn_back_kernel(
    dy_ref, h_ref, g_ref, u_ref, wgu_ref, wd_ref, wo_ref, gain_ref,
    dh_ref, da_ref, do_ref, dg_ref, gg_ref, df_scr, acc,
):
    blocks = wgu_ref.shape[0]
    hidden = wd_ref.shape[2]
    step = pl.program_id(0)

    @pl.when(step == 0)
    def _():
        df_scr[...] = dy_ref[...].astype(BF)
        acc[...] = jnp.zeros_like(acc)

    dz = dot_nt(df_scr[:, :ZB], wd_ref[0, 0])
    for z in range(1, blocks):
        dz = dz + dot_nt(df_scr[:, z * ZB : (z + 1) * ZB], wd_ref[z, 0])
    gate = g_ref[0].astype(F32)
    up = u_ref[0].astype(F32)
    s = 1.0 / (1.0 + jnp.exp(-gate))
    dgate = (dz * up * s * (1.0 + gate * (1.0 - s))).astype(BF)
    dup = (dz * gate * s).astype(BF)
    dg_ref[0, 0] = dgate
    dg_ref[0, 1] = dup
    for z in range(blocks):
        at = slice(z * ZB, (z + 1) * ZB)
        acc[:, at] = acc[:, at] + (
            dot(dgate, wgu_ref[z, 0, :hidden]) + dot(dup, wgu_ref[z, 0, hidden:])
        )

    @pl.when(step == pl.num_programs(0) - 1)
    def _():
        h = h_ref[...]
        r = row_rms(h)
        hn = h * r
        dn = acc[...]
        gg_ref[...] = jnp.sum(dn * hn, axis=0, keepdims=True)
        dhat = dn * gain_ref[...]
        dh = dy_ref[...] + r * (dhat - hn * jnp.mean(dhat * hn, axis=-1, keepdims=True))
        dh_ref[...] = dh
        da = dh.astype(BF)
        da_ref[...] = da
        tn, width = wo_ref.shape[1], wo_ref.shape[2]
        for t in range(tn):
            part = dot_nt(da[:, :ZB], wo_ref[0, t])
            for z in range(1, blocks):
                part = part + dot_nt(da[:, z * ZB : (z + 1) * ZB], wo_ref[z, t])
            do_ref[:, t * width : (t + 1) * width] = part.astype(BF)


def ffn_back_call(dy, h, g, u, wgu, wd, wo, gain):
    rows, model = dy.shape
    zb, tn, hidden, _ = wd.shape
    big = whole((rows, model))
    part = pl.BlockSpec((1, rows, hidden), lambda t: (t, 0, 0))
    return pl.pallas_call(
        ffn_back_kernel,
        grid=(tn,),
        in_specs=[
            big,
            big,
            part,
            part,
            pl.BlockSpec((zb, 1, 2 * hidden, ZB), lambda t: (0, t, 0, 0)),
            pl.BlockSpec((zb, 1, hidden, ZB), lambda t: (0, t, 0, 0)),
            whole(wo.shape),
            whole((1, model)),
        ],
        out_specs=[
            big,
            big,
            big,
            pl.BlockSpec((1, 2, rows, hidden), lambda t: (t, 0, 0, 0)),
            whole((1, model)),
        ],
        out_shape=[
            sds((rows, model), F32),
            sds((rows, model), BF),
            sds((rows, model), BF),
            sds((tn, 2, rows, hidden), BF),
            sds((1, model), F32),
        ],
        scratch_shapes=[pltpu.VMEM((rows, model), BF), pltpu.VMEM((rows, model), F32)],
        compiler_params=params(),
        cost_estimate=cost(
            2 * rows * model * (3 * tn * hidden + model), 6 * wd.size + 2 * wo.size + 20 * dy.size
        ),
    )(dy, h, g, u, wgu, wd, wo, gain)


def split3(value):
    hi = value.astype(BF).astype(F32)
    mid = (value - hi).astype(BF).astype(F32)
    return hi, mid, value - hi - mid


def attend_back_kernel(
    scale, q_ref, ko_ref, kx_ref, vo_ref, vx_ref, do_ref, o_ref, l_ref, aq_ref, ak_ref, hs_ref,
    add_ref, var_ref, dq_ref, dko_ref, dkx_ref, dvo_ref, dvx_ref, bias_ref,
):
    rows = q_ref.shape[0]
    kb = 256
    first = lax.broadcasted_iota(jnp.int32, (1, 128), 1) < HD
    lane = lax.broadcasted_iota(jnp.int32, (1, 128), 1) % HD
    q = q_ref[...].astype(F32)
    do = do_ref[...].astype(F32)
    inner = do * o_ref[...].astype(F32)
    base = aq_ref[...]
    hi, mid, low = split3(jnp.log2(l_ref[...]) * (-1.0 / scale))
    lse = jnp.where(lane == L_LSE, hi, 0.0)
    lse = jnp.where(lane == L_LSE + 1, mid, lse)
    lse = jnp.where(lane == L_LSE + 2, low, lse)
    dq_t = []
    dk = [[], []]
    dv = [[], []]
    for h in range(2):
        qh = pick(first, h, q, base * hs_ref[0, h : h + 1, :] + lse).astype(BF)
        d = jnp.sum(pick(first, h, inner, 0.0), axis=-1, keepdims=True)
        dhi, dmid, dlow = split3(-d)
        d_aug = jnp.where(lane == 0, dhi, 0.0)
        d_aug = jnp.where(lane == 1, dmid, d_aug)
        d_aug = jnp.where(lane == 2, dlow, d_aug)
        doh = pick(first, h, do, d_aug).astype(BF)
        total = None
        for half, (k_ref, v_ref) in enumerate(((ko_ref, vo_ref), (kx_ref, vx_ref))):
            for block in range(rows // kb):
                at = slice(block * kb, (block + 1) * kb)
                kk = slice(half * rows + block * kb, half * rows + (block + 1) * kb)
                kh = pick(first, h, k_ref[at, :].astype(F32), ak_ref[kk, :].astype(F32)).astype(BF)
                vh = pick(first, h, v_ref[at, :].astype(F32), 1.0).astype(BF)
                s = dot_nt(kh, qh)
                if half == 0:
                    s = s + add_ref[at, :]
                p = jnp.exp2(s * scale)
                ds = (p * dot_nt(vh, doh)).astype(BF)
                dv[h].append(dot(p.astype(BF), doh))
                dk[h].append(dot(ds, qh))
                part = dot_tn(kh, ds)
                total = part if total is None else total + part
        dq_t.append(total)
    scale_back = 1.0 / math.sqrt(HD)
    count = rows // kb
    for half, (dk_ref, dv_ref) in enumerate(((dko_ref, dvo_ref), (dkx_ref, dvx_ref))):
        for block in range(count):
            at = slice(block * kb, (block + 1) * kb)
            i = half * count + block
            dk_ref[at, :] = (jnp.where(first, dk[0][i], dk[1][i]) * scale_back).astype(dk_ref.dtype)
            dv_ref[at, :] = jnp.where(first, dv[0][i], dv[1][i]).astype(dv_ref.dtype)
    joined = jnp.concatenate([dq_t[0][:HD], dq_t[1][HD:]], axis=0)
    dq_ref[...] = joined.T * scale_back
    mine = var_ref[...]
    for h in range(2):
        begin = HD if h == 0 else 0
        r = dq_t[h][begin : begin + 8]
        same = jnp.sum(r * mine, axis=0, keepdims=True)
        every = jnp.sum(r[:N_VAR], axis=0, keepdims=True)
        bias_ref[0, 2 * h : 2 * h + 1, :] = same
        bias_ref[0, 2 * h + 1 : 2 * h + 2, :] = every - same


def attend_back_call(
    scale, q, k_own, k_oth, v_own, v_oth, do, o, sums, aug_q, aug_k, head_scale, add_own, var_q
):
    rows, total = q.shape
    pairs = total // 128
    col = pl.BlockSpec((rows, 128), lambda p: (0, p))
    return pl.pallas_call(
        functools.partial(attend_back_kernel, scale),
        grid=(pairs,),
        in_specs=[col] * 8
        + [
            whole(aug_q.shape),
            whole(aug_k.shape),
            pl.BlockSpec((1, 2, 128), lambda p: (p, 0, 0)),
            whole(add_own.shape),
            whole(var_q.shape),
        ],
        out_specs=[col] * 5 + [pl.BlockSpec((1, 4, rows), lambda p: (p, 0, 0))],
        out_shape=[
            sds((rows, total), F32),
            sds((rows, total), F32),
            sds((rows, total), BF),
            sds((rows, total), F32),
            sds((rows, total), BF),
            sds((pairs, 4, rows), F32),
        ],
        compiler_params=params(),
        cost_estimate=cost(
            10 * 2 * rows * rows * 2 * total, 40 * rows * total, rows * rows * 2 * pairs * 2
        ),
    )(q, k_own, k_oth, v_own, v_oth, do, o, sums, aug_q, aug_k, head_scale, add_own, var_q)


def qkv_back_kernel(
    dq_ref, dk_ref, dkr_ref, dv_ref, dvr_ref, q0_ref, k0_ref, cos_ref, sin_ref, w_ref, x_ref,
    dh_ref, gain_ref, dp_ref, dx_ref, gg_ref, acc,
):
    blocks = w_ref.shape[0]
    width = dq_ref.shape[1]
    step = pl.program_id(0)

    @pl.when(step == 0)
    def _():
        acc[...] = jnp.zeros_like(acc)

    cos, sin = cos_ref[...], sin_ref[...]
    for pair in range(width // 128):
        at = slice(pair * 128, (pair + 1) * 128)
        for which in range(2):
            grad = dq_ref[:, at] if which == 0 else dk_ref[:, at] + dkr_ref[:, at].astype(F32)
            u = (q0_ref if which == 0 else k0_ref)[:, at].astype(F32)
            r = lax.rsqrt(head_sum(u * u) * (1.0 / HD) + EPS)
            un = u * r
            grad = grad * cos - half_swap(grad) * sin
            out = r * (grad - un * (head_sum(grad * un) * (1.0 / HD)))
            dp_ref[0, :, which * width + pair * 128 : which * width + (pair + 1) * 128] = out.astype(
                BF
            )
    dp_ref[0, :, 2 * width :] = (dv_ref[...] + dvr_ref[...].astype(F32)).astype(BF)
    dp = dp_ref[0]
    for z in range(blocks):
        at = slice(z * ZB, (z + 1) * ZB)
        acc[:, at] = acc[:, at] + dot(dp, w_ref[z, 0])

    @pl.when(step == pl.num_programs(0) - 1)
    def _():
        x = x_ref[...]
        r = row_rms(x)
        xn = x * r
        dn = acc[...]
        gg_ref[...] = jnp.sum(dn * xn, axis=0, keepdims=True)
        dhat = dn * gain_ref[...]
        dx_ref[...] = dh_ref[...] + r * (dhat - xn * jnp.mean(dhat * xn, axis=-1, keepdims=True))


def qkv_back_call(dq, dk, dkr, dv, dvr, q0, k0, cos, sin, w, x, dh, gain):
    rows, model = x.shape
    zb, tn, feats, _ = w.shape
    width = feats // 3
    big = whole((rows, model))
    col = pl.BlockSpec((rows, width), lambda t: (0, t))
    return pl.pallas_call(
        qkv_back_kernel,
        grid=(tn,),
        in_specs=[col] * 7
        + [
            whole((rows, 128)),
            whole((rows, 128)),
            pl.BlockSpec((zb, 1, feats, ZB), lambda t: (0, t, 0, 0)),
            big,
            big,
            whole((1, model)),
        ],
        out_specs=[pl.BlockSpec((1, rows, feats), lambda t: (t, 0, 0)), big, whole((1, model))],
        out_shape=[sds((tn, rows, feats), BF), sds((rows, model), F32), sds((1, model), F32)],
        scratch_shapes=[pltpu.VMEM((rows, model), F32)],
        compiler_params=params(),
        cost_estimate=cost(2 * rows * model * tn * feats, 2 * w.size + 40 * x.size),
    )(dq, dk, dkr, dv, dvr, q0, k0, cos, sin, w, x, dh, gain)


def wgrad_kernel(ao_ref, bo_ref, ax_ref, bx_ref, g_ref):
    a = ao_ref[0]
    ax = ax_ref[0]
    for z in range(g_ref.shape[1]):
        at = slice(z * ZB, (z + 1) * ZB)
        g_ref[0, z] = (dot_tn(a, bo_ref[:, at]) + dot_tn(ax, bx_ref[:, at])).astype(BF)


def wgrad_call(a_own, b_own, a_oth, b_oth):
    n, rows, feats = a_own.shape
    model = b_own.shape[1]
    part = pl.BlockSpec((1, rows, feats), lambda i: (i, 0, 0))
    big = whole((rows, model))
    return pl.pallas_call(
        wgrad_kernel,
        grid=(n,),
        in_specs=[part, big, part, big],
        out_specs=pl.BlockSpec((1, model // ZB, feats, ZB), lambda i: (i, 0, 0, 0)),
        out_shape=sds((n, model // ZB, feats, ZB), BF),
        compiler_params=params(),
        cost_estimate=cost(4 * n * rows * feats * model, 2 * n * feats * model),
    )(a_own, b_own, a_oth, b_oth)


def core_swap(value):
    n = lax.axis_size("tensor")
    return lax.ppermute(value, "tensor", [(i, i ^ 1) for i in range(n)])


def y_swap(value):
    n = lax.axis_size("tensor")
    return lax.ppermute(value, "tensor", [(i, i ^ 2) for i in range(n)])


def ring(value):
    n = lax.axis_size("dp")
    return lax.ppermute(value, "dp", [(i, (i + 1) % n) for i in range(n)])


def gather_weight(piece):
    n = lax.axis_size("dp")
    tn = lax.axis_size("tensor")
    zi = lax.axis_index("dp")
    ti = lax.axis_index("tensor")
    feats, cols = piece.shape
    if n > 8:
        every = lax.all_gather(lax.all_gather(piece, "dp"), "tensor")
        every = every.transpose(0, 2, 1, 3).reshape(tn, feats, n * cols // ZB, ZB)
        return every.transpose(2, 0, 1, 3)
    out = jnp.zeros((n, tn, feats, cols), piece.dtype)
    held = piece
    for step in range(n):
        if step:
            held = ring(held)
        across = y_swap(held)
        both = core_swap(jnp.stack([held, across]))
        at = lax.rem(zi - step + n, n)
        for t, part in ((ti, held), (ti ^ 2, across), (ti ^ 1, both[0]), (ti ^ 3, both[1])):
            out = lax.dynamic_update_slice(out, part[None, None], (at, t, 0, 0))
    return out


def scatter_grad(grad):
    n = lax.axis_size("dp")
    zi = lax.axis_index("dp")
    yi = lax.axis_index("tensor") // 2
    mine = lax.dynamic_index_in_dim(grad, yi, 0, keepdims=False)
    other = lax.dynamic_index_in_dim(grad, 1 - yi, 0, keepdims=False)
    got = y_swap(other)
    total = mine.astype(F32) + got.astype(F32)
    blocks, feats, cols = total.shape
    if n > 8:
        flat = total.transpose(1, 0, 2).reshape(feats, blocks * cols).astype(BF)
        return lax.psum_scatter(flat, "dp", scatter_dimension=1, tiled=True).astype(F32)

    def chunk(index):
        return lax.dynamic_index_in_dim(total, lax.rem(index + 2 * n, n), 0, keepdims=False)

    running = chunk(zi - 1)
    for step in range(2, n + 1):
        running = ring(running.astype(BF)).astype(F32) + chunk(zi - step)
    return running


def small_sum(value):
    n = lax.axis_size("dp")
    value = value + core_swap(value)
    value = value + y_swap(value)
    if n & (n - 1):
        return lax.psum(value, "dp")
    bit = 1
    while bit < n:
        value = value + lax.ppermute(value, "dp", [(i, i ^ bit) for i in range(n)])
        bit *= 2
    return value


def own_rows(row, core):
    quarters = row.reshape(2, 2, row.shape[0] // 4)
    own = lax.dynamic_index_in_dim(quarters, core, 1, keepdims=False).reshape(-1)
    oth = lax.dynamic_index_in_dim(quarters, 1 - core, 1, keepdims=False).reshape(-1)
    return own, oth


def tables(segment, variate, time_row, pad, var_bias, core):
    seg_own, seg_oth = own_rows(segment, core)
    var_own, var_oth = own_rows(variate, core)
    pad_own, pad_oth = own_rows(pad, core)
    time_own, _ = own_rows(time_row, core)
    rows = seg_own.shape[0]
    half = HD // 2
    frequency = jnp.exp(-jnp.log(10000.0) * jnp.arange(half, dtype=F32) / half)
    phases = time_own.astype(F32)[:, None] * frequency[None, :]
    cos, sin = jnp.cos(phases), jnp.sin(phases)
    cos = jnp.concatenate([cos] * 4, axis=1)
    sin = jnp.concatenate([-sin, sin, -sin, sin], axis=1)
    lane = (jnp.arange(128, dtype=jnp.int32) % HD)[None, :]
    seg_k = jnp.concatenate([seg_own, seg_oth])[:, None]
    var_k = jnp.concatenate([var_own, var_oth])[:, None]
    pad_k = jnp.concatenate([jnp.ones_like(pad_own), pad_oth])[:, None]
    is_var = lane < 2 * N_VAR
    is_seg = (lane >= L_SEG) & (lane < L_PAD)
    is_lse = (lane >= L_LSE) & (lane < L_LSE + 3)
    aug_k = jnp.where(
        is_var,
        jnp.where(var_k == lane % N_VAR, 1.0, 0.0),
        jnp.where(
            is_seg,
            jnp.where(seg_k == lane - L_SEG, 0.0, -BIG),
            jnp.where(
                lane == L_PAD, jnp.where(pad_k == 1, 0.0, -BIG), jnp.where(is_lse, 1.0, 0.0)
            ),
        ),
    ).astype(BF)
    aug_q = jnp.where(
        is_var,
        jnp.where(var_own[:, None] == lane % N_VAR, 1.0, 0.0),
        jnp.where(
            is_seg,
            jnp.where(seg_own[:, None] == lane - L_SEG, 1.0, 0.0),
            jnp.where(lane == L_PAD, 1.0, 0.0),
        ),
    ).astype(F32)
    delta = (var_bias[:, 0] - var_bias[:, 1]) * math.sqrt(HD)
    hi = delta.astype(BF).astype(F32)
    low = (delta - hi).astype(BF).astype(F32)
    head_scale = jnp.where(
        lane < N_VAR, hi[:, None], jnp.where(lane < 2 * N_VAR, low[:, None], 1.0)
    ).reshape(-1, 2, 128)
    place = jnp.arange(rows, dtype=jnp.int32)
    neg = jnp.where(pad_own == 1, 0.0, -BIG).astype(F32)
    eye = place[:, None] == place[None, :]
    add_q = jnp.where(eye, 0.0, neg[None, :])
    add_k = jnp.where(eye, 0.0, neg[:, None])
    var_q = jnp.where(
        var_own[None, :] == jnp.arange(8, dtype=jnp.int32)[:, None], 1.0, 0.0
    ).astype(F32)
    return cos, sin, aug_q, aug_k, head_scale, add_q, add_k, var_q


def forward(save, x, weights, gains, tab, scale):
    w_qkv, w_out, w_gu, w_down = weights
    cos, sin, aug_q, aug_k, head_scale, add_q, _, _ = tab
    res = qkv_call(save, x, gains[0], w_qkv, cos, sin)
    if save:
        n1, q, k, v, q0, k0 = res
    else:
        q, k, v = res
    k_oth, v_oth = core_swap(k), core_swap(v)
    o, sums = attend_call(scale, q, k, k_oth, v, v_oth, aug_q, aug_k, head_scale, add_q)
    res = ffn_call(save, x, o, w_out, gains[1], w_gu, w_down)
    if not save:
        return res[0]
    y, h, n2, g, u, z = res
    return y, (x, n1, q, k, v, k_oth, v_oth, q0, k0, o, sums, h, n2, g, u, z)


def backward(dy, state, weights, gains, tab, scale):
    x, n1, q, k, v, k_oth, v_oth, q0, k0, o, sums, h, n2, g, u, z = state
    w_qkv, w_out, w_gu, w_down = weights
    cos, sin, aug_q, aug_k, head_scale, _, add_k, var_q = tab
    dh, da, do, dgu, gain_f = ffn_back_call(dy, h, g, u, w_gu, w_down, w_out, gains[1])
    dq, dk, dk_send, dv, dv_send, bias = attend_back_call(
        scale, q, k, k_oth, v, v_oth, do, o, sums, aug_q, aug_k, head_scale, add_k, var_q
    )
    dk_got, dv_got = core_swap(dk_send), core_swap(dv_send)
    dp, dx, gain_a = qkv_back_call(
        dq, dk, dk_got, dv, dv_got, q0, k0, cos, sin, w_qkv, x, dh, gains[0]
    )
    return dx, da, dgu, dp, jnp.concatenate([gain_a, gain_f], axis=0), bias


def per_device(
    boundary, w_qkv, w_out, w_gate_up, w_down, norm_gains, variate_bias,
    segment_ids, variate_ids, time_ids, padding_mask,
):
    ti = lax.axis_index("tensor")
    tn = lax.axis_size("tensor")
    yi, core = ti // 2, ti % 2
    zi, n = lax.axis_index("dp"), lax.axis_size("dp")
    is_first = lax.axis_index("section") == 0
    local = boundary[0]
    rows, model = local.shape[1:]
    scale = LOG2E / math.sqrt(HD)

    own = lax.dynamic_index_in_dim(local, yi, 0, keepdims=False)
    away = lax.dynamic_index_in_dim(local, 1 - yi, 0, keepdims=False)
    came = y_swap(away.astype(BF)).astype(F32)
    ends = jnp.where(
        yi == 0, jnp.concatenate([own, came], axis=0), jnp.concatenate([came, own], axis=0)
    )

    cols = w_qkv.shape[1]
    width = w_qkv.shape[3]
    hidden = w_gate_up.shape[3]
    p_qkv = w_qkv[0].transpose(1, 2, 0).reshape(3 * width, cols)
    p_gain = jnp.pad(norm_gains[0], ((0, 14), (0, 0)))
    full_qkv = gather_weight(jnp.concatenate([p_qkv, p_gain], axis=0))
    full_out = gather_weight(w_out[0])
    full_gu = gather_weight(w_gate_up[0].transpose(1, 2, 0).reshape(2 * hidden, cols))
    full_down = gather_weight(w_down[0])
    gains_all = full_qkv[:, 0, 3 * width : 3 * width + 2].transpose(1, 0, 2).reshape(2, model)
    gains = [gains_all[i : i + 1].astype(F32) for i in range(2)]
    full_qkv = full_qkv[:, :, : 3 * width]
    weights = (full_qkv, full_out, full_gu, full_down)

    bias_all = lax.all_gather(variate_bias[0], "tensor", axis=0, tiled=True).astype(F32)

    def row_of(array):
        return lax.dynamic_index_in_dim(array, yi, 0, keepdims=False)

    tab = tables(
        row_of(segment_ids), row_of(variate_ids), row_of(time_ids), row_of(padding_mask),
        bias_all, core,
    )

    y_low = forward(False, ends, weights, gains, tab, scale)
    got = lax.ppermute(y_low, "section", [(0, 1)]).astype(F32)
    x_in = jnp.where(is_first, ends, got)
    y, state = forward(True, x_in, weights, gains, tab, scale)
    dx = backward(ends, state, weights, gains, tab, scale)[0]
    got = lax.ppermute(dx.astype(BF), "section", [(1, 0)]).astype(F32)
    dy = jnp.where(is_first, got, ends)
    x, n1, q, k, v, k_oth, v_oth, q0, k0, o, sums, h, n2, g, u, z = state

    def by_core(array, index):
        parts = array.reshape((2, 2) + array.shape[1:])
        return lax.dynamic_index_in_dim(parts, index, 1, keepdims=False)

    def halves(array):
        return by_core(array, core), core_swap(by_core(array, 1 - core))

    def heads(array):
        return array.reshape(array.shape[0], tn, -1).transpose(1, 0, 2)

    df = dy.astype(BF)
    df_oth = core_swap(df)
    z_own, z_oth = halves(z)
    g_down = scatter_grad(wgrad_call(z_own, df, z_oth, df_oth))
    dx, da, dgu, dp, gain_grads, bias = backward(dy, state, weights, gains, tab, scale)
    n2_oth, n1_oth, da_oth = core_swap(n2), core_swap(n1), core_swap(da)
    gu_own, gu_oth = halves(dgu)
    flat = (4, h.shape[0], hidden)
    g_gu = wgrad_call(gu_own.reshape(flat), n2, gu_oth.reshape(flat), n2_oth)
    g_gu = g_gu.reshape(2, 2, model // ZB, hidden, ZB).transpose(0, 2, 1, 3, 4)
    g_gu = scatter_grad(g_gu.reshape(2, model // ZB, 2 * hidden, ZB))
    o_own, o_oth = halves(heads(o))
    g_out = scatter_grad(wgrad_call(o_own, da, o_oth, da_oth))
    dp_own, dp_oth = halves(dp)
    g_qkv = scatter_grad(wgrad_call(dp_own, n1, dp_oth, n1_oth))

    out_rows = jnp.where(is_first, dx, y)
    lower, upper = out_rows[:rows], out_rows[rows:]
    keep = jnp.where(yi == 0, lower, upper)
    send = jnp.where(yi == 0, upper, lower)
    back = y_swap(send.astype(BF)).astype(F32)
    boundary_out = jnp.where(
        yi == 0, jnp.stack([keep, back]), jnp.stack([back, keep])
    )[None]

    bias_sum = bias.sum(axis=-1).reshape(1, -1)
    small = jnp.concatenate(
        [gain_grads, jnp.pad(bias_sum, ((0, 0), (0, model - bias_sum.shape[1])))], axis=0
    )
    small = small_sum(small)
    piece = model // (n * tn)
    gain_piece = lax.dynamic_slice_in_dim(small[:2], (zi * tn + ti) * piece, piece, 1)
    heads_local = variate_bias.shape[1]
    bias_piece = lax.dynamic_slice_in_dim(
        small[2, : bias_sum.shape[1]].reshape(-1, 2), ti * heads_local, heads_local, 0
    )
    return (
        boundary_out,
        g_qkv.reshape(3, width, cols).transpose(2, 0, 1)[None],
        g_out[None],
        g_gu.reshape(2, hidden, cols).transpose(2, 0, 1)[None],
        g_down[None],
        gain_piece[None],
        bias_piece[None],
    )


def solution(mesh):
    placed = (
        P("section", "dp", "tensor", None),
        P("section", "dp", None, "tensor"),
        P("section", "tensor", "dp"),
        P("section", "dp", None, "tensor"),
        P("section", "tensor", "dp"),
        P("section", None, "dp"),
        P("section", "tensor", None),
        P("dp", None),
        P("dp", None),
        P("dp", None),
        P("dp", None),
    )
    return jax.shard_map(
        per_device,
        mesh=mesh,
        in_specs=placed,
        out_specs=(
            P("section", "dp", "tensor", None),
            P("section", "dp", None, "tensor"),
            P("section", "tensor", "dp"),
            P("section", "dp", None, "tensor"),
            P("section", "tensor", "dp"),
            P("section", None, ("dp", "tensor")),
            P("section", "tensor", None),
        ),
        check_vma=False,
    )
```

time: 1700 us -> 883 us (0.52)
  waiting for transfers between devices: 793 us -> 367 us
  matrix products: 397 us -> 0 us
  Pallas kernels: 0 us -> 249 us
  other arithmetic: 189 us -> 56.6 us
  local copies, waits for them, and re-layouts: 198 us -> 132 us
  blocking collectives: 68.2 us -> 8.46 us
  starting transfers between devices: 19.6 us -> 57.5 us
    dot_general x103 -> x0, matrix products: 397 us -> none  [the longest x16 65.6 us: masked_scores(): jnp.einsum('qhd,khd->hqk', q_block, k, preferred_element_type=jnp.float32)]
    reduce_scatter x19 -> x0, waiting for transfers between devices: 390 us -> none  [the longest x4 125 us: forward(): lax.psum_scatter(jnp.dot(attended, w_out, preferred_element_type=jnp.floa...]
    all_gather x19 -> x0, waiting for transfers between devices: 335 us -> none  [the longest x4 73.8 us: forward(): lax.all_gather((normed_a * gains_f[0]).astype(jnp.bfloat16), 'tensor', ax...]
    ppermute x6 -> x84, waiting for transfers between devices: 65.5 us -> 367 us  [the longest x23 196 us: y_swap(): return lax.ppermute(value, 'tensor', [(i, i ^ 2) for i in range(n)])]
    pallas_call x0 -> x16, Pallas kernels: none -> 249 us  [the longest x2 54.3 us: attend_back_call(): pl.pallas_call(functools.partial(attend_back_kernel, scale), grid=(pairs,...]
    reduce_sum x42 -> x1, other arithmetic: 99.3 us -> 0.93 us  [per_device(): bias_sum = bias.sum(axis=-1).reshape(1, -1)]
    ppermute x6 -> x84, starting transfers between devices: 15.8 us -> 57.5 us  [the longest x23 28.8 us: y_swap(): return lax.ppermute(value, 'tensor', [(i, i ^ 2) for i in range(n)])]
    unnamed x648 -> x97, local copies, waits for them, and re-layouts: 49.8 us -> 12.2 us
  transfers between devices with their start and end apart: 44 -> 84, of which waited for: 38 -> 35; matrix products, arithmetic and copies ran while one was open for 22% -> 19% of each run, Pallas kernels for 0% -> 14%
where the time goes in v1:
time: 883 us; the launch traced here: 874 us
  waiting for transfers between devices  367 us (42%)
  Pallas kernels  249 us (28%)
  local copies, waits for them, and re-layouts  132 us (15%)
  starting transfers between devices  57.5 us (7%)
  other arithmetic  56.6 us (6%)
    ppermute x23, waiting for transfers between devices, y_swap(): return lax.ppermute(value, 'tensor', [(i, i ^ 2) for i in range(n)])  196 us
    ppermute x24, waiting for transfers between devices, ring(): return lax.ppermute(value, 'dp', [(i, (i + 1) % n) for i in range(n)])  116 us
    dynamic_update_slice x63, local copies, waits for them, and re-layouts, gather_weight(): out = lax.dynamic_update_slice(out, part[None, None], (at, t, 0, 0))  57.9 us
    pallas_call x2, Pallas kernels, attend_back_call(): pl.pallas_call(functools.partial(attend_back_kernel, scale), grid=(pairs,...  54.3 us
    pallas_call x2, Pallas kernels, ffn_back_call(): pl.pallas_call(ffn_back_kernel, grid=(tn,), in_specs=[big, big, part, par...  42.1 us
    pallas_call x2, Pallas kernels, ffn_call(): pl.pallas_call(functools.partial(ffn_kernel, save), grid=(tn,), in_specs=...  38.4 us
    pallas_call x2, Pallas kernels, attend_call(): pl.pallas_call(functools.partial(attend_kernel, scale), grid=(pairs,), in...  35 us
    pallas_call x2, Pallas kernels, qkv_back_call(): pl.pallas_call(qkv_back_kernel, grid=(tn,), in_specs=[col] * 7 + [whole((...  29.9 us
  transfers between devices with their start and end apart: 84, of which 35 were waited for; matrix products, arithmetic and copies ran while one was open for 19% of the time, Pallas kernels for 14%

profile of v1, /device:TPU:0, one launch (start us, length us, event | category | flops | bytes accessed | tf_op | source)
XLA Modules:
  0.0 873.5 jit_solution(17704235071234624346)
XLA Ops:
  0.6 3.0 collective-permute-start.25
  23.6 8.5 all-gather
  34.7 3.0 broadcast_in_dim.312
  40.1 5.3 broadcast_in_dim.358
  46.4 2.9 broadcast_in_dim.366
  59.0 8.7 collective-permute-done.17
  71.3 5.6 collective-permute-done.19
  82.4 11.0 %collective-permute-done.20 = bf16[256,256]{1,0:T(8,128)(2,1)S(1)} collective-permute-done((bf16[256,256]{1,0:T(8,128)(2,1)S(1)}, bf16[256,256]{1,0:T(8,128)(2,1)S(1)}, u32[]{:S(2)}, u32[]{:S(2)}) %collective-permute-start.20) | collective-permute-done | bytes 131104 | tf_op jit(solution)/shard_map/ppermute | solution.py:568
  97.7 3.5 collective-permute-done.22
  107.0 10.7 %collective-permute-done.38 = bf16[688,256]{1,0:T(8,128)(2,1)S(1)} collective-permute-done((bf16[688,256]{1,0:T(8,128)(2,1)S(1)}, bf16[688,256]{1,0:T(8,128)(2,1)S(1)}, u32[]{:S(2)}, u32[]{:S(2)}) %collective-permute-start.38) | collective-permute-done | bytes 352288 | tf_op jit(solution)/shard_map/ppermute | solution.py:573
  125.3 3.0 collective-permute-done.39
  131.4 8.8 %collective-permute-done.4 = bf16[784,256]{1,0:T(8,128)(2,1)S(1)} collective-permute-done((bf16[784,256]{1,0:T(8,128)(2,1)S(1)}, bf16[784,256]{1,0:T(8,128)(2,1)S(1)}, u32[]{:S(2)}, u32[]{:S(2)}) %collective-permute-start.4) | collective-permute-done | bytes 401440 | tf_op jit(solution)/shard_map/ppermute | solution.py:568
  144.9 6.7 collective-permute-done.42
  159.1 22.3 %collective-permute-done.7 = bf16[784,256]{1,0:T(8,128)(2,1)S(1)} collective-permute-done((bf16[784,256]{1,0:T(8,128)(2,1)S(1)}, bf16[784,256]{1,0:T(8,128)(2,1)S(1)}, u32[]{:S(2)}, u32[]{:S(2)}) %collective-permute-start.7) | collective-permute-done | bytes 401440 | tf_op jit(solution)/shard_map/ppermute | solution.py:568
  189.0 6.8 collective-permute-done.9
  199.1 7.8 collective-permute-done.10
  210.6 4.7 collective-permute-done.30
  223.2 10.3 %collective-permute-done.31 = bf16[1376,256]{1,0:T(8,128)(2,1)S(1)} collective-permute-done((bf16[1376,256]{1,0:T(8,128)(2,1)S(1)}, bf16[1376,256]{1,0:T(8,128)(2,1)S(1)}, u32[]{:S(2)}, u32[]{:S(2)}) %collective-permute-start.31) | collective-permute-done | bytes 704544 | tf_op jit(solution)/shard_map/ppermute | solution.py:568
  237.1 2.7 collective-permute-done.33
  246.3 6.0 slice.180.w_ref
  253.7 11.0 %shard_map.162 = (bf16[512,1024]{1,0:T(8,128)(2,1)}, bf16[512,1024]{1,0:T(8,128)(2,1)}, bf16[512,1024]{1,0:T(8,128)(2,1)}) custom-call(f32[512,1024]{1,0:T(8,128)} %maximum_select_fusion.x_ref.dy_ref, f32[1,1024]{1,0:T(1,128)} %convert.10.gain_ref, bf16[4,4,768,256]{3,2,1,0:T(8,128)(2,1)} %slice.180.w_ref, f32[512,128]{1,0:T(8,128)} %pad_maximum_fusion.12.cos_ref, ...), custom_call_target="tpu_custom_call" | custom-call | flops 3221225472 | bytes 14680064 | tf_op jit(solution)/shard_map/pallas_call | solution.py:116
  271.7 17.5 %shard_map.163 = (bf16[512,1024]{1,0:T(8,128)(2,1)}, f32[512,1024]{1,0:T(8,128)}) custom-call(bf16[512,1024]{1,0:T(8,128)(2,1)} %get-tuple-element.47.q_ref, bf16[512,1024]{1,0:T(8,128)(2,1)} %get-tuple-element.48.ko_ref, bf16[512,1024]{1,0:T(8,128)(2,1)} %copy-done.45, bf16[512,1024]{1,0:T(8,128)(2,1)} %get-tuple-element.49.vo_ref, ...), custom_call_target="tpu_custom_call" | custom-call | flops 4294967296 | bytes 10485760 | tf_op jit(solution)/shard_map/pallas_call | solution.py:174
  299.2 17.9 %shard_map.164 = bf16[512,1024]{1,0:T(8,128)(2,1)} custom-call(f32[512,1024]{1,0:T(8,128)} %maximum_select_fusion.x_ref.dy_ref, bf16[512,1024]{1,0:T(8,128)(2,1)} %get-tuple-element.50.o_ref, bf16[4,4,256,256]{3,2,1,0:T(8,128)(2,1)} %fusion.43.wo_ref, f32[1,1024]{1,0:T(1,128)} %convert.9.gain_ref, bf16[4,4,1376,256]{3,2,1,0:T(8,128)(2,1)} %fusion.8.wgu_ref, ...), custom_call_target="tpu_custom_call" | custom-call | flops 9730785280 | bytes 29491200 | tf_op jit(solution)/shard_map/pallas_call | solution.py:256
  317.0 3.7 collective-permute-start.47
  320.8 22.8 %collective-permute-done.47 = bf16[512,1024]{1,0:T(8,128)(2,1)S(1)} collective-permute-done((bf16[512,1024]{1,0:T(8,128)(2,1)}, bf16[512,1024]{1,0:T(8,128)(2,1)S(1)}, u32[]{:S(2)}, u32[]{:S(2)}) %collective-permute-start.47) | collective-permute-done | bytes 1048608 | tf_op jit(solution)/shard_map/ppermute | solution.py:774
  345.4 11.1 %shard_map.165 = (bf16[512,1024]{1,0:T(8,128)(2,1)}, bf16[512,1024]{1,0:T(8,128)(2,1)}, bf16[512,1024]{1,0:T(8,128)(2,1)}, bf16[512,1024]{1,0:T(8,128)(2,1)}, bf...) custom-call(f32[512,1024]{1,0:T(8,128)} %convert_select_fusion.1.x_ref, f32[1,1024]{1,0:T(1,128)} %convert.10.gain_ref, ...), custom_call_target="tpu_custom_call" | custom-call | flops 3221225472 | bytes 14680064 | tf_op jit(solution)/shard_map/pallas_call | solution.py:116
  362.0 17.4 %shard_map.166 = (bf16[512,1024]{1,0:T(8,128)(2,1)}, f32[512,1024]{1,0:T(8,128)}) custom-call(bf16[512,1024]{1,0:T(8,128)(2,1)} %get-tuple-element.51.q_ref, bf16[512,1024]{1,0:T(8,128)(2,1)} %get-tuple-element.52.ko_ref, bf16[512,1024]{1,0:T(8,128)(2,1)} %copy-done.42, bf16[512,1024]{1,0:T(8,128)(2,1)} %get-tuple-element.53.vo_ref, ...), custom_call_target="tpu_custom_call" | custom-call | flops 4294967296 | bytes 10485760 | tf_op jit(solution)/shard_map/pallas_call | solution.py:174
  379.4 20.6 %shard_map.167 = (f32[512,1024]{1,0:T(8,128)}, f32[512,1024]{1,0:T(8,128)}, bf16[512,1024]{1,0:T(8,128)(2,1)}, bf16[4,512,688]{2,1,0:T(8,128)(2,1)}, bf16[4,512,...) custom-call(f32[512,1024]{1,0:T(8,128)} %convert_select_fusion.1.x_ref, bf16[512,1024]{1,0:T(8,128)(2,1)} %get-tuple-element.54.o_ref, ...), custom_call_target="tpu_custom_call" | custom-call | flops 9730785280 | bytes 29491200 | tf_op jit(solution)/shard_map/pallas_call | solution.py:256
  400.0 21.2 %shard_map.168 = (f32[512,1024]{1,0:T(8,128)}, bf16[512,1024]{1,0:T(8,128)(2,1)}, bf16[512,1024]{1,0:T(8,128)(2,1)}, bf16[4,2,512,688]{3,2,1,0:T(8,128)(2,1)}, f32[1,1024]{1,0:T(1,128)}) custom-call(f32[512,1024]{1,0:T(8,128)} %maximum_select_fusion.x_ref.dy_ref, f32[512,1024]{1,0:T(8,128)} %get-tuple-element.55.h_ref, ...), custom_call_target="tpu_custom_call" | custom-call | flops 9730785280 | bytes 29491200 | tf_op jit(solution)/shard_map/pallas_call | solution.py:331
  421.1 27.2 %shard_map.169 = (f32[512,1024]{1,0:T(8,128)}, f32[512,1024]{1,0:T(8,128)}, bf16[512,1024]{1,0:T(8,128)(2,1)}, f32[512,1024]{1,0:T(8,128)}, bf16[512,1024]{1,0:T(8,128)(2,1)}, /*index=5*/f32[8,4,512]{2,1,0:T(4,128)}) custom-call(bf16[512,1024]{1,0:T(8,128)(2,1)} %get-tuple-element.51.q_ref, bf16[512,1024]{1,0:T(8,128)(2,1)} %get-tuple-element.52.ko_ref, ...), custom_call_target="tpu_custom_call" | custom-call | flops 10737418240 | bytes 20971520 | tf_op jit(solution)/shard_map/pallas_call | solution.py:442
  453.7 14.8 %shard_map.170 = (bf16[4,512,768]{2,1,0:T(8,128)(2,1)}, f32[512,1024]{1,0:T(8,128)}, f32[1,1024]{1,0:T(1,128)}) custom-call(f32[512,1024]{1,0:T(8,128)} %get-tuple-element.60.dq_ref, f32[512,1024]{1,0:T(8,128)} %get-tuple-element.61.dk_ref, bf16[512,1024]{1,0:T(8,128)(2,1)} %copy-done.19, f32[512,1024]{1,0:T(8,128)} %get-tuple-element.63.dv_ref, ...), custom_call_target="tpu_custom_call" | custom-call | flops 3221225472 | bytes 27262976 | tf_op jit(solution)/shard_map/pallas_call | solution.py:517
  468.5 2.9 convert_element_type.206
  474.6 2.7 copy.64
  477.5 21.4 %collective-permute-done.52 = bf16[512,1024]{1,0:T(8,128)(2,1)} collective-permute-done((bf16[512,1024]{1,0:T(8,128)(2,1)}, bf16[512,1024]{1,0:T(8,128)(2,1)}, u32[]{:S(2)}, u32[]{:S(2)}) %collective-permute-start.52) | collective-permute-done | bytes 1048608 | tf_op jit(solution)/shard_map/ppermute | solution.py:778
  498.9 3.5 fusion.63
  502.4 20.9 %shard_map.171 = (f32[512,1024]{1,0:T(8,128)}, bf16[512,1024]{1,0:T(8,128)(2,1)}, bf16[512,1024]{1,0:T(8,128)(2,1)}, bf16[4,2,512,688]{3,2,1,0:T(8,128)(2,1)}, f32[1,1024]{1,0:T(1,128)}) custom-call(f32[512,1024]{1,0:T(8,128)} %get-tuple-element.90.dy_ref, f32[512,1024]{1,0:T(8,128)} %get-tuple-element.55.h_ref, ...), custom_call_target="tpu_custom_call" | custom-call | flops 9730785280 | bytes 29491200 | tf_op jit(solution)/shard_map/pallas_call | solution.py:331
  523.3 27.1 %shard_map.172 = (f32[512,1024]{1,0:T(8,128)}, f32[512,1024]{1,0:T(8,128)}, bf16[512,1024]{1,0:T(8,128)(2,1)}, f32[512,1024]{1,0:T(8,128)}, bf16[512,1024]{1,0:T(8,128)(2,1)}, /*index=5*/f32[8,4,512]{2,1,0:T(4,128)}) custom-call(bf16[512,1024]{1,0:T(8,128)(2,1)} %get-tuple-element.51.q_ref, bf16[512,1024]{1,0:T(8,128)(2,1)} %get-tuple-element.52.ko_ref, ...), custom_call_target="tpu_custom_call" | custom-call | flops 10737418240 | bytes 20971520 | tf_op jit(solution)/shard_map/pallas_call | solution.py:442
  551.1 6.0 constant_dynamic-slice_fusion.3
  557.1 4.6 copy.60
  568.1 15.1 %shard_map.173 = (bf16[4,512,768]{2,1,0:T(8,128)(2,1)}, f32[512,1024]{1,0:T(8,128)}, f32[1,1024]{1,0:T(1,128)}) custom-call(f32[512,1024]{1,0:T(8,128)} %get-tuple-element.70.dq_ref, f32[512,1024]{1,0:T(8,128)} %get-tuple-element.71.dk_ref, bf16[512,1024]{1,0:T(8,128)(2,1)} %copy-done.18, f32[512,1024]{1,0:T(8,128)} %get-tuple-element.73.dv_ref, ...), custom_call_target="tpu_custom_call" | custom-call | flops 3221225472 | bytes 27262976 | tf_op jit(solution)/shard_map/pallas_call | solution.py:517
  590.5 6.4 shard_map.177
  600.5 4.6 copy.61
  606.8 10.0 %shard_map.176 = bf16[4,4,688,256]{3,2,1,0:T(8,128)(2,1)} custom-call(bf16[4,512,688]{2,1,0:T(8,128)(2,1)} %bitcast.398, bf16[512,1024]{1,0:T(8,128)(2,1)} %get-tuple-element.82.bo_ref, bf16[4,512,688]{2,1,0:T(8,128)(2,1)} %bitcast.396, bf16[512,1024]{1,0:T(8,128)(2,1)} %collective-permute-done.69.bx_ref), custom_call_target="tpu_custom_call" | custom-call | flops 5771362304 | bytes 5636096 | tf_op jit(solution)/shard_map/pallas_call | solution.py:550
  616.8 3.0 copy.62
  619.8 2.4 copy-done.2
  627.2 4.1 shard_map.175
  632.4 3.5 collective-permute-done.83
  638.1 6.9 shard_map.174
  644.9 2.8 dynamic-slice_bitcast_fusion.2
  649.5 80.2 %collective-permute-done.64 = bf16[4,256,256]{2,1,0:T(8,128)(2,1)} collective-permute-done((bf16[4,256,256]{2,1,0:T(8,128)(2,1)S(1)}, bf16[4,256,256]{2,1,0:T(8,128)(2,1)}, u32[]{:S(2)}, u32[]{:S(2)}) %collective-permute-start.64) | collective-permute-done | bytes 524320 | tf_op jit(solution)/shard_map/ppermute | solution.py:568
  731.0 10.0 %collective-permute-done.55 = bf16[256,1024]{1,0:T(8,128)(2,1)} collective-permute-done((bf16[256,1024]{1,0:T(8,128)(2,1)}, bf16[256,1024]{1,0:T(8,128)(2,1)}, u32[]{:S(2)}, u32[]{:S(2)}) %collective-permute-start.55) | collective-permute-done | bytes 524320 | tf_op jit(solution)/shard_map/ppermute | solution.py:568
  743.7 2.4 convert_add_fusion.2
  746.1 27.3 %collective-permute-done.58 = bf16[4,768,256]{2,1,0:T(8,128)(2,1)} collective-permute-done((bf16[4,768,256]{2,1,0:T(8,128)(2,1)}, bf16[4,768,256]{2,1,0:T(8,128)(2,1)}, u32[]{:S(2)}, u32[]{:S(2)}) %collective-permute-start.58) | collective-permute-done | bytes 1572896 | tf_op jit(solution)/shard_map/ppermute | solution.py:568
  778.9 4.4 collective-permute-start.78
  783.3 6.1 collective-permute-done.59
  789.6 14.9 %collective-permute-done.71 = bf16[1376,256]{1,0:T(8,128)(2,1)S(1)} collective-permute-done((bf16[1376,256]{1,0:T(8,128)(2,1)S(1)}, bf16[1376,256]{1,0:T(8,128)(2,1)S(1)}, u32[]{:S(2)}, u32[]{:S(2)}) %collective-permute-start.71) | collective-permute-done | bytes 704544 | tf_op jit(solution)/shard_map/ppermute | solution.py:573
  804.8 2.5 collective-permute-done.66
  807.4 7.4 collective-permute-done.78
  815.1 8.3 collective-permute-done.60
  823.5 14.9 %collective-permute-done.72 = bf16[1376,256]{1,0:T(8,128)(2,1)S(1)} collective-permute-done((bf16[1376,256]{1,0:T(8,128)(2,1)S(1)}, bf16[1376,256]{1,0:T(8,128)(2,1)S(1)}, u32[]{:S(2)}, u32[]{:S(2)}) %collective-permute-start.72) | collective-permute-done | bytes 704544 | tf_op jit(solution)/shard_map/ppermute | solution.py:573
  841.9 6.8 collective-permute-done.79
  849.7 7.5 collective-permute-done.61
  858.4 11.9 %collective-permute-done.73 = bf16[1376,256]{1,0:T(8,128)(2,1)} collective-permute-done((bf16[1376,256]{1,0:T(8,128)(2,1)}, bf16[1376,256]{1,0:T(8,128)(2,1)}, u32[]{:S(2)}, u32[]{:S(2)}) %collective-permute-start.73) | collective-permute-done | bytes 704544 | tf_op jit(solution)/shard_map/ppermute | solution.py:573
  870.3 2.8 bitcast_add_fusion
  (403 shorter events, 189.5 us)
Async XLA Ops:
  0.6 121.2 %collective-permute-start.25 = (bf16[1376,256]{1,0:T(8,128)(2,1)}, bf16[1376,256]{1,0:T(8,128)(2,1)}, u32[]{:S(2)}, u32[]{:S(2)}) collective-permute-start(bf16[1376,256]{1,0:T(8,128)(2,1)} %bitcast.402), channel_id=1, source_target_pairs={{0,2},{1,3},{2,0},{3,1},{4,6},{5,7},{6,4},{7,5},{8,10},{9,11},{10,... | collective-permute-start | bytes 2113544 | tf_op jit(solution)/shard_map/ppermute | solution.py:568
  3.7 148.8 %collective-permute-start.27 = (bf16[1376,256]{1,0:T(8,128)(2,1)}, bf16[1376,256]{1,0:T(8,128)(2,1)}, u32[]{:S(2)}, u32[]{:S(2)}) collective-permute-start(bf16[1376,256]{1,0:T(8,128)(2,1)} %bitcast.403), channel_id=1, source_target_pairs={{0,4},{4,8},{8,12},{12,0},{1,5},{5,9},{9,13},{13,1},{2,6},{6,10},{... | collective-permute-start | bytes 2113544 | tf_op jit(solution)/shard_map/ppermute | solution.py:573
  5.3 49.0 %collective-permute-start.14 = (bf16[256,256]{1,0:T(8,128)(2,1)}, bf16[256,256]{1,0:T(8,128)(2,1)}, u32[]{:S(2)}, u32[]{:S(2)}) collective-permute-start(bf16[256,256]{1,0:T(8,128)(2,1)} %bitcast.430), channel_id=1, source_target_pairs={{0,2},{1,3},{2,0},{3,1},{4,6},{5,7},{6,4},{7,5},{8,10},{9,11},{10,... | collective-permute-start | bytes 393224 | tf_op jit(solution)/shard_map/ppermute | solution.py:568
  5.8 50.3 %collective-permute-start.16 = (bf16[256,256]{1,0:T(8,128)(2,1)}, bf16[256,256]{1,0:T(8,128)(2,1)}, u32[]{:S(2)}, u32[]{:S(2)}) collective-permute-start(bf16[256,256]{1,0:T(8,128)(2,1)} %bitcast.431), channel_id=1, source_target_pairs={{0,4},{4,8},{8,12},{12,0},{1,5},{5,9},{9,13},{13,1},{2,6},{6,10},{... | collective-permute-start | bytes 393224 | tf_op jit(solution)/shard_map/ppermute | solution.py:573
  10.1 83.3 %collective-permute-start.1 = (bf16[784,256]{1,0:T(8,128)(2,1)}, bf16[784,256]{1,0:T(8,128)(2,1)}, u32[]{:S(2)}, u32[]{:S(2)}) collective-permute-start(bf16[784,256]{1,0:T(8,128)(2,1)} %get-tuple-element.100), channel_id=1, source_target_pairs={{0,2},{1,3},{2,0},{3,1},{4,6},{5,7},{6,4},{7,5},{8,10},{9,11},{10,... | collective-permute-start | bytes 1204232 | tf_op jit(solution)/shard_map/ppermute | solution.py:568
  54.3 14.3 %collective-permute-start.36 = (bf16[688,256]{1,0:T(8,128)(2,1)S(1)}, bf16[688,256]{1,0:T(8,128)(2,1)S(1)}, u32[]{:S(2)}, u32[]{:S(2)}) collective-permute-start(bf16[688,256]{1,0:T(8,128)(2,1)S(1)} %bitcast.418), channel_id=1, source_target_pairs={{0,2},{1,3},{2,0},{3,1},{4,6},{5,7},{6,4},{7,5},{8,10},{9,11},{10,... | collective-permute-start | bytes 1056776 | tf_op jit(solution)/shard_map/ppermute | solution.py:568
  76.8 19.5 %collective-permute-start = (bf16[256,1024]{1,0:T(8,128)(2,1)S(1)}, bf16[256,1024]{1,0:T(8,128)(2,1)S(1)}, u32[]{:S(2)}, u32[]{:S(2)}) collective-permute-start(bf16[256,1024]{1,0:T(8,128)(2,1)S(1)} %fusion.19), channel_id=1, source_target_pairs={{0,2},{1,3},{2,0},{3,1},{4,6},{5,7},{6,4},{7,5},{8,10},{9,11},{10,... | collective-permute-start | bytes 1572872 | tf_op jit(solution)/shard_map/ppermute | solution.py:568
  78.5 14.9 %collective-permute-start.20 = (bf16[256,256]{1,0:T(8,128)(2,1)S(1)}, bf16[256,256]{1,0:T(8,128)(2,1)S(1)}, u32[]{:S(2)}, u32[]{:S(2)}) collective-permute-start(bf16[256,256]{1,0:T(8,128)(2,1)S(1)} %collective-permute-done.19), channel_id=1, source_target_pairs={{0,2},{1,3},{2,0},{3,1},{4,6},{5,7},{6,4},{7,5},{8,10},{9,11},{10,... | collective-permute-start | bytes 393224 | tf_op jit(solution)/shard_map/ppermute | solution.py:568
  96.4 32.1 %collective-permute-start.3 = (bf16[784,256]{1,0:T(8,128)(2,1)}, bf16[784,256]{1,0:T(8,128)(2,1)S(1)}, u32[]{:S(2)}, u32[]{:S(2)}) collective-permute-start(bf16[784,256]{1,0:T(8,128)(2,1)} %get-tuple-element.100), channel_id=1, source_target_pairs={{0,4},{4,8},{8,12},{12,0},{1,5},{5,9},{9,13},{13,1},{2,6},{6,10},{... | collective-permute-start | bytes 1204232 | tf_op jit(solution)/shard_map/ppermute | solution.py:573
  101.2 16.5 %collective-permute-start.38 = (bf16[688,256]{1,0:T(8,128)(2,1)S(1)}, bf16[688,256]{1,0:T(8,128)(2,1)S(1)}, u32[]{:S(2)}, u32[]{:S(2)}) collective-permute-start(bf16[688,256]{1,0:T(8,128)(2,1)S(1)} %bitcast.419), channel_id=1, source_target_pairs={{0,4},{4,8},{8,12},{12,0},{1,5},{5,9},{9,13},{13,1},{2,6},{6,10},{... | collective-permute-start | bytes 1056776 | tf_op jit(solution)/shard_map/ppermute | solution.py:573
  117.7 23.3 %collective-permute-start.37 = (bf16[2,688,256]{2,1,0:T(8,128)(2,1)S(1)}, bf16[2,688,256]{2,1,0:T(8,128)(2,1)S(1)}, u32[]{:S(2)}, u32[]{:S(2)}) collective-permute-start(bf16[2,688,256]{2,1,0:T(8,128)(2,1)S(1)} %pad_maximum_fusion.8), channel_id=1, source_target_pairs={{0,1},{1,0},{2,3},{3,2},{4,5},{5,4},{6,7},{7,6},{8,9},{9,8},{10,11... | collective-permute-start | bytes 2113544 | tf_op jit(solution)/shard_map/ppermute | solution.py:563
  128.4 12.5 %collective-permute-start.41 = (bf16[688,256]{1,0:T(8,128)(2,1)S(1)}, bf16[688,256]{1,0:T(8,128)(2,1)S(1)}, u32[]{:S(2)}, u32[]{:S(2)}) collective-permute-start(bf16[688,256]{1,0:T(8,128)(2,1)S(1)} %collective-permute-done.38), channel_id=1, source_target_pairs={{0,4},{4,8},{8,12},{12,0},{1,5},{5,9},{9,13},{13,1},{2,6},{6,10},{... | collective-permute-start | bytes 1056776 | tf_op jit(solution)/shard_map/ppermute | solution.py:573
  128.4 27.8 %collective-permute-start.2 = (bf16[2,784,256]{2,1,0:T(8,128)(2,1)S(1)}, bf16[2,784,256]{2,1,0:T(8,128)(2,1)S(1)}, u32[]{:S(2)}, u32[]{:S(2)}) collective-permute-start(bf16[2,784,256]{2,1,0:T(8,128)(2,1)S(1)} %pad_maximum_fusion.4), channel_id=1, source_target_pairs={{0,1},{1,0},{2,3},{3,2},{4,5},{5,4},{6,7},{7,6},{8,9},{9,8},{10,11... | collective-permute-start | bytes 2408456 | tf_op jit(solution)/shard_map/ppermute | solution.py:563
  128.5 11.7 %collective-permute-start.4 = (bf16[784,256]{1,0:T(8,128)(2,1)S(1)}, bf16[784,256]{1,0:T(8,128)(2,1)S(1)}, u32[]{:S(2)}, u32[]{:S(2)}) collective-permute-start(bf16[784,256]{1,0:T(8,128)(2,1)S(1)} %collective-permute-done.3), channel_id=1, source_target_pairs={{0,2},{1,3},{2,0},{3,1},{4,6},{5,7},{6,4},{7,5},{8,10},{9,11},{10,... | collective-permute-start | bytes 1204232 | tf_op jit(solution)/shard_map/ppermute | solution.py:568
  140.2 14.5 %collective-permute-start.6 = (bf16[784,256]{1,0:T(8,128)(2,1)S(1)}, bf16[784,256]{1,0:T(8,128)(2,1)S(1)}, u32[]{:S(2)}, u32[]{:S(2)}) collective-permute-start(bf16[784,256]{1,0:T(8,128)(2,1)S(1)} %collective-permute-done.3), channel_id=1, source_target_pairs={{0,4},{4,8},{8,12},{12,0},{1,5},{5,9},{9,13},{13,1},{2,6},{6,10},{... | collective-permute-start | bytes 1204232 | tf_op jit(solution)/shard_map/ppermute | solution.py:573
  140.9 93.8 %collective-permute-start.26 = (bf16[2,1376,256]{2,1,0:T(8,128)(2,1)S(1)}, bf16[2,1376,256]{2,1,0:T(8,128)(2,1)S(1)}, u32[]{:S(2)}, u32[]{:S(2)}) collective-permute-start(bf16[2,1376,256]{2,1,0:T(8,128)(2,1)S(1)} %pad_maximum_fusion), channel_id=1, source_target_pairs={{0,1},{1,0},{2,3},{3,2},{4,5},{5,4},{6,7},{7,6},{8,9},{9,8},{10,11... | collective-permute-start | bytes 4227080 | tf_op jit(solution)/shard_map/ppermute | solution.py:563
  151.6 32.8 %collective-permute-start.40 = (bf16[2,688,256]{2,1,0:T(8,128)(2,1)S(1)}, bf16[2,688,256]{2,1,0:T(8,128)(2,1)S(1)}, u32[]{:S(2)}, u32[]{:S(2)}) collective-permute-start(bf16[2,688,256]{2,1,0:T(8,128)(2,1)S(1)} %pad_maximum_fusion.9), channel_id=1, source_target_pairs={{0,1},{1,0},{2,3},{3,2},{4,5},{5,4},{6,7},{7,6},{8,9},{9,8},{10,11... | collective-permute-start | bytes 2113544 | tf_op jit(solution)/shard_map/ppermute | solution.py:563
  152.5 29.9 %collective-permute-start.44 = (bf16[688,256]{1,0:T(8,128)(2,1)S(1)}, bf16[688,256]{1,0:T(8,128)(2,1)S(1)}, u32[]{:S(2)}, u32[]{:S(2)}) collective-permute-start(bf16[688,256]{1,0:T(8,128)(2,1)S(1)} %collective-permute-done.41), channel_id=1, source_target_pairs={{0,4},{4,8},{8,12},{12,0},{1,5},{5,9},{9,13},{13,1},{2,6},{6,10},{... | collective-permute-start | bytes 1056776 | tf_op jit(solution)/shard_map/ppermute | solution.py:573
  154.8 43.0 %collective-permute-start.28 = (bf16[1376,256]{1,0:T(8,128)(2,1)}, bf16[1376,256]{1,0:T(8,128)(2,1)S(1)}, u32[]{:S(2)}, u32[]{:S(2)}) collective-permute-start(bf16[1376,256]{1,0:T(8,128)(2,1)} %collective-permute-done.27), channel_id=1, source_target_pairs={{0,2},{1,3},{2,0},{3,1},{4,6},{5,7},{6,4},{7,5},{8,10},{9,11},{10,... | collective-permute-start | bytes 2113544 | tf_op jit(solution)/shard_map/ppermute | solution.py:568
  156.3 25.2 %collective-permute-start.7 = (bf16[784,256]{1,0:T(8,128)(2,1)S(1)}, bf16[784,256]{1,0:T(8,128)(2,1)S(1)}, u32[]{:S(2)}, u32[]{:S(2)}) collective-permute-start(bf16[784,256]{1,0:T(8,128)(2,1)S(1)} %collective-permute-done.6), channel_id=1, source_target_pairs={{0,2},{1,3},{2,0},{3,1},{4,6},{5,7},{6,4},{7,5},{8,10},{9,11},{10,... | collective-permute-start | bytes 1204232 | tf_op jit(solution)/shard_map/ppermute | solution.py:568
  181.5 25.4 %collective-permute-start.5 = (bf16[2,784,256]{2,1,0:T(8,128)(2,1)S(1)}, bf16[2,784,256]{2,1,0:T(8,128)(2,1)S(1)}, u32[]{:S(2)}, u32[]{:S(2)}) collective-permute-start(bf16[2,784,256]{2,1,0:T(8,128)(2,1)S(1)} %pad_maximum_fusion.5), channel_id=1, source_target_pairs={{0,1},{1,0},{2,3},{3,2},{4,5},{5,4},{6,7},{7,6},{8,9},{9,8},{10,11... | collective-permute-start | bytes 2408456 | tf_op jit(solution)/shard_map/ppermute | solution.py:563
  182.4 13.5 %collective-permute-start.9 = (bf16[784,256]{1,0:T(8,128)(2,1)S(1)}, bf16[784,256]{1,0:T(8,128)(2,1)S(1)}, u32[]{:S(2)}, u32[]{:S(2)}) collective-permute-start(bf16[784,256]{1,0:T(8,128)(2,1)S(1)} %collective-permute-done.6), channel_id=1, source_target_pairs={{0,4},{4,8},{8,12},{12,0},{1,5},{5,9},{9,13},{13,1},{2,6},{6,10},{... | collective-permute-start | bytes 1204232 | tf_op jit(solution)/shard_map/ppermute | solution.py:573
  184.4 11.7 %collective-permute-start.45 = (bf16[688,256]{1,0:T(8,128)(2,1)S(1)}, bf16[688,256]{1,0:T(8,128)(2,1)S(1)}, u32[]{:S(2)}, u32[]{:S(2)}) collective-permute-start(bf16[688,256]{1,0:T(8,128)(2,1)S(1)} %collective-permute-done.44), channel_id=1, source_target_pairs={{0,2},{1,3},{2,0},{3,1},{4,6},{5,7},{6,4},{7,5},{8,10},{9,11},{10,... | collective-permute-start | bytes 1056776 | tf_op jit(solution)/shard_map/ppermute | solution.py:568
  195.9 19.4 %collective-permute-start.30 = (bf16[1376,256]{1,0:T(8,128)(2,1)}, bf16[1376,256]{1,0:T(8,128)(2,1)S(1)}, u32[]{:S(2)}, u32[]{:S(2)}) collective-permute-start(bf16[1376,256]{1,0:T(8,128)(2,1)} %collective-permute-done.27), channel_id=1, source_target_pairs={{0,4},{4,8},{8,12},{12,0},{1,5},{5,9},{9,13},{13,1},{2,6},{6,10},{... | collective-permute-start | bytes 2113544 | tf_op jit(solution)/shard_map/ppermute | solution.py:573
  197.8 17.6 %collective-permute-start.43 = (bf16[2,688,256]{2,1,0:T(8,128)(2,1)S(1)}, bf16[2,688,256]{2,1,0:T(8,128)(2,1)S(1)}, u32[]{:S(2)}, u32[]{:S(2)}) collective-permute-start(bf16[2,688,256]{2,1,0:T(8,128)(2,1)S(1)} %pad_maximum_fusion.10), channel_id=1, source_target_pairs={{0,1},{1,0},{2,3},{3,2},{4,5},{5,4},{6,7},{7,6},{8,9},{9,8},{10,11... | collective-permute-start | bytes 2113544 | tf_op jit(solution)/shard_map/ppermute | solution.py:563
  206.8 13.1 %collective-permute-start.8 = (bf16[2,784,256]{2,1,0:T(8,128)(2,1)S(1)}, bf16[2,784,256]{2,1,0:T(8,128)(2,1)S(1)}, u32[]{:S(2)}, u32[]{:S(2)}) collective-permute-start(bf16[2,784,256]{2,1,0:T(8,128)(2,1)S(1)} %pad_maximum_fusion.6), channel_id=1, source_target_pairs={{0,1},{1,0},{2,3},{3,2},{4,5},{5,4},{6,7},{7,6},{8,9},{9,8},{10,11... | collective-permute-start | bytes 2408456 | tf_op jit(solution)/shard_map/ppermute | solution.py:563
  206.9 60.2 %collective-permute-start.29 = (bf16[2,1376,256]{2,1,0:T(8,128)(2,1)S(1)}, bf16[2,1376,256]{2,1,0:T(8,128)(2,1)S(1)}, u32[]{:S(2)}, u32[]{:S(2)}) collective-permute-start(bf16[2,1376,256]{2,1,0:T(8,128)(2,1)S(1)} %pad_maximum_fusion.1), channel_id=1, source_target_pairs={{0,1},{1,0},{2,3},{3,2},{4,5},{5,4},{6,7},{7,6},{8,9},{9,8},{10,11... | collective-permute-start | bytes 4227080 | tf_op jit(solution)/shard_map/ppermute | solution.py:563
  215.3 27.0 %collective-permute-start.46 = (bf16[2,688,256]{2,1,0:T(8,128)(2,1)S(1)}, bf16[2,688,256]{2,1,0:T(8,128)(2,1)S(1)}, u32[]{:S(2)}, u32[]{:S(2)}) collective-permute-start(bf16[2,688,256]{2,1,0:T(8,128)(2,1)S(1)} %pad_maximum_fusion.11), channel_id=1, source_target_pairs={{0,1},{1,0},{2,3},{3,2},{4,5},{5,4},{6,7},{7,6},{8,9},{9,8},{10,11... | collective-permute-start | bytes 2113544 | tf_op jit(solution)/shard_map/ppermute | solution.py:563
  215.3 18.2 %collective-permute-start.31 = (bf16[1376,256]{1,0:T(8,128)(2,1)S(1)}, bf16[1376,256]{1,0:T(8,128)(2,1)S(1)}, u32[]{:S(2)}, u32[]{:S(2)}) collective-permute-start(bf16[1376,256]{1,0:T(8,128)(2,1)S(1)} %collective-permute-done.30), channel_id=1, source_target_pairs={{0,2},{1,3},{2,0},{3,1},{4,6},{5,7},{6,4},{7,5},{8,10},{9,11},{10,... | collective-permute-start | bytes 2113544 | tf_op jit(solution)/shard_map/ppermute | solution.py:568
  219.9 19.9 %collective-permute-start.33 = (bf16[1376,256]{1,0:T(8,128)(2,1)S(1)}, bf16[1376,256]{1,0:T(8,128)(2,1)S(1)}, u32[]{:S(2)}, u32[]{:S(2)}) collective-permute-start(bf16[1376,256]{1,0:T(8,128)(2,1)S(1)} %collective-permute-done.30), channel_id=1, source_target_pairs={{0,4},{4,8},{8,12},{12,0},{1,5},{5,9},{9,13},{13,1},{2,6},{6,10},{... | collective-permute-start | bytes 2113544 | tf_op jit(solution)/shard_map/ppermute | solution.py:573
  234.7 54.5 %collective-permute-start.32 = (bf16[2,1376,256]{2,1,0:T(8,128)(2,1)}, bf16[2,1376,256]{2,1,0:T(8,128)(2,1)}, u32[]{:S(2)}, u32[]{:S(2)}) collective-permute-start(bf16[2,1376,256]{2,1,0:T(8,128)(2,1)} %pad_maximum_fusion.2), channel_id=1, source_target_pairs={{0,1},{1,0},{2,3},{3,2},{4,5},{5,4},{6,7},{7,6},{8,9},{9,8},{10,11... | collective-permute-start | bytes 4227080 | tf_op jit(solution)/shard_map/ppermute | solution.py:563
  239.8 26.0 %collective-permute-start.34 = (bf16[1376,256]{1,0:T(8,128)(2,1)S(1)}, bf16[1376,256]{1,0:T(8,128)(2,1)S(1)}, u32[]{:S(2)}, u32[]{:S(2)}) collective-permute-start(bf16[1376,256]{1,0:T(8,128)(2,1)S(1)} %collective-permute-done.33), channel_id=1, source_target_pairs={{0,2},{1,3},{2,0},{3,1},{4,6},{5,7},{6,4},{7,5},{8,10},{9,11},{10,... | collective-permute-start | bytes 2113544 | tf_op jit(solution)/shard_map/ppermute | solution.py:568
  267.0 28.1 %collective-permute-start.35 = (bf16[2,1376,256]{2,1,0:T(8,128)(2,1)}, bf16[2,1376,256]{2,1,0:T(8,128)(2,1)}, u32[]{:S(2)}, u32[]{:S(2)}) collective-permute-start(bf16[2,1376,256]{2,1,0:T(8,128)(2,1)} %pad_maximum_fusion.3), channel_id=1, source_target_pairs={{0,1},{1,0},{2,3},{3,2},{4,5},{5,4},{6,7},{7,6},{8,9},{9,8},{10,11... | collective-permute-start | bytes 4227080 | tf_op jit(solution)/shard_map/ppermute | solution.py:563
  317.0 26.6 %collective-permute-start.47 = (bf16[512,1024]{1,0:T(8,128)(2,1)}, bf16[512,1024]{1,0:T(8,128)(2,1)S(1)}, u32[]{:S(2)}, u32[]{:S(2)}) collective-permute-start(bf16[512,1024]{1,0:T(8,128)(2,1)} %shard_map.164), channel_id=1, source_target_pairs={{0,16},{1,17},{2,18},{3,19},{4,20},{5,21},{6,22},{7,23},{8,24},{9,... | collective-permute-start | bytes 3145736 | tf_op jit(solution)/shard_map/ppermute | solution.py:774
  471.5 27.4 %collective-permute-start.52 = (bf16[512,1024]{1,0:T(8,128)(2,1)}, bf16[512,1024]{1,0:T(8,128)(2,1)}, u32[]{:S(2)}, u32[]{:S(2)}) collective-permute-start(bf16[512,1024]{1,0:T(8,128)(2,1)} %convert_element_type.206), channel_id=1, source_target_pairs={{16,0},{17,1},{18,2},{19,3},{20,4},{21,5},{22,6},{23,7},{24,8},{25... | collective-permute-start | bytes 3145736 | tf_op jit(solution)/shard_map/ppermute | solution.py:778
  477.3 87.2 %collective-permute-start.74 = (bf16[2,512,688]{1,2,0:T(8,128)(2,1)}, bf16[2,512,688]{1,2,0:T(8,128)(2,1)S(1)}, u32[]{:S(2)}, u32[]{:S(2)}) collective-permute-start(bf16[2,512,688]{1,2,0:T(8,128)(2,1)} %bitcast.417), channel_id=1, source_target_pairs={{0,1},{1,0},{2,3},{3,2},{4,5},{5,4},{6,7},{7,6},{8,9},{9,8},{10,11... | collective-permute-start | bytes 4227080 | tf_op jit(solution)/shard_map/ppermute | solution.py:563
  550.5 16.7 %collective-permute-start.53 = (bf16[512,1024]{1,0:T(8,128)(2,1)}, bf16[512,1024]{1,0:T(8,128)(2,1)S(1)}, u32[]{:S(2)}, u32[]{:S(2)}) collective-permute-start(bf16[512,1024]{1,0:T(8,128)(2,1)} %get-tuple-element.72), channel_id=1, source_target_pairs={{0,1},{1,0},{2,3},{3,2},{4,5},{5,4},{6,7},{7,6},{8,9},{9,8},{10,11... | collective-permute-start | bytes 3145736 | tf_op jit(solution)/shard_map/ppermute | solution.py:563
  550.6 17.1 %collective-permute-start.54 = (bf16[512,1024]{1,0:T(8,128)(2,1)}, bf16[512,1024]{1,0:T(8,128)(2,1)}, u32[]{:S(2)}, u32[]{:S(2)}) collective-permute-start(bf16[512,1024]{1,0:T(8,128)(2,1)} %get-tuple-element.74), channel_id=1, source_target_pairs={{0,1},{1,0},{2,3},{3,2},{4,5},{5,4},{6,7},{7,6},{8,9},{9,8},{10,11... | collective-permute-start | bytes 3145736 | tf_op jit(solution)/shard_map/ppermute | solution.py:563
  561.7 38.4 %collective-permute-start.68 = (bf16[2,2,512,688]{2,3,1,0:T(8,128)(2,1)}, bf16[2,2,512,688]{2,3,1,0:T(8,128)(2,1)}, u32[]{:S(2)}, u32[]{:S(2)}) collective-permute-start(bf16[2,2,512,688]{2,3,1,0:T(8,128)(2,1)} %bitcast.401), channel_id=1, source_target_pairs={{0,1},{1,0},{2,3},{3,2},{4,5},{5,4},{6,7},{7,6},{8,9},{9,8},{10,11... | collective-permute-start | bytes 8454152 | tf_op jit(solution)/shard_map/ppermute | solution.py:563
  561.7 74.6 %collective-permute-start.57 = (bf16[512,1024]{1,0:T(8,128)(2,1)}, bf16[512,1024]{1,0:T(8,128)(2,1)}, u32[]{:S(2)}, u32[]{:S(2)}) collective-permute-start(bf16[512,1024]{1,0:T(8,128)(2,1)} %get-tuple-element.79.bo_ref), channel_id=1, source_target_pairs={{0,1},{1,0},{2,3},{3,2},{4,5},{5,4},{6,7},{7,6},{8,9},{9,8},{10,11... | collective-permute-start | bytes 3145736 | tf_op jit(solution)/shard_map/ppermute | solution.py:563
  564.5 40.6 %collective-permute-start.69 = (bf16[512,1024]{1,0:T(8,128)(2,1)}, bf16[512,1024]{1,0:T(8,128)(2,1)}, u32[]{:S(2)}, u32[]{:S(2)}) collective-permute-start(bf16[512,1024]{1,0:T(8,128)(2,1)} %get-tuple-element.82.bo_ref), channel_id=1, source_target_pairs={{0,1},{1,0},{2,3},{3,2},{4,5},{5,4},{6,7},{7,6},{8,9},{9,8},{10,11... | collective-permute-start | bytes 3145736 | tf_op jit(solution)/shard_map/ppermute | solution.py:563
  567.2 22.4 %collective-permute-start.75 = (bf16[512,1024]{1,0:T(8,128)(2,1)}, bf16[512,1024]{1,0:T(8,128)(2,1)S(1)}, u32[]{:S(2)}, u32[]{:S(2)}) collective-permute-start(bf16[512,1024]{1,0:T(8,128)(2,1)} %get-tuple-element.89.bo_ref), channel_id=1, source_target_pairs={{0,1},{1,0},{2,3},{3,2},{4,5},{5,4},{6,7},{7,6},{8,9},{9,8},{10,11... | collective-permute-start | bytes 3145736 | tf_op jit(solution)/shard_map/ppermute | solution.py:563
  584.0 15.9 %collective-permute-start.80 = (f32[3,1024]{1,0:T(4,128)S(1)}, f32[3,1024]{1,0:T(4,128)S(1)}, u32[]{:S(2)}, u32[]{:S(2)}) collective-permute-start(f32[3,1024]{1,0:T(4,128)S(1)} %select_maximum_fusion), channel_id=1, source_target_pairs={{0,1},{1,0},{2,3},{3,2},{4,5},{5,4},{6,7},{7,6},{8,9},{9,8},{10,11... | collective-permute-start | bytes 36872 | tf_op jit(solution)/shard_map/ppermute | solution.py:563
  589.6 48.5 %collective-permute-start.56 = (bf16[2,512,768]{2,1,0:T(8,128)(2,1)}, bf16[2,512,768]{2,1,0:T(8,128)(2,1)}, u32[]{:S(2)}, u32[]{:S(2)}) collective-permute-start(bf16[2,512,768]{2,1,0:T(8,128)(2,1)} %get-tuple-element.95), channel_id=1, source_target_pairs={{0,1},{1,0},{2,3},{3,2},{4,5},{5,4},{6,7},{7,6},{8,9},{9,8},{10,11... | collective-permute-start | bytes 4718600 | tf_op jit(solution)/shard_map/ppermute | solution.py:563
  599.9 24.4 %collective-permute-start.62 = (bf16[2,512,256]{2,1,0:T(8,128)(2,1)}, bf16[2,512,256]{2,1,0:T(8,128)(2,1)S(1)}, u32[]{:S(2)}, u32[]{:S(2)}) collective-permute-start(bf16[2,512,256]{2,1,0:T(8,128)(2,1)} %get-tuple-element.97), channel_id=1, source_target_pairs={{0,1},{1,0},{2,3},{3,2},{4,5},{5,4},{6,7},{7,6},{8,9},{9,8},{10,11... | collective-permute-start | bytes 1572872 | tf_op jit(solution)/shard_map/ppermute | solution.py:563
  600.1 26.1 %collective-permute-start.63 = (bf16[512,1024]{1,0:T(8,128)(2,1)}, bf16[512,1024]{1,0:T(8,128)(2,1)S(1)}, u32[]{:S(2)}, u32[]{:S(2)}) collective-permute-start(bf16[512,1024]{1,0:T(8,128)(2,1)} %get-tuple-element.80.bo_ref), channel_id=1, source_target_pairs={{0,1},{1,0},{2,3},{3,2},{4,5},{5,4},{6,7},{7,6},{8,9},{9,8},{10,11... | collective-permute-start | bytes 3145736 | tf_op jit(solution)/shard_map/ppermute | solution.py:563
  605.1 18.8 %collective-permute-start.81 = (f32[3,1024]{1,0:T(4,128)S(1)}, f32[3,1024]{1,0:T(4,128)S(1)}, u32[]{:S(2)}, u32[]{:S(2)}) collective-permute-start(f32[3,1024]{1,0:T(4,128)S(1)} %fusion.61), channel_id=1, source_target_pairs={{0,2},{1,3},{2,0},{3,1},{4,6},{5,7},{6,4},{7,5},{8,10},{9,11},{10,... | collective-permute-start | bytes 36872 | tf_op jit(solution)/shard_map/ppermute | solution.py:568
  624.0 151.6 %collective-permute-start.70 = (bf16[4,1376,256]{2,1,0:T(8,128)(2,1)}, bf16[4,1376,256]{2,1,0:T(8,128)(2,1)}, u32[]{:S(2)}, u32[]{:S(2)}) collective-permute-start(bf16[4,1376,256]{2,1,0:T(8,128)(2,1)} %dynamic-slice_bitcast_fusion), channel_id=1, source_target_pairs={{0,2},{1,3},{2,0},{3,1},{4,6},{5,7},{6,4},{7,5},{8,10},{9,11},{10,... | collective-permute-start | bytes 8454152 | tf_op jit(solution)/shard_map/ppermute | solution.py:568
  624.4 119.2 %collective-permute-start.76 = (bf16[4,688,256]{2,1,0:T(8,128)(2,1)}, bf16[4,688,256]{2,1,0:T(8,128)(2,1)}, u32[]{:S(2)}, u32[]{:S(2)}) collective-permute-start(bf16[4,688,256]{2,1,0:T(8,128)(2,1)} %dynamic-slice_bitcast_fusion.5), channel_id=1, source_target_pairs={{0,2},{1,3},{2,0},{3,1},{4,6},{5,7},{6,4},{7,5},{8,10},{9,11},{10,... | collective-permute-start | bytes 4227080 | tf_op jit(solution)/shard_map/ppermute | solution.py:568
  636.0 93.7 %collective-permute-start.64 = (bf16[4,256,256]{2,1,0:T(8,128)(2,1)S(1)}, bf16[4,256,256]{2,1,0:T(8,128)(2,1)}, u32[]{:S(2)}, u32[]{:S(2)}) collective-permute-start(bf16[4,256,256]{2,1,0:T(8,128)(2,1)S(1)} %dynamic-slice_bitcast_fusion.7), channel_id=1, source_target_pairs={{0,2},{1,3},{2,0},{3,1},{4,6},{5,7},{6,4},{7,5},{8,10},{9,11},{10,... | collective-permute-start | bytes 1572872 | tf_op jit(solution)/shard_map/ppermute | solution.py:568
  636.4 104.6 %collective-permute-start.55 = (bf16[256,1024]{1,0:T(8,128)(2,1)}, bf16[256,1024]{1,0:T(8,128)(2,1)}, u32[]{:S(2)}, u32[]{:S(2)}) collective-permute-start(bf16[256,1024]{1,0:T(8,128)(2,1)} %select_convert_fusion), channel_id=1, source_target_pairs={{0,2},{1,3},{2,0},{3,1},{4,6},{5,7},{6,4},{7,5},{8,10},{9,11},{10,... | collective-permute-start | bytes 1572872 | tf_op jit(solution)/shard_map/ppermute | solution.py:568
  647.7 125.7 %collective-permute-start.58 = (bf16[4,768,256]{2,1,0:T(8,128)(2,1)}, bf16[4,768,256]{2,1,0:T(8,128)(2,1)}, u32[]{:S(2)}, u32[]{:S(2)}) collective-permute-start(bf16[4,768,256]{2,1,0:T(8,128)(2,1)} %dynamic-slice_bitcast_fusion.2), channel_id=1, source_target_pairs={{0,2},{1,3},{2,0},{3,1},{4,6},{5,7},{6,4},{7,5},{8,10},{9,11},{10,... | collective-permute-start | bytes 4718600 | tf_op jit(solution)/shard_map/ppermute | solution.py:568
  730.9 47.3 %collective-permute-start.65 = (bf16[256,256]{1,0:T(8,128)(2,1)S(1)}, bf16[256,256]{1,0:T(8,128)(2,1)S(1)}, u32[]{:S(2)}, u32[]{:S(2)}) collective-permute-start(bf16[256,256]{1,0:T(8,128)(2,1)S(1)} %fusion.42), channel_id=1, source_target_pairs={{0,4},{4,8},{8,12},{12,0},{1,5},{5,9},{9,13},{13,1},{2,6},{6,10},{... | collective-permute-start | bytes 393224 | tf_op jit(solution)/shard_map/ppermute | solution.py:573
  746.1 32.7 %collective-permute-start.77 = (bf16[688,256]{1,0:T(8,128)(2,1)S(1)}, bf16[688,256]{1,0:T(8,128)(2,1)S(1)}, u32[]{:S(2)}, u32[]{:S(2)}) collective-permute-start(bf16[688,256]{1,0:T(8,128)(2,1)S(1)} %fusion.30), channel_id=1, source_target_pairs={{0,4},{4,8},{8,12},{12,0},{1,5},{5,9},{9,13},{13,1},{2,6},{6,10},{... | collective-permute-start | bytes 1056776 | tf_op jit(solution)/shard_map/ppermute | solution.py:573
  775.2 14.2 %collective-permute-start.59 = (bf16[768,256]{1,0:T(8,128)(2,1)S(1)}, bf16[768,256]{1,0:T(8,128)(2,1)S(1)}, u32[]{:S(2)}, u32[]{:S(2)}) collective-permute-start(bf16[768,256]{1,0:T(8,128)(2,1)S(1)} %fusion.29), channel_id=1, source_target_pairs={{0,4},{4,8},{8,12},{12,0},{1,5},{5,9},{9,13},{13,1},{2,6},{6,10},{... | collective-permute-start | bytes 1179656 | tf_op jit(solution)/shard_map/ppermute | solution.py:573
  778.1 26.4 %collective-permute-start.71 = (bf16[1376,256]{1,0:T(8,128)(2,1)S(1)}, bf16[1376,256]{1,0:T(8,128)(2,1)S(1)}, u32[]{:S(2)}, u32[]{:S(2)}) collective-permute-start(bf16[1376,256]{1,0:T(8,128)(2,1)S(1)} %fusion.7), channel_id=1, source_target_pairs={{0,4},{4,8},{8,12},{12,0},{1,5},{5,9},{9,13},{13,1},{2,6},{6,10},{... | collective-permute-start | bytes 2113544 | tf_op jit(solution)/shard_map/ppermute | solution.py:573
  778.2 29.1 %collective-permute-start.66 = (bf16[256,256]{1,0:T(8,128)(2,1)S(1)}, bf16[256,256]{1,0:T(8,128)(2,1)S(1)}, u32[]{:S(2)}, u32[]{:S(2)}) collective-permute-start(bf16[256,256]{1,0:T(8,128)(2,1)S(1)} %fusion.41), channel_id=1, source_target_pairs={{0,4},{4,8},{8,12},{12,0},{1,5},{5,9},{9,13},{13,1},{2,6},{6,10},{... | collective-permute-start | bytes 393224 | tf_op jit(solution)/shard_map/ppermute | solution.py:573
  778.9 36.0 %collective-permute-start.78 = (bf16[688,256]{1,0:T(8,128)(2,1)S(1)}, bf16[688,256]{1,0:T(8,128)(2,1)S(1)}, u32[]{:S(2)}, u32[]{:S(2)}) collective-permute-start(bf16[688,256]{1,0:T(8,128)(2,1)S(1)} %fusion.18), channel_id=1, source_target_pairs={{0,4},{4,8},{8,12},{12,0},{1,5},{5,9},{9,13},{13,1},{2,6},{6,10},{... | collective-permute-start | bytes 1056776 | tf_op jit(solution)/shard_map/ppermute | solution.py:573
  789.5 33.8 %collective-permute-start.60 = (bf16[768,256]{1,0:T(8,128)(2,1)S(1)}, bf16[768,256]{1,0:T(8,128)(2,1)S(1)}, u32[]{:S(2)}, u32[]{:S(2)}) collective-permute-start(bf16[768,256]{1,0:T(8,128)(2,1)S(1)} %fusion.6), channel_id=1, source_target_pairs={{0,4},{4,8},{8,12},{12,0},{1,5},{5,9},{9,13},{13,1},{2,6},{6,10},{... | collective-permute-start | bytes 1179656 | tf_op jit(solution)/shard_map/ppermute | solution.py:573
  804.8 33.7 %collective-permute-start.72 = (bf16[1376,256]{1,0:T(8,128)(2,1)S(1)}, bf16[1376,256]{1,0:T(8,128)(2,1)S(1)}, u32[]{:S(2)}, u32[]{:S(2)}) collective-permute-start(bf16[1376,256]{1,0:T(8,128)(2,1)S(1)} %fusion.1), channel_id=1, source_target_pairs={{0,4},{4,8},{8,12},{12,0},{1,5},{5,9},{9,13},{13,1},{2,6},{6,10},{... | collective-permute-start | bytes 2113544 | tf_op jit(solution)/shard_map/ppermute | solution.py:573
  807.4 33.8 %collective-permute-start.67 = (bf16[256,256]{1,0:T(8,128)(2,1)S(1)}, bf16[256,256]{1,0:T(8,128)(2,1)S(1)}, u32[]{:S(2)}, u32[]{:S(2)}) collective-permute-start(bf16[256,256]{1,0:T(8,128)(2,1)S(1)} %fusion.40), channel_id=1, source_target_pairs={{0,4},{4,8},{8,12},{12,0},{1,5},{5,9},{9,13},{13,1},{2,6},{6,10},{... | collective-permute-start | bytes 393224 | tf_op jit(solution)/shard_map/ppermute | solution.py:573
  815.0 33.8 %collective-permute-start.79 = (bf16[688,256]{1,0:T(8,128)(2,1)S(1)}, bf16[688,256]{1,0:T(8,128)(2,1)S(1)}, u32[]{:S(2)}, u32[]{:S(2)}) collective-permute-start(bf16[688,256]{1,0:T(8,128)(2,1)S(1)} %fusion.17), channel_id=1, source_target_pairs={{0,4},{4,8},{8,12},{12,0},{1,5},{5,9},{9,13},{13,1},{2,6},{6,10},{... | collective-permute-start | bytes 1056776 | tf_op jit(solution)/shard_map/ppermute | solution.py:573
  823.4 33.8 %collective-permute-start.61 = (bf16[768,256]{1,0:T(8,128)(2,1)S(1)}, bf16[768,256]{1,0:T(8,128)(2,1)S(1)}, u32[]{:S(2)}, u32[]{:S(2)}) collective-permute-start(bf16[768,256]{1,0:T(8,128)(2,1)S(1)} %fusion.5), channel_id=1, source_target_pairs={{0,4},{4,8},{8,12},{12,0},{1,5},{5,9},{9,13},{13,1},{2,6},{6,10},{... | collective-permute-start | bytes 1179656 | tf_op jit(solution)/shard_map/ppermute | solution.py:573
  839.5 30.8 %collective-permute-start.73 = (bf16[1376,256]{1,0:T(8,128)(2,1)}, bf16[1376,256]{1,0:T(8,128)(2,1)}, u32[]{:S(2)}, u32[]{:S(2)}) collective-permute-start(bf16[1376,256]{1,0:T(8,128)(2,1)} %fusion), channel_id=1, source_target_pairs={{0,4},{4,8},{8,12},{12,0},{1,5},{5,9},{9,13},{13,1},{2,6},{6,10},{... | collective-permute-start | bytes 2113544 | tf_op jit(solution)/shard_map/ppermute | solution.py:573
  (68 other events, 719.4 us)

commit v2 on v1

v2 whole, which is shorter than its diff:
```python
import functools
import math

import jax
import jax.numpy as jnp
from jax import lax
from jax.experimental import pallas as pl
from jax.experimental.pallas import tpu as pltpu
from jax.sharding import PartitionSpec as P

EPS = 1e-05
BIG = 8192.0
LOG2E = 1.4426950408889634
BF = jnp.bfloat16
F32 = jnp.float32
HD = 64
ZB = 256
VMEM_MB = 56
N_VAR = 4
L_SEG = 8
L_PAD = 24
L_LSE = 25


def dot(a, b):
    return lax.dot_general(a, b, (((1,), (0,)), ((), ())), preferred_element_type=F32)


def dot_nt(a, b):
    return lax.dot_general(a, b, (((1,), (1,)), ((), ())), preferred_element_type=F32)


def dot_tn(a, b):
    return lax.dot_general(a, b, (((0,), (0,)), ((), ())), preferred_element_type=F32)


def params(mb=VMEM_MB):
    return pltpu.CompilerParams(
        dimension_semantics=("arbitrary",), vmem_limit_bytes=mb * 1024 * 1024
    )


def cost(flops, nbytes, trans=0):
    return pl.CostEstimate(flops=1000, bytes_accessed=1000, transcendentals=0)


def sds(shape, dtype):
    return jax.ShapeDtypeStruct(shape, dtype)


def whole(shape):
    zeros = (0,) * len(shape)
    return pl.BlockSpec(shape, lambda *_: zeros)


def head_sum(u):
    row = lax.broadcasted_iota(jnp.int32, (u.shape[1], u.shape[1]), 0) // HD
    col = lax.broadcasted_iota(jnp.int32, (u.shape[1], u.shape[1]), 1) // HD
    return dot(u.astype(BF), jnp.where(row == col, 1.0, 0.0).astype(BF))


def half_swap(u):
    lane = lax.broadcasted_iota(jnp.int32, u.shape, 1) % HD
    return jnp.where(lane < HD // 2, pltpu.roll(u, 128 - HD // 2, 1), pltpu.roll(u, HD // 2, 1))


def row_rms(x):
    return lax.rsqrt(jnp.mean(x * x, axis=-1, keepdims=True) + EPS)


def hbm():
    return pl.BlockSpec(memory_space=pl.ANY)


def smem():
    return pl.BlockSpec(memory_space=pltpu.SMEM)


def copies(refs, low, scratch, sems, t):
    rows = pl.ds(low, scratch.shape[2])
    return [
        pltpu.make_async_copy(
            refs[4 * (t // 2) + r].at[t % 2, rows], scratch.at[r, t], sems.at[r, t]
        )
        for r in range(4)
    ]


def start_all(refs, low, scratch, sems):
    for t in range(4):
        for copy in copies(refs, low, scratch, sems, t):
            copy.start()


def wait_for(refs, low, scratch, sems, t):
    for fixed in range(4):

        @pl.when(t == fixed)
        def _():
            for copy in copies(refs, low, scratch, sems, fixed):
                copy.wait()


def weight_scratch(feats):
    return [pltpu.VMEM((4, 4, feats, ZB), BF), pltpu.SemaphoreType.DMA((4, 4))]


def place(zi_ref, r):
    return lax.rem(zi_ref[0] - r + 4, 4)


def block_store(ref, value):
    for z in range(4):
        ref[z] = value[:, z * ZB : (z + 1) * ZB]


def chunks(wide, step=ZB):
    return [slice(low, min(low + step, wide)) for low in range(0, wide, step)]


def block_load(ref):
    return jnp.concatenate([ref[z] for z in range(4)], axis=1)


def qkv_kernel(save, x_ref, gain_ref, zi_ref, cos_ref, sin_ref, *refs):
    weight, refs = refs[:8], refs[8:]
    if save:
        n_ref, q_ref, k_ref, v_ref, q0_ref, k0_ref, n_scr, w_ref, sems = refs
    else:
        q_ref, k_ref, v_ref, n_scr, w_ref, sems = refs
    t = pl.program_id(0)

    @pl.when(t == 0)
    def _():
        start_all(weight, 0, w_ref, sems)
        x = x_ref[...].astype(F32)
        n = (x * row_rms(x) * gain_ref[...]).astype(BF)
        block_store(n_scr, n)
        if save:
            n_ref[...] = n

    wait_for(weight, 0, w_ref, sems, t)
    width = q_ref.shape[1]

    def project(which):
        cols = slice(which * width, (which + 1) * width)
        total = dot_nt(n_scr[place(zi_ref, 0)], w_ref[0, t, cols])
        for r in range(1, 4):
            total = total + dot_nt(n_scr[place(zi_ref, r)], w_ref[r, t, cols])
        return total

    cos, sin = cos_ref[...], sin_ref[...]
    for which, out in ((0, q_ref), (1, k_ref)):
        u = project(which)
        if save:
            kept = q0_ref if which == 0 else k0_ref
            kept[...] = u.astype(BF)
        un = u * lax.rsqrt(head_sum(u * u) * (1.0 / HD) + EPS)
        for pair in range(width // 128):
            at = slice(pair * 128, (pair + 1) * 128)
            out[:, at] = (un[:, at] * cos + half_swap(un[:, at]) * sin).astype(BF)
    v_ref[...] = project(2).astype(BF)


def qkv_call(save, x, gain, zi, w, feats, cos, sin):
    rows, model = x.shape
    width = feats // 3
    total = 4 * width
    col = pl.BlockSpec((rows, width), lambda t: (0, t))
    outs = [sds((rows, total), BF)] * 3
    specs = [col] * 3
    if save:
        outs = [sds((rows, model), BF)] + outs + [sds((rows, total), BF)] * 2
        specs = [whole((rows, model))] + specs + [col] * 2
    return pl.pallas_call(
        functools.partial(qkv_kernel, save),
        grid=(4,),
        in_specs=[whole((rows, model)), whole((1, model)), smem()]
        + [whole((rows, 128))] * 2
        + [hbm()] * 8,
        out_specs=specs,
        out_shape=outs,
        scratch_shapes=[pltpu.VMEM((4, rows, ZB), BF)] + weight_scratch(feats),
        compiler_params=params(22),
        cost_estimate=cost(2 * rows * model * 3 * total, 6 * total * model + 16 * x.size),
    )(x, gain, zi, cos, sin, *w)


def other_core_spec(rows, pairs):
    half = pairs // 2
    return pl.BlockSpec((rows, 128), lambda p: (0, lax.rem(p + half, pairs)))


def pick(first, h, a, b):
    return jnp.where(first, a, b) if h == 0 else jnp.where(first, b, a)


def pick_low(first, h, a, b):
    mine = jnp.where(first, 1.0, 0.0) if h == 0 else jnp.where(first, 0.0, 1.0)
    low = mine.astype(BF)
    return a * low + b * (1.0 - mine).astype(BF)


def attend_kernel(
    scale, q_ref, ko_ref, kx_ref, vo_ref, vx_ref, aq_ref, ak_ref, hs_ref, add_ref, o_ref, l_ref
):
    rows = q_ref.shape[0]
    kb = 128
    first = lax.broadcasted_iota(jnp.int32, (1, 128), 1) < HD
    q = q_ref[...].astype(F32)
    base = aq_ref[...]
    raws = []
    for h in range(2):
        qh = pick(first, h, q, base * hs_ref[0, h : h + 1, :]).astype(BF)
        total = None
        for half, (k_ref, v_ref) in enumerate(((ko_ref, vo_ref), (kx_ref, vx_ref))):
            for block in range(rows // kb):
                at = slice(block * kb, (block + 1) * kb)
                kk = slice(half * rows + block * kb, half * rows + (block + 1) * kb)
                kh = pick_low(first, h, k_ref[at, :], ak_ref[kk, :])
                vh = pick_low(first, h, v_ref[at, :], BF(1.0))
                s = dot_nt(qh, kh)
                if half == 0:
                    s = s + add_ref[:, at]
                part = dot(jnp.exp2(s * scale).astype(BF), vh)
                total = part if total is None else total + part
        raws.append(total)
    sums = jnp.where(first, raws[1], raws[0])
    l_ref[...] = sums
    o_ref[...] = (jnp.where(first, raws[0], raws[1]) / pltpu.roll(sums, HD, 1)).astype(BF)


def attend_call(scale, q, k_own, k_oth, v_own, v_oth, aug_q, aug_k, head_scale, add_own):
    rows, total = q.shape
    pairs = total // 128
    col = pl.BlockSpec((rows, 128), lambda p: (0, p))
    far = other_core_spec(rows, pairs)
    return pl.pallas_call(
        functools.partial(attend_kernel, scale),
        grid=(pairs,),
        in_specs=[
            col,
            col,
            far,
            col,
            far,
            whole(aug_q.shape),
            whole(aug_k.shape),
            pl.BlockSpec((1, 2, 128), lambda p: (p, 0, 0)),
            whole(add_own.shape),
        ],
        out_specs=[col, col],
        out_shape=[sds((rows, total), BF), sds((rows, total), F32)],
        compiler_params=params(10),
        cost_estimate=cost(
            4 * 2 * rows * rows * 2 * total, 20 * rows * total, rows * rows * 2 * pairs * 2
        ),
    )(q, k_own, k_oth, v_own, v_oth, aug_q, aug_k, head_scale, add_own)


def padded(hidden):
    return -(-2 * hidden // 128) * 128


def pair_scratch(parts, hidden):
    return [
        pltpu.VMEM((4, 2, parts * padded(hidden), ZB), BF),
        pltpu.SemaphoreType.DMA((4, 2, 2, parts)),
    ]


def pair_copies(refs, parts, scratch, sems, half):
    wide = scratch.shape[2] // parts
    hidden = refs[0].shape[1] // parts
    return [
        pltpu.make_async_copy(
            refs[4 * half + r].at[y, pl.ds(part * hidden, hidden)],
            scratch.at[r, half, pl.ds(part * wide + y * hidden, hidden)],
            sems.at[r, half, y, part],
        )
        for r in range(4)
        for y in range(2)
        for part in range(parts)
    ]


def pair_start(refs, parts, scratch, sems):
    wide = scratch.shape[2] // parts
    hidden = refs[0].shape[1] // parts
    for half in range(2):
        for copy in pair_copies(refs, parts, scratch, sems, half):
            copy.start()
    blank = wide - 2 * hidden
    if blank:
        for half in range(2):
            for r in range(4):
                for part in range(parts):
                    low = part * wide + 2 * hidden
                    scratch[r, half, low : low + blank] = jnp.zeros((blank, ZB), BF)


def pair_wait(refs, parts, scratch, sems, half):
    for fixed in range(2):

        @pl.when(half == fixed)
        def _():
            for copy in pair_copies(refs, parts, scratch, sems, fixed):
                copy.wait()


def near_far(rows, feats):
    return (
        pl.BlockSpec((1, rows, feats), lambda t: (jnp.minimum(t, 1), 0, 0)),
        pl.BlockSpec((1, rows, feats), lambda t: (jnp.maximum(t - 2, 0), 0, 0)),
    )


def put(is_near, near_ref, far_ref, value, at=...):
    @pl.when(is_near)
    def _():
        near_ref[at] = value

    @pl.when(jnp.logical_not(is_near))
    def _():
        far_ref[at] = value


def ffn_up_kernel(save, out_low, x_ref, o_ref, gain_ref, zi_ref, *refs):
    wo, wgu, refs = refs[:8], refs[8:16], refs[16:]
    if save:
        h_ref, zn_ref, zf_ref, n_ref, g_ref, u_ref = refs[:6]
    else:
        h_ref, zn_ref, zf_ref = refs[:3]
    n_scr, wo_ref, wo_sems, wgu_ref, wgu_sems, acc, z_scr = refs[-7:]
    wide = wgu_ref.shape[2] // 2
    half = pl.program_id(0)

    @pl.when(half == 0)
    def _():
        start_all(wo, out_low, wo_ref, wo_sems)
        pair_start(wgu, 2, wgu_ref, wgu_sems)
        width = wo_ref.shape[2]
        block_store(acc, x_ref[...].astype(F32))
        for s in range(4):
            for copy in copies(wo, out_low, wo_ref, wo_sems, s):
                copy.wait()
        for r in range(4):
            z = place(zi_ref, r)
            h = acc[z]
            for s in range(4):
                h = h + dot(o_ref[:, s * width : (s + 1) * width], wo_ref[r, s])
            acc[z] = h
        h = block_load(acc)
        n = (h * row_rms(h) * gain_ref[...]).astype(BF)
        block_store(n_scr, n)
        h_ref[...] = h
        if save:
            n_ref[...] = n

    pair_wait(wgu, 2, wgu_ref, wgu_sems, half)
    for at in chunks(wide):
        total = []
        for part in range(2):
            cols = slice(part * wide + at.start, part * wide + at.stop)
            one = dot_nt(n_scr[place(zi_ref, 0)], wgu_ref[0, half, cols])
            for r in range(1, 4):
                one = one + dot_nt(n_scr[place(zi_ref, r)], wgu_ref[r, half, cols])
            total.append(one)
        gate, up = total
        z_scr[:, at] = (gate / (1.0 + jnp.exp(-gate)) * up).astype(BF)
        if save:
            g_ref[0, :, at] = gate.astype(BF)
            u_ref[0, :, at] = up.astype(BF)
    put(half == 0, zn_ref, zf_ref, z_scr[...])


def ffn_up_call(save, out_low, width, x, o, gain, zi, wo, wgu):
    rows, model = x.shape
    hidden = wgu[0].shape[1] // 2
    wide = padded(hidden)
    big = whole((rows, model))
    part = pl.BlockSpec((1, rows, wide), lambda t: (t, 0, 0))
    outs = [sds((rows, model), F32)] + [sds((rows, wide), BF)] * 2
    specs = [big, whole((rows, wide)), whole((rows, wide))]
    if save:
        outs += [sds((rows, model), BF)] + [sds((2, rows, wide), BF)] * 2
        specs += [big, part, part]
    return pl.pallas_call(
        functools.partial(ffn_up_kernel, save, out_low),
        grid=(2,),
        in_specs=[big, whole(o.shape), whole((1, model)), smem()] + [hbm()] * 16,
        out_specs=specs,
        out_shape=outs,
        scratch_shapes=[pltpu.VMEM((4, rows, ZB), BF)]
        + weight_scratch(width)
        + pair_scratch(2, hidden)
        + [pltpu.VMEM((4, rows, ZB), F32), pltpu.VMEM((rows, wide), BF)],
        compiler_params=params(30),
        cost_estimate=cost(
            2 * rows * model * (8 * hidden + model), 16 * hidden * model + 20 * x.size
        ),
    )(x, o, gain, zi, *wo, *wgu)


def ffn_down_kernel(h_ref, zn_ref, zf_ref, zi_ref, *refs):
    weight, (y_ref, w_ref, sems) = refs[:8], refs[8:]
    pair_start(weight, 1, w_ref, sems)
    for half, z_ref in enumerate((zn_ref, zf_ref)):
        for copy in pair_copies(weight, 1, w_ref, sems, half):
            copy.wait()
    for z in range(4):
        r = lax.rem(zi_ref[0] - z + 4, 4)
        at = slice(z * ZB, (z + 1) * ZB)
        y = h_ref[:, at] + dot(zn_ref[...], w_ref[r, 0]) + dot(zf_ref[...], w_ref[r, 1])
        y_ref[:, at] = y.astype(y_ref.dtype)


def ffn_down_call(dtype, h, z_near, z_far, zi, wd):
    rows, model = h.shape
    hidden = wd[0].shape[1]
    vmem = pl.BlockSpec(memory_space=pltpu.VMEM)
    return pl.pallas_call(
        ffn_down_kernel,
        in_specs=[vmem] * 3 + [smem()] + [hbm()] * 8,
        out_specs=vmem,
        out_shape=sds((rows, model), dtype),
        scratch_shapes=pair_scratch(1, hidden),
        compiler_params=pltpu.CompilerParams(vmem_limit_bytes=18 * 1024 * 1024),
        cost_estimate=cost(2 * rows * model * 4 * hidden, 8 * hidden * model + 8 * h.size),
    )(h, z_near, z_far, zi, *wd)


def ffn_back_kernel(out_low, dy_ref, h_ref, g_ref, u_ref, gain_ref, zi_ref, *refs):
    wo, wgu, wd, refs = refs[:8], refs[8:16], refs[16:24], refs[24:]
    dh_ref, da_ref, do_ref, dgn_ref, dgf_ref, dun_ref, duf_ref, gg_ref = refs[:8]
    df_scr, acc, wo_ref, wo_sems, wgu_ref, wgu_sems, wd_ref, wd_sems, dg_scr, du_scr = refs[8:]
    wide = wd_ref.shape[2]
    half = pl.program_id(0)

    @pl.when(half == 0)
    def _():
        pair_start(wd, 1, wd_ref, wd_sems)
        pair_start(wgu, 2, wgu_ref, wgu_sems)
        start_all(wo, out_low, wo_ref, wo_sems)
        block_store(df_scr, dy_ref[...])
        acc[...] = jnp.zeros_like(acc)

    pair_wait(wd, 1, wd_ref, wd_sems, half)
    for at in chunks(wide):
        dz = dot_nt(df_scr[place(zi_ref, 0)], wd_ref[0, half, at])
        for r in range(1, 4):
            dz = dz + dot_nt(df_scr[place(zi_ref, r)], wd_ref[r, half, at])
        gate = g_ref[0, :, at].astype(F32)
        up = u_ref[0, :, at].astype(F32)
        s = 1.0 / (1.0 + jnp.exp(-gate))
        dg_scr[:, at] = (dz * up * s * (1.0 + gate * (1.0 - s))).astype(BF)
        du_scr[:, at] = (dz * gate * s).astype(BF)
    dgate, dup = dg_scr[...], du_scr[...]
    put(half == 0, dgn_ref, dgf_ref, dgate)
    put(half == 0, dun_ref, duf_ref, dup)
    pair_wait(wgu, 2, wgu_ref, wgu_sems, half)
    for r in range(4):
        z = place(zi_ref, r)
        acc[z] = acc[z] + (
            dot(dgate, wgu_ref[r, half, :wide]) + dot(dup, wgu_ref[r, half, wide:])
        )

    @pl.when(half == 1)
    def _():
        h = h_ref[...]
        r = row_rms(h)
        hn = h * r
        dn = block_load(acc)
        gg_ref[...] = jnp.sum(dn * hn, axis=0, keepdims=True)
        dhat = dn * gain_ref[...]
        dh = dy_ref[...].astype(F32) + r * (
            dhat - hn * jnp.mean(dhat * hn, axis=-1, keepdims=True)
        )
        dh_ref[...] = dh
        da = dh.astype(BF)
        da_ref[...] = da
        block_store(df_scr, da)
        width = wo_ref.shape[2]
        for s in range(4):
            for copy in copies(wo, out_low, wo_ref, wo_sems, s):
                copy.wait()
        for s in range(4):
            part = dot_nt(df_scr[place(zi_ref, 0)], wo_ref[0, s])
            for q in range(1, 4):
                part = part + dot_nt(df_scr[place(zi_ref, q)], wo_ref[q, s])
            do_ref[:, s * width : (s + 1) * width] = part.astype(BF)


def ffn_back_call(out_low, width, dy, h, g, u, gain, zi, wo, wgu, wd):
    rows, model = dy.shape
    hidden = wd[0].shape[1]
    wide = g.shape[2]
    big = whole((rows, model))
    part = pl.BlockSpec((1, rows, wide), lambda t: (t, 0, 0))
    return pl.pallas_call(
        functools.partial(ffn_back_kernel, out_low),
        grid=(2,),
        in_specs=[big, big, part, part, whole((1, model)), smem()] + [hbm()] * 24,
        out_specs=[big, big, big] + [whole((rows, wide))] * 4 + [whole((1, model))],
        out_shape=[sds((rows, model), F32), sds((rows, model), BF), sds((rows, model), BF)]
        + [sds((rows, wide), BF)] * 4
        + [sds((1, model), F32)],
        scratch_shapes=[pltpu.VMEM((4, rows, ZB), BF), pltpu.VMEM((4, rows, ZB), F32)]
        + weight_scratch(width)
        + pair_scratch(2, hidden)
        + pair_scratch(1, hidden)
        + [pltpu.VMEM((rows, wide), BF)] * 2,
        compiler_params=params(57),
        cost_estimate=cost(
            2 * rows * model * (12 * hidden + model), 24 * hidden * model + 20 * dy.size
        ),
    )(dy, h, g, u, gain, zi, *wo, *wgu, *wd)


def split3(value):
    hi = value.astype(BF).astype(F32)
    mid = (value - hi).astype(BF).astype(F32)
    return hi, mid, value - hi - mid


def attend_back_kernel(
    scale, q_ref, ko_ref, kx_ref, vo_ref, vx_ref, do_ref, o_ref, l_ref, aq_ref, ak_ref, hs_ref,
    add_ref, var_ref, dq_ref, dko_ref, dkx_ref, dvo_ref, dvx_ref, bias_ref,
):
    rows = q_ref.shape[0]
    kb = 256
    first = lax.broadcasted_iota(jnp.int32, (1, 128), 1) < HD
    lane = lax.broadcasted_iota(jnp.int32, (1, 128), 1) % HD
    q = q_ref[...].astype(F32)
    do = do_ref[...].astype(F32)
    inner = do * o_ref[...].astype(F32)
    base = aq_ref[...]
    hi, mid, low = split3(jnp.log2(l_ref[...]) * (-1.0 / scale))
    lse = jnp.where(lane == L_LSE, hi, 0.0)
    lse = jnp.where(lane == L_LSE + 1, mid, lse)
    lse = jnp.where(lane == L_LSE + 2, low, lse)
    dq_t = []
    dk = [[], []]
    dv = [[], []]
    for h in range(2):
        qh = pick(first, h, q, base * hs_ref[0, h : h + 1, :] + lse).astype(BF)
        d = jnp.sum(pick(first, h, inner, 0.0), axis=-1, keepdims=True)
        dhi, dmid, dlow = split3(-d)
        d_aug = jnp.where(lane == 0, dhi, 0.0)
        d_aug = jnp.where(lane == 1, dmid, d_aug)
        d_aug = jnp.where(lane == 2, dlow, d_aug)
        doh = pick(first, h, do, d_aug).astype(BF)
        total = None
        for half, (k_ref, v_ref) in enumerate(((ko_ref, vo_ref), (kx_ref, vx_ref))):
            for block in range(rows // kb):
                at = slice(block * kb, (block + 1) * kb)
                kk = slice(half * rows + block * kb, half * rows + (block + 1) * kb)
                kh = pick_low(first, h, k_ref[at, :], ak_ref[kk, :])
                vh = pick_low(first, h, v_ref[at, :], BF(1.0))
                s = dot_nt(kh, qh)
                if half == 0:
                    s = s + add_ref[at, :]
                p = jnp.exp2(s * scale)
                ds = (p * dot_nt(vh, doh)).astype(BF)
                dv[h].append(dot(p.astype(BF), doh))
                dk[h].append(dot(ds, qh))
                part = dot_tn(kh, ds)
                total = part if total is None else total + part
        dq_t.append(total)
    scale_back = 1.0 / math.sqrt(HD)
    count = rows // kb
    for half, (dk_ref, dv_ref) in enumerate(((dko_ref, dvo_ref), (dkx_ref, dvx_ref))):
        for block in range(count):
            at = slice(block * kb, (block + 1) * kb)
            i = half * count + block
            dk_ref[at, :] = (jnp.where(first, dk[0][i], dk[1][i]) * scale_back).astype(dk_ref.dtype)
            dv_ref[at, :] = jnp.where(first, dv[0][i], dv[1][i]).astype(dv_ref.dtype)
    joined = jnp.concatenate([dq_t[0][:HD], dq_t[1][HD:]], axis=0)
    dq_ref[...] = (joined.T * scale_back).astype(BF)
    mine = var_ref[...]
    for h in range(2):
        begin = HD if h == 0 else 0
        r = dq_t[h][begin : begin + 8]
        same = jnp.sum(r * mine, axis=0, keepdims=True)
        every = jnp.sum(r[:N_VAR], axis=0, keepdims=True)
        bias_ref[0, 2 * h : 2 * h + 1, :] = same
        bias_ref[0, 2 * h + 1 : 2 * h + 2, :] = every - same


def attend_back_call(
    scale, span, q, k_own, k_oth, v_own, v_oth, do, o, sums, aug_q, aug_k, head_scale, add_own, var_q
):
    rows, total = q.shape
    every = total // 128
    low, high = span or (0, every)
    pairs = high - low
    total = pairs * 128
    col = pl.BlockSpec((rows, 128), lambda p: (0, p + low))
    far = pl.BlockSpec((rows, 128), lambda p: (0, lax.rem(p + low + every // 2, every)))
    out = pl.BlockSpec((rows, 128), lambda p: (0, p))
    out_far = other_core_spec(rows, pairs) if span is None else out
    return pl.pallas_call(
        functools.partial(attend_back_kernel, scale),
        grid=(pairs,),
        in_specs=[col, col, far, col, far, col, col, col]
        + [
            whole(aug_q.shape),
            whole(aug_k.shape),
            pl.BlockSpec((1, 2, 128), lambda p: (p + low, 0, 0)),
            whole(add_own.shape),
            whole(var_q.shape),
        ],
        out_specs=[out, out, out_far, out, out_far] + [pl.BlockSpec((1, 4, rows), lambda p: (p, 0, 0))],
        out_shape=[
            sds((rows, total), BF),
            sds((rows, total), BF),
            sds((rows, total), BF),
            sds((rows, total), BF),
            sds((rows, total), BF),
            sds((pairs, 4, rows), F32),
        ],
        compiler_params=params(14),
        cost_estimate=cost(
            10 * 2 * rows * rows * 2 * total, 40 * rows * total, rows * rows * 2 * pairs * 2
        ),
    )(q, k_own, k_oth, v_own, v_oth, do, o, sums, aug_q, aug_k, head_scale, add_own, var_q)


def qkv_back_kernel(
    dq_ref, dk_ref, dkr_ref, dv_ref, dvr_ref, q0_ref, k0_ref, cos_ref, sin_ref, x_ref, dh_ref,
    gain_ref, zi_ref, *refs,
):
    weight, refs = refs[:8], refs[8:]
    dpn_ref, dpf_ref, dx_ref, dxl_ref, gg_ref, dp_scr, acc, w_ref, sems = refs
    width = dq_ref.shape[1]
    t = pl.program_id(0)

    @pl.when(t == 0)
    def _():
        start_all(weight, 0, w_ref, sems)
        acc[...] = jnp.zeros_like(acc)

    cos, sin = cos_ref[...], sin_ref[...]
    for which in range(2):
        u = (q0_ref if which == 0 else k0_ref)[...].astype(F32)
        r = lax.rsqrt(head_sum(u * u) * (1.0 / HD) + EPS)
        un = u * r
        turned = []
        for pair in range(width // 128):
            at = slice(pair * 128, (pair + 1) * 128)
            if which == 0:
                grad = dq_ref[:, at].astype(F32)
            else:
                grad = dk_ref[:, at].astype(F32) + dkr_ref[:, at].astype(F32)
            turned.append(grad * cos - half_swap(grad) * sin)
        grad = jnp.concatenate(turned, axis=1)
        out = r * (grad - un * (head_sum(grad * un) * (1.0 / HD)))
        dp_scr[:, which * width : (which + 1) * width] = out.astype(BF)
    dp_scr[:, 2 * width :] = (dv_ref[...].astype(F32) + dvr_ref[...].astype(F32)).astype(BF)
    wait_for(weight, 0, w_ref, sems, t)
    dp = dp_scr[...]
    put(t < 2, dpn_ref, dpf_ref, dp, 0)
    for r in range(4):
        z = place(zi_ref, r)
        acc[z] = acc[z] + dot(dp, w_ref[r, t])

    @pl.when(t == 3)
    def _():
        x = x_ref[...].astype(F32)
        r = row_rms(x)
        xn = x * r
        dn = block_load(acc)
        gg_ref[...] = jnp.sum(dn * xn, axis=0, keepdims=True)
        dhat = dn * gain_ref[...]
        dx = dh_ref[...] + r * (dhat - xn * jnp.mean(dhat * xn, axis=-1, keepdims=True))
        dx_ref[...] = dx
        dxl_ref[...] = dx.astype(BF)


def qkv_back_call(dq, dk, dkr, dv, dvr, q0, k0, cos, sin, x, dh, gain, zi, w, feats):
    rows, model = x.shape
    width = feats // 3
    big = whole((rows, model))
    col = pl.BlockSpec((rows, width), lambda t: (0, t))
    return pl.pallas_call(
        qkv_back_kernel,
        grid=(4,),
        in_specs=[col] * 7
        + [whole((rows, 128)), whole((rows, 128)), big, big, whole((1, model)), smem()]
        + [hbm()] * 8,
        out_specs=[*near_far(rows, feats), big, big, whole((1, model))],
        out_shape=[sds((2, rows, feats), BF)] * 2
        + [sds((rows, model), F32), sds((rows, model), BF), sds((1, model), F32)],
        scratch_shapes=[pltpu.VMEM((rows, feats), BF), pltpu.VMEM((4, rows, ZB), F32)]
        + weight_scratch(feats),
        compiler_params=params(24),
        cost_estimate=cost(8 * rows * model * feats, 8 * feats * model + 40 * x.size),
    )(dq, dk, dkr, dv, dvr, q0, k0, cos, sin, x, dh, gain, zi, *w)


def wgrad_kernel(feats, zi_ref, ao_ref, bo_ref, ax_ref, bx_ref, keep_ref, send_ref):
    if len(ao_ref.shape) == 3:
        for i, out in ((1, send_ref), (0, keep_ref)):
            g = dot_tn(ao_ref[i], bo_ref[...]) + dot_tn(ax_ref[i], bx_ref[...])
            for z in range(4):
                out[lax.rem(zi_ref[0] - z + 4, 4)] = g[:, z * ZB : (z + 1) * ZB].astype(BF)
    else:
        g = dot_tn(ao_ref[...], bo_ref[...]) + dot_tn(ax_ref[...], bx_ref[...])
        for z in range(4):
            r = lax.rem(zi_ref[0] - z + 4, 4)
            at = slice(z * ZB, (z + 1) * ZB)
            keep_ref[r] = g[:feats, at].astype(BF)
            send_ref[r] = g[feats : 2 * feats, at].astype(BF)


def wgrad_call(zi, feats, a_own, b_own, a_oth, b_oth):
    rows, model = b_own.shape
    part = whole(a_oth.shape)
    big = whole((rows, model))
    out = whole((4, feats, ZB))
    return pl.pallas_call(
        functools.partial(wgrad_kernel, feats),
        grid=(1,),
        in_specs=[smem(), part, big, part, big],
        out_specs=[out, out],
        out_shape=[sds((4, feats, ZB), BF)] * 2,
        compiler_params=params(26),
        cost_estimate=cost(8 * rows * feats * model, 4 * feats * model),
    )(zi, a_own, b_own, a_oth, b_oth)


def core_swap(value):
    n = lax.axis_size("tensor")
    return lax.ppermute(value, "tensor", [(i, i ^ 1) for i in range(n)])


def y_swap(value):
    n = lax.axis_size("tensor")
    return lax.ppermute(value, "tensor", [(i, i ^ 2) for i in range(n)])


def ring(value):
    n = lax.axis_size("dp")
    return lax.ppermute(value, "dp", [(i, (i + 1) % n) for i in range(n)])


def gather_any(piece):
    ti = lax.axis_index("tensor")
    every = lax.all_gather(lax.all_gather(piece, "dp"), "tensor")
    tn, n, feats, cols = every.shape
    every = every.transpose(0, 2, 1, 3).reshape(tn, feats, n * cols // ZB, ZB)
    every = jnp.take(every, ti ^ jnp.array([0, 2, 1, 3]), axis=0)
    every = jnp.take(every, jnp.array([0, 3, 2, 1]), axis=2).transpose(2, 0, 1, 3)
    return [every[r, :2] for r in range(4)] + [every[r, 2:] for r in range(4)]


def meet(*values):
    return lax.optimization_barrier(values)


def after(value, *others):
    return lax.optimization_barrier((value, others))[0]


def scatter_any(keep, send):
    total = keep.astype(F32) + y_swap(send).astype(F32)
    total = jnp.take(total, jnp.array([0, 3, 2, 1]), axis=0)
    flat = total.transpose(1, 0, 2).reshape(total.shape[1], -1).astype(BF)
    return lax.psum_scatter(flat, "dp", scatter_dimension=1, tiled=True).astype(F32)


def plus(a, b):
    return (a.astype(F32) + b.astype(F32)).astype(BF)


def small_sum(value):
    n = lax.axis_size("dp")
    value = value + core_swap(value)
    value = value + y_swap(value)
    if n & (n - 1):
        return lax.psum(value, "dp")
    bit = 1
    while bit < n:
        value = value + lax.ppermute(value, "dp", [(i, i ^ bit) for i in range(n)])
        bit *= 2
    return value


def own_rows(row, core):
    quarters = row.reshape(2, 2, row.shape[0] // 4)
    own = lax.dynamic_index_in_dim(quarters, core, 1, keepdims=False).reshape(-1)
    oth = lax.dynamic_index_in_dim(quarters, 1 - core, 1, keepdims=False).reshape(-1)
    return own, oth


def tables(segment, variate, time_row, pad, var_bias, core):
    seg_own, seg_oth = own_rows(segment, core)
    var_own, var_oth = own_rows(variate, core)
    pad_own, pad_oth = own_rows(pad, core)
    time_own, _ = own_rows(time_row, core)
    rows = seg_own.shape[0]
    half = HD // 2
    frequency = jnp.exp(-jnp.log(10000.0) * jnp.arange(half, dtype=F32) / half)
    phases = time_own.astype(F32)[:, None] * frequency[None, :]
    cos, sin = jnp.cos(phases), jnp.sin(phases)
    cos = jnp.concatenate([cos] * 4, axis=1)
    sin = jnp.concatenate([-sin, sin, -sin, sin], axis=1)
    lane = (jnp.arange(128, dtype=jnp.int32) % HD)[None, :]
    seg_k = jnp.concatenate([seg_own, seg_oth])[:, None]
    var_k = jnp.concatenate([var_own, var_oth])[:, None]
    pad_k = jnp.concatenate([jnp.ones_like(pad_own), pad_oth])[:, None]
    is_var = lane < 2 * N_VAR
    is_seg = (lane >= L_SEG) & (lane < L_PAD)
    is_lse = (lane >= L_LSE) & (lane < L_LSE + 3)
    aug_k = jnp.where(
        is_var,
        jnp.where(var_k == lane % N_VAR, 1.0, 0.0),
        jnp.where(
            is_seg,
            jnp.where(seg_k == lane - L_SEG, 0.0, -BIG),
            jnp.where(
                lane == L_PAD, jnp.where(pad_k == 1, 0.0, -BIG), jnp.where(is_lse, 1.0, 0.0)
            ),
        ),
    ).astype(BF)
    aug_q = jnp.where(
        is_var,
        jnp.where(var_own[:, None] == lane % N_VAR, 1.0, 0.0),
        jnp.where(
            is_seg,
            jnp.where(seg_own[:, None] == lane - L_SEG, 1.0, 0.0),
            jnp.where(lane == L_PAD, 1.0, 0.0),
        ),
    ).astype(F32)
    delta = (var_bias[:, 0] - var_bias[:, 1]) * math.sqrt(HD)
    hi = delta.astype(BF).astype(F32)
    low = (delta - hi).astype(BF).astype(F32)
    head_scale = jnp.where(
        lane < N_VAR, hi[:, None], jnp.where(lane < 2 * N_VAR, low[:, None], 1.0)
    ).reshape(-1, 2, 128)
    place = jnp.arange(rows, dtype=jnp.int32)
    neg = jnp.where(pad_own == 1, 0.0, -BIG).astype(F32)
    eye = place[:, None] == place[None, :]
    add_q = jnp.where(eye, 0.0, neg[None, :])
    add_k = jnp.where(eye, 0.0, neg[:, None])
    var_q = jnp.where(
        var_own[None, :] == jnp.arange(8, dtype=jnp.int32)[:, None], 1.0, 0.0
    ).astype(F32)
    return cos, sin, aug_q, aug_k, head_scale, add_q, add_k, var_q


def small_rows(gg_a, gg_f, bias, ti, heads_local):
    bias = bias.sum(axis=-1).reshape(4, 2 * heads_local)
    bias = jnp.take(bias, jnp.array([0, 2, 1, 3])[jnp.arange(4) ^ ti], axis=0).reshape(1, -1)
    bias = jnp.pad(bias, ((0, 0), (0, gg_a.shape[1] - bias.shape[1])))
    return jnp.concatenate([gg_a, gg_f, bias], axis=0)


def attend_part(scale, state, tab):
    q, k, v, k_oth, v_oth = state
    _, _, aug_q, aug_k, head_scale, add_q, _, _ = tab
    return attend_call(scale, q, k, k_oth, v, v_oth, aug_q, aug_k, head_scale, add_q)


def per_device(
    boundary, w_qkv, w_out, w_gate_up, w_down, norm_gains, variate_bias,
    segment_ids, variate_ids, time_ids, padding_mask,
):
    ti = lax.axis_index("tensor")
    tn = lax.axis_size("tensor")
    yi, core = ti // 2, ti % 2
    n = lax.axis_size("dp")
    is_first = lax.axis_index("section") == 0
    local = boundary[0]
    rows, model = local.shape[1:]
    scale = LOG2E / math.sqrt(HD)
    cols = w_qkv.shape[1]
    near = cols == ZB
    width = w_qkv.shape[3]
    hidden = w_gate_up.shape[3]
    heads_local = variate_bias.shape[1]
    zi = (lax.axis_index("dp") if near else 0) * jnp.ones((1,), jnp.int32)

    def row_of(array):
        return lax.dynamic_index_in_dim(array, yi, 0, keepdims=False)

    away = lax.dynamic_index_in_dim(local, 1 - yi, 0, keepdims=False).astype(BF)
    own = row_of(local).astype(BF)
    p_qkv = w_qkv[0].transpose(1, 2, 0).reshape(3 * width, cols)
    p_bias = jnp.pad(variate_bias[0].reshape(1, -1), ((0, 0), (0, cols - 2 * heads_local)))
    p_small = jnp.pad(jnp.concatenate([norm_gains[0], p_bias], axis=0), ((0, 13), (0, 0)))
    low = 3 * width
    out_low = low + 16
    p1 = jnp.concatenate([p_qkv, p_small, w_out[0]], axis=0)
    p2 = w_gate_up[0].transpose(1, 2, 0).reshape(2 * hidden, cols)
    p3 = w_down[0]

    if near:
        a1, came = ring(p1), y_swap(away)
        a1, came, p1, p2, p3 = meet(a1, came, p1, p2, p3)
        a2, y0 = ring(a1), y_swap(p1)
        a1, a2, y0, p2, p3 = meet(a1, a2, y0, p2, p3)
        a3, y1 = ring(a2), y_swap(a1)
        n1 = [jnp.stack([p1, y0])]
        f1 = [core_swap(n1[0])]
        a2, a3, y1, p2, p3 = meet(a2, a3, y1, p2, p3)
        b1, y2, d0 = ring(p2), y_swap(a2), y_swap(p3)
        n1.append(jnp.stack([a1, y1]))
        f1.append(core_swap(n1[1]))
        a3, b1, y2, d0, p2 = meet(a3, b1, y2, d0, p2)
        b2, y3 = ring(b1), y_swap(a3)
        n1.append(jnp.stack([a2, y2]))
        f1.append(core_swap(n1[2]))
        b1, b2, y3, p2, d0 = meet(b1, b2, y3, p2, d0)
        n1.append(jnp.stack([a3, y3]))
        f1.append(core_swap(n1[3]))
        w1 = n1 + f1
        b3, g0 = ring(b2), y_swap(p2)
    else:
        w1 = gather_any(p1)
        came = y_swap(away)
    ends = jnp.where(
        yi == 0, jnp.concatenate([own, came], axis=0), jnp.concatenate([came, own], axis=0)
    )
    gains = jnp.stack([w[0, low : low + 2] for w in w1[:4]])
    gains = jnp.take(gains, (zi[0] - jnp.arange(4)) % 4, axis=0)
    gains = gains.transpose(1, 0, 2).reshape(2, model).astype(F32)
    gain_a, gain_f = gains[:1], gains[1:]
    bias = [w[:, low + 2, : 2 * heads_local] for w in (w1[0], w1[4])]
    bias = jnp.concatenate(bias).reshape(4 * heads_local, 2).astype(F32)
    tab = tables(
        row_of(segment_ids), row_of(variate_ids), row_of(time_ids), row_of(padding_mask),
        bias, core,
    )
    cos, sin, aug_q, aug_k, head_scale, add_q, add_k, var_q = tab

    q, k, v = qkv_call(False, ends, gain_a, zi, w1, low, cos, sin)
    if near:
        b1, b2, b3, g0, d0, q, k, v = meet(b1, b2, b3, g0, d0, q, k, v)
        n3 = [jnp.stack([p3, d0])]
        c1, g1 = ring(n3[0]), y_swap(b1)
        n2 = [jnp.stack([p2, g0])]
        f2 = [core_swap(n2[0])]
        f3 = [core_swap(n3[0])]
    k_oth, v_oth = core_swap(k), core_swap(v)
    o, _ = attend_part(scale, (q, k, v, k_oth, v_oth), tab)
    if near:
        b2, b3, c1, g1, o = meet(b2, b3, c1, g1, o)
        c2, g2 = ring(c1), y_swap(b2)
        n2.append(jnp.stack([b1, g1]))
        f2.append(core_swap(n2[1]))
        f3.append(core_swap(c1))
        b3, c2, g2 = meet(b3, c2, g2)
        c3, g3 = ring(c2), y_swap(b3)
        n2.append(jnp.stack([b2, g2]))
        f2.append(core_swap(n2[2]))
        f3.append(core_swap(c2))
        n2.append(jnp.stack([b3, g3]))
        f2.append(core_swap(n2[3]))
        f3.append(core_swap(c3))
        w2, w3 = n2 + f2, n3 + [c1, c2, c3] + f3
    else:
        w2, w3 = gather_any(p2), gather_any(p3)
    h, z_near, z_far = ffn_up_call(False, out_low, width, ends, o, gain_f, zi, w1, w2)
    y_low = ffn_down_call(BF, h, z_near, z_far, zi, w3)
    got = lax.ppermute(y_low, "section", [(0, 1)])

    x = jnp.where(is_first, ends, got)
    n1, q, k, v, q0, k0 = qkv_call(True, x, gain_a, zi, w1, low, cos, sin)
    k_oth, v_oth = core_swap(k), core_swap(v)
    o, sums = attend_part(scale, (q, k, v, k_oth, v_oth), tab)
    h, z_near, z_far, n2, g, u = ffn_up_call(True, out_low, width, x, o, gain_f, zi, w1, w2)
    y = ffn_down_call(F32, h, z_near, z_far, zi, w3)

    def qkv_back(dq, dk, dk_got, dv, dv_got, dh):
        return qkv_back_call(
            dq, dk, dk_got, dv, dv_got, q0, k0, cos, sin, x, dh, gain_a, zi, w1, low
        )

    dh, _, do = ffn_back_call(out_low, width, ends, h, g, u, gain_f, zi, w1, w2, w3)[:3]
    dq, dk, dk_send, dv, dv_send, _ = attend_back_call(
        scale, None, q, k, k_oth, v, v_oth, do, o, sums, aug_q, aug_k, head_scale, add_k, var_q
    )
    dx_low = qkv_back(dq, dk, core_swap(dk_send), dv, core_swap(dv_send), dh)[3]
    got = lax.ppermute(dx_low, "section", [(1, 0)])
    z_oth, n2_oth, n1_oth = core_swap(z_far), core_swap(n2), core_swap(n1)
    o_oth = core_swap(o[:, 2 * width :])

    df = jnp.where(is_first, got, ends)
    down_keep, down_send = wgrad_call(zi, hidden, z_near, df, z_oth, core_swap(df))
    df, down_keep, down_send = meet(df, down_keep, down_send)
    down_got = y_swap(down_send)
    dh, da, do, dg_near, dg_far, du_near, du_far, gg_f = ffn_back_call(
        out_low, width, df, h, g, u, gain_f, zi, w1, w2, w3
    )
    gate_keep, gate_send = wgrad_call(zi, hidden, dg_near, n2, core_swap(dg_far), n2_oth)
    du_oth, da_oth = core_swap(du_far), core_swap(da)
    cut = width * 3 // 2
    if near:
        down_keep, down_got, gate_keep, gate_send, du_oth, da_oth, do = meet(
            down_keep, down_got, gate_keep, gate_send, du_oth, da_oth, do
        )
        gate_got = y_swap(gate_send)
        down = [plus(down_keep[r], down_got[r]) for r in range(4)]
        down_run = ring(down[1])
    up_keep, up_send = wgrad_call(zi, hidden, du_near, n2, du_oth, n2_oth)
    out_keep, out_send = wgrad_call(zi, width, o, da, o_oth, da_oth)

    def attend_back(do, low, high):
        return attend_back_call(
            scale, (low, high), q, k, k_oth, v, v_oth, do, o, sums, aug_q, aug_k, head_scale,
            add_k, var_q,
        )

    pairs = do.shape[1] // 128
    if near:
        up = [jnp.stack([up_keep[r], up_send[r]]) for r in range(4)]
        down_run, do, *up = meet(down_run, do, *up, out_send)[:6]
        down_run = ring(plus(down_run, down[2]))
        up_run = ring(up[1])
        first = attend_back(do, 0, pairs // 2)
        down_run, up_run, gate_got, do, out_send, *first = meet(
            down_run, up_run, gate_got, do, out_send, *first
        )
        out_got = y_swap(out_send)
        down_run = ring(plus(down_run, down[3]))
        up_run = ring(plus(up_run, up[2]))
        gate = [plus(gate_keep[r], gate_got[r]) for r in range(4)]
    else:
        first = attend_back(do, 0, pairs // 2)
    second = attend_back(do, pairs // 2, pairs)
    if near:
        down_run, up_run, out_got, first, second, *gate = meet(
            down_run, up_run, out_got, first, second, *gate
        )
        gate_run = ring(gate[1])
        up_run = ring(plus(up_run, up[3]))
        g_down = down_run.astype(F32) + down[0].astype(F32)
        out = [plus(out_keep[r], out_got[r]) for r in range(4)]
    dq, dk, dk_send, dv, dv_send, bias = (
        jnp.concatenate([b, a] if i in (2, 4) else [a, b], axis=0 if i == 5 else 1)
        for i, (a, b) in enumerate(zip(first, second))
    )
    dp_near, dp_far, dx, dx_low, gg_a = qkv_back(
        dq, dk, core_swap(dk_send), dv, core_swap(dv_send), dh
    )
    out_low_rows = jnp.where(is_first, dx_low, y.astype(BF))
    send = jnp.where(yi == 0, out_low_rows[rows:], out_low_rows[:rows])
    if near:
        gate_run, up_run, send, dp_near, dp_far, *out = meet(
            gate_run, up_run, send, dp_near, dp_far, *out
        )
        rows_got = y_swap(send)
        gate_run = ring(plus(gate_run, gate[2]))
        out_run = ring(out[1])
        up_run = plus(up_run, up[0])
    qkv_keep, qkv_send = wgrad_call(zi, 3 * width, dp_near, n1, core_swap(dp_far), n1_oth)
    small = small_rows(gg_a, gg_f, bias, ti, heads_local)
    if near:
        rows_got, gate_run, out_run, up_run, qkv_keep, qkv_send, small = meet(
            rows_got, gate_run, out_run, up_run, qkv_keep, qkv_send, small
        )
        head_got = y_swap(qkv_send[:, :cut])
        up_got = y_swap(up_run[1])
        tails = [jnp.stack([qkv_keep[r, cut:], qkv_send[r, cut:]]) for r in range(4)]
        tail_run = ring(tails[1])
        gate_run = ring(plus(gate_run, gate[3]))
        out_run = ring(plus(out_run, out[2]))
        g_gu_up = up_run[0].astype(F32)
        tail_run, gate_run, out_run, head_got = meet(tail_run, gate_run, out_run, head_got)
        tail_run = ring(plus(tail_run, tails[2]))
        out_run = ring(plus(out_run, out[3]))
        heads_sum = [plus(qkv_keep[r, :cut], head_got[r]) for r in range(4)]
        head_run = ring(heads_sum[1])
        tail_run, head_run, out_run = meet(tail_run, head_run, out_run)
        tail_run = ring(plus(tail_run, tails[3]))
        head_run = ring(plus(head_run, heads_sum[2]))
        tail_run, head_run, small = meet(tail_run, head_run, small)
        tail_run = plus(tail_run, tails[0])
        tail_got = y_swap(tail_run[1])
        head_run = ring(plus(head_run, heads_sum[3]))
        small = small_sum(small)
        g_qkv = jnp.concatenate(
            [
                head_run.astype(F32) + heads_sum[0].astype(F32),
                tail_run[0].astype(F32) + tail_got.astype(F32),
            ],
            axis=0,
        )
        g_out = out_run.astype(F32) + out[0].astype(F32)
        g_gu = jnp.stack(
            [gate_run.astype(F32) + gate[0].astype(F32), g_gu_up + up_got.astype(F32)]
        )
    else:
        rows_got = y_swap(send)
        g_down = scatter_any(down_keep, down_send)
        g_gu = jnp.stack([scatter_any(gate_keep, gate_send), scatter_any(up_keep, up_send)])
        g_out = scatter_any(out_keep, out_send)
        g_qkv = scatter_any(qkv_keep, qkv_send)
        small = small_sum(small)

    out_rows = jnp.where(is_first, dx, y)
    keep = jnp.where(yi == 0, out_rows[:rows], out_rows[rows:])
    back = rows_got.astype(F32)
    boundary_out = jnp.where(yi == 0, jnp.stack([keep, back]), jnp.stack([back, keep]))[None]
    piece = model // (n * tn)
    gain_piece = lax.dynamic_slice_in_dim(
        small[:2], (lax.axis_index("dp") * tn + ti) * piece, piece, 1
    )
    bias_piece = lax.dynamic_slice_in_dim(
        small[2, : 8 * heads_local].reshape(-1, 2), ti * heads_local, heads_local, 0
    )
    return (
        boundary_out,
        g_qkv.reshape(3, width, cols).transpose(2, 0, 1)[None],
        g_out[None],
        g_gu.transpose(2, 0, 1)[None],
        g_down[None],
        gain_piece[None],
        bias_piece[None],
    )


def solution(mesh):
    placed = (
        P("section", "dp", "tensor", None),
        P("section", "dp", None, "tensor"),
        P("section", "tensor", "dp"),
        P("section", "dp", None, "tensor"),
        P("section", "tensor", "dp"),
        P("section", None, "dp"),
        P("section", "tensor", None),
        P("dp", None),
        P("dp", None),
        P("dp", None),
        P("dp", None),
    )
    return jax.shard_map(
        per_device,
        mesh=mesh,
        in_specs=placed,
        out_specs=(
            P("section", "dp", "tensor", None),
            P("section", "dp", None, "tensor"),
            P("section", "tensor", "dp"),
            P("section", "dp", None, "tensor"),
            P("section", "tensor", "dp"),
            P("section", None, ("dp", "tensor")),
            P("section", "tensor", None),
        ),
        check_vma=False,
    )
```

time: 883 us -> 697 us (0.79)
  waiting for transfers between devices: 367 us -> 268 us
  local copies, waits for them, and re-layouts: 132 us -> 58.1 us
    ppermute x23 -> x18, waiting for transfers between devices: 196 us -> 74.6 us  [y_swap(): return lax.ppermute(value, 'tensor', [(i, i ^ 2) for i in range(n)])]
    dynamic_update_slice x63 -> x0, local copies, waits for them, and re-layouts: 57.9 us -> none  [gather_weight(): out = lax.dynamic_update_slice(out, part[None, None], (at, t, 0, 0))]
    unnamed x97 -> x339, local copies, waits for them, and re-layouts: 12.2 us -> 44.9 us
    dynamic_slice x6 -> x2, local copies, waits for them, and re-layouts: 15.8 us -> 1.92 us  [per_device(): lax.dynamic_slice_in_dim(small[2, :8 * heads_local].reshape(-1, 2), ti *...]
    pallas_call x12 -> x15, Pallas kernels: 160 us -> 172 us  [the longest x2 56.6 us: ffn_back_call(): pl.pallas_call(functools.partial(ffn_back_kernel, out_low), grid=(2,), in...]
    broadcast_in_dim x4 -> x0, local copies, waits for them, and re-layouts: 11.4 us -> none  [gather_weight(): out = jnp.zeros((n, tn, feats, cols), piece.dtype)]
    add x6 -> x2, other arithmetic: 10.4 us -> 0.11 us  [the longest x1 0.07 us: per_device(): head_run.astype(F32) + heads_sum[0].astype(F32)]
    squeeze x7 -> x2, local copies, waits for them, and re-layouts: 9.76 us -> 0.04 us  [the longest x1 0.02 us: per_device(): up_got = y_swap(up_run[1])]
  transfers between devices with their start and end apart: 84 -> 79, of which waited for: 35 -> 34; matrix products, arithmetic and copies ran while one was open for 19% -> 8% of each run, Pallas kernels for 14% -> 15%
where the time goes in v2:
time: 697 us; the launch traced here: 688 us
  waiting for transfers between devices  268 us (38%)
  Pallas kernels  256 us (37%)
  local copies, waits for them, and re-layouts  58.1 us (8%)
  starting transfers between devices  53.2 us (8%)
  other arithmetic  48.3 us (7%)
    ppermute x27, waiting for transfers between devices, ring(): return lax.ppermute(value, 'dp', [(i, (i + 1) % n) for i in range(n)])  123 us
    ppermute x18, waiting for transfers between devices, y_swap(): return lax.ppermute(value, 'tensor', [(i, i ^ 2) for i in range(n)])  74.6 us
    pallas_call x2, Pallas kernels, ffn_back_call(): pl.pallas_call(functools.partial(ffn_back_kernel, out_low), grid=(2,), in...  56.6 us
    pallas_call x3, Pallas kernels, attend_back_call(): pl.pallas_call(functools.partial(attend_back_kernel, scale), grid=(pairs,...  55.8 us
    unnamed x339, local copies, waits for them, and re-layouts  44.9 us
    pallas_call x2, Pallas kernels, ffn_up_call(): pl.pallas_call(functools.partial(ffn_up_kernel, save, out_low), grid=(2,)...  36.4 us
    pallas_call x2, Pallas kernels, qkv_back_call(): pl.pallas_call(qkv_back_kernel, grid=(4,), in_specs=[col] * 7 + [whole((r...  30.3 us
    pallas_call x2, Pallas kernels, attend_call(): pl.pallas_call(functools.partial(attend_kernel, scale), grid=(pairs,), in...  29 us
  transfers between devices with their start and end apart: 79, of which 34 were waited for; matrix products, arithmetic and copies ran while one was open for 8% of the time, Pallas kernels for 15%

profile of v2, /device:TPU:0, one launch (start us, length us, event | category | flops | bytes accessed | tf_op | source)
XLA Modules:
  0.0 687.8 jit_solution(15374189166871190910)
XLA Ops:
  0.7 2.5 fusion.11
  3.3 3.0 collective-permute-start.1
  9.3 8.9 %collective-permute-done.1 = bf16[256,1024]{1,0:T(8,128)(2,1)S(1)} collective-permute-done((bf16[256,1024]{1,0:T(8,128)(2,1)S(1)}, bf16[256,1024]{1,0:T(8,128)(2,1)S(1)}, u32[]{:S(2)}, u32[]{:S(2)}) %collective-permute-start.1) | collective-permute-done | bytes 524320 | tf_op jit(solution)/shard_map/ppermute | solution.py:739
  18.2 4.0 collective-permute-done
  22.8 13.9 %collective-permute-done.2 = bf16[1040,256]{1,0:T(8,128)(2,1)S(1)} collective-permute-done((bf16[1040,256]{1,0:T(8,128)(2,1)S(1)}, bf16[1040,256]{1,0:T(8,128)(2,1)S(1)}, u32[]{:S(2)}, u32[]{:S(2)}) %collective-permute-start.2) | collective-permute-done | bytes 532512 | tf_op jit(solution)/shard_map/ppermute | solution.py:744
  38.7 11.7 %collective-permute-done.4 = bf16[1040,256]{1,0:T(8,128)(2,1)S(1)} collective-permute-done((bf16[1040,256]{1,0:T(8,128)(2,1)S(1)}, bf16[1040,256]{1,0:T(8,128)(2,1)S(1)}, u32[]{:S(2)}, u32[]{:S(2)}) %collective-permute-start.4) | collective-permute-done | bytes 532512 | tf_op jit(solution)/shard_map/ppermute | solution.py:744
  53.9 15.3 %collective-permute-done.8 = bf16[688,256]{1,0:T(8,128)(2,1)S(1)} collective-permute-done((bf16[688,256]{1,0:T(8,128)(2,1)S(1)}, bf16[688,256]{1,0:T(8,128)(2,1)S(1)}, u32[]{:S(2)}, u32[]{:S(2)}) %collective-permute-start.8) | collective-permute-done | bytes 352288 | tf_op jit(solution)/shard_map/ppermute | solution.py:739
  72.3 12.3 %collective-permute-done.10 = bf16[1040,256]{1,0:T(8,128)(2,1)S(1)} collective-permute-done((bf16[1040,256]{1,0:T(8,128)(2,1)S(1)}, bf16[1040,256]{1,0:T(8,128)(2,1)S(1)}, u32[]{:S(2)}, u32[]{:S(2)}) %collective-permute-start.10) | collective-permute-done | bytes 532512 | tf_op jit(solution)/shard_map/ppermute | solution.py:739
  91.9 3.0 maximum_select_fusion.1.x_ref.dy_ref
  101.1 9.8 %shard_map.171 = (bf16[512,1024]{1,0:T(8,128)(2,1)S(1)}, bf16[512,1024]{1,0:T(8,128)(2,1)}, bf16[512,1024]{1,0:T(8,128)(2,1)}) custom-call(bf16[512,1024]{1,0:T(8,128)(2,1)S(1)} %copy-done.15, f32[1,1024]{1,0:T(1,128)S(1)} %bitcast.146, s32[1]{0:T(128)} %bitcast.18.zi_ref, f32[512,128]{1,0:T(8,128)S(1)} %pad_maximum_fusion.20.cos_ref, ...), custom_call_target="tpu_custom_call" | custom-call | flops 1000 | bytes 1000 | tf_op jit(solution)/shard_map/pallas_call | solution.py:175
  113.3 2.4 collective-permute-start.17
  121.4 14.7 %shard_map.172 = (bf16[512,1024]{1,0:T(8,128)(2,1)S(1)}, f32[512,1024]{1,0:T(8,128)}) custom-call(bf16[512,1024]{1,0:T(8,128)(2,1)S(1)} %copy-done.120, bf16[512,1024]{1,0:T(8,128)(2,1)} %get-tuple-element.217.ko_ref, bf16[512,1024]{1,0:T(8,128)(2,1)} %collective-permute-done.19.kx_ref, bf16[512,1024]{1,0:T(8,128)(2,1)} %get-tuple-element.218.vo_ref, ...), custom_call_target="tpu_custom_call" | custom-call | flops 1000 | bytes 1000 | tf_op jit(solution)/shard_map/pallas_call | solution.py:238
  139.6 15.8 %collective-permute-done.21.refs_2_.refs_18_ = bf16[2,688,256]{2,1,0:T(8,128)(2,1)S(1)} collective-permute-done((bf16[2,688,256]{2,1,0:T(8,128)(2,1)}, bf16[2,688,256]{2,1,0:T(8,128)(2,1)S(1)}, u32[]{:S(2)}, u32[]{:S(2)}) %collective-permute-start.21) | collective-permute-done | bytes 704544 | tf_op jit(solution)/shard_map/ppermute | solution.py:744
  158.2 1.7 pad_maximum_fusion.2.refs_10_
  160.0 11.9 %collective-permute-done.23 = bf16[1376,256]{1,0:T(8,128)(2,1)S(1)} collective-permute-done((bf16[1376,256]{1,0:T(8,128)(2,1)}, bf16[1376,256]{1,0:T(8,128)(2,1)S(1)}, u32[]{:S(2)}, u32[]{:S(2)}) %collective-permute-start.23) | collective-permute-done | bytes 704544 | tf_op jit(solution)/shard_map/ppermute | solution.py:739
  174.3 19.3 %collective-permute-done.28.refs_3_.refs_19_ = bf16[2,688,256]{2,1,0:T(8,128)(2,1)S(1)} collective-permute-done((bf16[2,688,256]{2,1,0:T(8,128)(2,1)S(1)}, bf16[2,688,256]{2,1,0:T(8,128)(2,1)S(1)}, u32[]{:S(2)}, u32[]{:S(2)}) %collective-permute-start.28) | collective-permute-done | bytes 704544 | tf_op jit(solution)/shard_map/ppermute | solution.py:744
  194.1 17.2 %shard_map.173 = (f32[512,1024]{1,0:T(8,128)}, bf16[512,1408]{1,0:T(8,128)(2,1)S(1)}, bf16[512,1408]{1,0:T(8,128)(2,1)S(1)}) custom-call(bf16[512,1024]{1,0:T(8,128)(2,1)S(1)} %copy-done.16, bf16[512,1024]{1,0:T(8,128)(2,1)S(1)} %get-tuple-element.220.o_ref, f32[1,1024]{1,0:T(1,128)S(1)} %bitcast.150, s32[1]{0:T(128)} %bitcast.18.zi_ref, ...), custom_call_target="tpu_custom_call" | custom-call | flops 1000 | bytes 1000 | tf_op jit(solution)/shard_map/pallas_call | solution.py:388
  211.5 2.5 copy-done.106
  214.0 6.2 shard_map.174
  220.2 4.8 collective-permute-start.33
  225.0 21.5 %collective-permute-done.33 = bf16[512,1024]{1,0:T(8,128)(2,1)} collective-permute-done((bf16[512,1024]{1,0:T(8,128)(2,1)}, bf16[512,1024]{1,0:T(8,128)(2,1)}, u32[]{:S(2)}, u32[]{:S(2)}) %collective-permute-start.33) | collective-permute-done | bytes 1048608 | tf_op jit(solution)/shard_map/ppermute | solution.py:966
  248.0 10.5 %shard_map.175 = (bf16[512,1024]{1,0:T(8,128)(2,1)}, bf16[512,1024]{1,0:T(8,128)(2,1)S(1)}, bf16[512,1024]{1,0:T(8,128)(2,1)S(1)}, bf16[512,1024]{1,0:T(8,128)(2...) custom-call(bf16[512,1024]{1,0:T(8,128)(2,1)S(1)} %broadcast_select_fusion.2.x_ref, ...), custom_call_target="tpu_custom_call" | custom-call | flops 1000 | bytes 1000 | tf_op jit(solution)/shard_map/pallas_call | solution.py:175
  261.0 2.1 collective-permute-done.34.kx_ref
  264.7 14.2 %shard_map.176 = (bf16[512,1024]{1,0:T(8,128)(2,1)S(1)}, f32[512,1024]{1,0:T(8,128)S(1)}) custom-call(bf16[512,1024]{1,0:T(8,128)(2,1)S(1)} %get-tuple-element.232.q_ref, bf16[512,1024]{1,0:T(8,128)(2,1)S(1)} %get-tuple-element.233.ko_ref, bf16[512,1024]{1,0:T(8,128)(2,1)S(1)} %collective-permute-done.34.kx_ref, ...), custom_call_target="tpu_custom_call" | custom-call | flops 1000 | bytes 1000 | tf_op jit(solution)/shard_map/pallas_call | solution.py:238
  280.5 19.2 %shard_map.177 = (f32[512,1024]{1,0:T(8,128)}, bf16[512,1408]{1,0:T(8,128)(2,1)S(1)}, bf16[512,1408]{1,0:T(8,128)(2,1)}, bf16[512,1024]{1,0:T(8,128)(2,1)S(1)}, ...) custom-call(bf16[512,1024]{1,0:T(8,128)(2,1)S(1)} %broadcast_select_fusion.2.x_ref, ...), custom_call_target="tpu_custom_call" | custom-call | flops 1000 | bytes 1000 | tf_op jit(solution)/shard_map/pallas_call | solution.py:388
  301.8 28.6 %shard_map.178 = (f32[512,1024]{1,0:T(8,128)}, bf16[512,1024]{1,0:T(8,128)(2,1)}, bf16[512,1024]{1,0:T(8,128)(2,1)}, bf16[512,1408]{1,0:T(8,128)(2,1)}, bf16[512...) custom-call(bf16[512,1024]{1,0:T(8,128)(2,1)} %maximum_select_fusion.1.x_ref.dy_re, ...), custom_call_target="tpu_custom_call" | custom-call | flops 1000 | bytes 1000 | tf_op jit(solution)/shard_map/pallas_call | solution.py:500
  336.7 28.5 %shard_map.179 = (bf16[512,1024]{1,0:T(8,128)(2,1)S(1)}, bf16[512,1024]{1,0:T(8,128)(2,1)S(1)}, bf16[512,1024]{1,0:T(8,128)(2,1)S(1)}, bf16[512,1024]{1,0:T(8,12...) custom-call(bf16[512,1024]{1,0:T(8,128)(2,1)S(1)} %copy-done.47, bf16[512,1024]{1,0:T(8,128)(2,1)S(1)} %copy-done.50, ...), custom_call_target="tpu_custom_call" | custom-call | flops 1000 | bytes 1000 | tf_op jit(solution)/shard_map/pallas_call | solution.py:602
  365.7 2.1 collective-permute-done.36.dkr_ref
  369.4 15.6 %shard_map.180 = (bf16[2,512,768]{2,1,0:T(8,128)(2,1)}, bf16[2,512,768]{2,1,0:T(8,128)(2,1)}, f32[512,1024]{1,0:T(8,128)}, bf16[512,1024]{1,0:T(8,128)(2,1)S(1)}, f32[1,1024]{1,0:T(1,128)}) custom-call(bf16[512,1024]{1,0:T(8,128)(2,1)S(1)} %get-tuple-element.241.dq_ref, bf16[512,1024]{1,0:T(8,128)(2,1)S(1)} %get-tuple-element.242.dk_ref, ...), custom_call_target="tpu_custom_call" | custom-call | flops 1000 | bytes 1000 | tf_op jit(solution)/shard_map/pallas_call | solution.py:685
  386.5 25.7 %collective-permute-done.38 = bf16[512,1024]{1,0:T(8,128)(2,1)S(1)} collective-permute-done((bf16[512,1024]{1,0:T(8,128)(2,1)S(1)}, bf16[512,1024]{1,0:T(8,128)(2,1)S(1)}, u32[]{:S(2)}, u32[]{:S(2)}) %collective-permute-start.38) | collective-permute-done | bytes 1048608 | tf_op jit(solution)/shard_map/ppermute | solution.py:985
  412.4 2.6 collective-permute-done.40.bx_ref
  415.1 3.2 shard_map.181
  420.5 27.9 %shard_map.182 = (f32[512,1024]{1,0:T(8,128)}, bf16[512,1024]{1,0:T(8,128)(2,1)}, bf16[512,1024]{1,0:T(8,128)(2,1)}, bf16[512,1408]{1,0:T(8,128)(2,1)}, bf16[512...) custom-call(bf16[512,1024]{1,0:T(8,128)(2,1)} %copy-done.77, ...), custom_call_target="tpu_custom_call" | custom-call | flops 1000 | bytes 1000 | tf_op jit(solution)/shard_map/pallas_call | solution.py:500
  450.1 5.4 collective-permute-done.43.bx_ref
  457.0 3.2 shard_map.183
  460.2 21.9 %collective-permute-done.41 = bf16[4,688,256]{2,1,0:T(8,128)(2,1)S(1)} collective-permute-done((bf16[4,688,256]{2,1,0:T(8,128)(2,1)}, bf16[4,688,256]{2,1,0:T(8,128)(2,1)S(1)}, u32[]{:S(2)}, u32[]{:S(2)}) %collective-permute-start.41) | collective-permute-done | bytes 1409056 | tf_op jit(solution)/shard_map/ppermute | solution.py:739
  483.1 3.2 shard_map.184
  487.5 2.1 shard_map.185
  494.1 13.6 %shard_map.186 = (bf16[512,512]{1,0:T(8,128)(2,1)S(1)}, bf16[512,512]{1,0:T(8,128)(2,1)S(1)}, bf16[512,512]{1,0:T(8,128)(2,1)S(1)}, bf16[512,512]{1,0:T(8,128)(2...) custom-call(bf16[512,1024]{1,0:T(8,128)(2,1)S(1)} %copy-done.47, bf16[512,1024]{1,0:T(8,128)(2,1)S(1)} %copy-done.51, ...), custom_call_target="tpu_custom_call" | custom-call | flops 1000 | bytes 1000 | tf_op jit(solution)/shard_map/pallas_call | solution.py:602
  507.8 11.4 %collective-permute-done.48 = bf16[688,256]{1,0:T(8,128)(2,1)S(1)} collective-permute-done((bf16[688,256]{1,0:T(8,128)(2,1)S(1)}, bf16[688,256]{1,0:T(8,128)(2,1)S(1)}, u32[]{:S(2)}, u32[]{:S(2)}) %collective-permute-start.48) | collective-permute-done | bytes 352288 | tf_op jit(solution)/shard_map/ppermute | solution.py:744
  532.7 13.7 %shard_map.187 = (bf16[512,512]{1,0:T(8,128)(2,1)S(1)}, bf16[512,512]{1,0:T(8,128)(2,1)S(1)}, bf16[512,512]{1,0:T(8,128)(2,1)S(1)}, bf16[512,512]{1,0:T(8,128)(2...) custom-call(bf16[512,1024]{1,0:T(8,128)(2,1)S(1)} %copy-done.48, bf16[512,1024]{1,0:T(8,128)(2,1)S(1)} %copy-done.52, ...), custom_call_target="tpu_custom_call" | custom-call | flops 1000 | bytes 1000 | tf_op jit(solution)/shard_map/pallas_call | solution.py:602
  551.9 5.2 shard_map.189
  558.7 2.5 add_convert_fusion.1
  561.2 2.5 collective-permute-start.57
  563.6 2.4 collective-permute-start.56
  569.6 2.0 fusion.30
  573.3 14.7 %shard_map.188 = (bf16[2,512,768]{2,1,0:T(8,128)(2,1)S(1)}, bf16[2,512,768]{2,1,0:T(8,128)(2,1)}, f32[512,1024]{1,0:T(8,128)S(1)}, bf16[512,1024]{1,0:T(8,128)(2,1)S(1)}, f32[1,1024]{1,0:T(1,128)S(1)}) custom-call(bf16[512,1024]{1,0:T(8,128)(2,1)S(1)} %pad_maximum_fusion.8.dq_ref, bf16[512,1024]{1,0:T(8,128)(2,1)S(1)} %pad_maximum_fusion.9.dk_ref, ...), custom_call_target="tpu_custom_call" | custom-call | flops 1000 | bytes 1000 | tf_op jit(solution)/shard_map/pallas_call | solution.py:685
  590.9 2.3 fusion.5
  596.2 2.1 broadcast_select_fusion
  601.0 5.0 shard_map.190
  606.0 3.6 collective-permute-done.60
  610.7 1.8 collective-permute-start.64
  613.2 2.9 collective-permute-start.63
  618.8 7.5 %collective-permute-done.64 = bf16[688,256]{1,0:T(8,128)(2,1)S(1)} collective-permute-done((bf16[688,256]{1,0:T(8,128)(2,1)S(1)}, bf16[688,256]{1,0:T(8,128)(2,1)S(1)}, u32[]{:S(2)}, u32[]{:S(2)}) %collective-permute-start.64) | collective-permute-done | bytes 352288 | tf_op jit(solution)/shard_map/ppermute | solution.py:744
  626.3 7.1 %collective-permute-done.63 = bf16[2,384,256]{2,1,0:T(8,128)(2,1)S(1)} collective-permute-done((bf16[2,384,256]{2,1,0:T(8,128)(2,1)S(1)}, bf16[2,384,256]{2,1,0:T(8,128)(2,1)S(1)}, u32[]{:S(2)}, u32[]{:S(2)}) %collective-permute-start.63) | collective-permute-done | bytes 393248 | tf_op jit(solution)/shard_map/ppermute | solution.py:744
  633.5 1.9 collective-permute-start.69
  636.7 1.8 collective-permute-done.74
  638.6 3.2 collective-permute-done.69
  641.8 10.4 %collective-permute-done.68 = bf16[384,256]{1,0:T(8,128)(2,1)S(1)} collective-permute-done((bf16[384,256]{1,0:T(8,128)(2,1)S(1)}, bf16[384,256]{1,0:T(8,128)(2,1)S(1)}, u32[]{:S(2)}, u32[]{:S(2)}) %collective-permute-start.68) | collective-permute-done | bytes 196640 | tf_op jit(solution)/shard_map/ppermute | solution.py:744
  653.9 8.1 %collective-permute-done.71 = bf16[384,256]{1,0:T(8,128)(2,1)S(1)} collective-permute-done((bf16[384,256]{1,0:T(8,128)(2,1)S(1)}, bf16[384,256]{1,0:T(8,128)(2,1)S(1)}, u32[]{:S(2)}, u32[]{:S(2)}) %collective-permute-start.71) | collective-permute-done | bytes 196640 | tf_op jit(solution)/shard_map/ppermute | solution.py:744
  662.0 5.3 collective-permute-done.70
  669.8 2.4 collective-permute-done.76
  672.4 5.2 collective-permute-done.77
  680.2 2.0 collective-permute-done.78
  (587 shorter events, 124.9 us)
Async XLA Ops:
  3.3 15.0 %collective-permute-start.1 = (bf16[256,1024]{1,0:T(8,128)(2,1)S(1)}, bf16[256,1024]{1,0:T(8,128)(2,1)S(1)}, u32[]{:S(2)}, u32[]{:S(2)}) collective-permute-start(bf16[256,1024]{1,0:T(8,128)(2,1)S(1)} %get-tuple-element.368), channel_id=1, source_target_pairs={{0,2},{1,3},{2,0},{3,1},{4,6},{5,7},{6,4},{7,5},{8,10},{9,11},{10,... | collective-permute-start | bytes 1572872 | tf_op jit(solution)/shard_map/ppermute | solution.py:739
  6.8 15.5 %collective-permute-start = (bf16[1040,256]{1,0:T(8,128)(2,1)S(1)}, bf16[1040,256]{1,0:T(8,128)(2,1)S(1)}, u32[]{:S(2)}, u32[]{:S(2)}) collective-permute-start(bf16[1040,256]{1,0:T(8,128)(2,1)S(1)} %fusion.10), channel_id=1, source_target_pairs={{0,4},{4,8},{8,12},{12,0},{1,5},{5,9},{9,13},{13,1},{2,6},{6,10},{... | collective-permute-start | bytes 1597448 | tf_op jit(solution)/shard_map/ppermute | solution.py:744
  22.2 14.5 %collective-permute-start.2 = (bf16[1040,256]{1,0:T(8,128)(2,1)S(1)}, bf16[1040,256]{1,0:T(8,128)(2,1)S(1)}, u32[]{:S(2)}, u32[]{:S(2)}) collective-permute-start(bf16[1040,256]{1,0:T(8,128)(2,1)S(1)} %collective-permute-done), channel_id=1, source_target_pairs={{0,4},{4,8},{8,12},{12,0},{1,5},{5,9},{9,13},{13,1},{2,6},{6,10},{... | collective-permute-start | bytes 1597448 | tf_op jit(solution)/shard_map/ppermute | solution.py:744
  22.2 14.5 %collective-permute-start.3 = (bf16[1040,256]{1,0:T(8,128)(2,1)S(1)}, bf16[1040,256]{1,0:T(8,128)(2,1)S(1)}, u32[]{:S(2)}, u32[]{:S(2)}) collective-permute-start(bf16[1040,256]{1,0:T(8,128)(2,1)S(1)} %fusion.10), channel_id=1, source_target_pairs={{0,2},{1,3},{2,0},{3,1},{4,6},{5,7},{6,4},{7,5},{8,10},{9,11},{10,... | collective-permute-start | bytes 1597448 | tf_op jit(solution)/shard_map/ppermute | solution.py:739
  36.8 13.6 %collective-permute-start.4 = (bf16[1040,256]{1,0:T(8,128)(2,1)S(1)}, bf16[1040,256]{1,0:T(8,128)(2,1)S(1)}, u32[]{:S(2)}, u32[]{:S(2)}) collective-permute-start(bf16[1040,256]{1,0:T(8,128)(2,1)S(1)} %collective-permute-done.2), channel_id=1, source_target_pairs={{0,4},{4,8},{8,12},{12,0},{1,5},{5,9},{9,13},{13,1},{2,6},{6,10},{... | collective-permute-start | bytes 1597448 | tf_op jit(solution)/shard_map/ppermute | solution.py:744
  36.8 13.6 %collective-permute-start.5 = (bf16[1040,256]{1,0:T(8,128)(2,1)S(1)}, bf16[1040,256]{1,0:T(8,128)(2,1)S(1)}, u32[]{:S(2)}, u32[]{:S(2)}) collective-permute-start(bf16[1040,256]{1,0:T(8,128)(2,1)S(1)} %collective-permute-done), channel_id=1, source_target_pairs={{0,2},{1,3},{2,0},{3,1},{4,6},{5,7},{6,4},{7,5},{8,10},{9,11},{10,... | collective-permute-start | bytes 1597448 | tf_op jit(solution)/shard_map/ppermute | solution.py:739
  50.4 18.8 %collective-permute-start.6 = (bf16[1376,256]{1,0:T(8,128)(2,1)}, bf16[1376,256]{1,0:T(8,128)(2,1)}, u32[]{:S(2)}, u32[]{:S(2)}) collective-permute-start(bf16[1376,256]{1,0:T(8,128)(2,1)} %bitcast.9), channel_id=1, source_target_pairs={{0,4},{4,8},{8,12},{12,0},{1,5},{5,9},{9,13},{13,1},{2,6},{6,10},{... | collective-permute-start | bytes 2113544 | tf_op jit(solution)/shard_map/ppermute | solution.py:744
  50.7 18.5 %collective-permute-start.7 = (bf16[1040,256]{1,0:T(8,128)(2,1)S(1)}, bf16[1040,256]{1,0:T(8,128)(2,1)S(1)}, u32[]{:S(2)}, u32[]{:S(2)}) collective-permute-start(bf16[1040,256]{1,0:T(8,128)(2,1)S(1)} %collective-permute-done.2), channel_id=1, source_target_pairs={{0,2},{1,3},{2,0},{3,1},{4,6},{5,7},{6,4},{7,5},{8,10},{9,11},{10,... | collective-permute-start | bytes 1597448 | tf_op jit(solution)/shard_map/ppermute | solution.py:739
  51.8 17.4 %collective-permute-start.8 = (bf16[688,256]{1,0:T(8,128)(2,1)S(1)}, bf16[688,256]{1,0:T(8,128)(2,1)S(1)}, u32[]{:S(2)}, u32[]{:S(2)}) collective-permute-start(bf16[688,256]{1,0:T(8,128)(2,1)S(1)} %bitcast.174), channel_id=1, source_target_pairs={{0,2},{1,3},{2,0},{3,1},{4,6},{5,7},{6,4},{7,5},{8,10},{9,11},{10,... | collective-permute-start | bytes 1056776 | tf_op jit(solution)/shard_map/ppermute | solution.py:739
  69.2 15.9 %collective-permute-start.9 = (bf16[1376,256]{1,0:T(8,128)(2,1)}, bf16[1376,256]{1,0:T(8,128)(2,1)}, u32[]{:S(2)}, u32[]{:S(2)}) collective-permute-start(bf16[1376,256]{1,0:T(8,128)(2,1)} %collective-permute-done.6), channel_id=1, source_target_pairs={{0,4},{4,8},{8,12},{12,0},{1,5},{5,9},{9,13},{13,1},{2,6},{6,10},{... | collective-permute-start | bytes 2113544 | tf_op jit(solution)/shard_map/ppermute | solution.py:744
  70.0 18.9 %collective-permute-start.13 = (bf16[2,1040,256]{2,1,0:T(8,128)(2,1)S(1)}, bf16[2,1040,256]{2,1,0:T(8,128)(2,1)S(1)}, u32[]{:S(2)}, u32[]{:S(2)}) collective-permute-start(bf16[2,1040,256]{2,1,0:T(8,128)(2,1)S(1)} %pad_maximum_fusion.4.refs_0_), channel_id=1, source_target_pairs={{0,1},{1,0},{2,3},{3,2},{4,5},{5,4},{6,7},{7,6},{8,9},{9,8},{10,11... | collective-permute-start | bytes 3194888 | tf_op jit(solution)/shard_map/ppermute | solution.py:734
  70.1 14.5 %collective-permute-start.10 = (bf16[1040,256]{1,0:T(8,128)(2,1)S(1)}, bf16[1040,256]{1,0:T(8,128)(2,1)S(1)}, u32[]{:S(2)}, u32[]{:S(2)}) collective-permute-start(bf16[1040,256]{1,0:T(8,128)(2,1)S(1)} %collective-permute-done.4), channel_id=1, source_target_pairs={{0,2},{1,3},{2,0},{3,1},{4,6},{5,7},{6,4},{7,5},{8,10},{9,11},{10,... | collective-permute-start | bytes 1597448 | tf_op jit(solution)/shard_map/ppermute | solution.py:739
  71.6 26.1 %collective-permute-start.14 = (bf16[2,1040,256]{2,1,0:T(8,128)(2,1)S(1)}, bf16[2,1040,256]{2,1,0:T(8,128)(2,1)}, u32[]{:S(2)}, u32[]{:S(2)}) collective-permute-start(bf16[2,1040,256]{2,1,0:T(8,128)(2,1)S(1)} %pad_maximum_fusion.5.refs_1_), channel_id=1, source_target_pairs={{0,1},{1,0},{2,3},{3,2},{4,5},{5,4},{6,7},{7,6},{8,9},{9,8},{10,11... | collective-permute-start | bytes 3194888 | tf_op jit(solution)/shard_map/ppermute | solution.py:734
  71.9 25.7 %collective-permute-start.15 = (bf16[2,1040,256]{2,1,0:T(8,128)(2,1)S(1)}, bf16[2,1040,256]{2,1,0:T(8,128)(2,1)}, u32[]{:S(2)}, u32[]{:S(2)}) collective-permute-start(bf16[2,1040,256]{2,1,0:T(8,128)(2,1)S(1)} %pad_maximum_fusion.6.refs_2_), channel_id=1, source_target_pairs={{0,1},{1,0},{2,3},{3,2},{4,5},{5,4},{6,7},{7,6},{8,9},{9,8},{10,11... | collective-permute-start | bytes 3194888 | tf_op jit(solution)/shard_map/ppermute | solution.py:734
  86.2 11.4 %collective-permute-start.16 = (bf16[2,1040,256]{2,1,0:T(8,128)(2,1)}, bf16[2,1040,256]{2,1,0:T(8,128)(2,1)}, u32[]{:S(2)}, u32[]{:S(2)}) collective-permute-start(bf16[2,1040,256]{2,1,0:T(8,128)(2,1)} %pad_maximum_fusion.7.refs_3_), channel_id=1, source_target_pairs={{0,1},{1,0},{2,3},{3,2},{4,5},{5,4},{6,7},{7,6},{8,9},{9,8},{10,11... | collective-permute-start | bytes 3194888 | tf_op jit(solution)/shard_map/ppermute | solution.py:734
  87.7 23.2 %collective-permute-start.11 = (bf16[1376,256]{1,0:T(8,128)(2,1)}, bf16[1376,256]{1,0:T(8,128)(2,1)}, u32[]{:S(2)}, u32[]{:S(2)}) collective-permute-start(bf16[1376,256]{1,0:T(8,128)(2,1)} %collective-permute-done.9), channel_id=1, source_target_pairs={{0,4},{4,8},{8,12},{12,0},{1,5},{5,9},{9,13},{13,1},{2,6},{6,10},{... | collective-permute-start | bytes 2113544 | tf_op jit(solution)/shard_map/ppermute | solution.py:744
  90.0 20.9 %collective-permute-start.12 = (bf16[1376,256]{1,0:T(8,128)(2,1)}, bf16[1376,256]{1,0:T(8,128)(2,1)}, u32[]{:S(2)}, u32[]{:S(2)}) collective-permute-start(bf16[1376,256]{1,0:T(8,128)(2,1)} %bitcast.9), channel_id=1, source_target_pairs={{0,2},{1,3},{2,0},{3,1},{4,6},{5,7},{6,4},{7,5},{8,10},{9,11},{10,... | collective-permute-start | bytes 2113544 | tf_op jit(solution)/shard_map/ppermute | solution.py:739
  113.3 22.8 %collective-permute-start.17 = (bf16[2,688,256]{2,1,0:T(8,128)(2,1)}, bf16[2,688,256]{2,1,0:T(8,128)(2,1)}, u32[]{:S(2)}, u32[]{:S(2)}) collective-permute-start(bf16[2,688,256]{2,1,0:T(8,128)(2,1)} %pad_maximum_fusion.14.refs_0_.refs_16_), channel_id=1, source_target_pairs={{0,4},{4,8},{8,12},{12,0},{1,5},{5,9},{9,13},{13,1},{2,6},{6,10},{... | collective-permute-start | bytes 2113544 | tf_op jit(solution)/shard_map/ppermute | solution.py:744
  115.7 20.5 %collective-permute-start.18 = (bf16[1376,256]{1,0:T(8,128)(2,1)}, bf16[1376,256]{1,0:T(8,128)(2,1)}, u32[]{:S(2)}, u32[]{:S(2)}) collective-permute-start(bf16[1376,256]{1,0:T(8,128)(2,1)} %collective-permute-done.6), channel_id=1, source_target_pairs={{0,2},{1,3},{2,0},{3,1},{4,6},{5,7},{6,4},{7,5},{8,10},{9,11},{10,... | collective-permute-start | bytes 2113544 | tf_op jit(solution)/shard_map/ppermute | solution.py:739
  136.1 19.3 %collective-permute-start.21 = (bf16[2,688,256]{2,1,0:T(8,128)(2,1)}, bf16[2,688,256]{2,1,0:T(8,128)(2,1)S(1)}, u32[]{:S(2)}, u32[]{:S(2)}) collective-permute-start(bf16[2,688,256]{2,1,0:T(8,128)(2,1)} %collective-permute-done.17.refs_1_.refs_17_), channel_id=1, source_target_pairs={{0,4},{4,8},{8,12},{12,0},{1,5},{5,9},{9,13},{13,1},{2,6},{6,10},{... | collective-permute-start | bytes 2113544 | tf_op jit(solution)/shard_map/ppermute | solution.py:744
  136.8 18.6 %collective-permute-start.22 = (bf16[1376,256]{1,0:T(8,128)(2,1)}, bf16[1376,256]{1,0:T(8,128)(2,1)S(1)}, u32[]{:S(2)}, u32[]{:S(2)}) collective-permute-start(bf16[1376,256]{1,0:T(8,128)(2,1)} %collective-permute-done.9), channel_id=1, source_target_pairs={{0,2},{1,3},{2,0},{3,1},{4,6},{5,7},{6,4},{7,5},{8,10},{9,11},{10,... | collective-permute-start | bytes 2113544 | tf_op jit(solution)/shard_map/ppermute | solution.py:739
  139.5 34.1 %collective-permute-start.24 = (bf16[2,1376,256]{2,1,0:T(8,128)(2,1)S(1)}, bf16[2,1376,256]{2,1,0:T(8,128)(2,1)S(1)}, u32[]{:S(2)}, u32[]{:S(2)}) collective-permute-start(bf16[2,1376,256]{2,1,0:T(8,128)(2,1)S(1)} %pad_maximum_fusion.refs_8_), channel_id=1, source_target_pairs={{0,1},{1,0},{2,3},{3,2},{4,5},{5,4},{6,7},{7,6},{8,9},{9,8},{10,11... | collective-permute-start | bytes 4227080 | tf_op jit(solution)/shard_map/ppermute | solution.py:734
  155.4 16.5 %collective-permute-start.23 = (bf16[1376,256]{1,0:T(8,128)(2,1)}, bf16[1376,256]{1,0:T(8,128)(2,1)S(1)}, u32[]{:S(2)}, u32[]{:S(2)}) collective-permute-start(bf16[1376,256]{1,0:T(8,128)(2,1)} %collective-permute-done.11), channel_id=1, source_target_pairs={{0,2},{1,3},{2,0},{3,1},{4,6},{5,7},{6,4},{7,5},{8,10},{9,11},{10,... | collective-permute-start | bytes 2113544 | tf_op jit(solution)/shard_map/ppermute | solution.py:739
  158.1 16.1 %collective-permute-start.25 = (bf16[2,1376,256]{2,1,0:T(8,128)(2,1)S(1)}, bf16[2,1376,256]{2,1,0:T(8,128)(2,1)S(1)}, u32[]{:S(2)}, u32[]{:S(2)}) collective-permute-start(bf16[2,1376,256]{2,1,0:T(8,128)(2,1)S(1)} %pad_maximum_fusion.1.refs_9_), channel_id=1, source_target_pairs={{0,1},{1,0},{2,3},{3,2},{4,5},{5,4},{6,7},{7,6},{8,9},{9,8},{10,11... | collective-permute-start | bytes 4227080 | tf_op jit(solution)/shard_map/ppermute | solution.py:734
  159.9 33.7 %collective-permute-start.26 = (bf16[2,1376,256]{2,1,0:T(8,128)(2,1)S(1)}, bf16[2,1376,256]{2,1,0:T(8,128)(2,1)S(1)}, u32[]{:S(2)}, u32[]{:S(2)}) collective-permute-start(bf16[2,1376,256]{2,1,0:T(8,128)(2,1)S(1)} %pad_maximum_fusion.2.refs_10_), channel_id=1, source_target_pairs={{0,1},{1,0},{2,3},{3,2},{4,5},{5,4},{6,7},{7,6},{8,9},{9,8},{10,11... | collective-permute-start | bytes 4227080 | tf_op jit(solution)/shard_map/ppermute | solution.py:734
  173.3 20.8 %collective-permute-start.27 = (bf16[2,1376,256]{2,1,0:T(8,128)(2,1)S(1)}, bf16[2,1376,256]{2,1,0:T(8,128)(2,1)S(1)}, u32[]{:S(2)}, u32[]{:S(2)}) collective-permute-start(bf16[2,1376,256]{2,1,0:T(8,128)(2,1)S(1)} %pad_maximum_fusion.3.refs_11_), channel_id=1, source_target_pairs={{0,1},{1,0},{2,3},{3,2},{4,5},{5,4},{6,7},{7,6},{8,9},{9,8},{10,11... | collective-permute-start | bytes 4227080 | tf_op jit(solution)/shard_map/ppermute | solution.py:734
  173.4 20.2 %collective-permute-start.28 = (bf16[2,688,256]{2,1,0:T(8,128)(2,1)S(1)}, bf16[2,688,256]{2,1,0:T(8,128)(2,1)S(1)}, u32[]{:S(2)}, u32[]{:S(2)}) collective-permute-start(bf16[2,688,256]{2,1,0:T(8,128)(2,1)S(1)} %collective-permute-done.21.refs_2_.refs_18_), channel_id=1, source_target_pairs={{0,4},{4,8},{8,12},{12,0},{1,5},{5,9},{9,13},{13,1},{2,6},{6,10},{... | collective-permute-start | bytes 2113544 | tf_op jit(solution)/shard_map/ppermute | solution.py:744
  173.7 37.7 %collective-permute-start.29 = (bf16[2,688,256]{2,1,0:T(8,128)(2,1)}, bf16[2,688,256]{2,1,0:T(8,128)(2,1)S(1)}, u32[]{:S(2)}, u32[]{:S(2)}) collective-permute-start(bf16[2,688,256]{2,1,0:T(8,128)(2,1)} %pad_maximum_fusion.14.refs_0_.refs_16_), channel_id=1, source_target_pairs={{0,1},{1,0},{2,3},{3,2},{4,5},{5,4},{6,7},{7,6},{8,9},{9,8},{10,11... | collective-permute-start | bytes 2113544 | tf_op jit(solution)/shard_map/ppermute | solution.py:734
  174.2 37.2 %collective-permute-start.30 = (bf16[2,688,256]{2,1,0:T(8,128)(2,1)}, bf16[2,688,256]{2,1,0:T(8,128)(2,1)S(1)}, u32[]{:S(2)}, u32[]{:S(2)}) collective-permute-start(bf16[2,688,256]{2,1,0:T(8,128)(2,1)} %collective-permute-done.17.refs_1_.refs_17_), channel_id=1, source_target_pairs={{0,1},{1,0},{2,3},{3,2},{4,5},{5,4},{6,7},{7,6},{8,9},{9,8},{10,11... | collective-permute-start | bytes 2113544 | tf_op jit(solution)/shard_map/ppermute | solution.py:734
  193.6 17.8 %collective-permute-start.31 = (bf16[2,688,256]{2,1,0:T(8,128)(2,1)S(1)}, bf16[2,688,256]{2,1,0:T(8,128)(2,1)S(1)}, u32[]{:S(2)}, u32[]{:S(2)}) collective-permute-start(bf16[2,688,256]{2,1,0:T(8,128)(2,1)S(1)} %collective-permute-done.21.refs_2_.refs_18_), channel_id=1, source_target_pairs={{0,1},{1,0},{2,3},{3,2},{4,5},{5,4},{6,7},{7,6},{8,9},{9,8},{10,11... | collective-permute-start | bytes 2113544 | tf_op jit(solution)/shard_map/ppermute | solution.py:734
  193.6 17.8 %collective-permute-start.32 = (bf16[2,688,256]{2,1,0:T(8,128)(2,1)S(1)}, bf16[2,688,256]{2,1,0:T(8,128)(2,1)S(1)}, u32[]{:S(2)}, u32[]{:S(2)}) collective-permute-start(bf16[2,688,256]{2,1,0:T(8,128)(2,1)S(1)} %collective-permute-done.28.refs_3_.refs_19_), channel_id=1, source_target_pairs={{0,1},{1,0},{2,3},{3,2},{4,5},{5,4},{6,7},{7,6},{8,9},{9,8},{10,11... | collective-permute-start | bytes 2113544 | tf_op jit(solution)/shard_map/ppermute | solution.py:734
  220.2 26.4 %collective-permute-start.33 = (bf16[512,1024]{1,0:T(8,128)(2,1)}, bf16[512,1024]{1,0:T(8,128)(2,1)}, u32[]{:S(2)}, u32[]{:S(2)}) collective-permute-start(bf16[512,1024]{1,0:T(8,128)(2,1)} %shard_map.174), channel_id=1, source_target_pairs={{0,16},{1,17},{2,18},{3,19},{4,20},{5,21},{6,22},{7,23},{8,24},{9,... | collective-permute-start | bytes 3145736 | tf_op jit(solution)/shard_map/ppermute | solution.py:966
  385.0 27.2 %collective-permute-start.38 = (bf16[512,1024]{1,0:T(8,128)(2,1)S(1)}, bf16[512,1024]{1,0:T(8,128)(2,1)S(1)}, u32[]{:S(2)}, u32[]{:S(2)}) collective-permute-start(bf16[512,1024]{1,0:T(8,128)(2,1)S(1)} %get-tuple-element.249), channel_id=1, source_target_pairs={{16,0},{17,1},{18,2},{19,3},{20,4},{21,5},{22,6},{23,7},{24,8},{25... | collective-permute-start | bytes 3145736 | tf_op jit(solution)/shard_map/ppermute | solution.py:985
  386.3 26.1 %collective-permute-start.39 = (bf16[512,1408]{1,0:T(8,128)(2,1)S(1)}, bf16[512,1408]{1,0:T(8,128)(2,1)S(1)}, u32[]{:S(2)}, u32[]{:S(2)}) collective-permute-start(bf16[512,1408]{1,0:T(8,128)(2,1)S(1)} %copy-done.109), channel_id=1, source_target_pairs={{0,1},{1,0},{2,3},{3,2},{4,5},{5,4},{6,7},{7,6},{8,9},{9,8},{10,11... | collective-permute-start | bytes 4325384 | tf_op jit(solution)/shard_map/ppermute | solution.py:734
  448.6 33.5 %collective-permute-start.44 = (bf16[512,1408]{1,0:T(8,128)(2,1)}, bf16[512,1408]{1,0:T(8,128)(2,1)S(1)}, u32[]{:S(2)}, u32[]{:S(2)}) collective-permute-start(bf16[512,1408]{1,0:T(8,128)(2,1)} %get-tuple-element.262), channel_id=1, source_target_pairs={{0,1},{1,0},{2,3},{3,2},{4,5},{5,4},{6,7},{7,6},{8,9},{9,8},{10,11... | collective-permute-start | bytes 4325384 | tf_op jit(solution)/shard_map/ppermute | solution.py:734
  449.0 33.1 %collective-permute-start.41 = (bf16[4,688,256]{2,1,0:T(8,128)(2,1)}, bf16[4,688,256]{2,1,0:T(8,128)(2,1)S(1)}, u32[]{:S(2)}, u32[]{:S(2)}) collective-permute-start(bf16[4,688,256]{2,1,0:T(8,128)(2,1)} %copy-done.134), channel_id=1, source_target_pairs={{0,2},{1,3},{2,0},{3,1},{4,6},{5,7},{6,4},{7,5},{8,10},{9,11},{10,... | collective-permute-start | bytes 4227080 | tf_op jit(solution)/shard_map/ppermute | solution.py:739
  449.5 10.7 %collective-permute-start.45 = (bf16[512,1024]{1,0:T(8,128)(2,1)}, bf16[512,1024]{1,0:T(8,128)(2,1)S(1)}, u32[]{:S(2)}, u32[]{:S(2)}) collective-permute-start(bf16[512,1024]{1,0:T(8,128)(2,1)} %get-tuple-element.263.bo_ref), channel_id=1, source_target_pairs={{0,1},{1,0},{2,3},{3,2},{4,5},{5,4},{6,7},{7,6},{8,9},{9,8},{10,11... | collective-permute-start | bytes 3145736 | tf_op jit(solution)/shard_map/ppermute | solution.py:734
  455.5 30.9 %collective-permute-start.47 = (bf16[512,512]{1,0:T(8,128)(2,1)S(1)}, bf16[512,512]{1,0:T(8,128)(2,1)S(1)}, u32[]{:S(2)}, u32[]{:S(2)}) collective-permute-start(bf16[512,512]{1,0:T(8,128)(2,1)S(1)} %slice.238), channel_id=1, source_target_pairs={{0,1},{1,0},{2,3},{3,2},{4,5},{5,4},{6,7},{7,6},{8,9},{9,8},{10,11... | collective-permute-start | bytes 1572872 | tf_op jit(solution)/shard_map/ppermute | solution.py:734
  482.3 11.5 %collective-permute-start.46 = (bf16[688,256]{1,0:T(8,128)(2,1)S(1)}, bf16[688,256]{1,0:T(8,128)(2,1)S(1)}, u32[]{:S(2)}, u32[]{:S(2)}) collective-permute-start(bf16[688,256]{1,0:T(8,128)(2,1)S(1)} %fusion.15), channel_id=1, source_target_pairs={{0,4},{4,8},{8,12},{12,0},{1,5},{5,9},{9,13},{13,1},{2,6},{6,10},{... | collective-permute-start | bytes 1056776 | tf_op jit(solution)/shard_map/ppermute | solution.py:744
  482.5 36.7 %collective-permute-start.50 = (bf16[4,688,256]{2,1,0:T(8,128)(2,1)S(1)}, bf16[4,688,256]{2,1,0:T(8,128)(2,1)S(1)}, u32[]{:S(2)}, u32[]{:S(2)}) collective-permute-start(bf16[4,688,256]{2,1,0:T(8,128)(2,1)S(1)} %get-tuple-element.276), channel_id=1, source_target_pairs={{0,2},{1,3},{2,0},{3,1},{4,6},{5,7},{6,4},{7,5},{8,10},{9,11},{10,... | collective-permute-start | bytes 4227080 | tf_op jit(solution)/shard_map/ppermute | solution.py:739
  493.7 25.4 %collective-permute-start.49 = (bf16[2,688,256]{2,1,0:T(8,128)(2,1)S(1)}, bf16[2,688,256]{2,1,0:T(8,128)(2,1)S(1)}, u32[]{:S(2)}, u32[]{:S(2)}) collective-permute-start(bf16[2,688,256]{2,1,0:T(8,128)(2,1)S(1)} %pad_maximum_fusion.16), channel_id=1, source_target_pairs={{0,4},{4,8},{8,12},{12,0},{1,5},{5,9},{9,13},{13,1},{2,6},{6,10},{... | collective-permute-start | bytes 2113544 | tf_op jit(solution)/shard_map/ppermute | solution.py:744
  493.9 25.3 %collective-permute-start.48 = (bf16[688,256]{1,0:T(8,128)(2,1)S(1)}, bf16[688,256]{1,0:T(8,128)(2,1)S(1)}, u32[]{:S(2)}, u32[]{:S(2)}) collective-permute-start(bf16[688,256]{1,0:T(8,128)(2,1)S(1)} %fusion.8), channel_id=1, source_target_pairs={{0,4},{4,8},{8,12},{12,0},{1,5},{5,9},{9,13},{13,1},{2,6},{6,10},{... | collective-permute-start | bytes 1056776 | tf_op jit(solution)/shard_map/ppermute | solution.py:744
  520.4 27.6 %collective-permute-start.52 = (bf16[2,688,256]{2,1,0:T(8,128)(2,1)}, bf16[2,688,256]{2,1,0:T(8,128)(2,1)}, u32[]{:S(2)}, u32[]{:S(2)}) collective-permute-start(bf16[2,688,256]{2,1,0:T(8,128)(2,1)} %add_convert_fusion.2), channel_id=1, source_target_pairs={{0,4},{4,8},{8,12},{12,0},{1,5},{5,9},{9,13},{13,1},{2,6},{6,10},{... | collective-permute-start | bytes 2113544 | tf_op jit(solution)/shard_map/ppermute | solution.py:744
  520.4 27.6 %collective-permute-start.53 = (bf16[4,256,256]{2,1,0:T(8,128)(2,1)}, bf16[4,256,256]{2,1,0:T(8,128)(2,1)}, u32[]{:S(2)}, u32[]{:S(2)}) collective-permute-start(bf16[4,256,256]{2,1,0:T(8,128)(2,1)} %get-tuple-element.287), channel_id=1, source_target_pairs={{0,2},{1,3},{2,0},{3,1},{4,6},{5,7},{6,4},{7,5},{8,10},{9,11},{10,... | collective-permute-start | bytes 1572872 | tf_op jit(solution)/shard_map/ppermute | solution.py:739
  522.2 25.9 %collective-permute-start.51 = (bf16[688,256]{1,0:T(8,128)(2,1)}, bf16[688,256]{1,0:T(8,128)(2,1)}, u32[]{:S(2)}, u32[]{:S(2)}) collective-permute-start(bf16[688,256]{1,0:T(8,128)(2,1)} %fusion.7), channel_id=1, source_target_pairs={{0,4},{4,8},{8,12},{12,0},{1,5},{5,9},{9,13},{13,1},{2,6},{6,10},{... | collective-permute-start | bytes 1056776 | tf_op jit(solution)/shard_map/ppermute | solution.py:744
  549.2 23.8 %collective-permute-start.55 = (bf16[512,1024]{1,0:T(8,128)(2,1)}, bf16[512,1024]{1,0:T(8,128)(2,1)}, u32[]{:S(2)}, u32[]{:S(2)}) collective-permute-start(bf16[512,1024]{1,0:T(8,128)(2,1)} %pad_maximum_fusion.12), channel_id=1, source_target_pairs={{0,1},{1,0},{2,3},{3,2},{4,5},{5,4},{6,7},{7,6},{8,9},{9,8},{10,11... | collective-permute-start | bytes 3145736 | tf_op jit(solution)/shard_map/ppermute | solution.py:734
  551.3 21.7 %collective-permute-start.54 = (bf16[512,1024]{1,0:T(8,128)(2,1)}, bf16[512,1024]{1,0:T(8,128)(2,1)}, u32[]{:S(2)}, u32[]{:S(2)}) collective-permute-start(bf16[512,1024]{1,0:T(8,128)(2,1)} %pad_maximum_fusion.10), channel_id=1, source_target_pairs={{0,1},{1,0},{2,3},{3,2},{4,5},{5,4},{6,7},{7,6},{8,9},{9,8},{10,11... | collective-permute-start | bytes 3145736 | tf_op jit(solution)/shard_map/ppermute | solution.py:734
  551.3 48.9 %collective-permute-start.62 = (bf16[512,1024]{1,0:T(8,128)(2,1)}, bf16[512,1024]{1,0:T(8,128)(2,1)}, u32[]{:S(2)}, u32[]{:S(2)}) collective-permute-start(bf16[512,1024]{1,0:T(8,128)(2,1)} %get-tuple-element.330.bo_ref), channel_id=1, source_target_pairs={{0,1},{1,0},{2,3},{3,2},{4,5},{5,4},{6,7},{7,6},{8,9},{9,8},{10,11... | collective-permute-start | bytes 3145736 | tf_op jit(solution)/shard_map/ppermute | solution.py:734
  561.2 29.6 %collective-permute-start.57 = (bf16[2,688,256]{2,1,0:T(8,128)(2,1)}, bf16[2,688,256]{2,1,0:T(8,128)(2,1)}, u32[]{:S(2)}, u32[]{:S(2)}) collective-permute-start(bf16[2,688,256]{2,1,0:T(8,128)(2,1)} %add_convert_fusion.1), channel_id=1, source_target_pairs={{0,4},{4,8},{8,12},{12,0},{1,5},{5,9},{9,13},{13,1},{2,6},{6,10},{... | collective-permute-start | bytes 2113544 | tf_op jit(solution)/shard_map/ppermute | solution.py:744
  563.6 27.1 %collective-permute-start.56 = (bf16[688,256]{1,0:T(8,128)(2,1)}, bf16[688,256]{1,0:T(8,128)(2,1)}, u32[]{:S(2)}, u32[]{:S(2)}) collective-permute-start(bf16[688,256]{1,0:T(8,128)(2,1)} %get-tuple-element.315), channel_id=1, source_target_pairs={{0,4},{4,8},{8,12},{12,0},{1,5},{5,9},{9,13},{13,1},{2,6},{6,10},{... | collective-permute-start | bytes 1056776 | tf_op jit(solution)/shard_map/ppermute | solution.py:744
  590.7 9.5 %collective-permute-start.61 = (bf16[2,512,768]{2,1,0:T(8,128)(2,1)}, bf16[2,512,768]{2,1,0:T(8,128)(2,1)S(1)}, u32[]{:S(2)}, u32[]{:S(2)}) collective-permute-start(bf16[2,512,768]{2,1,0:T(8,128)(2,1)} %get-tuple-element.331), channel_id=1, source_target_pairs={{0,1},{1,0},{2,3},{3,2},{4,5},{5,4},{6,7},{7,6},{8,9},{9,8},{10,11... | collective-permute-start | bytes 4718600 | tf_op jit(solution)/shard_map/ppermute | solution.py:734
  594.3 15.3 %collective-permute-start.59 = (bf16[688,256]{1,0:T(8,128)(2,1)S(1)}, bf16[688,256]{1,0:T(8,128)(2,1)S(1)}, u32[]{:S(2)}, u32[]{:S(2)}) collective-permute-start(bf16[688,256]{1,0:T(8,128)(2,1)S(1)} %add_convert_fusion.8), channel_id=1, source_target_pairs={{0,4},{4,8},{8,12},{12,0},{1,5},{5,9},{9,13},{13,1},{2,6},{6,10},{... | collective-permute-start | bytes 1056776 | tf_op jit(solution)/shard_map/ppermute | solution.py:744
  594.3 15.2 %collective-permute-start.58 = (bf16[256,1024]{1,0:T(8,128)(2,1)}, bf16[256,1024]{1,0:T(8,128)(2,1)S(1)}, u32[]{:S(2)}, u32[]{:S(2)}) collective-permute-start(bf16[256,1024]{1,0:T(8,128)(2,1)} %slice_select_fusion.1), channel_id=1, source_target_pairs={{0,2},{1,3},{2,0},{3,1},{4,6},{5,7},{6,4},{7,5},{8,10},{9,11},{10,... | collective-permute-start | bytes 1572872 | tf_op jit(solution)/shard_map/ppermute | solution.py:739
  595.6 14.0 %collective-permute-start.60 = (bf16[256,256]{1,0:T(8,128)(2,1)S(1)}, bf16[256,256]{1,0:T(8,128)(2,1)S(1)}, u32[]{:S(2)}, u32[]{:S(2)}) collective-permute-start(bf16[256,256]{1,0:T(8,128)(2,1)S(1)} %copy-done.159), channel_id=1, source_target_pairs={{0,4},{4,8},{8,12},{12,0},{1,5},{5,9},{9,13},{13,1},{2,6},{6,10},{... | collective-permute-start | bytes 393224 | tf_op jit(solution)/shard_map/ppermute | solution.py:744
  610.7 15.6 %collective-permute-start.64 = (bf16[688,256]{1,0:T(8,128)(2,1)S(1)}, bf16[688,256]{1,0:T(8,128)(2,1)S(1)}, u32[]{:S(2)}, u32[]{:S(2)}) collective-permute-start(bf16[688,256]{1,0:T(8,128)(2,1)S(1)} %add_convert_fusion.7), channel_id=1, source_target_pairs={{0,4},{4,8},{8,12},{12,0},{1,5},{5,9},{9,13},{13,1},{2,6},{6,10},{... | collective-permute-start | bytes 1056776 | tf_op jit(solution)/shard_map/ppermute | solution.py:744
  612.6 20.9 %collective-permute-start.66 = (bf16[4,384,256]{2,1,0:T(8,128)(2,1)S(1)}, bf16[4,384,256]{2,1,0:T(8,128)(2,1)S(1)}, u32[]{:S(2)}, u32[]{:S(2)}) collective-permute-start(bf16[4,384,256]{2,1,0:T(8,128)(2,1)S(1)} %slice.265), channel_id=1, source_target_pairs={{0,2},{1,3},{2,0},{3,1},{4,6},{5,7},{6,4},{7,5},{8,10},{9,11},{10,... | collective-permute-start | bytes 2359304 | tf_op jit(solution)/shard_map/ppermute | solution.py:739
  613.2 20.3 %collective-permute-start.63 = (bf16[2,384,256]{2,1,0:T(8,128)(2,1)S(1)}, bf16[2,384,256]{2,1,0:T(8,128)(2,1)S(1)}, u32[]{:S(2)}, u32[]{:S(2)}) collective-permute-start(bf16[2,384,256]{2,1,0:T(8,128)(2,1)S(1)} %pad_maximum_fusion.19), channel_id=1, source_target_pairs={{0,4},{4,8},{8,12},{12,0},{1,5},{5,9},{9,13},{13,1},{2,6},{6,10},{... | collective-permute-start | bytes 1179656 | tf_op jit(solution)/shard_map/ppermute | solution.py:744
  616.1 22.4 %collective-permute-start.74 = (bf16[688,256]{1,0:T(8,128)(2,1)S(1)}, bf16[688,256]{1,0:T(8,128)(2,1)S(1)}, u32[]{:S(2)}, u32[]{:S(2)}) collective-permute-start(bf16[688,256]{1,0:T(8,128)(2,1)S(1)} %slice_bitcast_fusion), channel_id=1, source_target_pairs={{0,2},{1,3},{2,0},{3,1},{4,6},{5,7},{6,4},{7,5},{8,10},{9,11},{10,... | collective-permute-start | bytes 1056776 | tf_op jit(solution)/shard_map/ppermute | solution.py:739
  633.5 8.3 %collective-permute-start.69 = (bf16[256,256]{1,0:T(8,128)(2,1)S(1)}, bf16[256,256]{1,0:T(8,128)(2,1)S(1)}, u32[]{:S(2)}, u32[]{:S(2)}) collective-permute-start(bf16[256,256]{1,0:T(8,128)(2,1)S(1)} %add_convert_fusion.20), channel_id=1, source_target_pairs={{0,4},{4,8},{8,12},{12,0},{1,5},{5,9},{9,13},{13,1},{2,6},{6,10},{... | collective-permute-start | bytes 393224 | tf_op jit(solution)/shard_map/ppermute | solution.py:744
  635.5 16.8 %collective-permute-start.67 = (bf16[2,384,256]{2,1,0:T(8,128)(2,1)S(1)}, bf16[2,384,256]{2,1,0:T(8,128)(2,1)S(1)}, u32[]{:S(2)}, u32[]{:S(2)}) collective-permute-start(bf16[2,384,256]{2,1,0:T(8,128)(2,1)S(1)} %add_convert_fusion.5), channel_id=1, source_target_pairs={{0,4},{4,8},{8,12},{12,0},{1,5},{5,9},{9,13},{13,1},{2,6},{6,10},{... | collective-permute-start | bytes 1179656 | tf_op jit(solution)/shard_map/ppermute | solution.py:744
  636.6 15.6 %collective-permute-start.68 = (bf16[384,256]{1,0:T(8,128)(2,1)S(1)}, bf16[384,256]{1,0:T(8,128)(2,1)S(1)}, u32[]{:S(2)}, u32[]{:S(2)}) collective-permute-start(bf16[384,256]{1,0:T(8,128)(2,1)S(1)} %fusion.23), channel_id=1, source_target_pairs={{0,4},{4,8},{8,12},{12,0},{1,5},{5,9},{9,13},{13,1},{2,6},{6,10},{... | collective-permute-start | bytes 589832 | tf_op jit(solution)/shard_map/ppermute | solution.py:744
  652.3 9.7 %collective-permute-start.71 = (bf16[384,256]{1,0:T(8,128)(2,1)S(1)}, bf16[384,256]{1,0:T(8,128)(2,1)S(1)}, u32[]{:S(2)}, u32[]{:S(2)}) collective-permute-start(bf16[384,256]{1,0:T(8,128)(2,1)S(1)} %fusion.14), channel_id=1, source_target_pairs={{0,4},{4,8},{8,12},{12,0},{1,5},{5,9},{9,13},{13,1},{2,6},{6,10},{... | collective-permute-start | bytes 589832 | tf_op jit(solution)/shard_map/ppermute | solution.py:744
  652.5 14.8 %collective-permute-start.70 = (bf16[2,384,256]{2,1,0:T(8,128)(2,1)S(1)}, bf16[2,384,256]{2,1,0:T(8,128)(2,1)S(1)}, u32[]{:S(2)}, u32[]{:S(2)}) collective-permute-start(bf16[2,384,256]{2,1,0:T(8,128)(2,1)S(1)} %add_convert_fusion.4), channel_id=1, source_target_pairs={{0,4},{4,8},{8,12},{12,0},{1,5},{5,9},{9,13},{13,1},{2,6},{6,10},{... | collective-permute-start | bytes 1179656 | tf_op jit(solution)/shard_map/ppermute | solution.py:744
  669.8 16.3 %collective-permute-start.72 = (bf16[384,256]{1,0:T(8,128)(2,1)S(1)}, bf16[384,256]{1,0:T(8,128)(2,1)S(1)}, u32[]{:S(2)}, u32[]{:S(2)}) collective-permute-start(bf16[384,256]{1,0:T(8,128)(2,1)S(1)} %fusion.13), channel_id=1, source_target_pairs={{0,4},{4,8},{8,12},{12,0},{1,5},{5,9},{9,13},{13,1},{2,6},{6,10},{... | collective-permute-start | bytes 589832 | tf_op jit(solution)/shard_map/ppermute | solution.py:744
  (183 other events, 3187.2 us)

commit v3 on v2

--- a/solution.py
+++ b/solution.py
@@ -41,7 +41,7 @@
 
 
 def cost(flops, nbytes, trans=0):
-    return pl.CostEstimate(flops=1000, bytes_accessed=1000, transcendentals=0)
+    return pl.CostEstimate(flops=int(flops), bytes_accessed=int(nbytes), transcendentals=0)
 
 
 def sds(shape, dtype):
@@ -181,7 +181,7 @@
         out_specs=specs,
         out_shape=outs,
         scratch_shapes=[pltpu.VMEM((4, rows, ZB), BF)] + weight_scratch(feats),
-        compiler_params=params(22),
+        compiler_params=params(),
         cost_estimate=cost(2 * rows * model * 3 * total, 6 * total * model + 16 * x.size),
     )(x, gain, zi, cos, sin, *w)
 
@@ -251,7 +251,7 @@
         ],
         out_specs=[col, col],
         out_shape=[sds((rows, total), BF), sds((rows, total), F32)],
-        compiler_params=params(10),
+        compiler_params=params(),
         cost_estimate=cost(
             4 * 2 * rows * rows * 2 * total, 20 * rows * total, rows * rows * 2 * pairs * 2
         ),
@@ -395,7 +395,7 @@
         + weight_scratch(width)
         + pair_scratch(2, hidden)
         + [pltpu.VMEM((4, rows, ZB), F32), pltpu.VMEM((rows, wide), BF)],
-        compiler_params=params(30),
+        compiler_params=params(),
         cost_estimate=cost(
             2 * rows * model * (8 * hidden + model), 16 * hidden * model + 20 * x.size
         ),
@@ -619,7 +619,7 @@
             sds((rows, total), BF),
             sds((pairs, 4, rows), F32),
         ],
-        compiler_params=params(14),
+        compiler_params=params(),
         cost_estimate=cost(
             10 * 2 * rows * rows * 2 * total, 40 * rows * total, rows * rows * 2 * pairs * 2
         ),
@@ -693,7 +693,7 @@
         + [sds((rows, model), F32), sds((rows, model), BF), sds((1, model), F32)],
         scratch_shapes=[pltpu.VMEM((rows, feats), BF), pltpu.VMEM((4, rows, ZB), F32)]
         + weight_scratch(feats),
-        compiler_params=params(24),
+        compiler_params=params(),
         cost_estimate=cost(8 * rows * model * feats, 8 * feats * model + 40 * x.size),
     )(dq, dk, dkr, dv, dvr, q0, k0, cos, sin, x, dh, gain, zi, *w)
 
@@ -755,11 +755,23 @@
 
 
 def meet(*values):
-    return lax.optimization_barrier(values)
+    return list(lax.optimization_barrier(values))
 
 
 def after(value, *others):
     return lax.optimization_barrier((value, others))[0]
+
+
+def to_owner(part, r):
+    n = lax.axis_size("dp")
+    return lax.ppermute(part, "dp", [(i, (i - r) % n) for i in range(n)])
+
+
+def add_all(own, others):
+    total = own.astype(F32)
+    for other in others:
+        total = total + other.astype(F32)
+    return total
 
 
 def scatter_any(keep, send):
@@ -793,7 +805,7 @@
     return own, oth
 
 
-def tables(segment, variate, time_row, pad, var_bias, core):
+def tables(segment, variate, time_row, pad, core):
     seg_own, seg_oth = own_rows(segment, core)
     var_own, var_oth = own_rows(variate, core)
     pad_own, pad_oth = own_rows(pad, core)
@@ -832,12 +844,6 @@
             jnp.where(lane == L_PAD, 1.0, 0.0),
         ),
     ).astype(F32)
-    delta = (var_bias[:, 0] - var_bias[:, 1]) * math.sqrt(HD)
-    hi = delta.astype(BF).astype(F32)
-    low = (delta - hi).astype(BF).astype(F32)
-    head_scale = jnp.where(
-        lane < N_VAR, hi[:, None], jnp.where(lane < 2 * N_VAR, low[:, None], 1.0)
-    ).reshape(-1, 2, 128)
     place = jnp.arange(rows, dtype=jnp.int32)
     neg = jnp.where(pad_own == 1, 0.0, -BIG).astype(F32)
     eye = place[:, None] == place[None, :]
@@ -846,7 +852,17 @@
     var_q = jnp.where(
         var_own[None, :] == jnp.arange(8, dtype=jnp.int32)[:, None], 1.0, 0.0
     ).astype(F32)
-    return cos, sin, aug_q, aug_k, head_scale, add_q, add_k, var_q
+    return cos, sin, aug_q, aug_k, add_q, add_k, var_q
+
+
+def head_scales(var_bias):
+    lane = (jnp.arange(128, dtype=jnp.int32) % HD)[None, :]
+    delta = (var_bias[:, 0] - var_bias[:, 1]) * math.sqrt(HD)
+    hi = delta.astype(BF).astype(F32)
+    low = (delta - hi).astype(BF).astype(F32)
+    return jnp.where(
+        lane < N_VAR, hi[:, None], jnp.where(lane < 2 * N_VAR, low[:, None], 1.0)
+    ).reshape(-1, 2, 128)
 
 
 def small_rows(gg_a, gg_f, bias, ti, heads_local):
@@ -895,15 +911,25 @@
     p2 = w_gate_up[0].transpose(1, 2, 0).reshape(2 * hidden, cols)
     p3 = w_down[0]
 
+    def both_ends(came):
+        return jnp.where(
+            yi == 0, jnp.concatenate([own, came], axis=0), jnp.concatenate([came, own], axis=0)
+        )
+
+    tab = tables(
+        row_of(segment_ids), row_of(variate_ids), row_of(time_ids), row_of(padding_mask), core
+    )
+
     if near:
         a1, came = ring(p1), y_swap(away)
         a1, came, p1, p2, p3 = meet(a1, came, p1, p2, p3)
         a2, y0 = ring(a1), y_swap(p1)
-        a1, a2, y0, p2, p3 = meet(a1, a2, y0, p2, p3)
+        a1, a2, y0, p2, p3, *tab = meet(a1, a2, y0, p2, p3, *tab)
+        ends = both_ends(came)
         a3, y1 = ring(a2), y_swap(a1)
         n1 = [jnp.stack([p1, y0])]
         f1 = [core_swap(n1[0])]
-        a2, a3, y1, p2, p3 = meet(a2, a3, y1, p2, p3)
+        a2, a3, y1, p2, p3, ends = meet(a2, a3, y1, p2, p3, ends)
         b1, y2, d0 = ring(p2), y_swap(a2), y_swap(p3)
         n1.append(jnp.stack([a1, y1]))
         f1.append(core_swap(n1[1]))
@@ -918,21 +944,16 @@
         b3, g0 = ring(b2), y_swap(p2)
     else:
         w1 = gather_any(p1)
-        came = y_swap(away)
-    ends = jnp.where(
-        yi == 0, jnp.concatenate([own, came], axis=0), jnp.concatenate([came, own], axis=0)
-    )
+        ends = both_ends(y_swap(away))
     gains = jnp.stack([w[0, low : low + 2] for w in w1[:4]])
     gains = jnp.take(gains, (zi[0] - jnp.arange(4)) % 4, axis=0)
     gains = gains.transpose(1, 0, 2).reshape(2, model).astype(F32)
     gain_a, gain_f = gains[:1], gains[1:]
     bias = [w[:, low + 2, : 2 * heads_local] for w in (w1[0], w1[4])]
     bias = jnp.concatenate(bias).reshape(4 * heads_local, 2).astype(F32)
-    tab = tables(
-        row_of(segment_ids), row_of(variate_ids), row_of(time_ids), row_of(padding_mask),
-        bias, core,
-    )
-    cos, sin, aug_q, aug_k, head_scale, add_q, add_k, var_q = tab
+    head_scale = head_scales(bias)
+    cos, sin, aug_q, aug_k, add_q, add_k, var_q = tab
+    tab = (cos, sin, aug_q, aug_k, head_scale, add_q, add_k, var_q)
 
     q, k, v = qkv_call(False, ends, gain_a, zi, w1, low, cos, sin)
     if near:
@@ -955,6 +976,7 @@
         n2.append(jnp.stack([b2, g2]))
         f2.append(core_swap(n2[2]))
         f3.append(core_swap(c2))
+        b3, c3, g3 = meet(b3, c3, g3)
         n2.append(jnp.stack([b3, g3]))
         f2.append(core_swap(n2[3]))
         f3.append(core_swap(c3))
@@ -986,111 +1008,95 @@
     z_oth, n2_oth, n1_oth = core_swap(z_far), core_swap(n2), core_swap(n1)
     o_oth = core_swap(o[:, 2 * width :])
 
+    got, y, z_oth, n2_oth, n1_oth, o_oth = meet(got, y, z_oth, n2_oth, n1_oth, o_oth)
+
     df = jnp.where(is_first, got, ends)
     down_keep, down_send = wgrad_call(zi, hidden, z_near, df, z_oth, core_swap(df))
     df, down_keep, down_send = meet(df, down_keep, down_send)
     down_got = y_swap(down_send)
-    dh, da, do, dg_near, dg_far, du_near, du_far, gg_f = ffn_back_call(
-        out_low, width, df, h, g, u, gain_f, zi, w1, w2, w3
+    back = ffn_back_call(out_low, width, df, h, g, u, gain_f, zi, w1, w2, w3)
+    down_keep, down_got, *back = meet(down_keep, down_got, *back)
+    dh, da, do, dg_near, dg_far, du_near, du_far, gg_f = back
+    dg_oth, du_oth, da_oth = core_swap(dg_far), core_swap(du_far), core_swap(da)
+    if near:
+        down = [plus(down_keep[r], down_got[r]) for r in range(4)]
+        down_run = ring(down[1])
+        dg_oth, du_oth, da_oth, down_run = meet(dg_oth, du_oth, da_oth, down_run)
+        down_run = ring(plus(down_run, down[2]))
+    else:
+        down_run = down_got
+    gate_keep, gate_send = wgrad_call(zi, hidden, dg_near, n2, dg_oth, n2_oth)
+    out_keep, out_send = wgrad_call(zi, width, o, da, o_oth, da_oth)
+    do, gate_keep, gate_send, out_keep, out_send, down_run = meet(
+        do, gate_keep, gate_send, out_keep, out_send, down_run
     )
-    gate_keep, gate_send = wgrad_call(zi, hidden, dg_near, n2, core_swap(dg_far), n2_oth)
-    du_oth, da_oth = core_swap(du_far), core_swap(da)
+    back = attend_back_call(
+        scale, None, q, k, k_oth, v, v_oth, do, o, sums, aug_q, aug_k, head_scale, add_k, var_q
+    )
+    half = hidden // 32 * 16
     cut = width * 3 // 2
     if near:
-        down_keep, down_got, gate_keep, gate_send, du_oth, da_oth, do = meet(
-            down_keep, down_got, gate_keep, gate_send, du_oth, da_oth, do
-        )
         gate_got = y_swap(gate_send)
-        down = [plus(down_keep[r], down_got[r]) for r in range(4)]
-        down_run = ring(down[1])
+        down_run = ring(plus(down_run, down[3]))
+        out = [jnp.stack([out_keep[r], out_send[r]]) for r in range(4)]
+        out_run = [to_owner(out[r], r) for r in (1, 2, 3)]
+        gate_got, down_run, *rest = meet(gate_got, down_run, *out_run, *back)
+        out_run, back = rest[:3], rest[3:]
+        g_down = down_run.astype(F32) + down[0].astype(F32)
+        out_sum = add_all(out[0], out_run)
+    dq, dk, dk_send, dv, dv_send, bias = back
+    dk_got, dv_got = core_swap(dk_send), core_swap(dv_send)
     up_keep, up_send = wgrad_call(zi, hidden, du_near, n2, du_oth, n2_oth)
-    out_keep, out_send = wgrad_call(zi, width, o, da, o_oth, da_oth)
-
-    def attend_back(do, low, high):
-        return attend_back_call(
-            scale, (low, high), q, k, k_oth, v, v_oth, do, o, sums, aug_q, aug_k, head_scale,
-            add_k, var_q,
-        )
-
-    pairs = do.shape[1] // 128
+    dk_got, dv_got, up_keep, up_send = meet(dk_got, dv_got, up_keep, up_send)
     if near:
-        up = [jnp.stack([up_keep[r], up_send[r]]) for r in range(4)]
-        down_run, do, *up = meet(down_run, do, *up, out_send)[:6]
-        down_run = ring(plus(down_run, down[2]))
-        up_run = ring(up[1])
-        first = attend_back(do, 0, pairs // 2)
-        down_run, up_run, gate_got, do, out_send, *first = meet(
-            down_run, up_run, gate_got, do, out_send, *first
-        )
-        out_got = y_swap(out_send)
-        down_run = ring(plus(down_run, down[3]))
-        up_run = ring(plus(up_run, up[2]))
+        up_got = [y_swap(up_send[:, :half])]
         gate = [plus(gate_keep[r], gate_got[r]) for r in range(4)]
-    else:
-        first = attend_back(do, 0, pairs // 2)
-    second = attend_back(do, pairs // 2, pairs)
+        gate_run = [to_owner(gate[r][:half], r) for r in (1, 2, 3)]
+    back = qkv_back(dq, dk, dk_got, dv, dv_got, dh)
     if near:
-        down_run, up_run, out_got, first, second, *gate = meet(
-            down_run, up_run, out_got, first, second, *gate
-        )
-        gate_run = ring(gate[1])
-        up_run = ring(plus(up_run, up[3]))
-        g_down = down_run.astype(F32) + down[0].astype(F32)
-        out = [plus(out_keep[r], out_got[r]) for r in range(4)]
-    dq, dk, dk_send, dv, dv_send, bias = (
-        jnp.concatenate([b, a] if i in (2, 4) else [a, b], axis=0 if i == 5 else 1)
-        for i, (a, b) in enumerate(zip(first, second))
-    )
-    dp_near, dp_far, dx, dx_low, gg_a = qkv_back(
-        dq, dk, core_swap(dk_send), dv, core_swap(dv_send), dh
-    )
+        rest = meet(*up_got, *gate_run, *back)
+        up_got, gate_run, back = rest[:1], rest[1:4], rest[4:]
+        up_got.append(y_swap(up_send[:, half:]))
+        gate_more = [to_owner(gate[r][half:], r) for r in (1, 2, 3)]
+    dp_near, dp_far, dx, dx_low, gg_a = back
+    dp_oth = core_swap(dp_far)
+    qkv_keep, qkv_send = wgrad_call(zi, 3 * width, dp_near, n1, dp_oth, n1_oth)
+    small = small_rows(gg_a, gg_f, bias, ti, heads_local)
     out_low_rows = jnp.where(is_first, dx_low, y.astype(BF))
     send = jnp.where(yi == 0, out_low_rows[rows:], out_low_rows[:rows])
     if near:
-        gate_run, up_run, send, dp_near, dp_far, *out = meet(
-            gate_run, up_run, send, dp_near, dp_far, *out
+        up_last, qkv_keep, qkv_send, small, send, *gate_more = meet(
+            up_got[1], qkv_keep, qkv_send, small, send, *gate_more
         )
-        rows_got = y_swap(send)
-        gate_run = ring(plus(gate_run, gate[2]))
-        out_run = ring(out[1])
-        up_run = plus(up_run, up[0])
-    qkv_keep, qkv_send = wgrad_call(zi, 3 * width, dp_near, n1, core_swap(dp_far), n1_oth)
-    small = small_rows(gg_a, gg_f, bias, ti, heads_local)
-    if near:
-        rows_got, gate_run, out_run, up_run, qkv_keep, qkv_send, small = meet(
-            rows_got, gate_run, out_run, up_run, qkv_keep, qkv_send, small
-        )
-        head_got = y_swap(qkv_send[:, :cut])
-        up_got = y_swap(up_run[1])
-        tails = [jnp.stack([qkv_keep[r, cut:], qkv_send[r, cut:]]) for r in range(4)]
-        tail_run = ring(tails[1])
-        gate_run = ring(plus(gate_run, gate[3]))
-        out_run = ring(plus(out_run, out[2]))
-        g_gu_up = up_run[0].astype(F32)
-        tail_run, gate_run, out_run, head_got = meet(tail_run, gate_run, out_run, head_got)
-        tail_run = ring(plus(tail_run, tails[2]))
-        out_run = ring(plus(out_run, out[3]))
-        heads_sum = [plus(qkv_keep[r, :cut], head_got[r]) for r in range(4)]
-        head_run = ring(heads_sum[1])
-        tail_run, head_run, out_run = meet(tail_run, head_run, out_run)
-        tail_run = ring(plus(tail_run, tails[3]))
-        head_run = ring(plus(head_run, heads_sum[2]))
-        tail_run, head_run, small = meet(tail_run, head_run, small)
-        tail_run = plus(tail_run, tails[0])
-        tail_got = y_swap(tail_run[1])
-        head_run = ring(plus(head_run, heads_sum[3]))
-        small = small_sum(small)
-        g_qkv = jnp.concatenate(
+        g_gate = jnp.concatenate(
             [
-                head_run.astype(F32) + heads_sum[0].astype(F32),
-                tail_run[0].astype(F32) + tail_got.astype(F32),
+                add_all(gate[0][:half], gate_run),
+                add_all(gate[0][half:], gate_more),
             ],
             axis=0,
         )
-        g_out = out_run.astype(F32) + out[0].astype(F32)
-        g_gu = jnp.stack(
-            [gate_run.astype(F32) + gate[0].astype(F32), g_gu_up + up_got.astype(F32)]
-        )
+        head_got = y_swap(qkv_send[:, :cut])
+        rows_got = y_swap(send)
+        up = [
+            plus(up_keep[r], jnp.concatenate([up_got[0][r], up_last[r]], axis=0))
+            for r in range(4)
+        ]
+        up_run = [to_owner(up[r], r) for r in (1, 2, 3)]
+        head_got, rows_got, *up_run = meet(head_got, rows_got, *up_run)
+        tail_got = y_swap(qkv_send[:, cut:])
+        head = [plus(qkv_keep[r, :cut], head_got[r]) for r in range(4)]
+        head_run = [to_owner(head[r], r) for r in (1, 2, 3)]
+        tail_got, small, out_sum, *head_run = meet(tail_got, small, out_sum, *head_run)
+        small = small + core_swap(small)
+        small = small + y_swap(small)
+        tail = [plus(qkv_keep[r, cut:], tail_got[r]) for r in range(4)]
+        tail_run = [to_owner(tail[r], r) for r in (1, 2, 3)]
+        out_got = y_swap(out_sum[1].astype(BF))
+        for bit in (1, 2):
+            small = small + lax.ppermute(small, "dp", [(i, i ^ bit) for i in range(4)])
+        g_gu = jnp.stack([g_gate, add_all(up[0], up_run)])
+        g_out = out_sum[0] + out_got.astype(F32)
+        g_qkv = jnp.concatenate([add_all(head[0], head_run), add_all(tail[0], tail_run)], axis=0)
     else:
         rows_got = y_swap(send)
         g_down = scatter_any(down_keep, down_send)

time: 697 us -> 656 us (0.941)
  waiting for transfers between devices: 268 us -> 216 us
  local copies, waits for them, and re-layouts: 58.1 us -> 37.3 us
  starting transfers between devices: 53.2 us -> 72.7 us
  Pallas kernels: 256 us -> 271 us
    ppermute x27 -> x12, waiting for transfers between devices: 123 us -> 65 us  [ring(): return lax.ppermute(value, 'dp', [(i, (i + 1) % n) for i in range(n)])]
    ppermute x2 -> x20, waiting for transfers between devices: 7.2 us -> 51.1 us  [the longest x18 37.2 us: to_owner(): return lax.ppermute(part, 'dp', [(i, (i - r) % n) for i in range(n)])]
    ppermute x2 -> x20, starting transfers between devices: 1.66 us -> 30.3 us  [the longest x18 28.8 us: to_owner(): return lax.ppermute(part, 'dp', [(i, (i - r) % n) for i in range(n)])]
    unnamed x339 -> x209, local copies, waits for them, and re-layouts: 44.9 us -> 18.2 us
    ppermute x18 -> x19, waiting for transfers between devices: 74.6 us -> 48.4 us  [y_swap(): return lax.ppermute(value, 'tensor', [(i, i ^ 2) for i in range(n)])]
    ppermute x27 -> x12, starting transfers between devices: 20.6 us -> 10 us  [ring(): return lax.ppermute(value, 'dp', [(i, (i + 1) % n) for i in range(n)])]
    ppermute x1, waiting for transfers between devices: 25.7 us -> 15.5 us  [per_device(): got = lax.ppermute(dx_low, 'section', [(1, 0)])]
    pallas_call x5, Pallas kernels: 16.6 us -> 23.6 us  [wgrad_call(): pl.pallas_call(functools.partial(wgrad_kernel, feats), grid=(1,), in_spec...]
  transfers between devices with their start and end apart: 79 -> 83, of which waited for: 34 -> 27; matrix products, arithmetic and copies ran while one was open for 8% -> 9% of each run, Pallas kernels for 15% -> 25%
where the time goes in v3:
time: 656 us; the launch traced here: 648 us
  Pallas kernels  271 us (41%)
  waiting for transfers between devices  216 us (33%)
  starting transfers between devices  72.7 us (11%)
  other arithmetic  47.6 us (7%)
  local copies, waits for them, and re-layouts  37.3 us (6%)
    ppermute x12, waiting for transfers between devices, ring(): return lax.ppermute(value, 'dp', [(i, (i + 1) % n) for i in range(n)])  65 us
    pallas_call x2, Pallas kernels, ffn_back_call(): pl.pallas_call(functools.partial(ffn_back_kernel, out_low), grid=(2,), in...  55.4 us
    pallas_call x2, Pallas kernels, attend_back_call(): pl.pallas_call(functools.partial(attend_back_kernel, scale), grid=(pairs,...  54.4 us
    ppermute x19, waiting for transfers between devices, y_swap(): return lax.ppermute(value, 'tensor', [(i, i ^ 2) for i in range(n)])  48.4 us
    pallas_call x2, Pallas kernels, ffn_up_call(): pl.pallas_call(functools.partial(ffn_up_kernel, save, out_low), grid=(2,)...  38.1 us
    ppermute x18, waiting for transfers between devices, to_owner(): return lax.ppermute(part, 'dp', [(i, (i - r) % n) for i in range(n)])  37.2 us
    pallas_call x2, Pallas kernels, qkv_back_call(): pl.pallas_call(qkv_back_kernel, grid=(4,), in_specs=[col] * 7 + [whole((r...  33.5 us
    pallas_call x2, Pallas kernels, attend_call(): pl.pallas_call(functools.partial(attend_kernel, scale), grid=(pairs,), in...  30.4 us
  transfers between devices with their start and end apart: 83, of which 27 were waited for; matrix products, arithmetic and copies ran while one was open for 9% of the time, Pallas kernels for 25%

profile of v3, /device:TPU:0, one launch (start us, length us, event | category | flops | bytes accessed | tf_op | source)
XLA Modules:
  0.0 647.5 jit_solution(17524090259062272587)
XLA Ops:
  4.3 3.1 collective-permute-start
  7.4 1.7 fusion.15
  15.6 7.0 %collective-permute-done.1 = bf16[256,1024]{1,0:T(8,128)(2,1)S(1)} collective-permute-done((bf16[256,1024]{1,0:T(8,128)(2,1)S(1)}, bf16[256,1024]{1,0:T(8,128)(2,1)S(1)}, u32[]{:S(2)}, u32[]{:S(2)}) %collective-permute-start.1) | collective-permute-done | bytes 524320 | tf_op jit(solution)/shard_map/ppermute | solution.py:739
  28.7 8.5 %collective-permute-done.2 = bf16[1040,256]{1,0:T(8,128)(2,1)} collective-permute-done((bf16[1040,256]{1,0:T(8,128)(2,1)S(1)}, bf16[1040,256]{1,0:T(8,128)(2,1)}, u32[]{:S(2)}, u32[]{:S(2)}) %collective-permute-start.2) | collective-permute-done | bytes 532512 | tf_op jit(solution)/shard_map/ppermute | solution.py:744
  39.7 2.6 maximum_select_fusion.1.x_ref.dy_ref
  42.3 8.7 %collective-permute-done.4 = bf16[1040,256]{1,0:T(8,128)(2,1)} collective-permute-done((bf16[1040,256]{1,0:T(8,128)(2,1)}, bf16[1040,256]{1,0:T(8,128)(2,1)}, u32[]{:S(2)}, u32[]{:S(2)}) %collective-permute-start.4) | collective-permute-done | bytes 532512 | tf_op jit(solution)/shard_map/ppermute | solution.py:744
  53.8 15.9 %collective-permute-done.8 = bf16[688,256]{1,0:T(8,128)(2,1)S(1)} collective-permute-done((bf16[688,256]{1,0:T(8,128)(2,1)S(1)}, bf16[688,256]{1,0:T(8,128)(2,1)S(1)}, u32[]{:S(2)}, u32[]{:S(2)}) %collective-permute-start.8) | collective-permute-done | bytes 352288 | tf_op jit(solution)/shard_map/ppermute | solution.py:739
  75.2 10.1 %collective-permute-done.10 = bf16[1040,256]{1,0:T(8,128)(2,1)S(1)} collective-permute-done((bf16[1040,256]{1,0:T(8,128)(2,1)}, bf16[1040,256]{1,0:T(8,128)(2,1)S(1)}, u32[]{:S(2)}, u32[]{:S(2)}) %collective-permute-start.10) | collective-permute-done | bytes 532512 | tf_op jit(solution)/shard_map/ppermute | solution.py:739
  85.4 2.4 pad_maximum_fusion.7.refs_3_
  96.5 10.7 %shard_map.171 = (bf16[512,1024]{1,0:T(8,128)(2,1)}, bf16[512,1024]{1,0:T(8,128)(2,1)}, bf16[512,1024]{1,0:T(8,128)(2,1)}) custom-call(bf16[512,1024]{1,0:T(8,128)(2,1)} %maximum_select_fusion.1.x_ref.dy_ref, f32[1,1024]{1,0:T(1,128)} %bitcast.204, s32[1]{0:T(128)} %bitcast.25.zi_ref, f32[512,128]{1,0:T(8,128)} %pad_maximum_fusion.10.cos_ref, ...), custom_call_target="tpu_custom_call" | custom-call | flops 3221225472 | bytes 14680064 | tf_op jit(solution)/shard_map/pallas_call | solution.py:175
  107.2 5.3 collective-permute-done.11
  118.4 15.3 %shard_map.172 = (bf16[512,1024]{1,0:T(8,128)(2,1)}, f32[512,1024]{1,0:T(8,128)}) custom-call(bf16[512,1024]{1,0:T(8,128)(2,1)} %get-tuple-element.224.q_ref, bf16[512,1024]{1,0:T(8,128)(2,1)} %get-tuple-element.225.ko_ref, bf16[512,1024]{1,0:T(8,128)(2,1)} %collective-permute-done.19.kx_ref, bf16[512,1024]{1,0:T(8,128)(2,1)} %get-tuple-element.226.vo_ref, ...), custom_call_target="tpu_custom_call" | custom-call | flops 4294967296 | bytes 10485760 | tf_op jit(solution)/shard_map/pallas_call | solution.py:238
  135.6 17.1 %collective-permute-done.21.refs_2_.refs_18_ = bf16[2,688,256]{2,1,0:T(8,128)(2,1)S(1)} collective-permute-done((bf16[2,688,256]{2,1,0:T(8,128)(2,1)S(1)}, bf16[2,688,256]{2,1,0:T(8,128)(2,1)S(1)}, u32[]{:S(2)}, u32[]{:S(2)}) %collective-permute-start.21) | collective-permute-done | bytes 704544 | tf_op jit(solution)/shard_map/ppermute | solution.py:744
  158.5 12.6 %collective-permute-done.23.refs_3_.refs_19_ = bf16[2,688,256]{2,1,0:T(8,128)(2,1)S(1)} collective-permute-done((bf16[2,688,256]{2,1,0:T(8,128)(2,1)S(1)}, bf16[2,688,256]{2,1,0:T(8,128)(2,1)S(1)}, u32[]{:S(2)}, u32[]{:S(2)}) %collective-permute-start.23) | collective-permute-done | bytes 704544 | tf_op jit(solution)/shard_map/ppermute | solution.py:744
  172.5 2.0 collective-permute-done.28.refs_15_
  175.6 18.4 %shard_map.173 = (f32[512,1024]{1,0:T(8,128)}, bf16[512,1408]{1,0:T(8,128)(2,1)}, bf16[512,1408]{1,0:T(8,128)(2,1)}) custom-call(bf16[512,1024]{1,0:T(8,128)(2,1)} %maximum_select_fusion.1.x_ref.dy_ref, bf16[512,1024]{1,0:T(8,128)(2,1)} %get-tuple-element.231.o_ref, f32[1,1024]{1,0:T(1,128)} %bitcast.218, s32[1]{0:T(128)} %bitcast.25.zi_ref, ...), custom_call_target="tpu_custom_call" | custom-call | flops 6845104128 | bytes 21757952 | tf_op jit(solution)/shard_map/pallas_call | solution.py:388
  194.2 2.5 copy-done.17
  199.4 6.7 %shard_map.174 = bf16[512,1024]{1,0:T(8,128)(2,1)} custom-call(f32[512,1024]{1,0:T(8,128)S(1)} %copy-done.17, bf16[512,1408]{1,0:T(8,128)(2,1)S(1)} %copy-done.20, bf16[512,1408]{1,0:T(8,128)(2,1)S(1)} %copy-done.21, s32[1]{0:T(128)} %bitcast.25.zi_ref, bf16[2,688,256]{2,1,0:T(8,128)(2,1)S(1)} %pad_maximum_fusion.9.refs_0_.refs_16_, ...), custom_call_target="tpu_custom_call" | custom-call | flops 2885681152 | bytes 9830400 | tf_op jit(solution)/shard_map/pallas_call | solution.py:422
  206.2 3.6 collective-permute-start.33
  209.8 22.8 %collective-permute-done.33 = bf16[512,1024]{1,0:T(8,128)(2,1)S(1)} collective-permute-done((bf16[512,1024]{1,0:T(8,128)(2,1)}, bf16[512,1024]{1,0:T(8,128)(2,1)S(1)}, u32[]{:S(2)}, u32[]{:S(2)}) %collective-permute-start.33) | collective-permute-done | bytes 1048608 | tf_op jit(solution)/shard_map/ppermute | solution.py:988
  233.7 11.1 %shard_map.175 = (bf16[512,1024]{1,0:T(8,128)(2,1)}, bf16[512,1024]{1,0:T(8,128)(2,1)}, bf16[512,1024]{1,0:T(8,128)(2,1)}, bf16[512,1024]{1,0:T(8,128)(2,1)}, bf...) custom-call(bf16[512,1024]{1,0:T(8,128)(2,1)} %broadcast_select_fusion.2.x_ref, f32[1,1024]{1,0:T(1,128)} %bitcast.205, ...), custom_call_target="tpu_custom_call" | custom-call | flops 3221225472 | bytes 14680064 | tf_op jit(solution)/shard_map/pallas_call | solution.py:175
  245.4 2.4 collective-permute-done.34.kx_ref
  250.2 15.1 %shard_map.176 = (bf16[512,1024]{1,0:T(8,128)(2,1)}, f32[512,1024]{1,0:T(8,128)}) custom-call(bf16[512,1024]{1,0:T(8,128)(2,1)} %get-tuple-element.246.q_ref, bf16[512,1024]{1,0:T(8,128)(2,1)} %get-tuple-element.247.ko_ref, bf16[512,1024]{1,0:T(8,128)(2,1)} %copy-done.101, bf16[512,1024]{1,0:T(8,128)(2,1)} %get-tuple-element.248.vo_ref, ...), custom_call_target="tpu_custom_call" | custom-call | flops 4294967296 | bytes 10485760 | tf_op jit(solution)/shard_map/pallas_call | solution.py:238
  265.4 19.7 %shard_map.177 = (f32[512,1024]{1,0:T(8,128)}, bf16[512,1408]{1,0:T(8,128)(2,1)}, bf16[512,1408]{1,0:T(8,128)(2,1)}, bf16[512,1024]{1,0:T(8,128)(2,1)}, bf16[2,5...) custom-call(bf16[512,1024]{1,0:T(8,128)(2,1)} %broadcast_select_fusion.2.x_ref, ...), custom_call_target="tpu_custom_call" | custom-call | flops 6845104128 | bytes 21757952 | tf_op jit(solution)/shard_map/pallas_call | solution.py:388
  285.0 27.8 %shard_map.178 = (f32[512,1024]{1,0:T(8,128)}, bf16[512,1024]{1,0:T(8,128)(2,1)}, bf16[512,1024]{1,0:T(8,128)(2,1)}, bf16[512,1408]{1,0:T(8,128)(2,1)}, bf16[512...) custom-call(bf16[512,1024]{1,0:T(8,128)(2,1)} %maximum_select_fusion.1.x_ref.dy_re, ...), custom_call_target="tpu_custom_call" | custom-call | flops 9730785280 | bytes 27394048 | tf_op jit(solution)/shard_map/pallas_call | solution.py:500
  312.9 27.2 %shard_map.179 = (bf16[512,1024]{1,0:T(8,128)(2,1)}, bf16[512,1024]{1,0:T(8,128)(2,1)}, bf16[512,1024]{1,0:T(8,128)(2,1)}, bf16[512,1024]{1,0:T(8,128)(2,1)}, bf...) custom-call(bf16[512,1024]{1,0:T(8,128)(2,1)} %get-tuple-element.246.q_ref, bf16[512,1024]{1,0:T(8,128)(2,1)} %get-tuple-element.247.ko_ref, ...), custom_call_target="tpu_custom_call" | custom-call | flops 10737418240 | bytes 20971520 | tf_op jit(solution)/shard_map/pallas_call | solution.py:602
  341.3 1.7 collective-permute-done.36.dkr_ref
  343.0 3.0 collective-permute-done.37.dvr_ref
  347.1 17.3 %shard_map.180 = (bf16[2,512,768]{2,1,0:T(8,128)(2,1)}, bf16[2,512,768]{2,1,0:T(8,128)(2,1)}, f32[512,1024]{1,0:T(8,128)}, bf16[512,1024]{1,0:T(8,128)(2,1)}, f32[1,1024]{1,0:T(1,128)}) custom-call(bf16[512,1024]{1,0:T(8,128)(2,1)} %get-tuple-element.257.dq_ref, bf16[512,1024]{1,0:T(8,128)(2,1)} %get-tuple-element.258.dk_ref, bf16[512,1024]{1,0:T(8,128)(2,1)} %copy-done.55, ...), custom_call_target="tpu_custom_call" | custom-call | flops 3221225472 | bytes 27262976 | tf_op jit(solution)/shard_map/pallas_call | solution.py:685
  369.1 7.2 %shard_map.181 = f32[512,1024]{1,0:T(8,128)S(1)} custom-call(f32[512,1024]{1,0:T(8,128)S(1)} %copy-done.16, bf16[512,1408]{1,0:T(8,128)(2,1)S(1)} %copy-done.18, bf16[512,1408]{1,0:T(8,128)(2,1)} %get-tuple-element.267.zf_ref, s32[1]{0:T(128)} %bitcast.25.zi_ref, bf16[2,688,256]{2,1,0:T(8,128)(2,1)S(1)} %copy-done.1, bf16[2,688,256]{2,1,0:T(8,128)(2,1)S(1)} %copy-done.3, ...), custom_call_target="tpu_custom_call" | custom-call | flops 2885681152 | bytes 9830400 | tf_op jit(solution)/shard_map/pallas_call | solution.py:422
  376.3 15.5 %collective-permute-done.38 = bf16[512,1024]{1,0:T(8,128)(2,1)S(1)} collective-permute-done((bf16[512,1024]{1,0:T(8,128)(2,1)}, bf16[512,1024]{1,0:T(8,128)(2,1)S(1)}, u32[]{:S(2)}, u32[]{:S(2)}) %collective-permute-start.38) | collective-permute-done | bytes 1048608 | tf_op jit(solution)/shard_map/ppermute | solution.py:1007
  392.0 2.6 collective-permute-done.43.bx_ref
  394.7 4.5 shard_map.182
  400.1 27.6 %shard_map.183 = (f32[512,1024]{1,0:T(8,128)}, bf16[512,1024]{1,0:T(8,128)(2,1)}, bf16[512,1024]{1,0:T(8,128)(2,1)}, bf16[512,1408]{1,0:T(8,128)(2,1)}, bf16[512...) custom-call(bf16[512,1024]{1,0:T(8,128)(2,1)} %copy-done.25, ...), custom_call_target="tpu_custom_call" | custom-call | flops 9730785280 | bytes 27394048 | tf_op jit(solution)/shard_map/pallas_call | solution.py:500
  427.8 4.6 collective-permute-done.44
  432.9 1.8 fusion.22
  434.7 12.7 %collective-permute-done.48 = bf16[688,256]{1,0:T(8,128)(2,1)} collective-permute-done((bf16[688,256]{1,0:T(8,128)(2,1)}, bf16[688,256]{1,0:T(8,128)(2,1)}, u32[]{:S(2)}, u32[]{:S(2)}) %collective-permute-start.48) | collective-permute-done | bytes 352288 | tf_op jit(solution)/shard_map/ppermute | solution.py:744
  450.5 6.3 shard_map.184
  456.8 2.6 shard_map.185
  459.5 5.2 shard_map.187
  465.5 2.0 fusion.10
  468.9 3.9 collective-permute-start.52
  473.3 2.1 collective-permute-start.54
  475.4 27.2 %shard_map.186 = (bf16[512,1024]{1,0:T(8,128)(2,1)}, bf16[512,1024]{1,0:T(8,128)(2,1)}, bf16[512,1024]{1,0:T(8,128)(2,1)}, bf16[512,1024]{1,0:T(8,128)(2,1)}, bf...) custom-call(bf16[512,1024]{1,0:T(8,128)(2,1)} %get-tuple-element.246.q_ref, bf16[512,1024]{1,0:T(8,128)(2,1)} %get-tuple-element.247.ko_ref, ...), custom_call_target="tpu_custom_call" | custom-call | flops 10737418240 | bytes 20971520 | tf_op jit(solution)/shard_map/pallas_call | solution.py:602
  503.5 2.4 add_convert_fusion.1
  506.6 1.8 collective-permute-start.58
  512.3 1.7 slice_bitcast_fusion.3
  516.4 4.1 collective-permute-start.63
  522.5 2.1 fusion.5
  524.6 16.2 %shard_map.188 = (bf16[2,512,768]{2,1,0:T(8,128)(2,1)}, bf16[2,512,768]{2,1,0:T(8,128)(2,1)}, f32[512,1024]{1,0:T(8,128)}, bf16[512,1024]{1,0:T(8,128)(2,1)}, f32[1,1024]{1,0:T(1,128)}) custom-call(bf16[512,1024]{1,0:T(8,128)(2,1)} %get-tuple-element.321.dq_ref, bf16[512,1024]{1,0:T(8,128)(2,1)} %get-tuple-element.322.dk_ref, ...), custom_call_target="tpu_custom_call" | custom-call | flops 3221225472 | bytes 27262976 | tf_op jit(solution)/shard_map/pallas_call | solution.py:685
  547.6 5.0 shard_map.189
  553.8 4.6 collective-permute-done.61
  561.0 3.4 collective-permute-start.68
  566.5 6.6 %collective-permute-done.68 = bf16[688,256]{1,0:T(8,128)(2,1)S(1)} collective-permute-done((bf16[688,256]{1,0:T(8,128)(2,1)S(1)}, bf16[688,256]{1,0:T(8,128)(2,1)S(1)}, u32[]{:S(2)}, u32[]{:S(2)}) %collective-permute-start.68) | collective-permute-done | bytes 352288 | tf_op jit(solution)/shard_map/ppermute | solution.py:767
  573.9 19.0 %collective-permute-done.69 = bf16[688,256]{1,0:T(8,128)(2,1)S(1)} collective-permute-done((bf16[688,256]{1,0:T(8,128)(2,1)S(1)}, bf16[688,256]{1,0:T(8,128)(2,1)S(1)}, u32[]{:S(2)}, u32[]{:S(2)}) %collective-permute-start.69) | collective-permute-done | bytes 352288 | tf_op jit(solution)/shard_map/ppermute | solution.py:767
  593.9 3.3 collective-permute-start.73
  597.2 1.9 collective-permute-start.74
  599.5 4.5 collective-permute-done.71
  604.0 10.3 %collective-permute-done.73 = bf16[384,256]{1,0:T(8,128)(2,1)S(1)} collective-permute-done((bf16[384,256]{1,0:T(8,128)(2,1)S(1)}, bf16[384,256]{1,0:T(8,128)(2,1)S(1)}, u32[]{:S(2)}, u32[]{:S(2)}) %collective-permute-start.73) | collective-permute-done | bytes 196640 | tf_op jit(solution)/shard_map/ppermute | solution.py:767
  618.1 1.7 collective-permute-done.80
  620.1 2.1 collective-permute-start.77
  622.2 2.4 collective-permute-start.75
  627.6 13.9 %collective-permute-done.82 = f32[3,1024]{1,0:T(4,128)S(1)} collective-permute-done((f32[3,1024]{1,0:T(4,128)S(1)}, f32[3,1024]{1,0:T(4,128)S(1)}, u32[]{:S(2)}, u32[]{:S(2)}) %collective-permute-start.82) | collective-permute-done | bytes 12320 | tf_op jit(solution)/shard_map/ppermute | solution.py:1096
  642.9 1.7 fusion.28
  (456 shorter events, 108.1 us)
Async XLA Ops:
  4.3 18.3 %collective-permute-start = (bf16[1040,256]{1,0:T(8,128)(2,1)S(1)}, bf16[1040,256]{1,0:T(8,128)(2,1)S(1)}, u32[]{:S(2)}, u32[]{:S(2)}) collective-permute-start(bf16[1040,256]{1,0:T(8,128)(2,1)S(1)} %fusion.13), channel_id=1, source_target_pairs={{0,4},{4,8},{8,12},{12,0},{1,5},{5,9},{9,13},{13,1},{2,6},{6,10},{... | collective-permute-start | bytes 1597448 | tf_op jit(solution)/shard_map/ppermute | solution.py:744
  9.1 13.4 %collective-permute-start.1 = (bf16[256,1024]{1,0:T(8,128)(2,1)S(1)}, bf16[256,1024]{1,0:T(8,128)(2,1)S(1)}, u32[]{:S(2)}, u32[]{:S(2)}) collective-permute-start(bf16[256,1024]{1,0:T(8,128)(2,1)S(1)} %get-tuple-element.384), channel_id=1, source_target_pairs={{0,2},{1,3},{2,0},{3,1},{4,6},{5,7},{6,4},{7,5},{8,10},{9,11},{10,... | collective-permute-start | bytes 1572872 | tf_op jit(solution)/shard_map/ppermute | solution.py:739
  22.6 14.6 %collective-permute-start.2 = (bf16[1040,256]{1,0:T(8,128)(2,1)S(1)}, bf16[1040,256]{1,0:T(8,128)(2,1)}, u32[]{:S(2)}, u32[]{:S(2)}) collective-permute-start(bf16[1040,256]{1,0:T(8,128)(2,1)S(1)} %collective-permute-done), channel_id=1, source_target_pairs={{0,4},{4,8},{8,12},{12,0},{1,5},{5,9},{9,13},{13,1},{2,6},{6,10},{... | collective-permute-start | bytes 1597448 | tf_op jit(solution)/shard_map/ppermute | solution.py:744
  24.2 13.0 %collective-permute-start.3 = (bf16[1040,256]{1,0:T(8,128)(2,1)S(1)}, bf16[1040,256]{1,0:T(8,128)(2,1)S(1)}, u32[]{:S(2)}, u32[]{:S(2)}) collective-permute-start(bf16[1040,256]{1,0:T(8,128)(2,1)S(1)} %fusion.13), channel_id=1, source_target_pairs={{0,2},{1,3},{2,0},{3,1},{4,6},{5,7},{6,4},{7,5},{8,10},{9,11},{10,... | collective-permute-start | bytes 1597448 | tf_op jit(solution)/shard_map/ppermute | solution.py:739
  37.2 13.8 %collective-permute-start.4 = (bf16[1040,256]{1,0:T(8,128)(2,1)}, bf16[1040,256]{1,0:T(8,128)(2,1)}, u32[]{:S(2)}, u32[]{:S(2)}) collective-permute-start(bf16[1040,256]{1,0:T(8,128)(2,1)} %collective-permute-done.2), channel_id=1, source_target_pairs={{0,4},{4,8},{8,12},{12,0},{1,5},{5,9},{9,13},{13,1},{2,6},{6,10},{... | collective-permute-start | bytes 1597448 | tf_op jit(solution)/shard_map/ppermute | solution.py:744
  51.0 18.6 %collective-permute-start.6 = (bf16[1376,256]{1,0:T(8,128)(2,1)S(1)}, bf16[1376,256]{1,0:T(8,128)(2,1)}, u32[]{:S(2)}, u32[]{:S(2)}) collective-permute-start(bf16[1376,256]{1,0:T(8,128)(2,1)S(1)} %bitcast.188), channel_id=1, source_target_pairs={{0,4},{4,8},{8,12},{12,0},{1,5},{5,9},{9,13},{13,1},{2,6},{6,10},{... | collective-permute-start | bytes 2113544 | tf_op jit(solution)/shard_map/ppermute | solution.py:744
  51.0 18.6 %collective-permute-start.7 = (bf16[1040,256]{1,0:T(8,128)(2,1)}, bf16[1040,256]{1,0:T(8,128)(2,1)S(1)}, u32[]{:S(2)}, u32[]{:S(2)}) collective-permute-start(bf16[1040,256]{1,0:T(8,128)(2,1)} %collective-permute-done.2), channel_id=1, source_target_pairs={{0,2},{1,3},{2,0},{3,1},{4,6},{5,7},{6,4},{7,5},{8,10},{9,11},{10,... | collective-permute-start | bytes 1597448 | tf_op jit(solution)/shard_map/ppermute | solution.py:739
  52.6 17.0 %collective-permute-start.8 = (bf16[688,256]{1,0:T(8,128)(2,1)S(1)}, bf16[688,256]{1,0:T(8,128)(2,1)S(1)}, u32[]{:S(2)}, u32[]{:S(2)}) collective-permute-start(bf16[688,256]{1,0:T(8,128)(2,1)S(1)} %bitcast.201), channel_id=1, source_target_pairs={{0,2},{1,3},{2,0},{3,1},{4,6},{5,7},{6,4},{7,5},{8,10},{9,11},{10,... | collective-permute-start | bytes 1056776 | tf_op jit(solution)/shard_map/ppermute | solution.py:739
  69.7 15.7 %collective-permute-start.9 = (bf16[1376,256]{1,0:T(8,128)(2,1)}, bf16[1376,256]{1,0:T(8,128)(2,1)S(1)}, u32[]{:S(2)}, u32[]{:S(2)}) collective-permute-start(bf16[1376,256]{1,0:T(8,128)(2,1)} %collective-permute-done.6), channel_id=1, source_target_pairs={{0,4},{4,8},{8,12},{12,0},{1,5},{5,9},{9,13},{13,1},{2,6},{6,10},{... | collective-permute-start | bytes 2113544 | tf_op jit(solution)/shard_map/ppermute | solution.py:744
  70.5 23.1 %collective-permute-start.13 = (bf16[2,1040,256]{2,1,0:T(8,128)(2,1)S(1)}, bf16[2,1040,256]{2,1,0:T(8,128)(2,1)}, u32[]{:S(2)}, u32[]{:S(2)}) collective-permute-start(bf16[2,1040,256]{2,1,0:T(8,128)(2,1)S(1)} %pad_maximum_fusion.4.refs_0_), channel_id=1, source_target_pairs={{0,1},{1,0},{2,3},{3,2},{4,5},{5,4},{6,7},{7,6},{8,9},{9,8},{10,11... | collective-permute-start | bytes 3194888 | tf_op jit(solution)/shard_map/ppermute | solution.py:734
  70.6 14.7 %collective-permute-start.10 = (bf16[1040,256]{1,0:T(8,128)(2,1)}, bf16[1040,256]{1,0:T(8,128)(2,1)S(1)}, u32[]{:S(2)}, u32[]{:S(2)}) collective-permute-start(bf16[1040,256]{1,0:T(8,128)(2,1)} %collective-permute-done.4), channel_id=1, source_target_pairs={{0,2},{1,3},{2,0},{3,1},{4,6},{5,7},{6,4},{7,5},{8,10},{9,11},{10,... | collective-permute-start | bytes 1597448 | tf_op jit(solution)/shard_map/ppermute | solution.py:739
  73.4 23.1 %collective-permute-start.14 = (bf16[2,1040,256]{2,1,0:T(8,128)(2,1)S(1)}, bf16[2,1040,256]{2,1,0:T(8,128)(2,1)}, u32[]{:S(2)}, u32[]{:S(2)}) collective-permute-start(bf16[2,1040,256]{2,1,0:T(8,128)(2,1)S(1)} %pad_maximum_fusion.5.refs_1_), channel_id=1, source_target_pairs={{0,1},{1,0},{2,3},{3,2},{4,5},{5,4},{6,7},{7,6},{8,9},{9,8},{10,11... | collective-permute-start | bytes 3194888 | tf_op jit(solution)/shard_map/ppermute | solution.py:734
  75.0 21.5 %collective-permute-start.15 = (bf16[2,1040,256]{2,1,0:T(8,128)(2,1)S(1)}, bf16[2,1040,256]{2,1,0:T(8,128)(2,1)}, u32[]{:S(2)}, u32[]{:S(2)}) collective-permute-start(bf16[2,1040,256]{2,1,0:T(8,128)(2,1)S(1)} %pad_maximum_fusion.6.refs_2_), channel_id=1, source_target_pairs={{0,1},{1,0},{2,3},{3,2},{4,5},{5,4},{6,7},{7,6},{8,9},{9,8},{10,11... | collective-permute-start | bytes 3194888 | tf_op jit(solution)/shard_map/ppermute | solution.py:734
  92.3 20.2 %collective-permute-start.11 = (bf16[1376,256]{1,0:T(8,128)(2,1)}, bf16[1376,256]{1,0:T(8,128)(2,1)S(1)}, u32[]{:S(2)}, u32[]{:S(2)}) collective-permute-start(bf16[1376,256]{1,0:T(8,128)(2,1)} %copy-done.61), channel_id=1, source_target_pairs={{0,4},{4,8},{8,12},{12,0},{1,5},{5,9},{9,13},{13,1},{2,6},{6,10},{... | collective-permute-start | bytes 2113544 | tf_op jit(solution)/shard_map/ppermute | solution.py:744
  93.6 18.9 %collective-permute-start.12 = (bf16[1376,256]{1,0:T(8,128)(2,1)}, bf16[1376,256]{1,0:T(8,128)(2,1)S(1)}, u32[]{:S(2)}, u32[]{:S(2)}) collective-permute-start(bf16[1376,256]{1,0:T(8,128)(2,1)} %bitcast.187), channel_id=1, source_target_pairs={{0,2},{1,3},{2,0},{3,1},{4,6},{5,7},{6,4},{7,5},{8,10},{9,11},{10,... | collective-permute-start | bytes 2113544 | tf_op jit(solution)/shard_map/ppermute | solution.py:739
  114.3 19.4 %collective-permute-start.17 = (bf16[2,688,256]{2,1,0:T(8,128)(2,1)S(1)}, bf16[2,688,256]{2,1,0:T(8,128)(2,1)S(1)}, u32[]{:S(2)}, u32[]{:S(2)}) collective-permute-start(bf16[2,688,256]{2,1,0:T(8,128)(2,1)S(1)} %pad_maximum_fusion.9.refs_0_.refs_16_), channel_id=1, source_target_pairs={{0,4},{4,8},{8,12},{12,0},{1,5},{5,9},{9,13},{13,1},{2,6},{6,10},{... | collective-permute-start | bytes 2113544 | tf_op jit(solution)/shard_map/ppermute | solution.py:744
  115.8 17.9 %collective-permute-start.18 = (bf16[1376,256]{1,0:T(8,128)(2,1)}, bf16[1376,256]{1,0:T(8,128)(2,1)S(1)}, u32[]{:S(2)}, u32[]{:S(2)}) collective-permute-start(bf16[1376,256]{1,0:T(8,128)(2,1)} %collective-permute-done.6), channel_id=1, source_target_pairs={{0,2},{1,3},{2,0},{3,1},{4,6},{5,7},{6,4},{7,5},{8,10},{9,11},{10,... | collective-permute-start | bytes 2113544 | tf_op jit(solution)/shard_map/ppermute | solution.py:739
  133.7 19.0 %collective-permute-start.21 = (bf16[2,688,256]{2,1,0:T(8,128)(2,1)S(1)}, bf16[2,688,256]{2,1,0:T(8,128)(2,1)S(1)}, u32[]{:S(2)}, u32[]{:S(2)}) collective-permute-start(bf16[2,688,256]{2,1,0:T(8,128)(2,1)S(1)} %collective-permute-done.17.refs_1_.refs_17_), channel_id=1, source_target_pairs={{0,4},{4,8},{8,12},{12,0},{1,5},{5,9},{9,13},{13,1},{2,6},{6,10},{... | collective-permute-start | bytes 2113544 | tf_op jit(solution)/shard_map/ppermute | solution.py:744
  134.4 18.3 %collective-permute-start.22 = (bf16[1376,256]{1,0:T(8,128)(2,1)S(1)}, bf16[1376,256]{1,0:T(8,128)(2,1)S(1)}, u32[]{:S(2)}, u32[]{:S(2)}) collective-permute-start(bf16[1376,256]{1,0:T(8,128)(2,1)S(1)} %copy-done.62), channel_id=1, source_target_pairs={{0,2},{1,3},{2,0},{3,1},{4,6},{5,7},{6,4},{7,5},{8,10},{9,11},{10,... | collective-permute-start | bytes 2113544 | tf_op jit(solution)/shard_map/ppermute | solution.py:739
  152.7 18.5 %collective-permute-start.23 = (bf16[2,688,256]{2,1,0:T(8,128)(2,1)S(1)}, bf16[2,688,256]{2,1,0:T(8,128)(2,1)S(1)}, u32[]{:S(2)}, u32[]{:S(2)}) collective-permute-start(bf16[2,688,256]{2,1,0:T(8,128)(2,1)S(1)} %collective-permute-done.21.refs_2_.refs_18_), channel_id=1, source_target_pairs={{0,4},{4,8},{8,12},{12,0},{1,5},{5,9},{9,13},{13,1},{2,6},{6,10},{... | collective-permute-start | bytes 2113544 | tf_op jit(solution)/shard_map/ppermute | solution.py:744
  153.1 18.0 %collective-permute-start.24 = (bf16[1376,256]{1,0:T(8,128)(2,1)S(1)}, bf16[1376,256]{1,0:T(8,128)(2,1)S(1)}, u32[]{:S(2)}, u32[]{:S(2)}) collective-permute-start(bf16[1376,256]{1,0:T(8,128)(2,1)S(1)} %copy-done.64), channel_id=1, source_target_pairs={{0,2},{1,3},{2,0},{3,1},{4,6},{5,7},{6,4},{7,5},{8,10},{9,11},{10,... | collective-permute-start | bytes 2113544 | tf_op jit(solution)/shard_map/ppermute | solution.py:739
  155.5 16.3 %collective-permute-start.25 = (bf16[2,1376,256]{2,1,0:T(8,128)(2,1)S(1)}, bf16[2,1376,256]{2,1,0:T(8,128)(2,1)S(1)}, u32[]{:S(2)}, u32[]{:S(2)}) collective-permute-start(bf16[2,1376,256]{2,1,0:T(8,128)(2,1)S(1)} %pad_maximum_fusion.refs_8_), channel_id=1, source_target_pairs={{0,1},{1,0},{2,3},{3,2},{4,5},{5,4},{6,7},{7,6},{8,9},{9,8},{10,11... | collective-permute-start | bytes 4227080 | tf_op jit(solution)/shard_map/ppermute | solution.py:734
  157.3 14.6 %collective-permute-start.26 = (bf16[2,1376,256]{2,1,0:T(8,128)(2,1)S(1)}, bf16[2,1376,256]{2,1,0:T(8,128)(2,1)S(1)}, u32[]{:S(2)}, u32[]{:S(2)}) collective-permute-start(bf16[2,1376,256]{2,1,0:T(8,128)(2,1)S(1)} %pad_maximum_fusion.1.refs_9_), channel_id=1, source_target_pairs={{0,1},{1,0},{2,3},{3,2},{4,5},{5,4},{6,7},{7,6},{8,9},{9,8},{10,11... | collective-permute-start | bytes 4227080 | tf_op jit(solution)/shard_map/ppermute | solution.py:734
  158.4 14.0 %collective-permute-start.27 = (bf16[2,1376,256]{2,1,0:T(8,128)(2,1)S(1)}, bf16[2,1376,256]{2,1,0:T(8,128)(2,1)S(1)}, u32[]{:S(2)}, u32[]{:S(2)}) collective-permute-start(bf16[2,1376,256]{2,1,0:T(8,128)(2,1)S(1)} %pad_maximum_fusion.2.refs_10_), channel_id=1, source_target_pairs={{0,1},{1,0},{2,3},{3,2},{4,5},{5,4},{6,7},{7,6},{8,9},{9,8},{10,11... | collective-permute-start | bytes 4227080 | tf_op jit(solution)/shard_map/ppermute | solution.py:734
  171.4 22.7 %collective-permute-start.29 = (bf16[2,688,256]{2,1,0:T(8,128)(2,1)S(1)}, bf16[2,688,256]{2,1,0:T(8,128)(2,1)S(1)}, u32[]{:S(2)}, u32[]{:S(2)}) collective-permute-start(bf16[2,688,256]{2,1,0:T(8,128)(2,1)S(1)} %pad_maximum_fusion.9.refs_0_.refs_16_), channel_id=1, source_target_pairs={{0,1},{1,0},{2,3},{3,2},{4,5},{5,4},{6,7},{7,6},{8,9},{9,8},{10,11... | collective-permute-start | bytes 2113544 | tf_op jit(solution)/shard_map/ppermute | solution.py:734
  171.9 22.2 %collective-permute-start.30 = (bf16[2,688,256]{2,1,0:T(8,128)(2,1)S(1)}, bf16[2,688,256]{2,1,0:T(8,128)(2,1)S(1)}, u32[]{:S(2)}, u32[]{:S(2)}) collective-permute-start(bf16[2,688,256]{2,1,0:T(8,128)(2,1)S(1)} %collective-permute-done.17.refs_1_.refs_17_), channel_id=1, source_target_pairs={{0,1},{1,0},{2,3},{3,2},{4,5},{5,4},{6,7},{7,6},{8,9},{9,8},{10,11... | collective-permute-start | bytes 2113544 | tf_op jit(solution)/shard_map/ppermute | solution.py:734
  172.0 22.1 %collective-permute-start.31 = (bf16[2,688,256]{2,1,0:T(8,128)(2,1)S(1)}, bf16[2,688,256]{2,1,0:T(8,128)(2,1)S(1)}, u32[]{:S(2)}, u32[]{:S(2)}) collective-permute-start(bf16[2,688,256]{2,1,0:T(8,128)(2,1)S(1)} %collective-permute-done.21.refs_2_.refs_18_), channel_id=1, source_target_pairs={{0,1},{1,0},{2,3},{3,2},{4,5},{5,4},{6,7},{7,6},{8,9},{9,8},{10,11... | collective-permute-start | bytes 2113544 | tf_op jit(solution)/shard_map/ppermute | solution.py:734
  172.5 21.6 %collective-permute-start.32 = (bf16[2,688,256]{2,1,0:T(8,128)(2,1)S(1)}, bf16[2,688,256]{2,1,0:T(8,128)(2,1)S(1)}, u32[]{:S(2)}, u32[]{:S(2)}) collective-permute-start(bf16[2,688,256]{2,1,0:T(8,128)(2,1)S(1)} %collective-permute-done.23.refs_3_.refs_19_), channel_id=1, source_target_pairs={{0,1},{1,0},{2,3},{3,2},{4,5},{5,4},{6,7},{7,6},{8,9},{9,8},{10,11... | collective-permute-start | bytes 2113544 | tf_op jit(solution)/shard_map/ppermute | solution.py:734
  206.2 26.4 %collective-permute-start.33 = (bf16[512,1024]{1,0:T(8,128)(2,1)}, bf16[512,1024]{1,0:T(8,128)(2,1)S(1)}, u32[]{:S(2)}, u32[]{:S(2)}) collective-permute-start(bf16[512,1024]{1,0:T(8,128)(2,1)} %shard_map.174), channel_id=1, source_target_pairs={{0,16},{1,17},{2,18},{3,19},{4,20},{5,21},{6,22},{7,23},{8,24},{9,... | collective-permute-start | bytes 3145736 | tf_op jit(solution)/shard_map/ppermute | solution.py:988
  340.7 35.7 %collective-permute-start.39 = (bf16[512,1408]{1,0:T(8,128)(2,1)}, bf16[512,1408]{1,0:T(8,128)(2,1)}, u32[]{:S(2)}, u32[]{:S(2)}) collective-permute-start(bf16[512,1408]{1,0:T(8,128)(2,1)} %get-tuple-element.267.zf_ref), channel_id=1, source_target_pairs={{0,1},{1,0},{2,3},{3,2},{4,5},{5,4},{6,7},{7,6},{8,9},{9,8},{10,11... | collective-permute-start | bytes 4325384 | tf_op jit(solution)/shard_map/ppermute | solution.py:734
  340.8 35.5 %collective-permute-start.41 = (bf16[512,1024]{1,0:T(8,128)(2,1)}, bf16[512,1024]{1,0:T(8,128)(2,1)}, u32[]{:S(2)}, u32[]{:S(2)}) collective-permute-start(bf16[512,1024]{1,0:T(8,128)(2,1)} %get-tuple-element.269.bo_ref), channel_id=1, source_target_pairs={{0,1},{1,0},{2,3},{3,2},{4,5},{5,4},{6,7},{7,6},{8,9},{9,8},{10,11... | collective-permute-start | bytes 3145736 | tf_op jit(solution)/shard_map/ppermute | solution.py:734
  341.2 35.1 %collective-permute-start.40 = (bf16[512,1024]{1,0:T(8,128)(2,1)}, bf16[512,1024]{1,0:T(8,128)(2,1)}, u32[]{:S(2)}, u32[]{:S(2)}) collective-permute-start(bf16[512,1024]{1,0:T(8,128)(2,1)} %get-tuple-element.268.bo_ref), channel_id=1, source_target_pairs={{0,1},{1,0},{2,3},{3,2},{4,5},{5,4},{6,7},{7,6},{8,9},{9,8},{10,11... | collective-permute-start | bytes 3145736 | tf_op jit(solution)/shard_map/ppermute | solution.py:734
  364.3 27.5 %collective-permute-start.38 = (bf16[512,1024]{1,0:T(8,128)(2,1)}, bf16[512,1024]{1,0:T(8,128)(2,1)S(1)}, u32[]{:S(2)}, u32[]{:S(2)}) collective-permute-start(bf16[512,1024]{1,0:T(8,128)(2,1)} %get-tuple-element.265), channel_id=1, source_target_pairs={{16,0},{17,1},{18,2},{19,3},{20,4},{21,5},{22,6},{23,7},{24,8},{25... | collective-permute-start | bytes 3145736 | tf_op jit(solution)/shard_map/ppermute | solution.py:1007
  399.2 33.1 %collective-permute-start.44 = (bf16[4,688,256]{2,1,0:T(8,128)(2,1)S(1)}, bf16[4,688,256]{2,1,0:T(8,128)(2,1)}, u32[]{:S(2)}, u32[]{:S(2)}) collective-permute-start(bf16[4,688,256]{2,1,0:T(8,128)(2,1)S(1)} %get-tuple-element.275), channel_id=1, source_target_pairs={{0,2},{1,3},{2,0},{3,1},{4,6},{5,7},{6,4},{7,5},{8,10},{9,11},{10,... | collective-permute-start | bytes 4227080 | tf_op jit(solution)/shard_map/ppermute | solution.py:739
  432.3 15.1 %collective-permute-start.45 = (bf16[512,1408]{1,0:T(8,128)(2,1)}, bf16[512,1408]{1,0:T(8,128)(2,1)}, u32[]{:S(2)}, u32[]{:S(2)}) collective-permute-start(bf16[512,1408]{1,0:T(8,128)(2,1)} %get-tuple-element.287), channel_id=1, source_target_pairs={{0,1},{1,0},{2,3},{3,2},{4,5},{5,4},{6,7},{7,6},{8,9},{9,8},{10,11... | collective-permute-start | bytes 4325384 | tf_op jit(solution)/shard_map/ppermute | solution.py:734
  432.3 15.1 %collective-permute-start.46 = (bf16[512,1408]{1,0:T(8,128)(2,1)}, bf16[512,1408]{1,0:T(8,128)(2,1)}, u32[]{:S(2)}, u32[]{:S(2)}) collective-permute-start(bf16[512,1408]{1,0:T(8,128)(2,1)} %get-tuple-element.288), channel_id=1, source_target_pairs={{0,1},{1,0},{2,3},{3,2},{4,5},{5,4},{6,7},{7,6},{8,9},{9,8},{10,11... | collective-permute-start | bytes 4325384 | tf_op jit(solution)/shard_map/ppermute | solution.py:734
  432.9 14.6 %collective-permute-start.47 = (bf16[512,1024]{1,0:T(8,128)(2,1)}, bf16[512,1024]{1,0:T(8,128)(2,1)}, u32[]{:S(2)}, u32[]{:S(2)}) collective-permute-start(bf16[512,1024]{1,0:T(8,128)(2,1)} %get-tuple-element.289.bo_ref), channel_id=1, source_target_pairs={{0,1},{1,0},{2,3},{3,2},{4,5},{5,4},{6,7},{7,6},{8,9},{9,8},{10,11... | collective-permute-start | bytes 3145736 | tf_op jit(solution)/shard_map/ppermute | solution.py:734
  448.7 15.9 %collective-permute-start.49 = (bf16[688,256]{1,0:T(8,128)(2,1)S(1)}, bf16[688,256]{1,0:T(8,128)(2,1)S(1)}, u32[]{:S(2)}, u32[]{:S(2)}) collective-permute-start(bf16[688,256]{1,0:T(8,128)(2,1)S(1)} %fusion.11), channel_id=1, source_target_pairs={{0,4},{4,8},{8,12},{12,0},{1,5},{5,9},{9,13},{13,1},{2,6},{6,10},{... | collective-permute-start | bytes 1056776 | tf_op jit(solution)/shard_map/ppermute | solution.py:744
  464.6 38.0 %collective-permute-start.50 = (bf16[4,688,256]{2,1,0:T(8,128)(2,1)}, bf16[4,688,256]{2,1,0:T(8,128)(2,1)}, u32[]{:S(2)}, u32[]{:S(2)}) collective-permute-start(bf16[4,688,256]{2,1,0:T(8,128)(2,1)} %get-tuple-element.301), channel_id=1, source_target_pairs={{0,2},{1,3},{2,0},{3,1},{4,6},{5,7},{6,4},{7,5},{8,10},{9,11},{10,... | collective-permute-start | bytes 4227080 | tf_op jit(solution)/shard_map/ppermute | solution.py:739
  467.5 35.1 %collective-permute-start.51 = (bf16[688,256]{1,0:T(8,128)(2,1)}, bf16[688,256]{1,0:T(8,128)(2,1)S(1)}, u32[]{:S(2)}, u32[]{:S(2)}) collective-permute-start(bf16[688,256]{1,0:T(8,128)(2,1)} %fusion.10), channel_id=1, source_target_pairs={{0,4},{4,8},{8,12},{12,0},{1,5},{5,9},{9,13},{13,1},{2,6},{6,10},{... | collective-permute-start | bytes 1056776 | tf_op jit(solution)/shard_map/ppermute | solution.py:744
  468.9 33.7 %collective-permute-start.52 = (bf16[2,256,256]{2,1,0:T(8,128)(2,1)S(1)}, bf16[2,256,256]{2,1,0:T(8,128)(2,1)S(1)}, u32[]{:S(2)}, u32[]{:S(2)}) collective-permute-start(bf16[2,256,256]{2,1,0:T(8,128)(2,1)S(1)} %pad_maximum_fusion.12), channel_id=1, source_target_pairs={{0,12},{4,0},{8,4},{12,8},{1,13},{5,1},{9,5},{13,9},{2,14},{6,2},{... | collective-permute-start | bytes 786440 | tf_op jit(solution)/shard_map/ppermute | solution.py:767
  472.8 29.8 %collective-permute-start.53 = (bf16[2,256,256]{2,1,0:T(8,128)(2,1)S(1)}, bf16[2,256,256]{2,1,0:T(8,128)(2,1)S(1)}, u32[]{:S(2)}, u32[]{:S(2)}) collective-permute-start(bf16[2,256,256]{2,1,0:T(8,128)(2,1)S(1)} %pad_maximum_fusion.13), channel_id=1, source_target_pairs={{0,8},{4,12},{8,0},{12,4},{1,9},{5,13},{9,1},{13,5},{2,10},{6,14},... | collective-permute-start | bytes 786440 | tf_op jit(solution)/shard_map/ppermute | solution.py:767
  473.3 29.3 %collective-permute-start.54 = (bf16[2,256,256]{2,1,0:T(8,128)(2,1)S(1)}, bf16[2,256,256]{2,1,0:T(8,128)(2,1)S(1)}, u32[]{:S(2)}, u32[]{:S(2)}) collective-permute-start(bf16[2,256,256]{2,1,0:T(8,128)(2,1)S(1)} %pad_maximum_fusion.14), channel_id=1, source_target_pairs={{0,4},{4,8},{8,12},{12,0},{1,5},{5,9},{9,13},{13,1},{2,6},{6,10},{... | collective-permute-start | bytes 786440 | tf_op jit(solution)/shard_map/ppermute | solution.py:767
  502.7 13.7 %collective-permute-start.55 = (bf16[512,1024]{1,0:T(8,128)(2,1)}, bf16[512,1024]{1,0:T(8,128)(2,1)}, u32[]{:S(2)}, u32[]{:S(2)}) collective-permute-start(bf16[512,1024]{1,0:T(8,128)(2,1)} %get-tuple-element.312), channel_id=1, source_target_pairs={{0,1},{1,0},{2,3},{3,2},{4,5},{5,4},{6,7},{7,6},{8,9},{9,8},{10,11... | collective-permute-start | bytes 3145736 | tf_op jit(solution)/shard_map/ppermute | solution.py:734
  503.5 17.0 %collective-permute-start.56 = (bf16[512,1024]{1,0:T(8,128)(2,1)}, bf16[512,1024]{1,0:T(8,128)(2,1)}, u32[]{:S(2)}, u32[]{:S(2)}) collective-permute-start(bf16[512,1024]{1,0:T(8,128)(2,1)} %get-tuple-element.313), channel_id=1, source_target_pairs={{0,1},{1,0},{2,3},{3,2},{4,5},{5,4},{6,7},{7,6},{8,9},{9,8},{10,11... | collective-permute-start | bytes 3145736 | tf_op jit(solution)/shard_map/ppermute | solution.py:734
  506.6 34.3 %collective-permute-start.58 = (bf16[336,256]{1,0:T(8,128)(2,1)}, bf16[336,256]{1,0:T(8,128)(2,1)}, u32[]{:S(2)}, u32[]{:S(2)}) collective-permute-start(bf16[336,256]{1,0:T(8,128)(2,1)} %slice_bitcast_fusion.11), channel_id=1, source_target_pairs={{0,12},{4,0},{8,4},{12,8},{1,13},{5,1},{9,5},{13,9},{2,14},{6,2},{... | collective-permute-start | bytes 516104 | tf_op jit(solution)/shard_map/ppermute | solution.py:767
  509.1 32.3 %collective-permute-start.59 = (bf16[336,256]{1,0:T(8,128)(2,1)}, bf16[336,256]{1,0:T(8,128)(2,1)}, u32[]{:S(2)}, u32[]{:S(2)}) collective-permute-start(bf16[336,256]{1,0:T(8,128)(2,1)} %slice_bitcast_fusion.10), channel_id=1, source_target_pairs={{0,8},{4,12},{8,0},{12,4},{1,9},{5,13},{9,1},{13,5},{2,10},{6,14},... | collective-permute-start | bytes 516104 | tf_op jit(solution)/shard_map/ppermute | solution.py:767
  510.5 31.1 %collective-permute-start.60 = (bf16[336,256]{1,0:T(8,128)(2,1)}, bf16[336,256]{1,0:T(8,128)(2,1)}, u32[]{:S(2)}, u32[]{:S(2)}) collective-permute-start(bf16[336,256]{1,0:T(8,128)(2,1)} %slice_bitcast_fusion.9), channel_id=1, source_target_pairs={{0,4},{4,8},{8,12},{12,0},{1,5},{5,9},{9,13},{13,1},{2,6},{6,10},{... | collective-permute-start | bytes 516104 | tf_op jit(solution)/shard_map/ppermute | solution.py:767
  516.4 36.2 %collective-permute-start.63 = (bf16[352,256]{1,0:T(8,128)(2,1)}, bf16[352,256]{1,0:T(8,128)(2,1)}, u32[]{:S(2)}, u32[]{:S(2)}) collective-permute-start(bf16[352,256]{1,0:T(8,128)(2,1)} %slice_bitcast_fusion.3), channel_id=1, source_target_pairs={{0,12},{4,0},{8,4},{12,8},{1,13},{5,1},{9,5},{13,9},{2,14},{6,2},{... | collective-permute-start | bytes 540680 | tf_op jit(solution)/shard_map/ppermute | solution.py:767
  520.5 21.9 %collective-permute-start.57 = (bf16[4,336,256]{2,1,0:T(8,128)(2,1)S(1)}, bf16[4,336,256]{2,1,0:T(8,128)(2,1)S(1)}, u32[]{:S(2)}, u32[]{:S(2)}) collective-permute-start(bf16[4,336,256]{2,1,0:T(8,128)(2,1)S(1)} %slice.301), channel_id=1, source_target_pairs={{0,2},{1,3},{2,0},{3,1},{4,6},{5,7},{6,4},{7,5},{8,10},{9,11},{10,... | collective-permute-start | bytes 2064392 | tf_op jit(solution)/shard_map/ppermute | solution.py:739
  540.9 13.0 %collective-permute-start.64 = (bf16[352,256]{1,0:T(8,128)(2,1)S(1)}, bf16[352,256]{1,0:T(8,128)(2,1)S(1)}, u32[]{:S(2)}, u32[]{:S(2)}) collective-permute-start(bf16[352,256]{1,0:T(8,128)(2,1)S(1)} %slice_bitcast_fusion.2), channel_id=1, source_target_pairs={{0,8},{4,12},{8,0},{12,4},{1,9},{5,13},{9,1},{13,5},{2,10},{6,14},... | collective-permute-start | bytes 540680 | tf_op jit(solution)/shard_map/ppermute | solution.py:767
  541.6 16.8 %collective-permute-start.61 = (bf16[4,352,256]{2,1,0:T(8,128)(2,1)S(1)}, bf16[4,352,256]{2,1,0:T(8,128)(2,1)S(1)}, u32[]{:S(2)}, u32[]{:S(2)}) collective-permute-start(bf16[4,352,256]{2,1,0:T(8,128)(2,1)S(1)} %slice.316), channel_id=1, source_target_pairs={{0,2},{1,3},{2,0},{3,1},{4,6},{5,7},{6,4},{7,5},{8,10},{9,11},{10,... | collective-permute-start | bytes 2162696 | tf_op jit(solution)/shard_map/ppermute | solution.py:739
  558.5 34.4 %collective-permute-start.66 = (bf16[4,384,256]{2,1,0:T(8,128)(2,1)S(1)}, bf16[4,384,256]{2,1,0:T(8,128)(2,1)S(1)}, u32[]{:S(2)}, u32[]{:S(2)}) collective-permute-start(bf16[4,384,256]{2,1,0:T(8,128)(2,1)S(1)} %get-tuple-element.388), channel_id=1, source_target_pairs={{0,2},{1,3},{2,0},{3,1},{4,6},{5,7},{6,4},{7,5},{8,10},{9,11},{10,... | collective-permute-start | bytes 2359304 | tf_op jit(solution)/shard_map/ppermute | solution.py:739
  559.4 33.5 %collective-permute-start.67 = (bf16[256,1024]{1,0:T(8,128)(2,1)S(1)}, bf16[256,1024]{1,0:T(8,128)(2,1)S(1)}, u32[]{:S(2)}, u32[]{:S(2)}) collective-permute-start(bf16[256,1024]{1,0:T(8,128)(2,1)S(1)} %slice_select_fusion.1), channel_id=1, source_target_pairs={{0,2},{1,3},{2,0},{3,1},{4,6},{5,7},{6,4},{7,5},{8,10},{9,11},{10,... | collective-permute-start | bytes 1572872 | tf_op jit(solution)/shard_map/ppermute | solution.py:739
  564.4 28.5 %collective-permute-start.69 = (bf16[688,256]{1,0:T(8,128)(2,1)S(1)}, bf16[688,256]{1,0:T(8,128)(2,1)S(1)}, u32[]{:S(2)}, u32[]{:S(2)}) collective-permute-start(bf16[688,256]{1,0:T(8,128)(2,1)S(1)} %get-tuple-element.390), channel_id=1, source_target_pairs={{0,8},{4,12},{8,0},{12,4},{1,9},{5,13},{9,1},{13,5},{2,10},{6,14},... | collective-permute-start | bytes 1056776 | tf_op jit(solution)/shard_map/ppermute | solution.py:767
  565.1 27.8 %collective-permute-start.70 = (bf16[688,256]{1,0:T(8,128)(2,1)S(1)}, bf16[688,256]{1,0:T(8,128)(2,1)S(1)}, u32[]{:S(2)}, u32[]{:S(2)}) collective-permute-start(bf16[688,256]{1,0:T(8,128)(2,1)S(1)} %get-tuple-element.389), channel_id=1, source_target_pairs={{0,4},{4,8},{8,12},{12,0},{1,5},{5,9},{9,13},{13,1},{2,6},{6,10},{... | collective-permute-start | bytes 1056776 | tf_op jit(solution)/shard_map/ppermute | solution.py:767
  573.1 30.9 %collective-permute-start.71 = (bf16[4,384,256]{2,1,0:T(8,128)(2,1)S(1)}, bf16[4,384,256]{2,1,0:T(8,128)(2,1)S(1)}, u32[]{:S(2)}, u32[]{:S(2)}) collective-permute-start(bf16[4,384,256]{2,1,0:T(8,128)(2,1)S(1)} %get-tuple-element.387), channel_id=1, source_target_pairs={{0,2},{1,3},{2,0},{3,1},{4,6},{5,7},{6,4},{7,5},{8,10},{9,11},{10,... | collective-permute-start | bytes 2359304 | tf_op jit(solution)/shard_map/ppermute | solution.py:739
  593.9 20.4 %collective-permute-start.73 = (bf16[384,256]{1,0:T(8,128)(2,1)S(1)}, bf16[384,256]{1,0:T(8,128)(2,1)S(1)}, u32[]{:S(2)}, u32[]{:S(2)}) collective-permute-start(bf16[384,256]{1,0:T(8,128)(2,1)S(1)} %get-tuple-element.381), channel_id=1, source_target_pairs={{0,8},{4,12},{8,0},{12,4},{1,9},{5,13},{9,1},{13,5},{2,10},{6,14},... | collective-permute-start | bytes 589832 | tf_op jit(solution)/shard_map/ppermute | solution.py:767
  597.2 17.2 %collective-permute-start.74 = (bf16[384,256]{1,0:T(8,128)(2,1)S(1)}, bf16[384,256]{1,0:T(8,128)(2,1)S(1)}, u32[]{:S(2)}, u32[]{:S(2)}) collective-permute-start(bf16[384,256]{1,0:T(8,128)(2,1)S(1)} %get-tuple-element.380), channel_id=1, source_target_pairs={{0,4},{4,8},{8,12},{12,0},{1,5},{5,9},{9,13},{13,1},{2,6},{6,10},{... | collective-permute-start | bytes 589832 | tf_op jit(solution)/shard_map/ppermute | solution.py:767
  620.1 24.5 %collective-permute-start.77 = (bf16[384,256]{1,0:T(8,128)(2,1)S(1)}, bf16[384,256]{1,0:T(8,128)(2,1)S(1)}, u32[]{:S(2)}, u32[]{:S(2)}) collective-permute-start(bf16[384,256]{1,0:T(8,128)(2,1)S(1)} %get-tuple-element.378), channel_id=1, source_target_pairs={{0,4},{4,8},{8,12},{12,0},{1,5},{5,9},{9,13},{13,1},{2,6},{6,10},{... | collective-permute-start | bytes 589832 | tf_op jit(solution)/shard_map/ppermute | solution.py:767
  622.1 22.4 %collective-permute-start.76 = (bf16[384,256]{1,0:T(8,128)(2,1)S(1)}, bf16[384,256]{1,0:T(8,128)(2,1)S(1)}, u32[]{:S(2)}, u32[]{:S(2)}) collective-permute-start(bf16[384,256]{1,0:T(8,128)(2,1)S(1)} %get-tuple-element.379), channel_id=1, source_target_pairs={{0,8},{4,12},{8,0},{12,4},{1,9},{5,13},{9,1},{13,5},{2,10},{6,14},... | collective-permute-start | bytes 589832 | tf_op jit(solution)/shard_map/ppermute | solution.py:767
  622.2 22.4 %collective-permute-start.75 = (bf16[384,256]{1,0:T(8,128)(2,1)S(1)}, bf16[384,256]{1,0:T(8,128)(2,1)S(1)}, u32[]{:S(2)}, u32[]{:S(2)}) collective-permute-start(bf16[384,256]{1,0:T(8,128)(2,1)S(1)} %get-tuple-element.377), channel_id=1, source_target_pairs={{0,12},{4,0},{8,4},{12,8},{1,13},{5,1},{9,5},{13,9},{2,14},{6,2},{... | collective-permute-start | bytes 589832 | tf_op jit(solution)/shard_map/ppermute | solution.py:767
  624.6 16.9 %collective-permute-start.82 = (f32[3,1024]{1,0:T(4,128)S(1)}, f32[3,1024]{1,0:T(4,128)S(1)}, u32[]{:S(2)}, u32[]{:S(2)}) collective-permute-start(f32[3,1024]{1,0:T(4,128)S(1)} %add.395), channel_id=1, source_target_pairs={{0,8},{4,12},{8,0},{12,4},{1,9},{5,13},{9,1},{13,5},{2,10},{6,14},... | collective-permute-start | bytes 36872 | tf_op jit(solution)/shard_map/ppermute | solution.py:1096
  626.7 16.2 %collective-permute-start.78 = (bf16[256,256]{1,0:T(8,128)(2,1)}, bf16[256,256]{1,0:T(8,128)(2,1)S(1)}, u32[]{:S(2)}, u32[]{:S(2)}) collective-permute-start(bf16[256,256]{1,0:T(8,128)(2,1)} %fusion.37), channel_id=1, source_target_pairs={{0,2},{1,3},{2,0},{3,1},{4,6},{5,7},{6,4},{7,5},{8,10},{9,11},{10,... | collective-permute-start | bytes 393224 | tf_op jit(solution)/shard_map/ppermute | solution.py:739
  (122 other events, 1575.6 us)

commit v4 on v3

--- a/solution.py
+++ b/solution.py
@@ -425,7 +425,7 @@
         out_specs=vmem,
         out_shape=sds((rows, model), dtype),
         scratch_shapes=pair_scratch(1, hidden),
-        compiler_params=pltpu.CompilerParams(vmem_limit_bytes=18 * 1024 * 1024),
+        compiler_params=pltpu.CompilerParams(vmem_limit_bytes=VMEM_MB * 1024 * 1024),
         cost_estimate=cost(2 * rows * model * 4 * hidden, 8 * hidden * model + 8 * h.size),
     )(h, z_near, z_far, zi, *wd)
 
@@ -1021,14 +1021,20 @@
     if near:
         down = [plus(down_keep[r], down_got[r]) for r in range(4)]
         down_run = ring(down[1])
-        dg_oth, du_oth, da_oth, down_run = meet(dg_oth, du_oth, da_oth, down_run)
-        down_run = ring(plus(down_run, down[2]))
     else:
         down_run = down_got
+    dg_oth, du_oth, da_oth = meet(dg_oth, du_oth, da_oth)
     gate_keep, gate_send = wgrad_call(zi, hidden, dg_near, n2, dg_oth, n2_oth)
+    down_run, do, gate_keep, gate_send, du_oth, da_oth = meet(
+        down_run, do, gate_keep, gate_send, du_oth, da_oth
+    )
+    if near:
+        gate_got = y_swap(gate_send)
+        down_run = ring(plus(down_run, down[2]))
     out_keep, out_send = wgrad_call(zi, width, o, da, o_oth, da_oth)
-    do, gate_keep, gate_send, out_keep, out_send, down_run = meet(
-        do, gate_keep, gate_send, out_keep, out_send, down_run
+    up_keep, up_send = wgrad_call(zi, hidden, du_near, n2, du_oth, n2_oth)
+    do, out_keep, out_send, up_keep, up_send, down_run = meet(
+        do, out_keep, out_send, up_keep, up_send, down_run
     )
     back = attend_back_call(
         scale, None, q, k, k_oth, v, v_oth, do, o, sums, aug_q, aug_k, head_scale, add_k, var_q
@@ -1036,28 +1042,21 @@
     half = hidden // 32 * 16
     cut = width * 3 // 2
     if near:
-        gate_got = y_swap(gate_send)
         down_run = ring(plus(down_run, down[3]))
         out = [jnp.stack([out_keep[r], out_send[r]]) for r in range(4)]
         out_run = [to_owner(out[r], r) for r in (1, 2, 3)]
         gate_got, down_run, *rest = meet(gate_got, down_run, *out_run, *back)
         out_run, back = rest[:3], rest[3:]
-        g_down = down_run.astype(F32) + down[0].astype(F32)
-        out_sum = add_all(out[0], out_run)
     dq, dk, dk_send, dv, dv_send, bias = back
     dk_got, dv_got = core_swap(dk_send), core_swap(dv_send)
-    up_keep, up_send = wgrad_call(zi, hidden, du_near, n2, du_oth, n2_oth)
-    dk_got, dv_got, up_keep, up_send = meet(dk_got, dv_got, up_keep, up_send)
     if near:
-        up_got = [y_swap(up_send[:, :half])]
+        up_got = y_swap(up_send)
         gate = [plus(gate_keep[r], gate_got[r]) for r in range(4)]
-        gate_run = [to_owner(gate[r][:half], r) for r in (1, 2, 3)]
+        gate_run = [to_owner(gate[r], r) for r in (1, 2, 3)]
     back = qkv_back(dq, dk, dk_got, dv, dv_got, dh)
     if near:
-        rest = meet(*up_got, *gate_run, *back)
-        up_got, gate_run, back = rest[:1], rest[1:4], rest[4:]
-        up_got.append(y_swap(up_send[:, half:]))
-        gate_more = [to_owner(gate[r][half:], r) for r in (1, 2, 3)]
+        up_got, *rest = meet(up_got, *gate_run, *back)
+        gate_run, back = rest[:3], rest[3:]
     dp_near, dp_far, dx, dx_low, gg_a = back
     dp_oth = core_swap(dp_far)
     qkv_keep, qkv_send = wgrad_call(zi, 3 * width, dp_near, n1, dp_oth, n1_oth)
@@ -1065,37 +1064,35 @@
     out_low_rows = jnp.where(is_first, dx_low, y.astype(BF))
     send = jnp.where(yi == 0, out_low_rows[rows:], out_low_rows[:rows])
     if near:
-        up_last, qkv_keep, qkv_send, small, send, *gate_more = meet(
-            up_got[1], qkv_keep, qkv_send, small, send, *gate_more
-        )
-        g_gate = jnp.concatenate(
-            [
-                add_all(gate[0][:half], gate_run),
-                add_all(gate[0][half:], gate_more),
-            ],
-            axis=0,
+        up = [plus(up_keep[r, :half], up_got[r, :half]) for r in range(4)]
+        up_run = [to_owner(up[r], r) for r in (1, 2, 3)]
+        rows_got = y_swap(send)
+        out_far = add_all(out[0][1], [run[1] for run in out_run]).astype(BF)
+        out_got = y_swap(out_far)
+        small = small + core_swap(small)
+        rows_got, out_got, qkv_keep, qkv_send, small, *up_run = meet(
+            rows_got, out_got, qkv_keep, qkv_send, small, *up_run
         )
         head_got = y_swap(qkv_send[:, :cut])
-        rows_got = y_swap(send)
-        up = [
-            plus(up_keep[r], jnp.concatenate([up_got[0][r], up_last[r]], axis=0))
-            for r in range(4)
-        ]
-        up_run = [to_owner(up[r], r) for r in (1, 2, 3)]
-        head_got, rows_got, *up_run = meet(head_got, rows_got, *up_run)
+        more = [plus(up_keep[r, half:], up_got[r, half:]) for r in range(4)]
+        more_run = [to_owner(more[r], r) for r in (1, 2, 3)]
+        small = small + y_swap(small)
+        head_got, small, *more_run = meet(head_got, small, *more_run)
         tail_got = y_swap(qkv_send[:, cut:])
         head = [plus(qkv_keep[r, :cut], head_got[r]) for r in range(4)]
         head_run = [to_owner(head[r], r) for r in (1, 2, 3)]
-        tail_got, small, out_sum, *head_run = meet(tail_got, small, out_sum, *head_run)
-        small = small + core_swap(small)
-        small = small + y_swap(small)
+        small = small + lax.ppermute(small, "dp", [(i, i ^ 1) for i in range(4)])
+        tail_got, small, down_run, out_got, *rest = meet(
+            tail_got, small, down_run, out_got, *head_run, *gate_run, *out_run, *up_run, *more_run
+        )
+        head_run, gate_run, out_run, up_run, more_run = (rest[i : i + 3] for i in range(0, 15, 3))
         tail = [plus(qkv_keep[r, cut:], tail_got[r]) for r in range(4)]
         tail_run = [to_owner(tail[r], r) for r in (1, 2, 3)]
-        out_got = y_swap(out_sum[1].astype(BF))
-        for bit in (1, 2):
-            small = small + lax.ppermute(small, "dp", [(i, i ^ bit) for i in range(4)])
-        g_gu = jnp.stack([g_gate, add_all(up[0], up_run)])
-        g_out = out_sum[0] + out_got.astype(F32)
+        small = small + lax.ppermute(small, "dp", [(i, i ^ 2) for i in range(4)])
+        g_down = down_run.astype(F32) + down[0].astype(F32)
+        g_up = [add_all(up[0], up_run), add_all(more[0], more_run)]
+        g_gu = jnp.stack([add_all(gate[0], gate_run), jnp.concatenate(g_up, axis=0)])
+        g_out = add_all(out[0][0], [run[0] for run in out_run] + [out_got])
         g_qkv = jnp.concatenate([add_all(head[0], head_run), add_all(tail[0], tail_run)], axis=0)
     else:
         rows_got = y_swap(send)

time: 656 us -> 633 us (0.965)
  waiting for transfers between devices: 216 us -> 206 us
  local copies, waits for them, and re-layouts: 37.3 us -> 27.5 us
    ppermute x18, waiting for transfers between devices: 37.2 us -> 18.4 us  [to_owner(): return lax.ppermute(part, 'dp', [(i, (i - r) % n) for i in range(n)])]
    ppermute x19 -> x18, waiting for transfers between devices: 48.4 us -> 60.8 us  [y_swap(): return lax.ppermute(value, 'tensor', [(i, i ^ 2) for i in range(n)])]
    ppermute x12, waiting for transfers between devices: 65 us -> 58.3 us  [ring(): return lax.ppermute(value, 'dp', [(i, (i + 1) % n) for i in range(n)])]
    unnamed x209 -> x189, local copies, waits for them, and re-layouts: 18.2 us -> 16.1 us
    ppermute x19 -> x18, starting transfers between devices: 22.1 us -> 21.5 us  [y_swap(): return lax.ppermute(value, 'tensor', [(i, i ^ 2) for i in range(n)])]
  transfers between devices with their start and end apart: 83 -> 82, of which waited for: 27 -> 29; matrix products, arithmetic and copies ran while one was open for 9% -> 8% of each run, Pallas kernels for 25% -> 25%
where the time goes in v4:
time: 633 us; the launch traced here: 625 us
  Pallas kernels  271 us (43%)
  waiting for transfers between devices  206 us (33%)
  starting transfers between devices  68.6 us (11%)
  other arithmetic  49.3 us (8%)
  local copies, waits for them, and re-layouts  27.5 us (4%)
    ppermute x18, waiting for transfers between devices, y_swap(): return lax.ppermute(value, 'tensor', [(i, i ^ 2) for i in range(n)])  60.8 us
    ppermute x12, waiting for transfers between devices, ring(): return lax.ppermute(value, 'dp', [(i, (i + 1) % n) for i in range(n)])  58.3 us
    pallas_call x2, Pallas kernels, ffn_back_call(): pl.pallas_call(functools.partial(ffn_back_kernel, out_low), grid=(2,), in...  55.5 us
    pallas_call x2, Pallas kernels, attend_back_call(): pl.pallas_call(functools.partial(attend_back_kernel, scale), grid=(pairs,...  54.6 us
    pallas_call x2, Pallas kernels, ffn_up_call(): pl.pallas_call(functools.partial(ffn_up_kernel, save, out_low), grid=(2,)...  38.1 us
    pallas_call x2, Pallas kernels, qkv_back_call(): pl.pallas_call(qkv_back_kernel, grid=(4,), in_specs=[col] * 7 + [whole((r...  32.8 us
    pallas_call x2, Pallas kernels, attend_call(): pl.pallas_call(functools.partial(attend_kernel, scale), grid=(pairs,), in...  30.4 us
    ppermute x18, starting transfers between devices, to_owner(): return lax.ppermute(part, 'dp', [(i, (i - r) % n) for i in range(n)])  23.4 us
  transfers between devices with their start and end apart: 82, of which 29 were waited for; matrix products, arithmetic and copies ran while one was open for 8% of the time, Pallas kernels for 25%

profile of v4, /device:TPU:0, one launch (start us, length us, event | category | flops | bytes accessed | tf_op | source)
XLA Modules:
  0.0 625.1 jit_solution(4380249491508264979)
XLA Ops:
  4.3 3.1 collective-permute-start
  7.4 1.7 fusion.14
  15.5 7.1 %collective-permute-done.1 = bf16[256,1024]{1,0:T(8,128)(2,1)S(1)} collective-permute-done((bf16[256,1024]{1,0:T(8,128)(2,1)S(1)}, bf16[256,1024]{1,0:T(8,128)(2,1)S(1)}, u32[]{:S(2)}, u32[]{:S(2)}) %collective-permute-start.1) | collective-permute-done | bytes 524320 | tf_op jit(solution)/shard_map/ppermute | solution.py:739
  29.5 8.3 %collective-permute-done.2 = bf16[1040,256]{1,0:T(8,128)(2,1)S(1)} collective-permute-done((bf16[1040,256]{1,0:T(8,128)(2,1)S(1)}, bf16[1040,256]{1,0:T(8,128)(2,1)S(1)}, u32[]{:S(2)}, u32[]{:S(2)}) %collective-permute-start.2) | collective-permute-done | bytes 532512 | tf_op jit(solution)/shard_map/ppermute | solution.py:744
  40.4 2.6 maximum_select_fusion.1.x_ref.dy_ref
  43.0 8.4 %collective-permute-done.4 = bf16[1040,256]{1,0:T(8,128)(2,1)} collective-permute-done((bf16[1040,256]{1,0:T(8,128)(2,1)S(1)}, bf16[1040,256]{1,0:T(8,128)(2,1)}, u32[]{:S(2)}, u32[]{:S(2)}) %collective-permute-start.4) | collective-permute-done | bytes 532512 | tf_op jit(solution)/shard_map/ppermute | solution.py:744
  54.3 15.6 %collective-permute-done.8 = bf16[688,256]{1,0:T(8,128)(2,1)S(1)} collective-permute-done((bf16[688,256]{1,0:T(8,128)(2,1)}, bf16[688,256]{1,0:T(8,128)(2,1)S(1)}, u32[]{:S(2)}, u32[]{:S(2)}) %collective-permute-start.8) | collective-permute-done | bytes 352288 | tf_op jit(solution)/shard_map/ppermute | solution.py:739
  75.4 10.2 %collective-permute-done.10 = bf16[1040,256]{1,0:T(8,128)(2,1)S(1)} collective-permute-done((bf16[1040,256]{1,0:T(8,128)(2,1)}, bf16[1040,256]{1,0:T(8,128)(2,1)S(1)}, u32[]{:S(2)}, u32[]{:S(2)}) %collective-permute-start.10) | collective-permute-done | bytes 532512 | tf_op jit(solution)/shard_map/ppermute | solution.py:739
  85.6 2.4 pad_maximum_fusion.7.refs_3_
  94.6 10.7 %shard_map.171 = (bf16[512,1024]{1,0:T(8,128)(2,1)}, bf16[512,1024]{1,0:T(8,128)(2,1)}, bf16[512,1024]{1,0:T(8,128)(2,1)}) custom-call(bf16[512,1024]{1,0:T(8,128)(2,1)} %maximum_select_fusion.1.x_ref.dy_ref, f32[1,1024]{1,0:T(1,128)} %bitcast.187, s32[1]{0:T(128)} %bitcast.25.zi_ref, f32[512,128]{1,0:T(8,128)} %pad_maximum_fusion.10.cos_ref, ...), custom_call_target="tpu_custom_call" | custom-call | flops 3221225472 | bytes 14680064 | tf_op jit(solution)/shard_map/pallas_call | solution.py:175
  105.3 5.7 collective-permute-done.11
  113.9 1.6 collective-permute-start.17
  118.2 15.3 %shard_map.172 = (bf16[512,1024]{1,0:T(8,128)(2,1)}, f32[512,1024]{1,0:T(8,128)}) custom-call(bf16[512,1024]{1,0:T(8,128)(2,1)} %get-tuple-element.238.q_ref, bf16[512,1024]{1,0:T(8,128)(2,1)} %get-tuple-element.239.ko_ref, bf16[512,1024]{1,0:T(8,128)(2,1)} %collective-permute-done.19.kx_ref, bf16[512,1024]{1,0:T(8,128)(2,1)} %get-tuple-element.240.vo_ref, ...), custom_call_target="tpu_custom_call" | custom-call | flops 4294967296 | bytes 10485760 | tf_op jit(solution)/shard_map/pallas_call | solution.py:238
  136.0 17.1 %collective-permute-done.21.refs_2_.refs_18_ = bf16[2,688,256]{2,1,0:T(8,128)(2,1)S(1)} collective-permute-done((bf16[2,688,256]{2,1,0:T(8,128)(2,1)S(1)}, bf16[2,688,256]{2,1,0:T(8,128)(2,1)S(1)}, u32[]{:S(2)}, u32[]{:S(2)}) %collective-permute-start.21) | collective-permute-done | bytes 704544 | tf_op jit(solution)/shard_map/ppermute | solution.py:744
  158.1 13.1 %collective-permute-done.23.refs_3_.refs_19_ = bf16[2,688,256]{2,1,0:T(8,128)(2,1)S(1)} collective-permute-done((bf16[2,688,256]{2,1,0:T(8,128)(2,1)S(1)}, bf16[2,688,256]{2,1,0:T(8,128)(2,1)S(1)}, u32[]{:S(2)}, u32[]{:S(2)}) %collective-permute-start.23) | collective-permute-done | bytes 704544 | tf_op jit(solution)/shard_map/ppermute | solution.py:744
  172.8 1.9 collective-permute-done.28.refs_15_
  175.8 18.4 %shard_map.173 = (f32[512,1024]{1,0:T(8,128)}, bf16[512,1408]{1,0:T(8,128)(2,1)}, bf16[512,1408]{1,0:T(8,128)(2,1)}) custom-call(bf16[512,1024]{1,0:T(8,128)(2,1)} %maximum_select_fusion.1.x_ref.dy_ref, bf16[512,1024]{1,0:T(8,128)(2,1)} %get-tuple-element.245.o_ref, f32[1,1024]{1,0:T(1,128)} %bitcast.201, s32[1]{0:T(128)} %bitcast.25.zi_ref, ...), custom_call_target="tpu_custom_call" | custom-call | flops 6845104128 | bytes 21757952 | tf_op jit(solution)/shard_map/pallas_call | solution.py:388
  195.8 9.6 %shard_map.174 = bf16[512,1024]{1,0:T(8,128)(2,1)} custom-call(f32[512,1024]{1,0:T(8,128)} %get-tuple-element.256.h_ref, bf16[512,1408]{1,0:T(8,128)(2,1)} %get-tuple-element.257.zn_ref, bf16[512,1408]{1,0:T(8,128)(2,1)} %get-tuple-element.258.zf_ref, s32[1]{0:T(128)} %bitcast.25.zi_ref, bf16[2,688,256]{2,1,0:T(8,128)(2,1)} %copy-done.27, ...), custom_call_target="tpu_custom_call" | custom-call | flops 2885681152 | bytes 9830400 | tf_op jit(solution)/shard_map/pallas_call | solution.py:422
  205.4 3.6 collective-permute-start.33
  209.0 22.8 %collective-permute-done.33 = bf16[512,1024]{1,0:T(8,128)(2,1)S(1)} collective-permute-done((bf16[512,1024]{1,0:T(8,128)(2,1)}, bf16[512,1024]{1,0:T(8,128)(2,1)S(1)}, u32[]{:S(2)}, u32[]{:S(2)}) %collective-permute-start.33) | collective-permute-done | bytes 1048608 | tf_op jit(solution)/shard_map/ppermute | solution.py:988
  232.9 11.1 %shard_map.175 = (bf16[512,1024]{1,0:T(8,128)(2,1)}, bf16[512,1024]{1,0:T(8,128)(2,1)}, bf16[512,1024]{1,0:T(8,128)(2,1)}, bf16[512,1024]{1,0:T(8,128)(2,1)}, bf...) custom-call(bf16[512,1024]{1,0:T(8,128)(2,1)} %broadcast_select_fusion.2.x_ref, f32[1,1024]{1,0:T(1,128)} %bitcast.188, ...), custom_call_target="tpu_custom_call" | custom-call | flops 3221225472 | bytes 14680064 | tf_op jit(solution)/shard_map/pallas_call | solution.py:175
  244.5 2.4 collective-permute-done.34.kx_ref
  249.4 15.1 %shard_map.176 = (bf16[512,1024]{1,0:T(8,128)(2,1)}, f32[512,1024]{1,0:T(8,128)}) custom-call(bf16[512,1024]{1,0:T(8,128)(2,1)} %get-tuple-element.260.q_ref, bf16[512,1024]{1,0:T(8,128)(2,1)} %get-tuple-element.261.ko_ref, bf16[512,1024]{1,0:T(8,128)(2,1)} %copy-done.91, bf16[512,1024]{1,0:T(8,128)(2,1)} %get-tuple-element.262.vo_ref, ...), custom_call_target="tpu_custom_call" | custom-call | flops 4294967296 | bytes 10485760 | tf_op jit(solution)/shard_map/pallas_call | solution.py:238
  264.5 19.6 %shard_map.177 = (f32[512,1024]{1,0:T(8,128)}, bf16[512,1408]{1,0:T(8,128)(2,1)}, bf16[512,1408]{1,0:T(8,128)(2,1)}, bf16[512,1024]{1,0:T(8,128)(2,1)}, bf16[2,5...) custom-call(bf16[512,1024]{1,0:T(8,128)(2,1)} %broadcast_select_fusion.2.x_ref, ...), custom_call_target="tpu_custom_call" | custom-call | flops 6845104128 | bytes 21757952 | tf_op jit(solution)/shard_map/pallas_call | solution.py:388
  284.2 27.8 %shard_map.178 = (f32[512,1024]{1,0:T(8,128)}, bf16[512,1024]{1,0:T(8,128)(2,1)}, bf16[512,1024]{1,0:T(8,128)(2,1)}, bf16[512,1408]{1,0:T(8,128)(2,1)}, bf16[512...) custom-call(bf16[512,1024]{1,0:T(8,128)(2,1)} %maximum_select_fusion.1.x_ref.dy_re, ...), custom_call_target="tpu_custom_call" | custom-call | flops 9730785280 | bytes 27394048 | tf_op jit(solution)/shard_map/pallas_call | solution.py:500
  312.0 27.3 %shard_map.179 = (bf16[512,1024]{1,0:T(8,128)(2,1)}, bf16[512,1024]{1,0:T(8,128)(2,1)}, bf16[512,1024]{1,0:T(8,128)(2,1)}, bf16[512,1024]{1,0:T(8,128)(2,1)}, bf...) custom-call(bf16[512,1024]{1,0:T(8,128)(2,1)} %get-tuple-element.260.q_ref, bf16[512,1024]{1,0:T(8,128)(2,1)} %get-tuple-element.261.ko_ref, ...), custom_call_target="tpu_custom_call" | custom-call | flops 10737418240 | bytes 20971520 | tf_op jit(solution)/shard_map/pallas_call | solution.py:602
  340.6 1.7 collective-permute-done.36.dkr_ref
  342.3 3.0 collective-permute-done.37.dvr_ref
  346.3 16.6 %shard_map.180 = (bf16[2,512,768]{2,1,0:T(8,128)(2,1)}, bf16[2,512,768]{2,1,0:T(8,128)(2,1)}, f32[512,1024]{1,0:T(8,128)}, bf16[512,1024]{1,0:T(8,128)(2,1)}, f32[1,1024]{1,0:T(1,128)}) custom-call(bf16[512,1024]{1,0:T(8,128)(2,1)} %get-tuple-element.271.dq_ref, bf16[512,1024]{1,0:T(8,128)(2,1)} %get-tuple-element.272.dk_ref, bf16[512,1024]{1,0:T(8,128)(2,1)} %copy-done.45, ...), custom_call_target="tpu_custom_call" | custom-call | flops 3221225472 | bytes 27262976 | tf_op jit(solution)/shard_map/pallas_call | solution.py:685
  364.4 9.9 %shard_map.181 = f32[512,1024]{1,0:T(8,128)} custom-call(f32[512,1024]{1,0:T(8,128)} %get-tuple-element.264.h_ref, bf16[512,1408]{1,0:T(8,128)(2,1)} %get-tuple-element.280.zn_ref.ao_ref, bf16[512,1408]{1,0:T(8,128)(2,1)} %get-tuple-element.281.zf_ref, s32[1]{0:T(128)} %bitcast.25.zi_ref, bf16[2,688,256]{2,1,0:T(8,128)(2,1)} %copy-done.27, ...), custom_call_target="tpu_custom_call" | custom-call | flops 2885681152 | bytes 9830400 | tf_op jit(solution)/shard_map/pallas_call | solution.py:422
  376.2 14.1 %collective-permute-done.38 = bf16[512,1024]{1,0:T(8,128)(2,1)} collective-permute-done((bf16[512,1024]{1,0:T(8,128)(2,1)}, bf16[512,1024]{1,0:T(8,128)(2,1)}, u32[]{:S(2)}, u32[]{:S(2)}) %collective-permute-start.38) | collective-permute-done | bytes 1048608 | tf_op jit(solution)/shard_map/ppermute | solution.py:1007
  391.7 2.6 collective-permute-done.43.bx_ref
  394.4 3.2 shard_map.182
  398.3 27.7 %shard_map.183 = (f32[512,1024]{1,0:T(8,128)}, bf16[512,1024]{1,0:T(8,128)(2,1)}, bf16[512,1024]{1,0:T(8,128)(2,1)}, bf16[512,1408]{1,0:T(8,128)(2,1)}, bf16[512...) custom-call(bf16[512,1024]{1,0:T(8,128)(2,1)} %copy-done.3, ...), custom_call_target="tpu_custom_call" | custom-call | flops 9730785280 | bytes 27394048 | tf_op jit(solution)/shard_map/pallas_call | solution.py:500
  426.0 4.8 collective-permute-done.44
  432.4 5.3 collective-permute-done.48.bx_ref
  440.4 4.3 shard_map.184
  444.8 1.7 fusion.10
  448.8 4.3 shard_map.186
  453.2 5.4 collective-permute-done.49
  459.8 3.9 collective-permute-start.53
  464.4 27.2 %shard_map.187 = (bf16[512,1024]{1,0:T(8,128)(2,1)}, bf16[512,1024]{1,0:T(8,128)(2,1)}, bf16[512,1024]{1,0:T(8,128)(2,1)}, bf16[512,1024]{1,0:T(8,128)(2,1)}, bf...) custom-call(bf16[512,1024]{1,0:T(8,128)(2,1)} %get-tuple-element.260.q_ref, bf16[512,1024]{1,0:T(8,128)(2,1)} %get-tuple-element.261.ko_ref, ...), custom_call_target="tpu_custom_call" | custom-call | flops 10737418240 | bytes 20971520 | tf_op jit(solution)/shard_map/pallas_call | solution.py:602
  493.3 2.3 fusion.26
  495.7 3.3 collective-permute-start.56
  501.0 16.2 %shard_map.188 = (bf16[2,512,768]{2,1,0:T(8,128)(2,1)}, bf16[2,512,768]{2,1,0:T(8,128)(2,1)}, f32[512,1024]{1,0:T(8,128)}, bf16[512,1024]{1,0:T(8,128)(2,1)}, f32[1,1024]{1,0:T(1,128)}) custom-call(bf16[512,1024]{1,0:T(8,128)(2,1)} %get-tuple-element.336.dq_ref, bf16[512,1024]{1,0:T(8,128)(2,1)} %get-tuple-element.337.dk_ref, bf16[512,1024]{1,0:T(8,128)(2,1)} %copy-done.44, ...), custom_call_target="tpu_custom_call" | custom-call | flops 3221225472 | bytes 27262976 | tf_op jit(solution)/shard_map/pallas_call | solution.py:685
  517.2 9.0 %collective-permute-done.50 = bf16[4,688,256]{2,1,0:T(8,128)(2,1)} collective-permute-done((bf16[4,688,256]{2,1,0:T(8,128)(2,1)}, bf16[4,688,256]{2,1,0:T(8,128)(2,1)}, u32[]{:S(2)}, u32[]{:S(2)}) %collective-permute-start.50) | collective-permute-done | bytes 1409056 | tf_op jit(solution)/shard_map/ppermute | solution.py:739
  526.2 5.2 collective-permute-done.57
  535.3 2.1 convert_select_fusion
  540.9 2.0 collective-permute-start.67
  542.9 5.0 shard_map.189
  548.0 8.9 %collective-permute-done.66 = bf16[336,256]{1,0:T(8,128)(2,1)S(1)} collective-permute-done((bf16[336,256]{1,0:T(8,128)(2,1)S(1)}, bf16[336,256]{1,0:T(8,128)(2,1)S(1)}, u32[]{:S(2)}, u32[]{:S(2)}) %collective-permute-start.66) | collective-permute-done | bytes 172064 | tf_op jit(solution)/shard_map/ppermute | solution.py:767
  561.8 1.8 collective-permute-start.71
  563.6 1.9 collective-permute-start.72
  565.5 11.3 %collective-permute-done.69 = f32[3,1024]{1,0:T(4,128)S(1)} collective-permute-done((f32[3,1024]{1,0:T(4,128)S(1)}, f32[3,1024]{1,0:T(4,128)S(1)}, u32[]{:S(2)}, u32[]{:S(2)}) %collective-permute-start.69) | collective-permute-done | bytes 12320 | tf_op jit(solution)/shard_map/ppermute | solution.py:739
  580.9 1.9 collective-permute-start.77
  585.0 7.4 %collective-permute-done.74 = f32[3,1024]{1,0:T(4,128)S(1)} collective-permute-done((f32[3,1024]{1,0:T(4,128)S(1)}, f32[3,1024]{1,0:T(4,128)S(1)}, u32[]{:S(2)}, u32[]{:S(2)}) %collective-permute-start.74) | collective-permute-done | bytes 12320 | tf_op jit(solution)/shard_map/ppermute | solution.py:1084
  592.4 2.9 collective-permute-done.73
  595.3 3.3 collective-permute-done.76
  600.6 2.9 collective-permute-start.78
  603.5 2.1 fusion.5
  605.6 2.0 collective-permute-start.81
  609.7 1.7 fusion.8
  611.5 1.7 fusion.31
  614.3 6.0 collective-permute-done.81
  (424 shorter events, 103.2 us)
Async XLA Ops:
  4.3 18.2 %collective-permute-start = (bf16[1040,256]{1,0:T(8,128)(2,1)S(1)}, bf16[1040,256]{1,0:T(8,128)(2,1)S(1)}, u32[]{:S(2)}, u32[]{:S(2)}) collective-permute-start(bf16[1040,256]{1,0:T(8,128)(2,1)S(1)} %fusion.12), channel_id=1, source_target_pairs={{0,4},{4,8},{8,12},{12,0},{1,5},{5,9},{9,13},{13,1},{2,6},{6,10},{... | collective-permute-start | bytes 1597448 | tf_op jit(solution)/shard_map/ppermute | solution.py:744
  9.1 13.4 %collective-permute-start.1 = (bf16[256,1024]{1,0:T(8,128)(2,1)S(1)}, bf16[256,1024]{1,0:T(8,128)(2,1)S(1)}, u32[]{:S(2)}, u32[]{:S(2)}) collective-permute-start(bf16[256,1024]{1,0:T(8,128)(2,1)S(1)} %get-tuple-element.417), channel_id=1, source_target_pairs={{0,2},{1,3},{2,0},{3,1},{4,6},{5,7},{6,4},{7,5},{8,10},{9,11},{10,... | collective-permute-start | bytes 1572872 | tf_op jit(solution)/shard_map/ppermute | solution.py:739
  23.4 14.4 %collective-permute-start.2 = (bf16[1040,256]{1,0:T(8,128)(2,1)S(1)}, bf16[1040,256]{1,0:T(8,128)(2,1)S(1)}, u32[]{:S(2)}, u32[]{:S(2)}) collective-permute-start(bf16[1040,256]{1,0:T(8,128)(2,1)S(1)} %collective-permute-done), channel_id=1, source_target_pairs={{0,4},{4,8},{8,12},{12,0},{1,5},{5,9},{9,13},{13,1},{2,6},{6,10},{... | collective-permute-start | bytes 1597448 | tf_op jit(solution)/shard_map/ppermute | solution.py:744
  24.9 12.9 %collective-permute-start.3 = (bf16[1040,256]{1,0:T(8,128)(2,1)S(1)}, bf16[1040,256]{1,0:T(8,128)(2,1)S(1)}, u32[]{:S(2)}, u32[]{:S(2)}) collective-permute-start(bf16[1040,256]{1,0:T(8,128)(2,1)S(1)} %fusion.12), channel_id=1, source_target_pairs={{0,2},{1,3},{2,0},{3,1},{4,6},{5,7},{6,4},{7,5},{8,10},{9,11},{10,... | collective-permute-start | bytes 1597448 | tf_op jit(solution)/shard_map/ppermute | solution.py:739
  37.8 13.7 %collective-permute-start.4 = (bf16[1040,256]{1,0:T(8,128)(2,1)S(1)}, bf16[1040,256]{1,0:T(8,128)(2,1)}, u32[]{:S(2)}, u32[]{:S(2)}) collective-permute-start(bf16[1040,256]{1,0:T(8,128)(2,1)S(1)} %collective-permute-done.2), channel_id=1, source_target_pairs={{0,4},{4,8},{8,12},{12,0},{1,5},{5,9},{9,13},{13,1},{2,6},{6,10},{... | collective-permute-start | bytes 1597448 | tf_op jit(solution)/shard_map/ppermute | solution.py:744
  38.9 12.6 %collective-permute-start.5 = (bf16[1040,256]{1,0:T(8,128)(2,1)S(1)}, bf16[1040,256]{1,0:T(8,128)(2,1)}, u32[]{:S(2)}, u32[]{:S(2)}) collective-permute-start(bf16[1040,256]{1,0:T(8,128)(2,1)S(1)} %collective-permute-done), channel_id=1, source_target_pairs={{0,2},{1,3},{2,0},{3,1},{4,6},{5,7},{6,4},{7,5},{8,10},{9,11},{10,... | collective-permute-start | bytes 1597448 | tf_op jit(solution)/shard_map/ppermute | solution.py:739
  51.5 18.4 %collective-permute-start.6 = (bf16[1376,256]{1,0:T(8,128)(2,1)S(1)}, bf16[1376,256]{1,0:T(8,128)(2,1)}, u32[]{:S(2)}, u32[]{:S(2)}) collective-permute-start(bf16[1376,256]{1,0:T(8,128)(2,1)S(1)} %bitcast.171), channel_id=1, source_target_pairs={{0,4},{4,8},{8,12},{12,0},{1,5},{5,9},{9,13},{13,1},{2,6},{6,10},{... | collective-permute-start | bytes 2113544 | tf_op jit(solution)/shard_map/ppermute | solution.py:744
  51.6 18.3 %collective-permute-start.7 = (bf16[1040,256]{1,0:T(8,128)(2,1)S(1)}, bf16[1040,256]{1,0:T(8,128)(2,1)}, u32[]{:S(2)}, u32[]{:S(2)}) collective-permute-start(bf16[1040,256]{1,0:T(8,128)(2,1)S(1)} %collective-permute-done.2), channel_id=1, source_target_pairs={{0,2},{1,3},{2,0},{3,1},{4,6},{5,7},{6,4},{7,5},{8,10},{9,11},{10,... | collective-permute-start | bytes 1597448 | tf_op jit(solution)/shard_map/ppermute | solution.py:739
  53.1 16.8 %collective-permute-start.8 = (bf16[688,256]{1,0:T(8,128)(2,1)}, bf16[688,256]{1,0:T(8,128)(2,1)S(1)}, u32[]{:S(2)}, u32[]{:S(2)}) collective-permute-start(bf16[688,256]{1,0:T(8,128)(2,1)} %bitcast.9), channel_id=1, source_target_pairs={{0,2},{1,3},{2,0},{3,1},{4,6},{5,7},{6,4},{7,5},{8,10},{9,11},{10,... | collective-permute-start | bytes 1056776 | tf_op jit(solution)/shard_map/ppermute | solution.py:739
  69.9 15.7 %collective-permute-start.9 = (bf16[1376,256]{1,0:T(8,128)(2,1)}, bf16[1376,256]{1,0:T(8,128)(2,1)S(1)}, u32[]{:S(2)}, u32[]{:S(2)}) collective-permute-start(bf16[1376,256]{1,0:T(8,128)(2,1)} %collective-permute-done.6), channel_id=1, source_target_pairs={{0,4},{4,8},{8,12},{12,0},{1,5},{5,9},{9,13},{13,1},{2,6},{6,10},{... | collective-permute-start | bytes 2113544 | tf_op jit(solution)/shard_map/ppermute | solution.py:744
  70.8 21.6 %collective-permute-start.13 = (bf16[2,1040,256]{2,1,0:T(8,128)(2,1)S(1)}, bf16[2,1040,256]{2,1,0:T(8,128)(2,1)}, u32[]{:S(2)}, u32[]{:S(2)}) collective-permute-start(bf16[2,1040,256]{2,1,0:T(8,128)(2,1)S(1)} %pad_maximum_fusion.4.refs_0_), channel_id=1, source_target_pairs={{0,1},{1,0},{2,3},{3,2},{4,5},{5,4},{6,7},{7,6},{8,9},{9,8},{10,11... | collective-permute-start | bytes 3194888 | tf_op jit(solution)/shard_map/ppermute | solution.py:734
  70.9 14.7 %collective-permute-start.10 = (bf16[1040,256]{1,0:T(8,128)(2,1)}, bf16[1040,256]{1,0:T(8,128)(2,1)S(1)}, u32[]{:S(2)}, u32[]{:S(2)}) collective-permute-start(bf16[1040,256]{1,0:T(8,128)(2,1)} %collective-permute-done.4), channel_id=1, source_target_pairs={{0,2},{1,3},{2,0},{3,1},{4,6},{5,7},{6,4},{7,5},{8,10},{9,11},{10,... | collective-permute-start | bytes 1597448 | tf_op jit(solution)/shard_map/ppermute | solution.py:739
  73.6 20.9 %collective-permute-start.14 = (bf16[2,1040,256]{2,1,0:T(8,128)(2,1)S(1)}, bf16[2,1040,256]{2,1,0:T(8,128)(2,1)}, u32[]{:S(2)}, u32[]{:S(2)}) collective-permute-start(bf16[2,1040,256]{2,1,0:T(8,128)(2,1)S(1)} %pad_maximum_fusion.5.refs_1_), channel_id=1, source_target_pairs={{0,1},{1,0},{2,3},{3,2},{4,5},{5,4},{6,7},{7,6},{8,9},{9,8},{10,11... | collective-permute-start | bytes 3194888 | tf_op jit(solution)/shard_map/ppermute | solution.py:734
  75.2 19.4 %collective-permute-start.15 = (bf16[2,1040,256]{2,1,0:T(8,128)(2,1)S(1)}, bf16[2,1040,256]{2,1,0:T(8,128)(2,1)}, u32[]{:S(2)}, u32[]{:S(2)}) collective-permute-start(bf16[2,1040,256]{2,1,0:T(8,128)(2,1)S(1)} %pad_maximum_fusion.6.refs_2_), channel_id=1, source_target_pairs={{0,1},{1,0},{2,3},{3,2},{4,5},{5,4},{6,7},{7,6},{8,9},{9,8},{10,11... | collective-permute-start | bytes 3194888 | tf_op jit(solution)/shard_map/ppermute | solution.py:734
  90.8 20.2 %collective-permute-start.11 = (bf16[1376,256]{1,0:T(8,128)(2,1)}, bf16[1376,256]{1,0:T(8,128)(2,1)S(1)}, u32[]{:S(2)}, u32[]{:S(2)}) collective-permute-start(bf16[1376,256]{1,0:T(8,128)(2,1)} %copy-done.51), channel_id=1, source_target_pairs={{0,4},{4,8},{8,12},{12,0},{1,5},{5,9},{9,13},{13,1},{2,6},{6,10},{... | collective-permute-start | bytes 2113544 | tf_op jit(solution)/shard_map/ppermute | solution.py:744
  92.4 18.7 %collective-permute-start.12 = (bf16[1376,256]{1,0:T(8,128)(2,1)}, bf16[1376,256]{1,0:T(8,128)(2,1)S(1)}, u32[]{:S(2)}, u32[]{:S(2)}) collective-permute-start(bf16[1376,256]{1,0:T(8,128)(2,1)} %bitcast.170), channel_id=1, source_target_pairs={{0,2},{1,3},{2,0},{3,1},{4,6},{5,7},{6,4},{7,5},{8,10},{9,11},{10,... | collective-permute-start | bytes 2113544 | tf_op jit(solution)/shard_map/ppermute | solution.py:739
  113.9 19.5 %collective-permute-start.17 = (bf16[2,688,256]{2,1,0:T(8,128)(2,1)S(1)}, bf16[2,688,256]{2,1,0:T(8,128)(2,1)S(1)}, u32[]{:S(2)}, u32[]{:S(2)}) collective-permute-start(bf16[2,688,256]{2,1,0:T(8,128)(2,1)S(1)} %pad_maximum_fusion.9.refs_0_.refs_16_), channel_id=1, source_target_pairs={{0,4},{4,8},{8,12},{12,0},{1,5},{5,9},{9,13},{13,1},{2,6},{6,10},{... | collective-permute-start | bytes 2113544 | tf_op jit(solution)/shard_map/ppermute | solution.py:744
  115.6 17.9 %collective-permute-start.18 = (bf16[1376,256]{1,0:T(8,128)(2,1)}, bf16[1376,256]{1,0:T(8,128)(2,1)S(1)}, u32[]{:S(2)}, u32[]{:S(2)}) collective-permute-start(bf16[1376,256]{1,0:T(8,128)(2,1)} %collective-permute-done.6), channel_id=1, source_target_pairs={{0,2},{1,3},{2,0},{3,1},{4,6},{5,7},{6,4},{7,5},{8,10},{9,11},{10,... | collective-permute-start | bytes 2113544 | tf_op jit(solution)/shard_map/ppermute | solution.py:739
  134.4 18.7 %collective-permute-start.21 = (bf16[2,688,256]{2,1,0:T(8,128)(2,1)S(1)}, bf16[2,688,256]{2,1,0:T(8,128)(2,1)S(1)}, u32[]{:S(2)}, u32[]{:S(2)}) collective-permute-start(bf16[2,688,256]{2,1,0:T(8,128)(2,1)S(1)} %collective-permute-done.17.refs_1_.refs_17_), channel_id=1, source_target_pairs={{0,4},{4,8},{8,12},{12,0},{1,5},{5,9},{9,13},{13,1},{2,6},{6,10},{... | collective-permute-start | bytes 2113544 | tf_op jit(solution)/shard_map/ppermute | solution.py:744
  135.1 18.0 %collective-permute-start.22 = (bf16[1376,256]{1,0:T(8,128)(2,1)S(1)}, bf16[1376,256]{1,0:T(8,128)(2,1)S(1)}, u32[]{:S(2)}, u32[]{:S(2)}) collective-permute-start(bf16[1376,256]{1,0:T(8,128)(2,1)S(1)} %copy-done.52), channel_id=1, source_target_pairs={{0,2},{1,3},{2,0},{3,1},{4,6},{5,7},{6,4},{7,5},{8,10},{9,11},{10,... | collective-permute-start | bytes 2113544 | tf_op jit(solution)/shard_map/ppermute | solution.py:739
  153.1 18.2 %collective-permute-start.23 = (bf16[2,688,256]{2,1,0:T(8,128)(2,1)S(1)}, bf16[2,688,256]{2,1,0:T(8,128)(2,1)S(1)}, u32[]{:S(2)}, u32[]{:S(2)}) collective-permute-start(bf16[2,688,256]{2,1,0:T(8,128)(2,1)S(1)} %collective-permute-done.21.refs_2_.refs_18_), channel_id=1, source_target_pairs={{0,4},{4,8},{8,12},{12,0},{1,5},{5,9},{9,13},{13,1},{2,6},{6,10},{... | collective-permute-start | bytes 2113544 | tf_op jit(solution)/shard_map/ppermute | solution.py:744
  153.5 17.7 %collective-permute-start.24 = (bf16[1376,256]{1,0:T(8,128)(2,1)S(1)}, bf16[1376,256]{1,0:T(8,128)(2,1)S(1)}, u32[]{:S(2)}, u32[]{:S(2)}) collective-permute-start(bf16[1376,256]{1,0:T(8,128)(2,1)S(1)} %copy-done.54), channel_id=1, source_target_pairs={{0,2},{1,3},{2,0},{3,1},{4,6},{5,7},{6,4},{7,5},{8,10},{9,11},{10,... | collective-permute-start | bytes 2113544 | tf_op jit(solution)/shard_map/ppermute | solution.py:739
  154.7 17.3 %collective-permute-start.25 = (bf16[2,1376,256]{2,1,0:T(8,128)(2,1)S(1)}, bf16[2,1376,256]{2,1,0:T(8,128)(2,1)S(1)}, u32[]{:S(2)}, u32[]{:S(2)}) collective-permute-start(bf16[2,1376,256]{2,1,0:T(8,128)(2,1)S(1)} %pad_maximum_fusion.refs_8_), channel_id=1, source_target_pairs={{0,1},{1,0},{2,3},{3,2},{4,5},{5,4},{6,7},{7,6},{8,9},{9,8},{10,11... | collective-permute-start | bytes 4227080 | tf_op jit(solution)/shard_map/ppermute | solution.py:734
  157.0 15.1 %collective-permute-start.26 = (bf16[2,1376,256]{2,1,0:T(8,128)(2,1)S(1)}, bf16[2,1376,256]{2,1,0:T(8,128)(2,1)S(1)}, u32[]{:S(2)}, u32[]{:S(2)}) collective-permute-start(bf16[2,1376,256]{2,1,0:T(8,128)(2,1)S(1)} %pad_maximum_fusion.1.refs_9_), channel_id=1, source_target_pairs={{0,1},{1,0},{2,3},{3,2},{4,5},{5,4},{6,7},{7,6},{8,9},{9,8},{10,11... | collective-permute-start | bytes 4227080 | tf_op jit(solution)/shard_map/ppermute | solution.py:734
  158.1 14.5 %collective-permute-start.27 = (bf16[2,1376,256]{2,1,0:T(8,128)(2,1)S(1)}, bf16[2,1376,256]{2,1,0:T(8,128)(2,1)S(1)}, u32[]{:S(2)}, u32[]{:S(2)}) collective-permute-start(bf16[2,1376,256]{2,1,0:T(8,128)(2,1)S(1)} %pad_maximum_fusion.2.refs_10_), channel_id=1, source_target_pairs={{0,1},{1,0},{2,3},{3,2},{4,5},{5,4},{6,7},{7,6},{8,9},{9,8},{10,11... | collective-permute-start | bytes 4227080 | tf_op jit(solution)/shard_map/ppermute | solution.py:734
  171.5 22.7 %collective-permute-start.29 = (bf16[2,688,256]{2,1,0:T(8,128)(2,1)S(1)}, bf16[2,688,256]{2,1,0:T(8,128)(2,1)S(1)}, u32[]{:S(2)}, u32[]{:S(2)}) collective-permute-start(bf16[2,688,256]{2,1,0:T(8,128)(2,1)S(1)} %pad_maximum_fusion.9.refs_0_.refs_16_), channel_id=1, source_target_pairs={{0,1},{1,0},{2,3},{3,2},{4,5},{5,4},{6,7},{7,6},{8,9},{9,8},{10,11... | collective-permute-start | bytes 2113544 | tf_op jit(solution)/shard_map/ppermute | solution.py:734
  172.0 22.2 %collective-permute-start.30 = (bf16[2,688,256]{2,1,0:T(8,128)(2,1)S(1)}, bf16[2,688,256]{2,1,0:T(8,128)(2,1)S(1)}, u32[]{:S(2)}, u32[]{:S(2)}) collective-permute-start(bf16[2,688,256]{2,1,0:T(8,128)(2,1)S(1)} %collective-permute-done.17.refs_1_.refs_17_), channel_id=1, source_target_pairs={{0,1},{1,0},{2,3},{3,2},{4,5},{5,4},{6,7},{7,6},{8,9},{9,8},{10,11... | collective-permute-start | bytes 2113544 | tf_op jit(solution)/shard_map/ppermute | solution.py:734
  172.2 22.1 %collective-permute-start.31 = (bf16[2,688,256]{2,1,0:T(8,128)(2,1)S(1)}, bf16[2,688,256]{2,1,0:T(8,128)(2,1)S(1)}, u32[]{:S(2)}, u32[]{:S(2)}) collective-permute-start(bf16[2,688,256]{2,1,0:T(8,128)(2,1)S(1)} %collective-permute-done.21.refs_2_.refs_18_), channel_id=1, source_target_pairs={{0,1},{1,0},{2,3},{3,2},{4,5},{5,4},{6,7},{7,6},{8,9},{9,8},{10,11... | collective-permute-start | bytes 2113544 | tf_op jit(solution)/shard_map/ppermute | solution.py:734
  172.6 21.6 %collective-permute-start.32 = (bf16[2,688,256]{2,1,0:T(8,128)(2,1)S(1)}, bf16[2,688,256]{2,1,0:T(8,128)(2,1)S(1)}, u32[]{:S(2)}, u32[]{:S(2)}) collective-permute-start(bf16[2,688,256]{2,1,0:T(8,128)(2,1)S(1)} %collective-permute-done.23.refs_3_.refs_19_), channel_id=1, source_target_pairs={{0,1},{1,0},{2,3},{3,2},{4,5},{5,4},{6,7},{7,6},{8,9},{9,8},{10,11... | collective-permute-start | bytes 2113544 | tf_op jit(solution)/shard_map/ppermute | solution.py:734
  205.4 26.4 %collective-permute-start.33 = (bf16[512,1024]{1,0:T(8,128)(2,1)}, bf16[512,1024]{1,0:T(8,128)(2,1)S(1)}, u32[]{:S(2)}, u32[]{:S(2)}) collective-permute-start(bf16[512,1024]{1,0:T(8,128)(2,1)} %shard_map.174), channel_id=1, source_target_pairs={{0,16},{1,17},{2,18},{3,19},{4,20},{5,21},{6,22},{7,23},{8,24},{9,... | collective-permute-start | bytes 3145736 | tf_op jit(solution)/shard_map/ppermute | solution.py:988
  339.9 36.3 %collective-permute-start.39 = (bf16[512,1408]{1,0:T(8,128)(2,1)}, bf16[512,1408]{1,0:T(8,128)(2,1)S(1)}, u32[]{:S(2)}, u32[]{:S(2)}) collective-permute-start(bf16[512,1408]{1,0:T(8,128)(2,1)} %get-tuple-element.281.zf_ref), channel_id=1, source_target_pairs={{0,1},{1,0},{2,3},{3,2},{4,5},{5,4},{6,7},{7,6},{8,9},{9,8},{10,11... | collective-permute-start | bytes 4325384 | tf_op jit(solution)/shard_map/ppermute | solution.py:734
  340.0 34.3 %collective-permute-start.41 = (bf16[512,1024]{1,0:T(8,128)(2,1)S(1)}, bf16[512,1024]{1,0:T(8,128)(2,1)S(1)}, u32[]{:S(2)}, u32[]{:S(2)}) collective-permute-start(bf16[512,1024]{1,0:T(8,128)(2,1)S(1)} %copy-done.6), channel_id=1, source_target_pairs={{0,1},{1,0},{2,3},{3,2},{4,5},{5,4},{6,7},{7,6},{8,9},{9,8},{10,11... | collective-permute-start | bytes 3145736 | tf_op jit(solution)/shard_map/ppermute | solution.py:734
  340.4 34.8 %collective-permute-start.40 = (bf16[512,1024]{1,0:T(8,128)(2,1)S(1)}, bf16[512,1024]{1,0:T(8,128)(2,1)S(1)}, u32[]{:S(2)}, u32[]{:S(2)}) collective-permute-start(bf16[512,1024]{1,0:T(8,128)(2,1)S(1)} %copy-done.10), channel_id=1, source_target_pairs={{0,1},{1,0},{2,3},{3,2},{4,5},{5,4},{6,7},{7,6},{8,9},{9,8},{10,11... | collective-permute-start | bytes 3145736 | tf_op jit(solution)/shard_map/ppermute | solution.py:734
  362.9 27.4 %collective-permute-start.38 = (bf16[512,1024]{1,0:T(8,128)(2,1)}, bf16[512,1024]{1,0:T(8,128)(2,1)}, u32[]{:S(2)}, u32[]{:S(2)}) collective-permute-start(bf16[512,1024]{1,0:T(8,128)(2,1)} %get-tuple-element.279), channel_id=1, source_target_pairs={{16,0},{17,1},{18,2},{19,3},{20,4},{21,5},{22,6},{23,7},{24,8},{25... | collective-permute-start | bytes 3145736 | tf_op jit(solution)/shard_map/ppermute | solution.py:1007
  364.2 10.2 %collective-permute-start.42 = (bf16[512,512]{1,0:T(8,128)(2,1)S(1)}, bf16[512,512]{1,0:T(8,128)(2,1)S(1)}, u32[]{:S(2)}, u32[]{:S(2)}) collective-permute-start(bf16[512,512]{1,0:T(8,128)(2,1)S(1)} %slice.261), channel_id=1, source_target_pairs={{0,1},{1,0},{2,3},{3,2},{4,5},{5,4},{6,7},{7,6},{8,9},{9,8},{10,11... | collective-permute-start | bytes 1572872 | tf_op jit(solution)/shard_map/ppermute | solution.py:734
  397.7 33.1 %collective-permute-start.44 = (bf16[4,688,256]{2,1,0:T(8,128)(2,1)S(1)}, bf16[4,688,256]{2,1,0:T(8,128)(2,1)}, u32[]{:S(2)}, u32[]{:S(2)}) collective-permute-start(bf16[4,688,256]{2,1,0:T(8,128)(2,1)S(1)} %get-tuple-element.289), channel_id=1, source_target_pairs={{0,2},{1,3},{2,0},{3,1},{4,6},{5,7},{6,4},{7,5},{8,10},{9,11},{10,... | collective-permute-start | bytes 4227080 | tf_op jit(solution)/shard_map/ppermute | solution.py:739
  432.3 12.5 %collective-permute-start.45 = (bf16[688,256]{1,0:T(8,128)(2,1)S(1)}, bf16[688,256]{1,0:T(8,128)(2,1)S(1)}, u32[]{:S(2)}, u32[]{:S(2)}) collective-permute-start(bf16[688,256]{1,0:T(8,128)(2,1)S(1)} %fusion.21), channel_id=1, source_target_pairs={{0,4},{4,8},{8,12},{12,0},{1,5},{5,9},{9,13},{13,1},{2,6},{6,10},{... | collective-permute-start | bytes 1056776 | tf_op jit(solution)/shard_map/ppermute | solution.py:744
  446.6 11.9 %collective-permute-start.49 = (bf16[688,256]{1,0:T(8,128)(2,1)S(1)}, bf16[688,256]{1,0:T(8,128)(2,1)S(1)}, u32[]{:S(2)}, u32[]{:S(2)}) collective-permute-start(bf16[688,256]{1,0:T(8,128)(2,1)S(1)} %fusion.10), channel_id=1, source_target_pairs={{0,4},{4,8},{8,12},{12,0},{1,5},{5,9},{9,13},{13,1},{2,6},{6,10},{... | collective-permute-start | bytes 1056776 | tf_op jit(solution)/shard_map/ppermute | solution.py:744
  446.9 44.9 %collective-permute-start.51 = (bf16[4,688,256]{2,1,0:T(8,128)(2,1)}, bf16[4,688,256]{2,1,0:T(8,128)(2,1)}, u32[]{:S(2)}, u32[]{:S(2)}) collective-permute-start(bf16[4,688,256]{2,1,0:T(8,128)(2,1)} %get-tuple-element.324), channel_id=1, source_target_pairs={{0,2},{1,3},{2,0},{3,1},{4,6},{5,7},{6,4},{7,5},{8,10},{9,11},{10,... | collective-permute-start | bytes 4227080 | tf_op jit(solution)/shard_map/ppermute | solution.py:739
  459.6 32.1 %collective-permute-start.52 = (bf16[688,256]{1,0:T(8,128)(2,1)S(1)}, bf16[688,256]{1,0:T(8,128)(2,1)S(1)}, u32[]{:S(2)}, u32[]{:S(2)}) collective-permute-start(bf16[688,256]{1,0:T(8,128)(2,1)S(1)} %fusion.9), channel_id=1, source_target_pairs={{0,4},{4,8},{8,12},{12,0},{1,5},{5,9},{9,13},{13,1},{2,6},{6,10},{... | collective-permute-start | bytes 1056776 | tf_op jit(solution)/shard_map/ppermute | solution.py:744
  459.8 31.8 %collective-permute-start.53 = (bf16[2,256,256]{2,1,0:T(8,128)(2,1)S(1)}, bf16[2,256,256]{2,1,0:T(8,128)(2,1)S(1)}, u32[]{:S(2)}, u32[]{:S(2)}) collective-permute-start(bf16[2,256,256]{2,1,0:T(8,128)(2,1)S(1)} %pad_maximum_fusion.12), channel_id=1, source_target_pairs={{0,12},{4,0},{8,4},{12,8},{1,13},{5,1},{9,5},{13,9},{2,14},{6,2},{... | collective-permute-start | bytes 786440 | tf_op jit(solution)/shard_map/ppermute | solution.py:767
  463.7 28.0 %collective-permute-start.54 = (bf16[2,256,256]{2,1,0:T(8,128)(2,1)S(1)}, bf16[2,256,256]{2,1,0:T(8,128)(2,1)S(1)}, u32[]{:S(2)}, u32[]{:S(2)}) collective-permute-start(bf16[2,256,256]{2,1,0:T(8,128)(2,1)S(1)} %pad_maximum_fusion.13), channel_id=1, source_target_pairs={{0,8},{4,12},{8,0},{12,4},{1,9},{5,13},{9,1},{13,5},{2,10},{6,14},... | collective-permute-start | bytes 786440 | tf_op jit(solution)/shard_map/ppermute | solution.py:767
  463.8 27.9 %collective-permute-start.55 = (bf16[2,256,256]{2,1,0:T(8,128)(2,1)S(1)}, bf16[2,256,256]{2,1,0:T(8,128)(2,1)S(1)}, u32[]{:S(2)}, u32[]{:S(2)}) collective-permute-start(bf16[2,256,256]{2,1,0:T(8,128)(2,1)S(1)} %pad_maximum_fusion.14), channel_id=1, source_target_pairs={{0,4},{4,8},{8,12},{12,0},{1,5},{5,9},{9,13},{13,1},{2,6},{6,10},{... | collective-permute-start | bytes 786440 | tf_op jit(solution)/shard_map/ppermute | solution.py:767
  492.6 33.6 %collective-permute-start.50 = (bf16[4,688,256]{2,1,0:T(8,128)(2,1)}, bf16[4,688,256]{2,1,0:T(8,128)(2,1)}, u32[]{:S(2)}, u32[]{:S(2)}) collective-permute-start(bf16[4,688,256]{2,1,0:T(8,128)(2,1)} %get-tuple-element.322), channel_id=1, source_target_pairs={{0,2},{1,3},{2,0},{3,1},{4,6},{5,7},{6,4},{7,5},{8,10},{9,11},{10,... | collective-permute-start | bytes 4227080 | tf_op jit(solution)/shard_map/ppermute | solution.py:739
  495.7 30.5 %collective-permute-start.56 = (bf16[688,256]{1,0:T(8,128)(2,1)}, bf16[688,256]{1,0:T(8,128)(2,1)}, u32[]{:S(2)}, u32[]{:S(2)}) collective-permute-start(bf16[688,256]{1,0:T(8,128)(2,1)} %get-tuple-element.409), channel_id=1, source_target_pairs={{0,12},{4,0},{8,4},{12,8},{1,13},{5,1},{9,5},{13,9},{2,14},{6,2},{... | collective-permute-start | bytes 1056776 | tf_op jit(solution)/shard_map/ppermute | solution.py:767
  498.9 32.5 %collective-permute-start.57 = (bf16[688,256]{1,0:T(8,128)(2,1)}, bf16[688,256]{1,0:T(8,128)(2,1)}, u32[]{:S(2)}, u32[]{:S(2)}) collective-permute-start(bf16[688,256]{1,0:T(8,128)(2,1)} %get-tuple-element.408), channel_id=1, source_target_pairs={{0,8},{4,12},{8,0},{12,4},{1,9},{5,13},{9,1},{13,5},{2,10},{6,14},... | collective-permute-start | bytes 1056776 | tf_op jit(solution)/shard_map/ppermute | solution.py:767
  500.0 31.4 %collective-permute-start.58 = (bf16[688,256]{1,0:T(8,128)(2,1)}, bf16[688,256]{1,0:T(8,128)(2,1)}, u32[]{:S(2)}, u32[]{:S(2)}) collective-permute-start(bf16[688,256]{1,0:T(8,128)(2,1)} %get-tuple-element.407), channel_id=1, source_target_pairs={{0,4},{4,8},{8,12},{12,0},{1,5},{5,9},{9,13},{13,1},{2,6},{6,10},{... | collective-permute-start | bytes 1056776 | tf_op jit(solution)/shard_map/ppermute | solution.py:767
  532.1 15.8 %collective-permute-start.62 = (bf16[256,256]{1,0:T(8,128)(2,1)}, bf16[256,256]{1,0:T(8,128)(2,1)}, u32[]{:S(2)}, u32[]{:S(2)}) collective-permute-start(bf16[256,256]{1,0:T(8,128)(2,1)} %fusion.48), channel_id=1, source_target_pairs={{0,2},{1,3},{2,0},{3,1},{4,6},{5,7},{6,4},{7,5},{8,10},{9,11},{10,... | collective-permute-start | bytes 393224 | tf_op jit(solution)/shard_map/ppermute | solution.py:739
  537.6 19.3 %collective-permute-start.61 = (bf16[256,1024]{1,0:T(8,128)(2,1)S(1)}, bf16[256,1024]{1,0:T(8,128)(2,1)S(1)}, u32[]{:S(2)}, u32[]{:S(2)}) collective-permute-start(bf16[256,1024]{1,0:T(8,128)(2,1)S(1)} %slice_select_fusion.1), channel_id=1, source_target_pairs={{0,2},{1,3},{2,0},{3,1},{4,6},{5,7},{6,4},{7,5},{8,10},{9,11},{10,... | collective-permute-start | bytes 1572872 | tf_op jit(solution)/shard_map/ppermute | solution.py:739
  539.6 17.3 %collective-permute-start.66 = (bf16[336,256]{1,0:T(8,128)(2,1)S(1)}, bf16[336,256]{1,0:T(8,128)(2,1)S(1)}, u32[]{:S(2)}, u32[]{:S(2)}) collective-permute-start(bf16[336,256]{1,0:T(8,128)(2,1)S(1)} %get-tuple-element.405), channel_id=1, source_target_pairs={{0,8},{4,12},{8,0},{12,4},{1,9},{5,13},{9,1},{13,5},{2,10},{6,14},... | collective-permute-start | bytes 516104 | tf_op jit(solution)/shard_map/ppermute | solution.py:767
  540.9 16.0 %collective-permute-start.67 = (bf16[336,256]{1,0:T(8,128)(2,1)S(1)}, bf16[336,256]{1,0:T(8,128)(2,1)S(1)}, u32[]{:S(2)}, u32[]{:S(2)}) collective-permute-start(bf16[336,256]{1,0:T(8,128)(2,1)S(1)} %get-tuple-element.404), channel_id=1, source_target_pairs={{0,4},{4,8},{8,12},{12,0},{1,5},{5,9},{9,13},{13,1},{2,6},{6,10},{... | collective-permute-start | bytes 516104 | tf_op jit(solution)/shard_map/ppermute | solution.py:767
  557.0 22.5 %collective-permute-start.68 = (bf16[4,384,256]{2,1,0:T(8,128)(2,1)S(1)}, bf16[4,384,256]{2,1,0:T(8,128)(2,1)S(1)}, u32[]{:S(2)}, u32[]{:S(2)}) collective-permute-start(bf16[4,384,256]{2,1,0:T(8,128)(2,1)S(1)} %get-tuple-element.420), channel_id=1, source_target_pairs={{0,2},{1,3},{2,0},{3,1},{4,6},{5,7},{6,4},{7,5},{8,10},{9,11},{10,... | collective-permute-start | bytes 2359304 | tf_op jit(solution)/shard_map/ppermute | solution.py:739
  559.0 17.8 %collective-permute-start.69 = (f32[3,1024]{1,0:T(4,128)S(1)}, f32[3,1024]{1,0:T(4,128)S(1)}, u32[]{:S(2)}, u32[]{:S(2)}) collective-permute-start(f32[3,1024]{1,0:T(4,128)S(1)} %fusion.65), channel_id=1, source_target_pairs={{0,2},{1,3},{2,0},{3,1},{4,6},{5,7},{6,4},{7,5},{8,10},{9,11},{10,... | collective-permute-start | bytes 36872 | tf_op jit(solution)/shard_map/ppermute | solution.py:739
  561.7 16.8 %collective-permute-start.70 = (bf16[352,256]{1,0:T(8,128)(2,1)S(1)}, bf16[352,256]{1,0:T(8,128)(2,1)S(1)}, u32[]{:S(2)}, u32[]{:S(2)}) collective-permute-start(bf16[352,256]{1,0:T(8,128)(2,1)S(1)} %get-tuple-element.403), channel_id=1, source_target_pairs={{0,12},{4,0},{8,4},{12,8},{1,13},{5,1},{9,5},{13,9},{2,14},{6,2},{... | collective-permute-start | bytes 540680 | tf_op jit(solution)/shard_map/ppermute | solution.py:767
  561.8 17.8 %collective-permute-start.71 = (bf16[352,256]{1,0:T(8,128)(2,1)S(1)}, bf16[352,256]{1,0:T(8,128)(2,1)S(1)}, u32[]{:S(2)}, u32[]{:S(2)}) collective-permute-start(bf16[352,256]{1,0:T(8,128)(2,1)S(1)} %get-tuple-element.402), channel_id=1, source_target_pairs={{0,8},{4,12},{8,0},{12,4},{1,9},{5,13},{9,1},{13,5},{2,10},{6,14},... | collective-permute-start | bytes 540680 | tf_op jit(solution)/shard_map/ppermute | solution.py:767
  563.6 16.0 %collective-permute-start.72 = (bf16[352,256]{1,0:T(8,128)(2,1)S(1)}, bf16[352,256]{1,0:T(8,128)(2,1)S(1)}, u32[]{:S(2)}, u32[]{:S(2)}) collective-permute-start(bf16[352,256]{1,0:T(8,128)(2,1)S(1)} %get-tuple-element.401), channel_id=1, source_target_pairs={{0,4},{4,8},{8,12},{12,0},{1,5},{5,9},{9,13},{13,1},{2,6},{6,10},{... | collective-permute-start | bytes 540680 | tf_op jit(solution)/shard_map/ppermute | solution.py:767
  576.8 18.5 %collective-permute-start.73 = (bf16[4,384,256]{2,1,0:T(8,128)(2,1)S(1)}, bf16[4,384,256]{2,1,0:T(8,128)(2,1)S(1)}, u32[]{:S(2)}, u32[]{:S(2)}) collective-permute-start(bf16[4,384,256]{2,1,0:T(8,128)(2,1)S(1)} %get-tuple-element.421), channel_id=1, source_target_pairs={{0,2},{1,3},{2,0},{3,1},{4,6},{5,7},{6,4},{7,5},{8,10},{9,11},{10,... | collective-permute-start | bytes 2359304 | tf_op jit(solution)/shard_map/ppermute | solution.py:739
  579.7 15.6 %collective-permute-start.75 = (bf16[384,256]{1,0:T(8,128)(2,1)S(1)}, bf16[384,256]{1,0:T(8,128)(2,1)S(1)}, u32[]{:S(2)}, u32[]{:S(2)}) collective-permute-start(bf16[384,256]{1,0:T(8,128)(2,1)S(1)} %get-tuple-element.415), channel_id=1, source_target_pairs={{0,12},{4,0},{8,4},{12,8},{1,13},{5,1},{9,5},{13,9},{2,14},{6,2},{... | collective-permute-start | bytes 589832 | tf_op jit(solution)/shard_map/ppermute | solution.py:767
  579.8 18.8 %collective-permute-start.76 = (bf16[384,256]{1,0:T(8,128)(2,1)S(1)}, bf16[384,256]{1,0:T(8,128)(2,1)S(1)}, u32[]{:S(2)}, u32[]{:S(2)}) collective-permute-start(bf16[384,256]{1,0:T(8,128)(2,1)S(1)} %get-tuple-element.414), channel_id=1, source_target_pairs={{0,8},{4,12},{8,0},{12,4},{1,9},{5,13},{9,1},{13,5},{2,10},{6,14},... | collective-permute-start | bytes 589832 | tf_op jit(solution)/shard_map/ppermute | solution.py:767
  580.9 17.6 %collective-permute-start.77 = (bf16[384,256]{1,0:T(8,128)(2,1)S(1)}, bf16[384,256]{1,0:T(8,128)(2,1)S(1)}, u32[]{:S(2)}, u32[]{:S(2)}) collective-permute-start(bf16[384,256]{1,0:T(8,128)(2,1)S(1)} %get-tuple-element.413), channel_id=1, source_target_pairs={{0,4},{4,8},{8,12},{12,0},{1,5},{5,9},{9,13},{13,1},{2,6},{6,10},{... | collective-permute-start | bytes 589832 | tf_op jit(solution)/shard_map/ppermute | solution.py:767
  599.6 22.2 %collective-permute-start.80 = (bf16[384,256]{1,0:T(8,128)(2,1)}, bf16[384,256]{1,0:T(8,128)(2,1)}, u32[]{:S(2)}, u32[]{:S(2)}) collective-permute-start(bf16[384,256]{1,0:T(8,128)(2,1)} %get-tuple-element.411), channel_id=1, source_target_pairs={{0,4},{4,8},{8,12},{12,0},{1,5},{5,9},{9,13},{13,1},{2,6},{6,10},{... | collective-permute-start | bytes 589832 | tf_op jit(solution)/shard_map/ppermute | solution.py:767
  599.6 22.2 %collective-permute-start.79 = (bf16[384,256]{1,0:T(8,128)(2,1)}, bf16[384,256]{1,0:T(8,128)(2,1)}, u32[]{:S(2)}, u32[]{:S(2)}) collective-permute-start(bf16[384,256]{1,0:T(8,128)(2,1)} %get-tuple-element.412), channel_id=1, source_target_pairs={{0,8},{4,12},{8,0},{12,4},{1,9},{5,13},{9,1},{13,5},{2,10},{6,14},... | collective-permute-start | bytes 589832 | tf_op jit(solution)/shard_map/ppermute | solution.py:767
  600.6 21.2 %collective-permute-start.78 = (bf16[384,256]{1,0:T(8,128)(2,1)}, bf16[384,256]{1,0:T(8,128)(2,1)}, u32[]{:S(2)}, u32[]{:S(2)}) collective-permute-start(bf16[384,256]{1,0:T(8,128)(2,1)} %get-tuple-element.410), channel_id=1, source_target_pairs={{0,12},{4,0},{8,4},{12,8},{1,13},{5,1},{9,5},{13,9},{2,14},{6,2},{... | collective-permute-start | bytes 589832 | tf_op jit(solution)/shard_map/ppermute | solution.py:767
  605.6 14.8 %collective-permute-start.81 = (f32[3,1024]{1,0:T(4,128)S(1)}, f32[3,1024]{1,0:T(4,128)S(1)}, u32[]{:S(2)}, u32[]{:S(2)}) collective-permute-start(f32[3,1024]{1,0:T(4,128)S(1)} %add.411), channel_id=1, source_target_pairs={{0,8},{4,12},{8,0},{12,4},{1,9},{5,13},{9,1},{13,5},{2,10},{6,14},... | collective-permute-start | bytes 36872 | tf_op jit(solution)/shard_map/ppermute | solution.py:1091
  (111 other events, 1287.4 us)

commit v5 on v4

--- a/solution.py
+++ b/solution.py
@@ -86,8 +86,8 @@
     ]
 
 
-def start_all(refs, low, scratch, sems):
-    for t in range(4):
+def start_all(refs, low, scratch, sems, shards=range(4)):
+    for t in shards:
         for copy in copies(refs, low, scratch, sems, t):
             copy.start()
 
@@ -132,7 +132,7 @@
 
     @pl.when(t == 0)
     def _():
-        start_all(weight, 0, w_ref, sems)
+        start_all(weight, 0, w_ref, sems, range(1))
         x = x_ref[...].astype(F32)
         n = (x * row_rms(x) * gain_ref[...]).astype(BF)
         block_store(n_scr, n)
@@ -140,6 +140,11 @@
             n_ref[...] = n
 
     wait_for(weight, 0, w_ref, sems, t)
+
+    @pl.when(t == 0)
+    def _():
+        start_all(weight, 0, w_ref, sems, range(1, 4))
+
     width = q_ref.shape[1]
 
     def project(which):
@@ -284,15 +289,15 @@
     ]
 
 
-def pair_start(refs, parts, scratch, sems):
+def pair_start(refs, parts, scratch, sems, halves=range(2)):
     wide = scratch.shape[2] // parts
     hidden = refs[0].shape[1] // parts
-    for half in range(2):
+    for half in halves:
         for copy in pair_copies(refs, parts, scratch, sems, half):
             copy.start()
     blank = wide - 2 * hidden
     if blank:
-        for half in range(2):
+        for half in halves:
             for r in range(4):
                 for part in range(parts):
                     low = part * wide + 2 * hidden
@@ -338,12 +343,13 @@
     @pl.when(half == 0)
     def _():
         start_all(wo, out_low, wo_ref, wo_sems)
-        pair_start(wgu, 2, wgu_ref, wgu_sems)
+        pair_start(wgu, 2, wgu_ref, wgu_sems, range(1))
         width = wo_ref.shape[2]
         block_store(acc, x_ref[...].astype(F32))
         for s in range(4):
             for copy in copies(wo, out_low, wo_ref, wo_sems, s):
                 copy.wait()
+        pair_start(wgu, 2, wgu_ref, wgu_sems, range(1, 2))
         for r in range(4):
             z = place(zi_ref, r)
             h = acc[z]
@@ -439,13 +445,19 @@
 
     @pl.when(half == 0)
     def _():
-        pair_start(wd, 1, wd_ref, wd_sems)
-        pair_start(wgu, 2, wgu_ref, wgu_sems)
-        start_all(wo, out_low, wo_ref, wo_sems)
+        pair_start(wd, 1, wd_ref, wd_sems, range(1))
         block_store(df_scr, dy_ref[...])
         acc[...] = jnp.zeros_like(acc)
 
     pair_wait(wd, 1, wd_ref, wd_sems, half)
+
+    @pl.when(half == 0)
+    def _():
+        pair_start(wgu, 2, wgu_ref, wgu_sems, range(1))
+        pair_start(wd, 1, wd_ref, wd_sems, range(1, 2))
+        pair_start(wgu, 2, wgu_ref, wgu_sems, range(1, 2))
+        start_all(wo, out_low, wo_ref, wo_sems)
+
     for at in chunks(wide):
         dz = dot_nt(df_scr[place(zi_ref, 0)], wd_ref[0, half, at])
         for r in range(1, 4):
@@ -528,7 +540,7 @@
     add_ref, var_ref, dq_ref, dko_ref, dkx_ref, dvo_ref, dvx_ref, bias_ref,
 ):
     rows = q_ref.shape[0]
-    kb = 256
+    kb = 512
     first = lax.broadcasted_iota(jnp.int32, (1, 128), 1) < HD
     lane = lax.broadcasted_iota(jnp.int32, (1, 128), 1) % HD
     q = q_ref[...].astype(F32)
@@ -955,24 +967,25 @@
     cos, sin, aug_q, aug_k, add_q, add_k, var_q = tab
     tab = (cos, sin, aug_q, aug_k, head_scale, add_q, add_k, var_q)
 
-    q, k, v = qkv_call(False, ends, gain_a, zi, w1, low, cos, sin)
     if near:
-        b1, b2, b3, g0, d0, q, k, v = meet(b1, b2, b3, g0, d0, q, k, v)
+        b1, b2, b3, g0, d0 = meet(b1, b2, b3, g0, d0)
         n3 = [jnp.stack([p3, d0])]
         c1, g1 = ring(n3[0]), y_swap(b1)
         n2 = [jnp.stack([p2, g0])]
         f2 = [core_swap(n2[0])]
         f3 = [core_swap(n3[0])]
+    q, k, v = qkv_call(False, ends, gain_a, zi, w1, low, cos, sin)
+    if near:
+        b2, b3, c1, g1, q, k, v = meet(b2, b3, c1, g1, q, k, v)
+        c2, g2 = ring(c1), y_swap(b2)
     k_oth, v_oth = core_swap(k), core_swap(v)
     o, _ = attend_part(scale, (q, k, v, k_oth, v_oth), tab)
     if near:
-        b2, b3, c1, g1, o = meet(b2, b3, c1, g1, o)
-        c2, g2 = ring(c1), y_swap(b2)
+        b3, c1, g1, c2, g2, o = meet(b3, c1, g1, c2, g2, o)
+        c3, g3 = ring(c2), y_swap(b3)
         n2.append(jnp.stack([b1, g1]))
         f2.append(core_swap(n2[1]))
         f3.append(core_swap(c1))
-        b3, c2, g2 = meet(b3, c2, g2)
-        c3, g3 = ring(c2), y_swap(b3)
         n2.append(jnp.stack([b2, g2]))
         f2.append(core_swap(n2[2]))
         f3.append(core_swap(c2))
@@ -1004,9 +1017,10 @@
         scale, None, q, k, k_oth, v, v_oth, do, o, sums, aug_q, aug_k, head_scale, add_k, var_q
     )
     dx_low = qkv_back(dq, dk, core_swap(dk_send), dv, core_swap(dv_send), dh)[3]
+    dx_low, z_far, n1_far, n2_far, o_far = meet(dx_low, z_far, n1, n2, o[:, 2 * width :])
     got = lax.ppermute(dx_low, "section", [(1, 0)])
-    z_oth, n2_oth, n1_oth = core_swap(z_far), core_swap(n2), core_swap(n1)
-    o_oth = core_swap(o[:, 2 * width :])
+    z_oth, n2_oth, n1_oth = core_swap(z_far), core_swap(n2_far), core_swap(n1_far)
+    o_oth = core_swap(o_far)
 
     got, y, z_oth, n2_oth, n1_oth, o_oth = meet(got, y, z_oth, n2_oth, n1_oth, o_oth)
 

time: 633 us -> 626 us (0.989)
  Pallas kernels: 271 us -> 262 us
    ppermute x12, waiting for transfers between devices: 58.3 us -> 51.8 us  [ring(): return lax.ppermute(value, 'dp', [(i, (i + 1) % n) for i in range(n)])]
    ppermute x18, waiting for transfers between devices: 60.8 us -> 67.4 us  [y_swap(): return lax.ppermute(value, 'tensor', [(i, i ^ 2) for i in range(n)])]
  transfers between devices with their start and end apart: 82 -> 82, of which waited for: 29 -> 31; matrix products, arithmetic and copies ran while one was open for 8% -> 8% of each run, Pallas kernels for 25% -> 22%
where the time goes in v5:
time: 626 us; the launch traced here: 618 us
  Pallas kernels  262 us (42%)
  waiting for transfers between devices  205 us (33%)
  starting transfers between devices  70.3 us (11%)
  other arithmetic  51.6 us (8%)
  local copies, waits for them, and re-layouts  26.4 us (4%)
    ppermute x18, waiting for transfers between devices, y_swap(): return lax.ppermute(value, 'tensor', [(i, i ^ 2) for i in range(n)])  67.4 us
    pallas_call x2, Pallas kernels, attend_back_call(): pl.pallas_call(functools.partial(attend_back_kernel, scale), grid=(pairs,...  53.3 us
    ppermute x12, waiting for transfers between devices, ring(): return lax.ppermute(value, 'dp', [(i, (i + 1) % n) for i in range(n)])  51.8 us
    pallas_call x2, Pallas kernels, ffn_back_call(): pl.pallas_call(functools.partial(ffn_back_kernel, out_low), grid=(2,), in...  50.5 us
    pallas_call x2, Pallas kernels, ffn_up_call(): pl.pallas_call(functools.partial(ffn_up_kernel, save, out_low), grid=(2,)...  34.9 us
    pallas_call x2, Pallas kernels, qkv_back_call(): pl.pallas_call(qkv_back_kernel, grid=(4,), in_specs=[col] * 7 + [whole((r...  33 us
    pallas_call x2, Pallas kernels, attend_call(): pl.pallas_call(functools.partial(attend_kernel, scale), grid=(pairs,), in...  30.4 us
    ppermute x18, starting transfers between devices, to_owner(): return lax.ppermute(part, 'dp', [(i, (i - r) % n) for i in range(n)])  23.4 us
  transfers between devices with their start and end apart: 82, of which 31 were waited for; matrix products, arithmetic and copies ran while one was open for 8% of the time, Pallas kernels for 22%

profile of v5, /device:TPU:0, one launch (start us, length us, event | category | flops | bytes accessed | tf_op | source)
XLA Modules:
  0.0 617.7 jit_solution(593600293355033894)
XLA Ops:
  4.3 3.1 collective-permute-start
  7.4 2.5 fusion.14
  16.2 7.3 %collective-permute-done.1 = bf16[256,1024]{1,0:T(8,128)(2,1)S(1)} collective-permute-done((bf16[256,1024]{1,0:T(8,128)(2,1)}, bf16[256,1024]{1,0:T(8,128)(2,1)S(1)}, u32[]{:S(2)}, u32[]{:S(2)}) %collective-permute-start.1) | collective-permute-done | bytes 524320 | tf_op jit(solution)/shard_map/ppermute | solution.py:751
  30.4 8.3 %collective-permute-done.2 = bf16[1040,256]{1,0:T(8,128)(2,1)S(1)} collective-permute-done((bf16[1040,256]{1,0:T(8,128)(2,1)S(1)}, bf16[1040,256]{1,0:T(8,128)(2,1)S(1)}, u32[]{:S(2)}, u32[]{:S(2)}) %collective-permute-start.2) | collective-permute-done | bytes 532512 | tf_op jit(solution)/shard_map/ppermute | solution.py:756
  41.3 2.7 maximum_select_fusion.1.x_ref.dy_ref
  44.0 8.4 %collective-permute-done.4 = bf16[1040,256]{1,0:T(8,128)(2,1)} collective-permute-done((bf16[1040,256]{1,0:T(8,128)(2,1)S(1)}, bf16[1040,256]{1,0:T(8,128)(2,1)}, u32[]{:S(2)}, u32[]{:S(2)}) %collective-permute-start.4) | collective-permute-done | bytes 532512 | tf_op jit(solution)/shard_map/ppermute | solution.py:756
  54.6 16.8 %collective-permute-done.8 = bf16[688,256]{1,0:T(8,128)(2,1)S(1)} collective-permute-done((bf16[688,256]{1,0:T(8,128)(2,1)S(1)}, bf16[688,256]{1,0:T(8,128)(2,1)S(1)}, u32[]{:S(2)}, u32[]{:S(2)}) %collective-permute-start.8) | collective-permute-done | bytes 352288 | tf_op jit(solution)/shard_map/ppermute | solution.py:751
  74.5 7.8 %collective-permute-done.10 = bf16[1040,256]{1,0:T(8,128)(2,1)} collective-permute-done((bf16[1040,256]{1,0:T(8,128)(2,1)}, bf16[1040,256]{1,0:T(8,128)(2,1)}, u32[]{:S(2)}, u32[]{:S(2)}) %collective-permute-start.10) | collective-permute-done | bytes 532512 | tf_op jit(solution)/shard_map/ppermute | solution.py:751
  82.3 5.6 collective-permute-done.9
  92.2 2.3 pad_maximum_fusion.7.refs_3_
  94.5 7.4 %collective-permute-done.11 = bf16[1376,256]{1,0:T(8,128)(2,1)S(1)} collective-permute-done((bf16[1376,256]{1,0:T(8,128)(2,1)}, bf16[1376,256]{1,0:T(8,128)(2,1)S(1)}, u32[]{:S(2)}, u32[]{:S(2)}) %collective-permute-start.11) | collective-permute-done | bytes 704544 | tf_op jit(solution)/shard_map/ppermute | solution.py:756
  104.0 5.0 collective-permute-done.12
  110.0 2.1 collective-permute-start.13
  114.3 10.7 %shard_map.171 = (bf16[512,1024]{1,0:T(8,128)(2,1)}, bf16[512,1024]{1,0:T(8,128)(2,1)}, bf16[512,1024]{1,0:T(8,128)(2,1)}) custom-call(bf16[512,1024]{1,0:T(8,128)(2,1)} %maximum_select_fusion.1.x_ref.dy_ref, f32[1,1024]{1,0:T(1,128)} %bitcast.184, s32[1]{0:T(128)} %bitcast.27.zi_ref, f32[512,128]{1,0:T(8,128)} %pad_maximum_fusion.10.cos_ref, ...), custom_call_target="tpu_custom_call" | custom-call | flops 3221225472 | bytes 14680064 | tf_op jit(solution)/shard_map/pallas_call | solution.py:180
  125.0 4.2 collective-permute-done.13.refs_1_.refs_17_
  130.8 2.2 collective-permute-start.19
  135.5 15.2 %shard_map.172 = (bf16[512,1024]{1,0:T(8,128)(2,1)}, f32[512,1024]{1,0:T(8,128)}) custom-call(bf16[512,1024]{1,0:T(8,128)(2,1)} %get-tuple-element.249.q_ref, bf16[512,1024]{1,0:T(8,128)(2,1)} %get-tuple-element.250.ko_ref, bf16[512,1024]{1,0:T(8,128)(2,1)} %collective-permute-done.21.kx_ref, bf16[512,1024]{1,0:T(8,128)(2,1)} %get-tuple-element.251.vo_ref, ...), custom_call_target="tpu_custom_call" | custom-call | flops 4294967296 | bytes 10485760 | tf_op jit(solution)/shard_map/pallas_call | solution.py:243
  156.0 1.7 pad_maximum_fusion.2.refs_10_
  157.8 12.4 %collective-permute-done.23.refs_3_.refs_19_ = bf16[2,688,256]{2,1,0:T(8,128)(2,1)S(1)} collective-permute-done((bf16[2,688,256]{2,1,0:T(8,128)(2,1)S(1)}, bf16[2,688,256]{2,1,0:T(8,128)(2,1)S(1)}, u32[]{:S(2)}, u32[]{:S(2)}) %collective-permute-start.23) | collective-permute-done | bytes 704544 | tf_op jit(solution)/shard_map/ppermute | solution.py:756
  174.7 16.8 %shard_map.173 = (f32[512,1024]{1,0:T(8,128)}, bf16[512,1408]{1,0:T(8,128)(2,1)}, bf16[512,1408]{1,0:T(8,128)(2,1)}) custom-call(bf16[512,1024]{1,0:T(8,128)(2,1)} %maximum_select_fusion.1.x_ref.dy_ref, bf16[512,1024]{1,0:T(8,128)(2,1)} %get-tuple-element.256.o_ref, f32[1,1024]{1,0:T(1,128)} %bitcast.198, s32[1]{0:T(128)} %bitcast.27.zi_ref, ...), custom_call_target="tpu_custom_call" | custom-call | flops 6845104128 | bytes 21757952 | tf_op jit(solution)/shard_map/pallas_call | solution.py:394
  193.2 9.6 %shard_map.174 = bf16[512,1024]{1,0:T(8,128)(2,1)} custom-call(f32[512,1024]{1,0:T(8,128)} %get-tuple-element.264.h_ref, bf16[512,1408]{1,0:T(8,128)(2,1)} %get-tuple-element.265.zn_ref, bf16[512,1408]{1,0:T(8,128)(2,1)} %get-tuple-element.266.zf_ref, s32[1]{0:T(128)} %bitcast.27.zi_ref, bf16[2,688,256]{2,1,0:T(8,128)(2,1)} %copy-done.26, ...), custom_call_target="tpu_custom_call" | custom-call | flops 2885681152 | bytes 9830400 | tf_op jit(solution)/shard_map/pallas_call | solution.py:428
  202.8 3.6 collective-permute-start.33
  206.4 22.8 %collective-permute-done.33 = bf16[512,1024]{1,0:T(8,128)(2,1)S(1)} collective-permute-done((bf16[512,1024]{1,0:T(8,128)(2,1)}, bf16[512,1024]{1,0:T(8,128)(2,1)S(1)}, u32[]{:S(2)}, u32[]{:S(2)}) %collective-permute-start.33) | collective-permute-done | bytes 1048608 | tf_op jit(solution)/shard_map/ppermute | solution.py:1001
  230.3 11.1 %shard_map.175 = (bf16[512,1024]{1,0:T(8,128)(2,1)}, bf16[512,1024]{1,0:T(8,128)(2,1)}, bf16[512,1024]{1,0:T(8,128)(2,1)}, bf16[512,1024]{1,0:T(8,128)(2,1)}, bf...) custom-call(bf16[512,1024]{1,0:T(8,128)(2,1)} %broadcast_select_fusion.2.x_ref, f32[1,1024]{1,0:T(1,128)} %bitcast.185, ...), custom_call_target="tpu_custom_call" | custom-call | flops 3221225472 | bytes 14680064 | tf_op jit(solution)/shard_map/pallas_call | solution.py:180
  242.0 2.4 collective-permute-done.34.kx_ref
  246.8 15.1 %shard_map.176 = (bf16[512,1024]{1,0:T(8,128)(2,1)}, f32[512,1024]{1,0:T(8,128)}) custom-call(bf16[512,1024]{1,0:T(8,128)(2,1)} %get-tuple-element.269.q_ref, bf16[512,1024]{1,0:T(8,128)(2,1)} %get-tuple-element.270.ko_ref, bf16[512,1024]{1,0:T(8,128)(2,1)} %copy-done.91, bf16[512,1024]{1,0:T(8,128)(2,1)} %get-tuple-element.271.vo_ref, ...), custom_call_target="tpu_custom_call" | custom-call | flops 4294967296 | bytes 10485760 | tf_op jit(solution)/shard_map/pallas_call | solution.py:243
  262.0 18.1 %shard_map.177 = (f32[512,1024]{1,0:T(8,128)}, bf16[512,1408]{1,0:T(8,128)(2,1)}, bf16[512,1408]{1,0:T(8,128)(2,1)}, bf16[512,1024]{1,0:T(8,128)(2,1)}, bf16[2,5...) custom-call(bf16[512,1024]{1,0:T(8,128)(2,1)} %broadcast_select_fusion.2.x_ref, ...), custom_call_target="tpu_custom_call" | custom-call | flops 6845104128 | bytes 21757952 | tf_op jit(solution)/shard_map/pallas_call | solution.py:394
  280.1 25.3 %shard_map.178 = (f32[512,1024]{1,0:T(8,128)}, bf16[512,1024]{1,0:T(8,128)(2,1)}, bf16[512,1024]{1,0:T(8,128)(2,1)}, bf16[512,1408]{1,0:T(8,128)(2,1)}, bf16[512...) custom-call(bf16[512,1024]{1,0:T(8,128)(2,1)} %maximum_select_fusion.1.x_ref.dy_re, ...), custom_call_target="tpu_custom_call" | custom-call | flops 9730785280 | bytes 27394048 | tf_op jit(solution)/shard_map/pallas_call | solution.py:512
  305.4 26.7 %shard_map.179 = (bf16[512,1024]{1,0:T(8,128)(2,1)}, bf16[512,1024]{1,0:T(8,128)(2,1)}, bf16[512,1024]{1,0:T(8,128)(2,1)}, bf16[512,1024]{1,0:T(8,128)(2,1)}, bf...) custom-call(bf16[512,1024]{1,0:T(8,128)(2,1)} %get-tuple-element.269.q_ref, bf16[512,1024]{1,0:T(8,128)(2,1)} %get-tuple-element.270.ko_ref, ...), custom_call_target="tpu_custom_call" | custom-call | flops 10737418240 | bytes 20971520 | tf_op jit(solution)/shard_map/pallas_call | solution.py:614
  332.7 2.3 collective-permute-done.36.dkr_ref
  337.5 16.8 %shard_map.180 = (bf16[2,512,768]{2,1,0:T(8,128)(2,1)}, bf16[2,512,768]{2,1,0:T(8,128)(2,1)}, f32[512,1024]{1,0:T(8,128)}, bf16[512,1024]{1,0:T(8,128)(2,1)}, f32[1,1024]{1,0:T(1,128)}) custom-call(bf16[512,1024]{1,0:T(8,128)(2,1)} %get-tuple-element.280.dq_ref, bf16[512,1024]{1,0:T(8,128)(2,1)} %get-tuple-element.281.dk_ref, bf16[512,1024]{1,0:T(8,128)(2,1)} %copy-done.45, ...), custom_call_target="tpu_custom_call" | custom-call | flops 3221225472 | bytes 27262976 | tf_op jit(solution)/shard_map/pallas_call | solution.py:697
  356.7 9.9 %shard_map.181 = f32[512,1024]{1,0:T(8,128)} custom-call(f32[512,1024]{1,0:T(8,128)} %get-tuple-element.273.h_ref, bf16[512,1408]{1,0:T(8,128)(2,1)} %get-tuple-element.293.zn_ref.ao_ref, bf16[512,1408]{1,0:T(8,128)(2,1)} %get-tuple-element.294.zf_ref, s32[1]{0:T(128)} %bitcast.27.zi_ref, bf16[2,688,256]{2,1,0:T(8,128)(2,1)} %copy-done.26, ...), custom_call_target="tpu_custom_call" | custom-call | flops 2885681152 | bytes 9830400 | tf_op jit(solution)/shard_map/pallas_call | solution.py:428
  367.5 14.6 %collective-permute-done.38 = bf16[512,1024]{1,0:T(8,128)(2,1)} collective-permute-done((bf16[512,1024]{1,0:T(8,128)(2,1)}, bf16[512,1024]{1,0:T(8,128)(2,1)}, u32[]{:S(2)}, u32[]{:S(2)}) %collective-permute-start.38) | collective-permute-done | bytes 1048608 | tf_op jit(solution)/shard_map/ppermute | solution.py:1021
  385.0 2.6 collective-permute-done.43.bx_ref
  387.6 3.2 shard_map.182
  391.6 25.2 %shard_map.183 = (f32[512,1024]{1,0:T(8,128)}, bf16[512,1024]{1,0:T(8,128)(2,1)}, bf16[512,1024]{1,0:T(8,128)(2,1)}, bf16[512,1408]{1,0:T(8,128)(2,1)}, bf16[512...) custom-call(bf16[512,1024]{1,0:T(8,128)(2,1)} %copy-done.3, ...), custom_call_target="tpu_custom_call" | custom-call | flops 9730785280 | bytes 27394048 | tf_op jit(solution)/shard_map/pallas_call | solution.py:512
  416.8 7.2 %collective-permute-done.44 = bf16[4,688,256]{2,1,0:T(8,128)(2,1)} collective-permute-done((bf16[4,688,256]{2,1,0:T(8,128)(2,1)S(1)}, bf16[4,688,256]{2,1,0:T(8,128)(2,1)}, u32[]{:S(2)}, u32[]{:S(2)}) %collective-permute-start.44) | collective-permute-done | bytes 1409056 | tf_op jit(solution)/shard_map/ppermute | solution.py:751
  425.6 5.3 collective-permute-done.48.bx_ref
  433.6 4.3 shard_map.184
  438.1 1.7 fusion.10
  442.2 4.3 shard_map.186
  446.5 5.3 collective-permute-done.49
  453.0 3.9 collective-permute-start.53
  457.7 26.6 %shard_map.187 = (bf16[512,1024]{1,0:T(8,128)(2,1)}, bf16[512,1024]{1,0:T(8,128)(2,1)}, bf16[512,1024]{1,0:T(8,128)(2,1)}, bf16[512,1024]{1,0:T(8,128)(2,1)}, bf...) custom-call(bf16[512,1024]{1,0:T(8,128)(2,1)} %get-tuple-element.269.q_ref, bf16[512,1024]{1,0:T(8,128)(2,1)} %get-tuple-element.270.ko_ref, ...), custom_call_target="tpu_custom_call" | custom-call | flops 10737418240 | bytes 20971520 | tf_op jit(solution)/shard_map/pallas_call | solution.py:614
  486.1 2.3 fusion.26
  488.4 3.3 collective-permute-start.56
  493.7 16.2 %shard_map.188 = (bf16[2,512,768]{2,1,0:T(8,128)(2,1)}, bf16[2,512,768]{2,1,0:T(8,128)(2,1)}, f32[512,1024]{1,0:T(8,128)}, bf16[512,1024]{1,0:T(8,128)(2,1)}, f32[1,1024]{1,0:T(1,128)}) custom-call(bf16[512,1024]{1,0:T(8,128)(2,1)} %get-tuple-element.350.dq_ref, bf16[512,1024]{1,0:T(8,128)(2,1)} %get-tuple-element.351.dk_ref, bf16[512,1024]{1,0:T(8,128)(2,1)} %copy-done.44, ...), custom_call_target="tpu_custom_call" | custom-call | flops 3221225472 | bytes 27262976 | tf_op jit(solution)/shard_map/pallas_call | solution.py:697
  509.9 8.9 %collective-permute-done.50 = bf16[4,688,256]{2,1,0:T(8,128)(2,1)} collective-permute-done((bf16[4,688,256]{2,1,0:T(8,128)(2,1)}, bf16[4,688,256]{2,1,0:T(8,128)(2,1)}, u32[]{:S(2)}, u32[]{:S(2)}) %collective-permute-start.50) | collective-permute-done | bytes 1409056 | tf_op jit(solution)/shard_map/ppermute | solution.py:751
  518.8 5.3 collective-permute-done.57
  528.0 2.1 convert_select_fusion
  533.7 2.0 collective-permute-start.67
  535.7 5.0 shard_map.189
  540.7 8.9 %collective-permute-done.66 = bf16[336,256]{1,0:T(8,128)(2,1)S(1)} collective-permute-done((bf16[336,256]{1,0:T(8,128)(2,1)S(1)}, bf16[336,256]{1,0:T(8,128)(2,1)S(1)}, u32[]{:S(2)}, u32[]{:S(2)}) %collective-permute-start.66) | collective-permute-done | bytes 172064 | tf_op jit(solution)/shard_map/ppermute | solution.py:779
  554.4 1.8 collective-permute-start.71
  556.2 1.9 collective-permute-start.72
  558.1 11.4 %collective-permute-done.69 = f32[3,1024]{1,0:T(4,128)S(1)} collective-permute-done((f32[3,1024]{1,0:T(4,128)S(1)}, f32[3,1024]{1,0:T(4,128)S(1)}, u32[]{:S(2)}, u32[]{:S(2)}) %collective-permute-start.69) | collective-permute-done | bytes 12320 | tf_op jit(solution)/shard_map/ppermute | solution.py:751
  573.6 1.9 collective-permute-start.77
  577.6 7.4 %collective-permute-done.74 = f32[3,1024]{1,0:T(4,128)S(1)} collective-permute-done((f32[3,1024]{1,0:T(4,128)S(1)}, f32[3,1024]{1,0:T(4,128)S(1)}, u32[]{:S(2)}, u32[]{:S(2)}) %collective-permute-start.74) | collective-permute-done | bytes 12320 | tf_op jit(solution)/shard_map/ppermute | solution.py:1098
  585.0 3.0 collective-permute-done.73
  588.1 3.2 collective-permute-done.76
  593.2 2.9 collective-permute-start.78
  596.1 2.1 fusion.5
  598.2 2.0 collective-permute-start.81
  607.0 6.0 collective-permute-done.81
  (424 shorter events, 106.9 us)
Async XLA Ops:
  4.3 19.2 %collective-permute-start = (bf16[1040,256]{1,0:T(8,128)(2,1)S(1)}, bf16[1040,256]{1,0:T(8,128)(2,1)S(1)}, u32[]{:S(2)}, u32[]{:S(2)}) collective-permute-start(bf16[1040,256]{1,0:T(8,128)(2,1)S(1)} %fusion.12), channel_id=1, source_target_pairs={{0,4},{4,8},{8,12},{12,0},{1,5},{5,9},{9,13},{13,1},{2,6},{6,10},{... | collective-permute-start | bytes 1597448 | tf_op jit(solution)/shard_map/ppermute | solution.py:756
  9.9 13.6 %collective-permute-start.1 = (bf16[256,1024]{1,0:T(8,128)(2,1)}, bf16[256,1024]{1,0:T(8,128)(2,1)S(1)}, u32[]{:S(2)}, u32[]{:S(2)}) collective-permute-start(bf16[256,1024]{1,0:T(8,128)(2,1)} %get-tuple-element.431), channel_id=1, source_target_pairs={{0,2},{1,3},{2,0},{3,1},{4,6},{5,7},{6,4},{7,5},{8,10},{9,11},{10,... | collective-permute-start | bytes 1572872 | tf_op jit(solution)/shard_map/ppermute | solution.py:751
  24.3 14.4 %collective-permute-start.2 = (bf16[1040,256]{1,0:T(8,128)(2,1)S(1)}, bf16[1040,256]{1,0:T(8,128)(2,1)S(1)}, u32[]{:S(2)}, u32[]{:S(2)}) collective-permute-start(bf16[1040,256]{1,0:T(8,128)(2,1)S(1)} %collective-permute-done), channel_id=1, source_target_pairs={{0,4},{4,8},{8,12},{12,0},{1,5},{5,9},{9,13},{13,1},{2,6},{6,10},{... | collective-permute-start | bytes 1597448 | tf_op jit(solution)/shard_map/ppermute | solution.py:756
  25.9 12.9 %collective-permute-start.3 = (bf16[1040,256]{1,0:T(8,128)(2,1)S(1)}, bf16[1040,256]{1,0:T(8,128)(2,1)S(1)}, u32[]{:S(2)}, u32[]{:S(2)}) collective-permute-start(bf16[1040,256]{1,0:T(8,128)(2,1)S(1)} %fusion.12), channel_id=1, source_target_pairs={{0,2},{1,3},{2,0},{3,1},{4,6},{5,7},{6,4},{7,5},{8,10},{9,11},{10,... | collective-permute-start | bytes 1597448 | tf_op jit(solution)/shard_map/ppermute | solution.py:751
  38.7 13.7 %collective-permute-start.4 = (bf16[1040,256]{1,0:T(8,128)(2,1)S(1)}, bf16[1040,256]{1,0:T(8,128)(2,1)}, u32[]{:S(2)}, u32[]{:S(2)}) collective-permute-start(bf16[1040,256]{1,0:T(8,128)(2,1)S(1)} %collective-permute-done.2), channel_id=1, source_target_pairs={{0,4},{4,8},{8,12},{12,0},{1,5},{5,9},{9,13},{13,1},{2,6},{6,10},{... | collective-permute-start | bytes 1597448 | tf_op jit(solution)/shard_map/ppermute | solution.py:756
  39.8 12.6 %collective-permute-start.5 = (bf16[1040,256]{1,0:T(8,128)(2,1)S(1)}, bf16[1040,256]{1,0:T(8,128)(2,1)}, u32[]{:S(2)}, u32[]{:S(2)}) collective-permute-start(bf16[1040,256]{1,0:T(8,128)(2,1)S(1)} %collective-permute-done), channel_id=1, source_target_pairs={{0,2},{1,3},{2,0},{3,1},{4,6},{5,7},{6,4},{7,5},{8,10},{9,11},{10,... | collective-permute-start | bytes 1597448 | tf_op jit(solution)/shard_map/ppermute | solution.py:751
  52.4 19.0 %collective-permute-start.6 = (bf16[1376,256]{1,0:T(8,128)(2,1)}, bf16[1376,256]{1,0:T(8,128)(2,1)S(1)}, u32[]{:S(2)}, u32[]{:S(2)}) collective-permute-start(bf16[1376,256]{1,0:T(8,128)(2,1)} %bitcast.8), channel_id=1, source_target_pairs={{0,4},{4,8},{8,12},{12,0},{1,5},{5,9},{9,13},{13,1},{2,6},{6,10},{... | collective-permute-start | bytes 2113544 | tf_op jit(solution)/shard_map/ppermute | solution.py:756
  52.5 18.9 %collective-permute-start.7 = (bf16[1040,256]{1,0:T(8,128)(2,1)S(1)}, bf16[1040,256]{1,0:T(8,128)(2,1)S(1)}, u32[]{:S(2)}, u32[]{:S(2)}) collective-permute-start(bf16[1040,256]{1,0:T(8,128)(2,1)S(1)} %collective-permute-done.2), channel_id=1, source_target_pairs={{0,2},{1,3},{2,0},{3,1},{4,6},{5,7},{6,4},{7,5},{8,10},{9,11},{10,... | collective-permute-start | bytes 1597448 | tf_op jit(solution)/shard_map/ppermute | solution.py:751
  54.0 17.5 %collective-permute-start.8 = (bf16[688,256]{1,0:T(8,128)(2,1)S(1)}, bf16[688,256]{1,0:T(8,128)(2,1)S(1)}, u32[]{:S(2)}, u32[]{:S(2)}) collective-permute-start(bf16[688,256]{1,0:T(8,128)(2,1)S(1)} %bitcast.181), channel_id=1, source_target_pairs={{0,2},{1,3},{2,0},{3,1},{4,6},{5,7},{6,4},{7,5},{8,10},{9,11},{10,... | collective-permute-start | bytes 1056776 | tf_op jit(solution)/shard_map/ppermute | solution.py:751
  72.1 15.7 %collective-permute-start.9 = (bf16[1376,256]{1,0:T(8,128)(2,1)S(1)}, bf16[1376,256]{1,0:T(8,128)(2,1)}, u32[]{:S(2)}, u32[]{:S(2)}) collective-permute-start(bf16[1376,256]{1,0:T(8,128)(2,1)S(1)} %collective-permute-done.6), channel_id=1, source_target_pairs={{0,4},{4,8},{8,12},{12,0},{1,5},{5,9},{9,13},{13,1},{2,6},{6,10},{... | collective-permute-start | bytes 2113544 | tf_op jit(solution)/shard_map/ppermute | solution.py:756
  74.4 37.8 %collective-permute-start.15 = (bf16[2,1040,256]{2,1,0:T(8,128)(2,1)S(1)}, bf16[2,1040,256]{2,1,0:T(8,128)(2,1)}, u32[]{:S(2)}, u32[]{:S(2)}) collective-permute-start(bf16[2,1040,256]{2,1,0:T(8,128)(2,1)S(1)} %pad_maximum_fusion.4.refs_0_), channel_id=1, source_target_pairs={{0,1},{1,0},{2,3},{3,2},{4,5},{5,4},{6,7},{7,6},{8,9},{9,8},{10,11... | collective-permute-start | bytes 3194888 | tf_op jit(solution)/shard_map/ppermute | solution.py:746
  87.9 14.0 %collective-permute-start.11 = (bf16[1376,256]{1,0:T(8,128)(2,1)}, bf16[1376,256]{1,0:T(8,128)(2,1)S(1)}, u32[]{:S(2)}, u32[]{:S(2)}) collective-permute-start(bf16[1376,256]{1,0:T(8,128)(2,1)} %collective-permute-done.9), channel_id=1, source_target_pairs={{0,4},{4,8},{8,12},{12,0},{1,5},{5,9},{9,13},{13,1},{2,6},{6,10},{... | collective-permute-start | bytes 2113544 | tf_op jit(solution)/shard_map/ppermute | solution.py:756
  89.0 25.2 %collective-permute-start.16 = (bf16[2,1040,256]{2,1,0:T(8,128)(2,1)S(1)}, bf16[2,1040,256]{2,1,0:T(8,128)(2,1)}, u32[]{:S(2)}, u32[]{:S(2)}) collective-permute-start(bf16[2,1040,256]{2,1,0:T(8,128)(2,1)S(1)} %pad_maximum_fusion.5.refs_1_), channel_id=1, source_target_pairs={{0,1},{1,0},{2,3},{3,2},{4,5},{5,4},{6,7},{7,6},{8,9},{9,8},{10,11... | collective-permute-start | bytes 3194888 | tf_op jit(solution)/shard_map/ppermute | solution.py:746
  90.4 23.8 %collective-permute-start.17 = (bf16[2,1040,256]{2,1,0:T(8,128)(2,1)}, bf16[2,1040,256]{2,1,0:T(8,128)(2,1)}, u32[]{:S(2)}, u32[]{:S(2)}) collective-permute-start(bf16[2,1040,256]{2,1,0:T(8,128)(2,1)} %pad_maximum_fusion.6.refs_2_), channel_id=1, source_target_pairs={{0,1},{1,0},{2,3},{3,2},{4,5},{5,4},{6,7},{7,6},{8,9},{9,8},{10,11... | collective-permute-start | bytes 3194888 | tf_op jit(solution)/shard_map/ppermute | solution.py:746
  90.8 18.2 %collective-permute-start.12 = (bf16[1376,256]{1,0:T(8,128)(2,1)}, bf16[1376,256]{1,0:T(8,128)(2,1)}, u32[]{:S(2)}, u32[]{:S(2)}) collective-permute-start(bf16[1376,256]{1,0:T(8,128)(2,1)} %bitcast.8), channel_id=1, source_target_pairs={{0,2},{1,3},{2,0},{3,1},{4,6},{5,7},{6,4},{7,5},{8,10},{9,11},{10,... | collective-permute-start | bytes 2113544 | tf_op jit(solution)/shard_map/ppermute | solution.py:751
  101.9 12.4 %collective-permute-start.18 = (bf16[2,1040,256]{2,1,0:T(8,128)(2,1)}, bf16[2,1040,256]{2,1,0:T(8,128)(2,1)}, u32[]{:S(2)}, u32[]{:S(2)}) collective-permute-start(bf16[2,1040,256]{2,1,0:T(8,128)(2,1)} %pad_maximum_fusion.7.refs_3_), channel_id=1, source_target_pairs={{0,1},{1,0},{2,3},{3,2},{4,5},{5,4},{6,7},{7,6},{8,9},{9,8},{10,11... | collective-permute-start | bytes 3194888 | tf_op jit(solution)/shard_map/ppermute | solution.py:746
  110.0 19.2 %collective-permute-start.13 = (bf16[2,688,256]{2,1,0:T(8,128)(2,1)S(1)}, bf16[2,688,256]{2,1,0:T(8,128)(2,1)S(1)}, u32[]{:S(2)}, u32[]{:S(2)}) collective-permute-start(bf16[2,688,256]{2,1,0:T(8,128)(2,1)S(1)} %pad_maximum_fusion.9.refs_0_.refs_16_), channel_id=1, source_target_pairs={{0,4},{4,8},{8,12},{12,0},{1,5},{5,9},{9,13},{13,1},{2,6},{6,10},{... | collective-permute-start | bytes 2113544 | tf_op jit(solution)/shard_map/ppermute | solution.py:756
  112.2 17.0 %collective-permute-start.14 = (bf16[1376,256]{1,0:T(8,128)(2,1)}, bf16[1376,256]{1,0:T(8,128)(2,1)S(1)}, u32[]{:S(2)}, u32[]{:S(2)}) collective-permute-start(bf16[1376,256]{1,0:T(8,128)(2,1)} %copy-done.49), channel_id=1, source_target_pairs={{0,2},{1,3},{2,0},{3,1},{4,6},{5,7},{6,4},{7,5},{8,10},{9,11},{10,... | collective-permute-start | bytes 2113544 | tf_op jit(solution)/shard_map/ppermute | solution.py:751
  130.8 19.9 %collective-permute-start.19 = (bf16[2,688,256]{2,1,0:T(8,128)(2,1)}, bf16[2,688,256]{2,1,0:T(8,128)(2,1)S(1)}, u32[]{:S(2)}, u32[]{:S(2)}) collective-permute-start(bf16[2,688,256]{2,1,0:T(8,128)(2,1)} %copy-done.29), channel_id=1, source_target_pairs={{0,4},{4,8},{8,12},{12,0},{1,5},{5,9},{9,13},{13,1},{2,6},{6,10},{... | collective-permute-start | bytes 2113544 | tf_op jit(solution)/shard_map/ppermute | solution.py:756
  133.1 17.7 %collective-permute-start.20 = (bf16[1376,256]{1,0:T(8,128)(2,1)}, bf16[1376,256]{1,0:T(8,128)(2,1)S(1)}, u32[]{:S(2)}, u32[]{:S(2)}) collective-permute-start(bf16[1376,256]{1,0:T(8,128)(2,1)} %collective-permute-done.9), channel_id=1, source_target_pairs={{0,2},{1,3},{2,0},{3,1},{4,6},{5,7},{6,4},{7,5},{8,10},{9,11},{10,... | collective-permute-start | bytes 2113544 | tf_op jit(solution)/shard_map/ppermute | solution.py:751
  150.8 19.5 %collective-permute-start.23 = (bf16[2,688,256]{2,1,0:T(8,128)(2,1)S(1)}, bf16[2,688,256]{2,1,0:T(8,128)(2,1)S(1)}, u32[]{:S(2)}, u32[]{:S(2)}) collective-permute-start(bf16[2,688,256]{2,1,0:T(8,128)(2,1)S(1)} %collective-permute-done.19.refs_2_.refs_18_), channel_id=1, source_target_pairs={{0,4},{4,8},{8,12},{12,0},{1,5},{5,9},{9,13},{13,1},{2,6},{6,10},{... | collective-permute-start | bytes 2113544 | tf_op jit(solution)/shard_map/ppermute | solution.py:756
  151.9 18.3 %collective-permute-start.24 = (bf16[1376,256]{1,0:T(8,128)(2,1)S(1)}, bf16[1376,256]{1,0:T(8,128)(2,1)S(1)}, u32[]{:S(2)}, u32[]{:S(2)}) collective-permute-start(bf16[1376,256]{1,0:T(8,128)(2,1)S(1)} %copy-done.52), channel_id=1, source_target_pairs={{0,2},{1,3},{2,0},{3,1},{4,6},{5,7},{6,4},{7,5},{8,10},{9,11},{10,... | collective-permute-start | bytes 2113544 | tf_op jit(solution)/shard_map/ppermute | solution.py:751
  154.9 16.0 %collective-permute-start.25 = (bf16[2,1376,256]{2,1,0:T(8,128)(2,1)S(1)}, bf16[2,1376,256]{2,1,0:T(8,128)(2,1)S(1)}, u32[]{:S(2)}, u32[]{:S(2)}) collective-permute-start(bf16[2,1376,256]{2,1,0:T(8,128)(2,1)S(1)} %pad_maximum_fusion.refs_8_), channel_id=1, source_target_pairs={{0,1},{1,0},{2,3},{3,2},{4,5},{5,4},{6,7},{7,6},{8,9},{9,8},{10,11... | collective-permute-start | bytes 4227080 | tf_op jit(solution)/shard_map/ppermute | solution.py:746
  156.0 15.1 %collective-permute-start.26 = (bf16[2,1376,256]{2,1,0:T(8,128)(2,1)S(1)}, bf16[2,1376,256]{2,1,0:T(8,128)(2,1)S(1)}, u32[]{:S(2)}, u32[]{:S(2)}) collective-permute-start(bf16[2,1376,256]{2,1,0:T(8,128)(2,1)S(1)} %pad_maximum_fusion.1.refs_9_), channel_id=1, source_target_pairs={{0,1},{1,0},{2,3},{3,2},{4,5},{5,4},{6,7},{7,6},{8,9},{9,8},{10,11... | collective-permute-start | bytes 4227080 | tf_op jit(solution)/shard_map/ppermute | solution.py:746
  157.8 14.1 %collective-permute-start.27 = (bf16[2,1376,256]{2,1,0:T(8,128)(2,1)S(1)}, bf16[2,1376,256]{2,1,0:T(8,128)(2,1)S(1)}, u32[]{:S(2)}, u32[]{:S(2)}) collective-permute-start(bf16[2,1376,256]{2,1,0:T(8,128)(2,1)S(1)} %pad_maximum_fusion.2.refs_10_), channel_id=1, source_target_pairs={{0,1},{1,0},{2,3},{3,2},{4,5},{5,4},{6,7},{7,6},{8,9},{9,8},{10,11... | collective-permute-start | bytes 4227080 | tf_op jit(solution)/shard_map/ppermute | solution.py:746
  170.5 21.1 %collective-permute-start.29 = (bf16[2,688,256]{2,1,0:T(8,128)(2,1)S(1)}, bf16[2,688,256]{2,1,0:T(8,128)(2,1)S(1)}, u32[]{:S(2)}, u32[]{:S(2)}) collective-permute-start(bf16[2,688,256]{2,1,0:T(8,128)(2,1)S(1)} %pad_maximum_fusion.9.refs_0_.refs_16_), channel_id=1, source_target_pairs={{0,1},{1,0},{2,3},{3,2},{4,5},{5,4},{6,7},{7,6},{8,9},{9,8},{10,11... | collective-permute-start | bytes 2113544 | tf_op jit(solution)/shard_map/ppermute | solution.py:746
  171.0 20.7 %collective-permute-start.31 = (bf16[2,688,256]{2,1,0:T(8,128)(2,1)S(1)}, bf16[2,688,256]{2,1,0:T(8,128)(2,1)S(1)}, u32[]{:S(2)}, u32[]{:S(2)}) collective-permute-start(bf16[2,688,256]{2,1,0:T(8,128)(2,1)S(1)} %collective-permute-done.19.refs_2_.refs_18_), channel_id=1, source_target_pairs={{0,1},{1,0},{2,3},{3,2},{4,5},{5,4},{6,7},{7,6},{8,9},{9,8},{10,11... | collective-permute-start | bytes 2113544 | tf_op jit(solution)/shard_map/ppermute | solution.py:746
  171.8 19.8 %collective-permute-start.30 = (bf16[2,688,256]{2,1,0:T(8,128)(2,1)S(1)}, bf16[2,688,256]{2,1,0:T(8,128)(2,1)S(1)}, u32[]{:S(2)}, u32[]{:S(2)}) collective-permute-start(bf16[2,688,256]{2,1,0:T(8,128)(2,1)S(1)} %copy-done.30), channel_id=1, source_target_pairs={{0,1},{1,0},{2,3},{3,2},{4,5},{5,4},{6,7},{7,6},{8,9},{9,8},{10,11... | collective-permute-start | bytes 2113544 | tf_op jit(solution)/shard_map/ppermute | solution.py:746
  171.9 19.8 %collective-permute-start.32 = (bf16[2,688,256]{2,1,0:T(8,128)(2,1)S(1)}, bf16[2,688,256]{2,1,0:T(8,128)(2,1)S(1)}, u32[]{:S(2)}, u32[]{:S(2)}) collective-permute-start(bf16[2,688,256]{2,1,0:T(8,128)(2,1)S(1)} %collective-permute-done.23.refs_3_.refs_19_), channel_id=1, source_target_pairs={{0,1},{1,0},{2,3},{3,2},{4,5},{5,4},{6,7},{7,6},{8,9},{9,8},{10,11... | collective-permute-start | bytes 2113544 | tf_op jit(solution)/shard_map/ppermute | solution.py:746
  202.8 26.4 %collective-permute-start.33 = (bf16[512,1024]{1,0:T(8,128)(2,1)}, bf16[512,1024]{1,0:T(8,128)(2,1)S(1)}, u32[]{:S(2)}, u32[]{:S(2)}) collective-permute-start(bf16[512,1024]{1,0:T(8,128)(2,1)} %shard_map.174), channel_id=1, source_target_pairs={{0,16},{1,17},{2,18},{3,19},{4,20},{5,21},{6,22},{7,23},{8,24},{9,... | collective-permute-start | bytes 3145736 | tf_op jit(solution)/shard_map/ppermute | solution.py:1001
  354.3 28.9 %collective-permute-start.39 = (bf16[512,1408]{1,0:T(8,128)(2,1)}, bf16[512,1408]{1,0:T(8,128)(2,1)S(1)}, u32[]{:S(2)}, u32[]{:S(2)}) collective-permute-start(bf16[512,1408]{1,0:T(8,128)(2,1)} %get-tuple-element.294.zf_ref), channel_id=1, source_target_pairs={{0,1},{1,0},{2,3},{3,2},{4,5},{5,4},{6,7},{7,6},{8,9},{9,8},{10,11... | collective-permute-start | bytes 4325384 | tf_op jit(solution)/shard_map/ppermute | solution.py:746
  354.5 27.6 %collective-permute-start.38 = (bf16[512,1024]{1,0:T(8,128)(2,1)}, bf16[512,1024]{1,0:T(8,128)(2,1)}, u32[]{:S(2)}, u32[]{:S(2)}) collective-permute-start(bf16[512,1024]{1,0:T(8,128)(2,1)} %get-tuple-element.292), channel_id=1, source_target_pairs={{16,0},{17,1},{18,2},{19,3},{20,4},{21,5},{22,6},{23,7},{24,8},{25... | collective-permute-start | bytes 3145736 | tf_op jit(solution)/shard_map/ppermute | solution.py:1021
  355.8 26.3 %collective-permute-start.40 = (bf16[512,1024]{1,0:T(8,128)(2,1)S(1)}, bf16[512,1024]{1,0:T(8,128)(2,1)S(1)}, u32[]{:S(2)}, u32[]{:S(2)}) collective-permute-start(bf16[512,1024]{1,0:T(8,128)(2,1)S(1)} %copy-done.10), channel_id=1, source_target_pairs={{0,1},{1,0},{2,3},{3,2},{4,5},{5,4},{6,7},{7,6},{8,9},{9,8},{10,11... | collective-permute-start | bytes 3145736 | tf_op jit(solution)/shard_map/ppermute | solution.py:746
  356.2 26.9 %collective-permute-start.41 = (bf16[512,1024]{1,0:T(8,128)(2,1)S(1)}, bf16[512,1024]{1,0:T(8,128)(2,1)S(1)}, u32[]{:S(2)}, u32[]{:S(2)}) collective-permute-start(bf16[512,1024]{1,0:T(8,128)(2,1)S(1)} %copy-done.6), channel_id=1, source_target_pairs={{0,1},{1,0},{2,3},{3,2},{4,5},{5,4},{6,7},{7,6},{8,9},{9,8},{10,11... | collective-permute-start | bytes 3145736 | tf_op jit(solution)/shard_map/ppermute | solution.py:746
  356.4 10.3 %collective-permute-start.42 = (bf16[512,512]{1,0:T(8,128)(2,1)S(1)}, bf16[512,512]{1,0:T(8,128)(2,1)S(1)}, u32[]{:S(2)}, u32[]{:S(2)}) collective-permute-start(bf16[512,512]{1,0:T(8,128)(2,1)S(1)} %slice.261), channel_id=1, source_target_pairs={{0,1},{1,0},{2,3},{3,2},{4,5},{5,4},{6,7},{7,6},{8,9},{9,8},{10,11... | collective-permute-start | bytes 1572872 | tf_op jit(solution)/shard_map/ppermute | solution.py:746
  390.9 33.1 %collective-permute-start.44 = (bf16[4,688,256]{2,1,0:T(8,128)(2,1)S(1)}, bf16[4,688,256]{2,1,0:T(8,128)(2,1)}, u32[]{:S(2)}, u32[]{:S(2)}) collective-permute-start(bf16[4,688,256]{2,1,0:T(8,128)(2,1)S(1)} %get-tuple-element.303), channel_id=1, source_target_pairs={{0,2},{1,3},{2,0},{3,1},{4,6},{5,7},{6,4},{7,5},{8,10},{9,11},{10,... | collective-permute-start | bytes 4227080 | tf_op jit(solution)/shard_map/ppermute | solution.py:751
  425.6 12.5 %collective-permute-start.45 = (bf16[688,256]{1,0:T(8,128)(2,1)S(1)}, bf16[688,256]{1,0:T(8,128)(2,1)S(1)}, u32[]{:S(2)}, u32[]{:S(2)}) collective-permute-start(bf16[688,256]{1,0:T(8,128)(2,1)S(1)} %fusion.21), channel_id=1, source_target_pairs={{0,4},{4,8},{8,12},{12,0},{1,5},{5,9},{9,13},{13,1},{2,6},{6,10},{... | collective-permute-start | bytes 1056776 | tf_op jit(solution)/shard_map/ppermute | solution.py:756
  439.8 11.9 %collective-permute-start.49 = (bf16[688,256]{1,0:T(8,128)(2,1)S(1)}, bf16[688,256]{1,0:T(8,128)(2,1)S(1)}, u32[]{:S(2)}, u32[]{:S(2)}) collective-permute-start(bf16[688,256]{1,0:T(8,128)(2,1)S(1)} %fusion.10), channel_id=1, source_target_pairs={{0,4},{4,8},{8,12},{12,0},{1,5},{5,9},{9,13},{13,1},{2,6},{6,10},{... | collective-permute-start | bytes 1056776 | tf_op jit(solution)/shard_map/ppermute | solution.py:756
  440.1 44.2 %collective-permute-start.51 = (bf16[4,688,256]{2,1,0:T(8,128)(2,1)}, bf16[4,688,256]{2,1,0:T(8,128)(2,1)}, u32[]{:S(2)}, u32[]{:S(2)}) collective-permute-start(bf16[4,688,256]{2,1,0:T(8,128)(2,1)} %get-tuple-element.338), channel_id=1, source_target_pairs={{0,2},{1,3},{2,0},{3,1},{4,6},{5,7},{6,4},{7,5},{8,10},{9,11},{10,... | collective-permute-start | bytes 4227080 | tf_op jit(solution)/shard_map/ppermute | solution.py:751
  452.9 31.5 %collective-permute-start.52 = (bf16[688,256]{1,0:T(8,128)(2,1)S(1)}, bf16[688,256]{1,0:T(8,128)(2,1)S(1)}, u32[]{:S(2)}, u32[]{:S(2)}) collective-permute-start(bf16[688,256]{1,0:T(8,128)(2,1)S(1)} %fusion.9), channel_id=1, source_target_pairs={{0,4},{4,8},{8,12},{12,0},{1,5},{5,9},{9,13},{13,1},{2,6},{6,10},{... | collective-permute-start | bytes 1056776 | tf_op jit(solution)/shard_map/ppermute | solution.py:756
  453.0 31.2 %collective-permute-start.53 = (bf16[2,256,256]{2,1,0:T(8,128)(2,1)S(1)}, bf16[2,256,256]{2,1,0:T(8,128)(2,1)S(1)}, u32[]{:S(2)}, u32[]{:S(2)}) collective-permute-start(bf16[2,256,256]{2,1,0:T(8,128)(2,1)S(1)} %pad_maximum_fusion.12), channel_id=1, source_target_pairs={{0,12},{4,0},{8,4},{12,8},{1,13},{5,1},{9,5},{13,9},{2,14},{6,2},{... | collective-permute-start | bytes 786440 | tf_op jit(solution)/shard_map/ppermute | solution.py:779
  456.9 27.4 %collective-permute-start.54 = (bf16[2,256,256]{2,1,0:T(8,128)(2,1)S(1)}, bf16[2,256,256]{2,1,0:T(8,128)(2,1)S(1)}, u32[]{:S(2)}, u32[]{:S(2)}) collective-permute-start(bf16[2,256,256]{2,1,0:T(8,128)(2,1)S(1)} %pad_maximum_fusion.13), channel_id=1, source_target_pairs={{0,8},{4,12},{8,0},{12,4},{1,9},{5,13},{9,1},{13,5},{2,10},{6,14},... | collective-permute-start | bytes 786440 | tf_op jit(solution)/shard_map/ppermute | solution.py:779
  457.0 27.3 %collective-permute-start.55 = (bf16[2,256,256]{2,1,0:T(8,128)(2,1)S(1)}, bf16[2,256,256]{2,1,0:T(8,128)(2,1)S(1)}, u32[]{:S(2)}, u32[]{:S(2)}) collective-permute-start(bf16[2,256,256]{2,1,0:T(8,128)(2,1)S(1)} %pad_maximum_fusion.14), channel_id=1, source_target_pairs={{0,4},{4,8},{8,12},{12,0},{1,5},{5,9},{9,13},{13,1},{2,6},{6,10},{... | collective-permute-start | bytes 786440 | tf_op jit(solution)/shard_map/ppermute | solution.py:779
  485.2 33.6 %collective-permute-start.50 = (bf16[4,688,256]{2,1,0:T(8,128)(2,1)}, bf16[4,688,256]{2,1,0:T(8,128)(2,1)}, u32[]{:S(2)}, u32[]{:S(2)}) collective-permute-start(bf16[4,688,256]{2,1,0:T(8,128)(2,1)} %get-tuple-element.336), channel_id=1, source_target_pairs={{0,2},{1,3},{2,0},{3,1},{4,6},{5,7},{6,4},{7,5},{8,10},{9,11},{10,... | collective-permute-start | bytes 4227080 | tf_op jit(solution)/shard_map/ppermute | solution.py:751
  488.4 30.4 %collective-permute-start.56 = (bf16[688,256]{1,0:T(8,128)(2,1)}, bf16[688,256]{1,0:T(8,128)(2,1)}, u32[]{:S(2)}, u32[]{:S(2)}) collective-permute-start(bf16[688,256]{1,0:T(8,128)(2,1)} %get-tuple-element.423), channel_id=1, source_target_pairs={{0,12},{4,0},{8,4},{12,8},{1,13},{5,1},{9,5},{13,9},{2,14},{6,2},{... | collective-permute-start | bytes 1056776 | tf_op jit(solution)/shard_map/ppermute | solution.py:779
  491.6 32.5 %collective-permute-start.57 = (bf16[688,256]{1,0:T(8,128)(2,1)}, bf16[688,256]{1,0:T(8,128)(2,1)}, u32[]{:S(2)}, u32[]{:S(2)}) collective-permute-start(bf16[688,256]{1,0:T(8,128)(2,1)} %get-tuple-element.422), channel_id=1, source_target_pairs={{0,8},{4,12},{8,0},{12,4},{1,9},{5,13},{9,1},{13,5},{2,10},{6,14},... | collective-permute-start | bytes 1056776 | tf_op jit(solution)/shard_map/ppermute | solution.py:779
  492.8 31.4 %collective-permute-start.58 = (bf16[688,256]{1,0:T(8,128)(2,1)}, bf16[688,256]{1,0:T(8,128)(2,1)}, u32[]{:S(2)}, u32[]{:S(2)}) collective-permute-start(bf16[688,256]{1,0:T(8,128)(2,1)} %get-tuple-element.421), channel_id=1, source_target_pairs={{0,4},{4,8},{8,12},{12,0},{1,5},{5,9},{9,13},{13,1},{2,6},{6,10},{... | collective-permute-start | bytes 1056776 | tf_op jit(solution)/shard_map/ppermute | solution.py:779
  524.9 15.8 %collective-permute-start.62 = (bf16[256,256]{1,0:T(8,128)(2,1)}, bf16[256,256]{1,0:T(8,128)(2,1)}, u32[]{:S(2)}, u32[]{:S(2)}) collective-permute-start(bf16[256,256]{1,0:T(8,128)(2,1)} %fusion.48), channel_id=1, source_target_pairs={{0,2},{1,3},{2,0},{3,1},{4,6},{5,7},{6,4},{7,5},{8,10},{9,11},{10,... | collective-permute-start | bytes 393224 | tf_op jit(solution)/shard_map/ppermute | solution.py:751
  530.2 19.4 %collective-permute-start.61 = (bf16[256,1024]{1,0:T(8,128)(2,1)S(1)}, bf16[256,1024]{1,0:T(8,128)(2,1)S(1)}, u32[]{:S(2)}, u32[]{:S(2)}) collective-permute-start(bf16[256,1024]{1,0:T(8,128)(2,1)S(1)} %slice_select_fusion.1), channel_id=1, source_target_pairs={{0,2},{1,3},{2,0},{3,1},{4,6},{5,7},{6,4},{7,5},{8,10},{9,11},{10,... | collective-permute-start | bytes 1572872 | tf_op jit(solution)/shard_map/ppermute | solution.py:751
  532.3 17.3 %collective-permute-start.66 = (bf16[336,256]{1,0:T(8,128)(2,1)S(1)}, bf16[336,256]{1,0:T(8,128)(2,1)S(1)}, u32[]{:S(2)}, u32[]{:S(2)}) collective-permute-start(bf16[336,256]{1,0:T(8,128)(2,1)S(1)} %get-tuple-element.419), channel_id=1, source_target_pairs={{0,8},{4,12},{8,0},{12,4},{1,9},{5,13},{9,1},{13,5},{2,10},{6,14},... | collective-permute-start | bytes 516104 | tf_op jit(solution)/shard_map/ppermute | solution.py:779
  533.7 16.0 %collective-permute-start.67 = (bf16[336,256]{1,0:T(8,128)(2,1)S(1)}, bf16[336,256]{1,0:T(8,128)(2,1)S(1)}, u32[]{:S(2)}, u32[]{:S(2)}) collective-permute-start(bf16[336,256]{1,0:T(8,128)(2,1)S(1)} %get-tuple-element.418), channel_id=1, source_target_pairs={{0,4},{4,8},{8,12},{12,0},{1,5},{5,9},{9,13},{13,1},{2,6},{6,10},{... | collective-permute-start | bytes 516104 | tf_op jit(solution)/shard_map/ppermute | solution.py:779
  549.8 22.4 %collective-permute-start.68 = (bf16[4,384,256]{2,1,0:T(8,128)(2,1)S(1)}, bf16[4,384,256]{2,1,0:T(8,128)(2,1)S(1)}, u32[]{:S(2)}, u32[]{:S(2)}) collective-permute-start(bf16[4,384,256]{2,1,0:T(8,128)(2,1)S(1)} %get-tuple-element.434), channel_id=1, source_target_pairs={{0,2},{1,3},{2,0},{3,1},{4,6},{5,7},{6,4},{7,5},{8,10},{9,11},{10,... | collective-permute-start | bytes 2359304 | tf_op jit(solution)/shard_map/ppermute | solution.py:751
  551.7 17.9 %collective-permute-start.69 = (f32[3,1024]{1,0:T(4,128)S(1)}, f32[3,1024]{1,0:T(4,128)S(1)}, u32[]{:S(2)}, u32[]{:S(2)}) collective-permute-start(f32[3,1024]{1,0:T(4,128)S(1)} %fusion.65), channel_id=1, source_target_pairs={{0,2},{1,3},{2,0},{3,1},{4,6},{5,7},{6,4},{7,5},{8,10},{9,11},{10,... | collective-permute-start | bytes 36872 | tf_op jit(solution)/shard_map/ppermute | solution.py:751
  554.3 16.8 %collective-permute-start.70 = (bf16[352,256]{1,0:T(8,128)(2,1)S(1)}, bf16[352,256]{1,0:T(8,128)(2,1)S(1)}, u32[]{:S(2)}, u32[]{:S(2)}) collective-permute-start(bf16[352,256]{1,0:T(8,128)(2,1)S(1)} %get-tuple-element.417), channel_id=1, source_target_pairs={{0,12},{4,0},{8,4},{12,8},{1,13},{5,1},{9,5},{13,9},{2,14},{6,2},{... | collective-permute-start | bytes 540680 | tf_op jit(solution)/shard_map/ppermute | solution.py:779
  554.4 17.8 %collective-permute-start.71 = (bf16[352,256]{1,0:T(8,128)(2,1)S(1)}, bf16[352,256]{1,0:T(8,128)(2,1)S(1)}, u32[]{:S(2)}, u32[]{:S(2)}) collective-permute-start(bf16[352,256]{1,0:T(8,128)(2,1)S(1)} %get-tuple-element.416), channel_id=1, source_target_pairs={{0,8},{4,12},{8,0},{12,4},{1,9},{5,13},{9,1},{13,5},{2,10},{6,14},... | collective-permute-start | bytes 540680 | tf_op jit(solution)/shard_map/ppermute | solution.py:779
  556.2 16.0 %collective-permute-start.72 = (bf16[352,256]{1,0:T(8,128)(2,1)S(1)}, bf16[352,256]{1,0:T(8,128)(2,1)S(1)}, u32[]{:S(2)}, u32[]{:S(2)}) collective-permute-start(bf16[352,256]{1,0:T(8,128)(2,1)S(1)} %get-tuple-element.415), channel_id=1, source_target_pairs={{0,4},{4,8},{8,12},{12,0},{1,5},{5,9},{9,13},{13,1},{2,6},{6,10},{... | collective-permute-start | bytes 540680 | tf_op jit(solution)/shard_map/ppermute | solution.py:779
  569.5 18.5 %collective-permute-start.73 = (bf16[4,384,256]{2,1,0:T(8,128)(2,1)S(1)}, bf16[4,384,256]{2,1,0:T(8,128)(2,1)S(1)}, u32[]{:S(2)}, u32[]{:S(2)}) collective-permute-start(bf16[4,384,256]{2,1,0:T(8,128)(2,1)S(1)} %get-tuple-element.435), channel_id=1, source_target_pairs={{0,2},{1,3},{2,0},{3,1},{4,6},{5,7},{6,4},{7,5},{8,10},{9,11},{10,... | collective-permute-start | bytes 2359304 | tf_op jit(solution)/shard_map/ppermute | solution.py:751
  572.3 15.7 %collective-permute-start.75 = (bf16[384,256]{1,0:T(8,128)(2,1)S(1)}, bf16[384,256]{1,0:T(8,128)(2,1)S(1)}, u32[]{:S(2)}, u32[]{:S(2)}) collective-permute-start(bf16[384,256]{1,0:T(8,128)(2,1)S(1)} %get-tuple-element.429), channel_id=1, source_target_pairs={{0,12},{4,0},{8,4},{12,8},{1,13},{5,1},{9,5},{13,9},{2,14},{6,2},{... | collective-permute-start | bytes 589832 | tf_op jit(solution)/shard_map/ppermute | solution.py:779
  572.4 18.8 %collective-permute-start.76 = (bf16[384,256]{1,0:T(8,128)(2,1)S(1)}, bf16[384,256]{1,0:T(8,128)(2,1)S(1)}, u32[]{:S(2)}, u32[]{:S(2)}) collective-permute-start(bf16[384,256]{1,0:T(8,128)(2,1)S(1)} %get-tuple-element.428), channel_id=1, source_target_pairs={{0,8},{4,12},{8,0},{12,4},{1,9},{5,13},{9,1},{13,5},{2,10},{6,14},... | collective-permute-start | bytes 589832 | tf_op jit(solution)/shard_map/ppermute | solution.py:779
  573.6 17.6 %collective-permute-start.77 = (bf16[384,256]{1,0:T(8,128)(2,1)S(1)}, bf16[384,256]{1,0:T(8,128)(2,1)S(1)}, u32[]{:S(2)}, u32[]{:S(2)}) collective-permute-start(bf16[384,256]{1,0:T(8,128)(2,1)S(1)} %get-tuple-element.427), channel_id=1, source_target_pairs={{0,4},{4,8},{8,12},{12,0},{1,5},{5,9},{9,13},{13,1},{2,6},{6,10},{... | collective-permute-start | bytes 589832 | tf_op jit(solution)/shard_map/ppermute | solution.py:779
  592.2 22.2 %collective-permute-start.80 = (bf16[384,256]{1,0:T(8,128)(2,1)}, bf16[384,256]{1,0:T(8,128)(2,1)}, u32[]{:S(2)}, u32[]{:S(2)}) collective-permute-start(bf16[384,256]{1,0:T(8,128)(2,1)} %get-tuple-element.425), channel_id=1, source_target_pairs={{0,4},{4,8},{8,12},{12,0},{1,5},{5,9},{9,13},{13,1},{2,6},{6,10},{... | collective-permute-start | bytes 589832 | tf_op jit(solution)/shard_map/ppermute | solution.py:779
  592.2 22.2 %collective-permute-start.79 = (bf16[384,256]{1,0:T(8,128)(2,1)}, bf16[384,256]{1,0:T(8,128)(2,1)}, u32[]{:S(2)}, u32[]{:S(2)}) collective-permute-start(bf16[384,256]{1,0:T(8,128)(2,1)} %get-tuple-element.426), channel_id=1, source_target_pairs={{0,8},{4,12},{8,0},{12,4},{1,9},{5,13},{9,1},{13,5},{2,10},{6,14},... | collective-permute-start | bytes 589832 | tf_op jit(solution)/shard_map/ppermute | solution.py:779
  593.2 21.2 %collective-permute-start.78 = (bf16[384,256]{1,0:T(8,128)(2,1)}, bf16[384,256]{1,0:T(8,128)(2,1)}, u32[]{:S(2)}, u32[]{:S(2)}) collective-permute-start(bf16[384,256]{1,0:T(8,128)(2,1)} %get-tuple-element.424), channel_id=1, source_target_pairs={{0,12},{4,0},{8,4},{12,8},{1,13},{5,1},{9,5},{13,9},{2,14},{6,2},{... | collective-permute-start | bytes 589832 | tf_op jit(solution)/shard_map/ppermute | solution.py:779
  598.2 14.8 %collective-permute-start.81 = (f32[3,1024]{1,0:T(4,128)S(1)}, f32[3,1024]{1,0:T(4,128)S(1)}, u32[]{:S(2)}, u32[]{:S(2)}) collective-permute-start(f32[3,1024]{1,0:T(4,128)S(1)} %add.411), channel_id=1, source_target_pairs={{0,8},{4,12},{8,0},{12,4},{1,9},{5,13},{9,1},{13,5},{2,10},{6,14},... | collective-permute-start | bytes 36872 | tf_op jit(solution)/shard_map/ppermute | solution.py:1105
  (111 other events, 1188.6 us)

commit v6 on v5

--- a/solution.py
+++ b/solution.py
@@ -942,14 +942,16 @@
         n1 = [jnp.stack([p1, y0])]
         f1 = [core_swap(n1[0])]
         a2, a3, y1, p2, p3, ends = meet(a2, a3, y1, p2, p3, ends)
-        b1, y2, d0 = ring(p2), y_swap(a2), y_swap(p3)
+        mid = p3.shape[0] // 32 * 16
+        b1, y2, d0 = ring(p2), y_swap(a2), y_swap(p3[:mid])
         n1.append(jnp.stack([a1, y1]))
         f1.append(core_swap(n1[1]))
-        a3, b1, y2, d0, p2 = meet(a3, b1, y2, d0, p2)
-        b2, y3 = ring(b1), y_swap(a3)
+        a3, b1, y2, d0, p2, p3 = meet(a3, b1, y2, d0, p2, p3)
+        b2, y3, d1 = ring(b1), y_swap(a3), y_swap(p3[mid:])
         n1.append(jnp.stack([a2, y2]))
         f1.append(core_swap(n1[2]))
-        b1, b2, y3, p2, d0 = meet(b1, b2, y3, p2, d0)
+        b1, b2, y3, p2, d0, d1 = meet(b1, b2, y3, p2, d0, d1)
+        d0 = jnp.concatenate([d0, d1], axis=0)
         n1.append(jnp.stack([a3, y3]))
         f1.append(core_swap(n1[3]))
         w1 = n1 + f1
@@ -1074,11 +1076,13 @@
     dp_near, dp_far, dx, dx_low, gg_a = back
     dp_oth = core_swap(dp_far)
     qkv_keep, qkv_send = wgrad_call(zi, 3 * width, dp_near, n1, dp_oth, n1_oth)
+    if near:
+        up = [plus(up_keep[r, :half], up_got[r, :half]) for r in range(4)]
+        dx_low, gg_a, *up = meet(dx_low, gg_a, *up)
     small = small_rows(gg_a, gg_f, bias, ti, heads_local)
     out_low_rows = jnp.where(is_first, dx_low, y.astype(BF))
     send = jnp.where(yi == 0, out_low_rows[rows:], out_low_rows[:rows])
     if near:
-        up = [plus(up_keep[r, :half], up_got[r, :half]) for r in range(4)]
         up_run = [to_owner(up[r], r) for r in (1, 2, 3)]
         rows_got = y_swap(send)
         out_far = add_all(out[0][1], [run[1] for run in out_run]).astype(BF)
@@ -1101,8 +1105,9 @@
         )
         head_run, gate_run, out_run, up_run, more_run = (rest[i : i + 3] for i in range(0, 15, 3))
         tail = [plus(qkv_keep[r, cut:], tail_got[r]) for r in range(4)]
+        small = small + lax.ppermute(small, "dp", [(i, i ^ 2) for i in range(4)])
+        small, *tail = meet(small, *tail)
         tail_run = [to_owner(tail[r], r) for r in (1, 2, 3)]
-        small = small + lax.ppermute(small, "dp", [(i, i ^ 2) for i in range(4)])
         g_down = down_run.astype(F32) + down[0].astype(F32)
         g_up = [add_all(up[0], up_run), add_all(more[0], more_run)]
         g_gu = jnp.stack([add_all(gate[0], gate_run), jnp.concatenate(g_up, axis=0)])

time: 626 us -> 619 us (0.989)
    ppermute x18, waiting for transfers between devices: 18.4 us -> 30.6 us  [to_owner(): return lax.ppermute(part, 'dp', [(i, (i - r) % n) for i in range(n)])]
    ppermute x18 -> x19, waiting for transfers between devices: 67.4 us -> 59.3 us  [y_swap(): return lax.ppermute(value, 'tensor', [(i, i ^ 2) for i in range(n)])]
    unnamed x189 -> x187, local copies, waits for them, and re-layouts: 15.7 us -> 13.4 us
    ppermute x18 -> x19, starting transfers between devices: 22.1 us -> 22.2 us  [y_swap(): return lax.ppermute(value, 'tensor', [(i, i ^ 2) for i in range(n)])]
  transfers between devices with their start and end apart: 82 -> 83, of which waited for: 31 -> 35; matrix products, arithmetic and copies ran while one was open for 8% -> 8% of each run, Pallas kernels for 22% -> 22%
where the time goes in v6:
time: 619 us; the launch traced here: 609 us
  Pallas kernels  261 us (42%)
  waiting for transfers between devices  207 us (33%)
  starting transfers between devices  68.3 us (11%)
  other arithmetic  46.2 us (7%)
  local copies, waits for them, and re-layouts  24.3 us (4%)
    ppermute x19, waiting for transfers between devices, y_swap(): return lax.ppermute(value, 'tensor', [(i, i ^ 2) for i in range(n)])  59.3 us
    ppermute x12, waiting for transfers between devices, ring(): return lax.ppermute(value, 'dp', [(i, (i + 1) % n) for i in range(n)])  54.2 us
    pallas_call x2, Pallas kernels, attend_back_call(): pl.pallas_call(functools.partial(attend_back_kernel, scale), grid=(pairs,...  53.3 us
    pallas_call x2, Pallas kernels, ffn_back_call(): pl.pallas_call(functools.partial(ffn_back_kernel, out_low), grid=(2,), in...  50.4 us
    pallas_call x2, Pallas kernels, ffn_up_call(): pl.pallas_call(functools.partial(ffn_up_kernel, save, out_low), grid=(2,)...  34.9 us
    pallas_call x2, Pallas kernels, qkv_back_call(): pl.pallas_call(qkv_back_kernel, grid=(4,), in_specs=[col] * 7 + [whole((r...  33 us
    ppermute x18, waiting for transfers between devices, to_owner(): return lax.ppermute(part, 'dp', [(i, (i - r) % n) for i in range(n)])  30.6 us
    pallas_call x2, Pallas kernels, attend_call(): pl.pallas_call(functools.partial(attend_kernel, scale), grid=(pairs,), in...  30.3 us
  transfers between devices with their start and end apart: 83, of which 35 were waited for; matrix products, arithmetic and copies ran while one was open for 8% of the time, Pallas kernels for 22%

profile of v6, /device:TPU:0, one launch (start us, length us, event | category | flops | bytes accessed | tf_op | source)
XLA Modules:
  0.0 609.3 jit_solution(7275413797536992693)
XLA Ops:
  4.3 3.1 collective-permute-start
  7.4 1.7 fusion.14
  9.1 1.6 collective-permute-start.1
  15.5 7.0 %collective-permute-done.1 = bf16[256,1024]{1,0:T(8,128)(2,1)S(1)} collective-permute-done((bf16[256,1024]{1,0:T(8,128)(2,1)S(1)}, bf16[256,1024]{1,0:T(8,128)(2,1)S(1)}, u32[]{:S(2)}, u32[]{:S(2)}) %collective-permute-start.1) | collective-permute-done | bytes 524320 | tf_op jit(solution)/shard_map/ppermute | solution.py:751
  28.7 8.3 %collective-permute-done.2 = bf16[1040,256]{1,0:T(8,128)(2,1)S(1)} collective-permute-done((bf16[1040,256]{1,0:T(8,128)(2,1)S(1)}, bf16[1040,256]{1,0:T(8,128)(2,1)S(1)}, u32[]{:S(2)}, u32[]{:S(2)}) %collective-permute-start.2) | collective-permute-done | bytes 532512 | tf_op jit(solution)/shard_map/ppermute | solution.py:756
  41.1 9.6 %collective-permute-done.4 = bf16[1040,256]{1,0:T(8,128)(2,1)} collective-permute-done((bf16[1040,256]{1,0:T(8,128)(2,1)S(1)}, bf16[1040,256]{1,0:T(8,128)(2,1)}, u32[]{:S(2)}, u32[]{:S(2)}) %collective-permute-start.4) | collective-permute-done | bytes 532512 | tf_op jit(solution)/shard_map/ppermute | solution.py:756
  52.9 12.3 %collective-permute-done.8 = bf16[336,256]{1,0:T(8,128)(2,1)S(1)} collective-permute-done((bf16[336,256]{1,0:T(8,128)(2,1)S(1)}, bf16[336,256]{1,0:T(8,128)(2,1)S(1)}, u32[]{:S(2)}, u32[]{:S(2)}) %collective-permute-start.8) | collective-permute-done | bytes 172064 | tf_op jit(solution)/shard_map/ppermute | solution.py:751
  65.2 2.0 collective-permute-done.6
  67.2 1.6 collective-permute-start.10
  70.8 10.4 %collective-permute-done.11 = bf16[352,256]{1,0:T(8,128)(2,1)S(1)} collective-permute-done((bf16[352,256]{1,0:T(8,128)(2,1)S(1)}, bf16[352,256]{1,0:T(8,128)(2,1)S(1)}, u32[]{:S(2)}, u32[]{:S(2)}) %collective-permute-start.11) | collective-permute-done | bytes 180256 | tf_op jit(solution)/shard_map/ppermute | solution.py:751
  81.3 1.7 collective-permute-done.9
  86.4 2.3 pad_maximum_fusion.7.refs_3_
  88.7 9.0 %collective-permute-done.12 = bf16[1376,256]{1,0:T(8,128)(2,1)S(1)} collective-permute-done((bf16[1376,256]{1,0:T(8,128)(2,1)}, bf16[1376,256]{1,0:T(8,128)(2,1)S(1)}, u32[]{:S(2)}, u32[]{:S(2)}) %collective-permute-start.12) | collective-permute-done | bytes 704544 | tf_op jit(solution)/shard_map/ppermute | solution.py:756
  106.6 10.7 %shard_map.171 = (bf16[512,1024]{1,0:T(8,128)(2,1)}, bf16[512,1024]{1,0:T(8,128)(2,1)}, bf16[512,1024]{1,0:T(8,128)(2,1)}) custom-call(bf16[512,1024]{1,0:T(8,128)(2,1)} %maximum_select_fusion.1.x_ref.dy_ref, f32[1,1024]{1,0:T(1,128)} %bitcast.179, s32[1]{0:T(128)} %bitcast.27.zi_ref, f32[512,128]{1,0:T(8,128)} %pad_maximum_fusion.11.cos_ref, ...), custom_call_target="tpu_custom_call" | custom-call | flops 3221225472 | bytes 14680064 | tf_op jit(solution)/shard_map/pallas_call | solution.py:180
  117.3 5.8 collective-permute-done.14.refs_1_.refs_17_
  128.3 15.2 %shard_map.172 = (bf16[512,1024]{1,0:T(8,128)(2,1)}, f32[512,1024]{1,0:T(8,128)}) custom-call(bf16[512,1024]{1,0:T(8,128)(2,1)} %get-tuple-element.264.q_ref, bf16[512,1024]{1,0:T(8,128)(2,1)} %get-tuple-element.265.ko_ref, bf16[512,1024]{1,0:T(8,128)(2,1)} %copy-done.91, bf16[512,1024]{1,0:T(8,128)(2,1)} %get-tuple-element.266.vo_ref, ...), custom_call_target="tpu_custom_call" | custom-call | flops 4294967296 | bytes 10485760 | tf_op jit(solution)/shard_map/pallas_call | solution.py:243
  148.8 1.7 pad_maximum_fusion.2.refs_10_
  150.7 12.4 %collective-permute-done.24.refs_3_.refs_19_ = bf16[2,688,256]{2,1,0:T(8,128)(2,1)S(1)} collective-permute-done((bf16[2,688,256]{2,1,0:T(8,128)(2,1)S(1)}, bf16[2,688,256]{2,1,0:T(8,128)(2,1)S(1)}, u32[]{:S(2)}, u32[]{:S(2)}) %collective-permute-start.24) | collective-permute-done | bytes 704544 | tf_op jit(solution)/shard_map/ppermute | solution.py:756
  167.5 16.8 %shard_map.173 = (f32[512,1024]{1,0:T(8,128)}, bf16[512,1408]{1,0:T(8,128)(2,1)}, bf16[512,1408]{1,0:T(8,128)(2,1)}) custom-call(bf16[512,1024]{1,0:T(8,128)(2,1)} %maximum_select_fusion.1.x_ref.dy_ref, bf16[512,1024]{1,0:T(8,128)(2,1)} %get-tuple-element.271.o_ref, f32[1,1024]{1,0:T(1,128)} %bitcast.193, s32[1]{0:T(128)} %bitcast.27.zi_ref, ...), custom_call_target="tpu_custom_call" | custom-call | flops 6845104128 | bytes 21757952 | tf_op jit(solution)/shard_map/pallas_call | solution.py:394
  185.9 9.6 %shard_map.174 = bf16[512,1024]{1,0:T(8,128)(2,1)} custom-call(f32[512,1024]{1,0:T(8,128)} %get-tuple-element.279.h_ref, bf16[512,1408]{1,0:T(8,128)(2,1)} %get-tuple-element.280.zn_ref, bf16[512,1408]{1,0:T(8,128)(2,1)} %get-tuple-element.281.zf_ref, s32[1]{0:T(128)} %bitcast.27.zi_ref, bf16[2,688,256]{2,1,0:T(8,128)(2,1)} %copy-done.25, ...), custom_call_target="tpu_custom_call" | custom-call | flops 2885681152 | bytes 9830400 | tf_op jit(solution)/shard_map/pallas_call | solution.py:428
  195.6 3.6 collective-permute-start.34
  199.2 22.8 %collective-permute-done.34 = bf16[512,1024]{1,0:T(8,128)(2,1)S(1)} collective-permute-done((bf16[512,1024]{1,0:T(8,128)(2,1)}, bf16[512,1024]{1,0:T(8,128)(2,1)S(1)}, u32[]{:S(2)}, u32[]{:S(2)}) %collective-permute-start.34) | collective-permute-done | bytes 1048608 | tf_op jit(solution)/shard_map/ppermute | solution.py:1003
  223.1 11.2 %shard_map.175 = (bf16[512,1024]{1,0:T(8,128)(2,1)}, bf16[512,1024]{1,0:T(8,128)(2,1)}, bf16[512,1024]{1,0:T(8,128)(2,1)}, bf16[512,1024]{1,0:T(8,128)(2,1)}, bf...) custom-call(bf16[512,1024]{1,0:T(8,128)(2,1)} %broadcast_select_fusion.2.x_ref, f32[1,1024]{1,0:T(1,128)} %bitcast.180, ...), custom_call_target="tpu_custom_call" | custom-call | flops 3221225472 | bytes 14680064 | tf_op jit(solution)/shard_map/pallas_call | solution.py:180
  234.8 2.4 collective-permute-done.35.kx_ref
  239.7 15.1 %shard_map.176 = (bf16[512,1024]{1,0:T(8,128)(2,1)}, f32[512,1024]{1,0:T(8,128)}) custom-call(bf16[512,1024]{1,0:T(8,128)(2,1)} %get-tuple-element.284.q_ref, bf16[512,1024]{1,0:T(8,128)(2,1)} %get-tuple-element.285.ko_ref, bf16[512,1024]{1,0:T(8,128)(2,1)} %copy-done.89, bf16[512,1024]{1,0:T(8,128)(2,1)} %get-tuple-element.286.vo_ref, ...), custom_call_target="tpu_custom_call" | custom-call | flops 4294967296 | bytes 10485760 | tf_op jit(solution)/shard_map/pallas_call | solution.py:243
  254.9 18.1 %shard_map.177 = (f32[512,1024]{1,0:T(8,128)}, bf16[512,1408]{1,0:T(8,128)(2,1)}, bf16[512,1408]{1,0:T(8,128)(2,1)}, bf16[512,1024]{1,0:T(8,128)(2,1)}, bf16[2,5...) custom-call(bf16[512,1024]{1,0:T(8,128)(2,1)} %broadcast_select_fusion.2.x_ref, ...), custom_call_target="tpu_custom_call" | custom-call | flops 6845104128 | bytes 21757952 | tf_op jit(solution)/shard_map/pallas_call | solution.py:394
  272.9 25.3 %shard_map.178 = (f32[512,1024]{1,0:T(8,128)}, bf16[512,1024]{1,0:T(8,128)(2,1)}, bf16[512,1024]{1,0:T(8,128)(2,1)}, bf16[512,1408]{1,0:T(8,128)(2,1)}, bf16[512...) custom-call(bf16[512,1024]{1,0:T(8,128)(2,1)} %maximum_select_fusion.1.x_ref.dy_re, ...), custom_call_target="tpu_custom_call" | custom-call | flops 9730785280 | bytes 27394048 | tf_op jit(solution)/shard_map/pallas_call | solution.py:512
  298.3 26.7 %shard_map.179 = (bf16[512,1024]{1,0:T(8,128)(2,1)}, bf16[512,1024]{1,0:T(8,128)(2,1)}, bf16[512,1024]{1,0:T(8,128)(2,1)}, bf16[512,1024]{1,0:T(8,128)(2,1)}, bf...) custom-call(bf16[512,1024]{1,0:T(8,128)(2,1)} %get-tuple-element.284.q_ref, bf16[512,1024]{1,0:T(8,128)(2,1)} %get-tuple-element.285.ko_ref, ...), custom_call_target="tpu_custom_call" | custom-call | flops 10737418240 | bytes 20971520 | tf_op jit(solution)/shard_map/pallas_call | solution.py:614
  325.6 2.3 collective-permute-done.37.dkr_ref
  330.4 16.7 %shard_map.180 = (bf16[2,512,768]{2,1,0:T(8,128)(2,1)}, bf16[2,512,768]{2,1,0:T(8,128)(2,1)}, f32[512,1024]{1,0:T(8,128)}, bf16[512,1024]{1,0:T(8,128)(2,1)}, f32[1,1024]{1,0:T(1,128)}) custom-call(bf16[512,1024]{1,0:T(8,128)(2,1)} %get-tuple-element.295.dq_ref, bf16[512,1024]{1,0:T(8,128)(2,1)} %get-tuple-element.296.dk_ref, bf16[512,1024]{1,0:T(8,128)(2,1)} %copy-done.46, ...), custom_call_target="tpu_custom_call" | custom-call | flops 3221225472 | bytes 27262976 | tf_op jit(solution)/shard_map/pallas_call | solution.py:697
  349.6 9.9 %shard_map.181 = f32[512,1024]{1,0:T(8,128)} custom-call(f32[512,1024]{1,0:T(8,128)} %get-tuple-element.288.h_ref, bf16[512,1408]{1,0:T(8,128)(2,1)} %get-tuple-element.308.zn_ref.ao_ref, bf16[512,1408]{1,0:T(8,128)(2,1)} %get-tuple-element.309.zf_ref, s32[1]{0:T(128)} %bitcast.27.zi_ref, bf16[2,688,256]{2,1,0:T(8,128)(2,1)} %copy-done.25, ...), custom_call_target="tpu_custom_call" | custom-call | flops 2885681152 | bytes 9830400 | tf_op jit(solution)/shard_map/pallas_call | solution.py:428
  359.5 15.4 %collective-permute-done.39 = bf16[512,1024]{1,0:T(8,128)(2,1)} collective-permute-done((bf16[512,1024]{1,0:T(8,128)(2,1)}, bf16[512,1024]{1,0:T(8,128)(2,1)}, u32[]{:S(2)}, u32[]{:S(2)}) %collective-permute-start.39) | collective-permute-done | bytes 1048608 | tf_op jit(solution)/shard_map/ppermute | solution.py:1023
  375.0 2.1 broadcast_select_fusion.1.bo_ref.dy_ref
  377.2 2.6 collective-permute-done.44.bx_ref
  379.9 3.2 shard_map.182
  384.7 25.1 %shard_map.183 = (f32[512,1024]{1,0:T(8,128)}, bf16[512,1024]{1,0:T(8,128)(2,1)}, bf16[512,1024]{1,0:T(8,128)(2,1)}, bf16[512,1408]{1,0:T(8,128)(2,1)}, bf16[512...) custom-call(bf16[512,1024]{1,0:T(8,128)(2,1)} %copy-done.2, ...), custom_call_target="tpu_custom_call" | custom-call | flops 9730785280 | bytes 27394048 | tf_op jit(solution)/shard_map/pallas_call | solution.py:512
  409.8 6.3 %collective-permute-done.45 = bf16[4,688,256]{2,1,0:T(8,128)(2,1)S(1)} collective-permute-done((bf16[4,688,256]{2,1,0:T(8,128)(2,1)S(1)}, bf16[4,688,256]{2,1,0:T(8,128)(2,1)S(1)}, u32[]{:S(2)}, u32[]{:S(2)}) %collective-permute-start.45) | collective-permute-done | bytes 1409056 | tf_op jit(solution)/shard_map/ppermute | solution.py:751
  417.1 6.0 collective-permute-done.49.bx_ref
  425.7 4.3 shard_map.184
  433.5 4.3 shard_map.186
  437.8 4.8 collective-permute-done.50
  443.8 3.9 collective-permute-start.54
  448.4 26.6 %shard_map.187 = (bf16[512,1024]{1,0:T(8,128)(2,1)}, bf16[512,1024]{1,0:T(8,128)(2,1)}, bf16[512,1024]{1,0:T(8,128)(2,1)}, bf16[512,1024]{1,0:T(8,128)(2,1)}, bf...) custom-call(bf16[512,1024]{1,0:T(8,128)(2,1)} %get-tuple-element.284.q_ref, bf16[512,1024]{1,0:T(8,128)(2,1)} %get-tuple-element.285.ko_ref, ...), custom_call_target="tpu_custom_call" | custom-call | flops 10737418240 | bytes 20971520 | tf_op jit(solution)/shard_map/pallas_call | solution.py:614
  477.0 2.3 fusion.24
  479.3 3.3 collective-permute-start.57
  484.6 16.3 %shard_map.188 = (bf16[2,512,768]{2,1,0:T(8,128)(2,1)}, bf16[2,512,768]{2,1,0:T(8,128)(2,1)}, f32[512,1024]{1,0:T(8,128)}, bf16[512,1024]{1,0:T(8,128)(2,1)}, f32[1,1024]{1,0:T(1,128)}) custom-call(bf16[512,1024]{1,0:T(8,128)(2,1)} %get-tuple-element.365.dq_ref, bf16[512,1024]{1,0:T(8,128)(2,1)} %get-tuple-element.366.dk_ref, ...), custom_call_target="tpu_custom_call" | custom-call | flops 3221225472 | bytes 27262976 | tf_op jit(solution)/shard_map/pallas_call | solution.py:697
  500.8 8.6 %collective-permute-done.51 = bf16[4,688,256]{2,1,0:T(8,128)(2,1)} collective-permute-done((bf16[4,688,256]{2,1,0:T(8,128)(2,1)}, bf16[4,688,256]{2,1,0:T(8,128)(2,1)}, u32[]{:S(2)}, u32[]{:S(2)}) %collective-permute-start.51) | collective-permute-done | bytes 1409056 | tf_op jit(solution)/shard_map/ppermute | solution.py:751
  509.4 5.7 collective-permute-done.58
  515.2 1.6 fusion.44
  525.3 2.1 collective-permute-start.68
  527.4 4.9 shard_map.189
  532.3 8.5 %collective-permute-done.67 = bf16[336,256]{1,0:T(8,128)(2,1)S(1)} collective-permute-done((bf16[336,256]{1,0:T(8,128)(2,1)S(1)}, bf16[336,256]{1,0:T(8,128)(2,1)S(1)}, u32[]{:S(2)}, u32[]{:S(2)}) %collective-permute-start.67) | collective-permute-done | bytes 172064 | tf_op jit(solution)/shard_map/ppermute | solution.py:779
  544.8 1.8 collective-permute-start.72
  546.6 1.9 collective-permute-start.73
  548.5 11.7 %collective-permute-done.70 = f32[3,1024]{1,0:T(4,128)S(1)} collective-permute-done((f32[3,1024]{1,0:T(4,128)S(1)}, f32[3,1024]{1,0:T(4,128)S(1)}, u32[]{:S(2)}, u32[]{:S(2)}) %collective-permute-start.70) | collective-permute-done | bytes 12320 | tf_op jit(solution)/shard_map/ppermute | solution.py:751
  563.6 1.9 collective-permute-start.78
  567.9 7.2 %collective-permute-done.75 = f32[3,1024]{1,0:T(4,128)S(1)} collective-permute-done((f32[3,1024]{1,0:T(4,128)S(1)}, f32[3,1024]{1,0:T(4,128)S(1)}, u32[]{:S(2)}, u32[]{:S(2)}) %collective-permute-start.75) | collective-permute-done | bytes 12320 | tf_op jit(solution)/shard_map/ppermute | solution.py:1102
  575.1 3.0 collective-permute-done.74
  578.1 2.8 collective-permute-done.77
  583.3 2.1 fusion.5
  586.7 1.6 fusion.8
  592.0 2.8 collective-permute-start.80
  596.2 4.1 collective-permute-done.82
  600.3 7.2 %collective-permute-done.81 = bf16[384,256]{1,0:T(8,128)(2,1)S(1)} collective-permute-done((bf16[384,256]{1,0:T(8,128)(2,1)}, bf16[384,256]{1,0:T(8,128)(2,1)S(1)}, u32[]{:S(2)}, u32[]{:S(2)}) %collective-permute-start.81) | collective-permute-done | bytes 196640 | tf_op jit(solution)/shard_map/ppermute | solution.py:779
  (428 shorter events, 103.9 us)
Async XLA Ops:
  4.3 18.2 %collective-permute-start = (bf16[1040,256]{1,0:T(8,128)(2,1)S(1)}, bf16[1040,256]{1,0:T(8,128)(2,1)S(1)}, u32[]{:S(2)}, u32[]{:S(2)}) collective-permute-start(bf16[1040,256]{1,0:T(8,128)(2,1)S(1)} %fusion.12), channel_id=1, source_target_pairs={{0,4},{4,8},{8,12},{12,0},{1,5},{5,9},{9,13},{13,1},{2,6},{6,10},{... | collective-permute-start | bytes 1597448 | tf_op jit(solution)/shard_map/ppermute | solution.py:756
  9.1 13.4 %collective-permute-start.1 = (bf16[256,1024]{1,0:T(8,128)(2,1)S(1)}, bf16[256,1024]{1,0:T(8,128)(2,1)S(1)}, u32[]{:S(2)}, u32[]{:S(2)}) collective-permute-start(bf16[256,1024]{1,0:T(8,128)(2,1)S(1)} %get-tuple-element.459), channel_id=1, source_target_pairs={{0,2},{1,3},{2,0},{3,1},{4,6},{5,7},{6,4},{7,5},{8,10},{9,11},{10,... | collective-permute-start | bytes 1572872 | tf_op jit(solution)/shard_map/ppermute | solution.py:751
  22.6 14.4 %collective-permute-start.2 = (bf16[1040,256]{1,0:T(8,128)(2,1)S(1)}, bf16[1040,256]{1,0:T(8,128)(2,1)S(1)}, u32[]{:S(2)}, u32[]{:S(2)}) collective-permute-start(bf16[1040,256]{1,0:T(8,128)(2,1)S(1)} %collective-permute-done), channel_id=1, source_target_pairs={{0,4},{4,8},{8,12},{12,0},{1,5},{5,9},{9,13},{13,1},{2,6},{6,10},{... | collective-permute-start | bytes 1597448 | tf_op jit(solution)/shard_map/ppermute | solution.py:756
  24.1 12.9 %collective-permute-start.3 = (bf16[1040,256]{1,0:T(8,128)(2,1)S(1)}, bf16[1040,256]{1,0:T(8,128)(2,1)S(1)}, u32[]{:S(2)}, u32[]{:S(2)}) collective-permute-start(bf16[1040,256]{1,0:T(8,128)(2,1)S(1)} %fusion.12), channel_id=1, source_target_pairs={{0,2},{1,3},{2,0},{3,1},{4,6},{5,7},{6,4},{7,5},{8,10},{9,11},{10,... | collective-permute-start | bytes 1597448 | tf_op jit(solution)/shard_map/ppermute | solution.py:751
  37.0 13.7 %collective-permute-start.4 = (bf16[1040,256]{1,0:T(8,128)(2,1)S(1)}, bf16[1040,256]{1,0:T(8,128)(2,1)}, u32[]{:S(2)}, u32[]{:S(2)}) collective-permute-start(bf16[1040,256]{1,0:T(8,128)(2,1)S(1)} %collective-permute-done.2), channel_id=1, source_target_pairs={{0,4},{4,8},{8,12},{12,0},{1,5},{5,9},{9,13},{13,1},{2,6},{6,10},{... | collective-permute-start | bytes 1597448 | tf_op jit(solution)/shard_map/ppermute | solution.py:756
  38.1 12.6 %collective-permute-start.5 = (bf16[1040,256]{1,0:T(8,128)(2,1)S(1)}, bf16[1040,256]{1,0:T(8,128)(2,1)}, u32[]{:S(2)}, u32[]{:S(2)}) collective-permute-start(bf16[1040,256]{1,0:T(8,128)(2,1)S(1)} %collective-permute-done), channel_id=1, source_target_pairs={{0,2},{1,3},{2,0},{3,1},{4,6},{5,7},{6,4},{7,5},{8,10},{9,11},{10,... | collective-permute-start | bytes 1597448 | tf_op jit(solution)/shard_map/ppermute | solution.py:751
  50.7 16.5 %collective-permute-start.6 = (bf16[1376,256]{1,0:T(8,128)(2,1)}, bf16[1376,256]{1,0:T(8,128)(2,1)S(1)}, u32[]{:S(2)}, u32[]{:S(2)}) collective-permute-start(bf16[1376,256]{1,0:T(8,128)(2,1)} %bitcast.8), channel_id=1, source_target_pairs={{0,4},{4,8},{8,12},{12,0},{1,5},{5,9},{9,13},{13,1},{2,6},{6,10},{... | collective-permute-start | bytes 2113544 | tf_op jit(solution)/shard_map/ppermute | solution.py:756
  50.8 14.4 %collective-permute-start.7 = (bf16[1040,256]{1,0:T(8,128)(2,1)S(1)}, bf16[1040,256]{1,0:T(8,128)(2,1)S(1)}, u32[]{:S(2)}, u32[]{:S(2)}) collective-permute-start(bf16[1040,256]{1,0:T(8,128)(2,1)S(1)} %collective-permute-done.2), channel_id=1, source_target_pairs={{0,2},{1,3},{2,0},{3,1},{4,6},{5,7},{6,4},{7,5},{8,10},{9,11},{10,... | collective-permute-start | bytes 1597448 | tf_op jit(solution)/shard_map/ppermute | solution.py:751
  52.2 13.0 %collective-permute-start.8 = (bf16[336,256]{1,0:T(8,128)(2,1)S(1)}, bf16[336,256]{1,0:T(8,128)(2,1)S(1)}, u32[]{:S(2)}, u32[]{:S(2)}) collective-permute-start(bf16[336,256]{1,0:T(8,128)(2,1)S(1)} %slice.255), channel_id=1, source_target_pairs={{0,2},{1,3},{2,0},{3,1},{4,6},{5,7},{6,4},{7,5},{8,10},{9,11},{10,... | collective-permute-start | bytes 516104 | tf_op jit(solution)/shard_map/ppermute | solution.py:751
  67.2 15.7 %collective-permute-start.9 = (bf16[1376,256]{1,0:T(8,128)(2,1)S(1)}, bf16[1376,256]{1,0:T(8,128)(2,1)}, u32[]{:S(2)}, u32[]{:S(2)}) collective-permute-start(bf16[1376,256]{1,0:T(8,128)(2,1)S(1)} %collective-permute-done.6), channel_id=1, source_target_pairs={{0,4},{4,8},{8,12},{12,0},{1,5},{5,9},{9,13},{13,1},{2,6},{6,10},{... | collective-permute-start | bytes 2113544 | tf_op jit(solution)/shard_map/ppermute | solution.py:756
  67.2 14.0 %collective-permute-start.10 = (bf16[1040,256]{1,0:T(8,128)(2,1)}, bf16[1040,256]{1,0:T(8,128)(2,1)}, u32[]{:S(2)}, u32[]{:S(2)}) collective-permute-start(bf16[1040,256]{1,0:T(8,128)(2,1)} %collective-permute-done.4), channel_id=1, source_target_pairs={{0,2},{1,3},{2,0},{3,1},{4,6},{5,7},{6,4},{7,5},{8,10},{9,11},{10,... | collective-permute-start | bytes 1597448 | tf_op jit(solution)/shard_map/ppermute | solution.py:751
  70.0 11.2 %collective-permute-start.11 = (bf16[352,256]{1,0:T(8,128)(2,1)S(1)}, bf16[352,256]{1,0:T(8,128)(2,1)S(1)}, u32[]{:S(2)}, u32[]{:S(2)}) collective-permute-start(bf16[352,256]{1,0:T(8,128)(2,1)S(1)} %slice.256), channel_id=1, source_target_pairs={{0,2},{1,3},{2,0},{3,1},{4,6},{5,7},{6,4},{7,5},{8,10},{9,11},{10,... | collective-permute-start | bytes 540680 | tf_op jit(solution)/shard_map/ppermute | solution.py:751
  70.7 33.6 %collective-permute-start.16 = (bf16[2,1040,256]{2,1,0:T(8,128)(2,1)S(1)}, bf16[2,1040,256]{2,1,0:T(8,128)(2,1)}, u32[]{:S(2)}, u32[]{:S(2)}) collective-permute-start(bf16[2,1040,256]{2,1,0:T(8,128)(2,1)S(1)} %pad_maximum_fusion.4.refs_0_), channel_id=1, source_target_pairs={{0,1},{1,0},{2,3},{3,2},{4,5},{5,4},{6,7},{7,6},{8,9},{9,8},{10,11... | collective-permute-start | bytes 3194888 | tf_op jit(solution)/shard_map/ppermute | solution.py:746
  82.9 14.7 %collective-permute-start.12 = (bf16[1376,256]{1,0:T(8,128)(2,1)}, bf16[1376,256]{1,0:T(8,128)(2,1)S(1)}, u32[]{:S(2)}, u32[]{:S(2)}) collective-permute-start(bf16[1376,256]{1,0:T(8,128)(2,1)} %collective-permute-done.9), channel_id=1, source_target_pairs={{0,4},{4,8},{8,12},{12,0},{1,5},{5,9},{9,13},{13,1},{2,6},{6,10},{... | collective-permute-start | bytes 2113544 | tf_op jit(solution)/shard_map/ppermute | solution.py:756
  84.1 22.4 %collective-permute-start.17 = (bf16[2,1040,256]{2,1,0:T(8,128)(2,1)S(1)}, bf16[2,1040,256]{2,1,0:T(8,128)(2,1)}, u32[]{:S(2)}, u32[]{:S(2)}) collective-permute-start(bf16[2,1040,256]{2,1,0:T(8,128)(2,1)S(1)} %pad_maximum_fusion.5.refs_1_), channel_id=1, source_target_pairs={{0,1},{1,0},{2,3},{3,2},{4,5},{5,4},{6,7},{7,6},{8,9},{9,8},{10,11... | collective-permute-start | bytes 3194888 | tf_op jit(solution)/shard_map/ppermute | solution.py:746
  84.3 22.2 %collective-permute-start.18 = (bf16[2,1040,256]{2,1,0:T(8,128)(2,1)S(1)}, bf16[2,1040,256]{2,1,0:T(8,128)(2,1)}, u32[]{:S(2)}, u32[]{:S(2)}) collective-permute-start(bf16[2,1040,256]{2,1,0:T(8,128)(2,1)S(1)} %pad_maximum_fusion.6.refs_2_), channel_id=1, source_target_pairs={{0,1},{1,0},{2,3},{3,2},{4,5},{5,4},{6,7},{7,6},{8,9},{9,8},{10,11... | collective-permute-start | bytes 3194888 | tf_op jit(solution)/shard_map/ppermute | solution.py:746
  84.9 18.1 %collective-permute-start.13 = (bf16[1376,256]{1,0:T(8,128)(2,1)}, bf16[1376,256]{1,0:T(8,128)(2,1)}, u32[]{:S(2)}, u32[]{:S(2)}) collective-permute-start(bf16[1376,256]{1,0:T(8,128)(2,1)} %bitcast.8), channel_id=1, source_target_pairs={{0,2},{1,3},{2,0},{3,1},{4,6},{5,7},{6,4},{7,5},{8,10},{9,11},{10,... | collective-permute-start | bytes 2113544 | tf_op jit(solution)/shard_map/ppermute | solution.py:751
  103.1 20.0 %collective-permute-start.14 = (bf16[2,688,256]{2,1,0:T(8,128)(2,1)S(1)}, bf16[2,688,256]{2,1,0:T(8,128)(2,1)S(1)}, u32[]{:S(2)}, u32[]{:S(2)}) collective-permute-start(bf16[2,688,256]{2,1,0:T(8,128)(2,1)S(1)} %pad_maximum_fusion.9.refs_0_.refs_16_), channel_id=1, source_target_pairs={{0,4},{4,8},{8,12},{12,0},{1,5},{5,9},{9,13},{13,1},{2,6},{6,10},{... | collective-permute-start | bytes 2113544 | tf_op jit(solution)/shard_map/ppermute | solution.py:756
  104.3 18.7 %collective-permute-start.15 = (bf16[1376,256]{1,0:T(8,128)(2,1)S(1)}, bf16[1376,256]{1,0:T(8,128)(2,1)S(1)}, u32[]{:S(2)}, u32[]{:S(2)}) collective-permute-start(bf16[1376,256]{1,0:T(8,128)(2,1)S(1)} %copy-done.49), channel_id=1, source_target_pairs={{0,2},{1,3},{2,0},{3,1},{4,6},{5,7},{6,4},{7,5},{8,10},{9,11},{10,... | collective-permute-start | bytes 2113544 | tf_op jit(solution)/shard_map/ppermute | solution.py:751
  124.7 19.5 %collective-permute-start.20 = (bf16[2,688,256]{2,1,0:T(8,128)(2,1)}, bf16[2,688,256]{2,1,0:T(8,128)(2,1)S(1)}, u32[]{:S(2)}, u32[]{:S(2)}) collective-permute-start(bf16[2,688,256]{2,1,0:T(8,128)(2,1)} %copy-done.29), channel_id=1, source_target_pairs={{0,4},{4,8},{8,12},{12,0},{1,5},{5,9},{9,13},{13,1},{2,6},{6,10},{... | collective-permute-start | bytes 2113544 | tf_op jit(solution)/shard_map/ppermute | solution.py:756
  124.7 19.5 %collective-permute-start.21 = (bf16[1376,256]{1,0:T(8,128)(2,1)}, bf16[1376,256]{1,0:T(8,128)(2,1)S(1)}, u32[]{:S(2)}, u32[]{:S(2)}) collective-permute-start(bf16[1376,256]{1,0:T(8,128)(2,1)} %collective-permute-done.9), channel_id=1, source_target_pairs={{0,2},{1,3},{2,0},{3,1},{4,6},{5,7},{6,4},{7,5},{8,10},{9,11},{10,... | collective-permute-start | bytes 2113544 | tf_op jit(solution)/shard_map/ppermute | solution.py:751
  144.2 18.9 %collective-permute-start.24 = (bf16[2,688,256]{2,1,0:T(8,128)(2,1)S(1)}, bf16[2,688,256]{2,1,0:T(8,128)(2,1)S(1)}, u32[]{:S(2)}, u32[]{:S(2)}) collective-permute-start(bf16[2,688,256]{2,1,0:T(8,128)(2,1)S(1)} %collective-permute-done.20.refs_2_.refs_18_), channel_id=1, source_target_pairs={{0,4},{4,8},{8,12},{12,0},{1,5},{5,9},{9,13},{13,1},{2,6},{6,10},{... | collective-permute-start | bytes 2113544 | tf_op jit(solution)/shard_map/ppermute | solution.py:756
  145.3 17.7 %collective-permute-start.25 = (bf16[1376,256]{1,0:T(8,128)(2,1)S(1)}, bf16[1376,256]{1,0:T(8,128)(2,1)S(1)}, u32[]{:S(2)}, u32[]{:S(2)}) collective-permute-start(bf16[1376,256]{1,0:T(8,128)(2,1)S(1)} %copy-done.52), channel_id=1, source_target_pairs={{0,2},{1,3},{2,0},{3,1},{4,6},{5,7},{6,4},{7,5},{8,10},{9,11},{10,... | collective-permute-start | bytes 2113544 | tf_op jit(solution)/shard_map/ppermute | solution.py:751
  147.8 16.9 %collective-permute-start.26 = (bf16[2,1376,256]{2,1,0:T(8,128)(2,1)S(1)}, bf16[2,1376,256]{2,1,0:T(8,128)(2,1)S(1)}, u32[]{:S(2)}, u32[]{:S(2)}) collective-permute-start(bf16[2,1376,256]{2,1,0:T(8,128)(2,1)S(1)} %pad_maximum_fusion.refs_8_), channel_id=1, source_target_pairs={{0,1},{1,0},{2,3},{3,2},{4,5},{5,4},{6,7},{7,6},{8,9},{9,8},{10,11... | collective-permute-start | bytes 4227080 | tf_op jit(solution)/shard_map/ppermute | solution.py:746
  148.8 16.4 %collective-permute-start.27 = (bf16[2,1376,256]{2,1,0:T(8,128)(2,1)S(1)}, bf16[2,1376,256]{2,1,0:T(8,128)(2,1)S(1)}, u32[]{:S(2)}, u32[]{:S(2)}) collective-permute-start(bf16[2,1376,256]{2,1,0:T(8,128)(2,1)S(1)} %pad_maximum_fusion.1.refs_9_), channel_id=1, source_target_pairs={{0,1},{1,0},{2,3},{3,2},{4,5},{5,4},{6,7},{7,6},{8,9},{9,8},{10,11... | collective-permute-start | bytes 4227080 | tf_op jit(solution)/shard_map/ppermute | solution.py:746
  150.6 14.7 %collective-permute-start.28 = (bf16[2,1376,256]{2,1,0:T(8,128)(2,1)S(1)}, bf16[2,1376,256]{2,1,0:T(8,128)(2,1)S(1)}, u32[]{:S(2)}, u32[]{:S(2)}) collective-permute-start(bf16[2,1376,256]{2,1,0:T(8,128)(2,1)S(1)} %pad_maximum_fusion.2.refs_10_), channel_id=1, source_target_pairs={{0,1},{1,0},{2,3},{3,2},{4,5},{5,4},{6,7},{7,6},{8,9},{9,8},{10,11... | collective-permute-start | bytes 4227080 | tf_op jit(solution)/shard_map/ppermute | solution.py:746
  164.7 19.7 %collective-permute-start.30 = (bf16[2,688,256]{2,1,0:T(8,128)(2,1)S(1)}, bf16[2,688,256]{2,1,0:T(8,128)(2,1)S(1)}, u32[]{:S(2)}, u32[]{:S(2)}) collective-permute-start(bf16[2,688,256]{2,1,0:T(8,128)(2,1)S(1)} %copy-done.26), channel_id=1, source_target_pairs={{0,1},{1,0},{2,3},{3,2},{4,5},{5,4},{6,7},{7,6},{8,9},{9,8},{10,11... | collective-permute-start | bytes 2113544 | tf_op jit(solution)/shard_map/ppermute | solution.py:746
  164.7 19.7 %collective-permute-start.32 = (bf16[2,688,256]{2,1,0:T(8,128)(2,1)S(1)}, bf16[2,688,256]{2,1,0:T(8,128)(2,1)S(1)}, u32[]{:S(2)}, u32[]{:S(2)}) collective-permute-start(bf16[2,688,256]{2,1,0:T(8,128)(2,1)S(1)} %collective-permute-done.20.refs_2_.refs_18_), channel_id=1, source_target_pairs={{0,1},{1,0},{2,3},{3,2},{4,5},{5,4},{6,7},{7,6},{8,9},{9,8},{10,11... | collective-permute-start | bytes 2113544 | tf_op jit(solution)/shard_map/ppermute | solution.py:746
  165.2 19.2 %collective-permute-start.31 = (bf16[2,688,256]{2,1,0:T(8,128)(2,1)S(1)}, bf16[2,688,256]{2,1,0:T(8,128)(2,1)S(1)}, u32[]{:S(2)}, u32[]{:S(2)}) collective-permute-start(bf16[2,688,256]{2,1,0:T(8,128)(2,1)S(1)} %copy-done.30), channel_id=1, source_target_pairs={{0,1},{1,0},{2,3},{3,2},{4,5},{5,4},{6,7},{7,6},{8,9},{9,8},{10,11... | collective-permute-start | bytes 2113544 | tf_op jit(solution)/shard_map/ppermute | solution.py:746
  165.3 19.1 %collective-permute-start.33 = (bf16[2,688,256]{2,1,0:T(8,128)(2,1)S(1)}, bf16[2,688,256]{2,1,0:T(8,128)(2,1)S(1)}, u32[]{:S(2)}, u32[]{:S(2)}) collective-permute-start(bf16[2,688,256]{2,1,0:T(8,128)(2,1)S(1)} %collective-permute-done.24.refs_3_.refs_19_), channel_id=1, source_target_pairs={{0,1},{1,0},{2,3},{3,2},{4,5},{5,4},{6,7},{7,6},{8,9},{9,8},{10,11... | collective-permute-start | bytes 2113544 | tf_op jit(solution)/shard_map/ppermute | solution.py:746
  195.6 26.4 %collective-permute-start.34 = (bf16[512,1024]{1,0:T(8,128)(2,1)}, bf16[512,1024]{1,0:T(8,128)(2,1)S(1)}, u32[]{:S(2)}, u32[]{:S(2)}) collective-permute-start(bf16[512,1024]{1,0:T(8,128)(2,1)} %shard_map.174), channel_id=1, source_target_pairs={{0,16},{1,17},{2,18},{3,19},{4,20},{5,21},{6,22},{7,23},{8,24},{9,... | collective-permute-start | bytes 3145736 | tf_op jit(solution)/shard_map/ppermute | solution.py:1003
  347.1 27.9 %collective-permute-start.40 = (bf16[512,1408]{1,0:T(8,128)(2,1)}, bf16[512,1408]{1,0:T(8,128)(2,1)S(1)}, u32[]{:S(2)}, u32[]{:S(2)}) collective-permute-start(bf16[512,1408]{1,0:T(8,128)(2,1)} %get-tuple-element.309.zf_ref), channel_id=1, source_target_pairs={{0,1},{1,0},{2,3},{3,2},{4,5},{5,4},{6,7},{7,6},{8,9},{9,8},{10,11... | collective-permute-start | bytes 4325384 | tf_op jit(solution)/shard_map/ppermute | solution.py:746
  347.3 27.6 %collective-permute-start.39 = (bf16[512,1024]{1,0:T(8,128)(2,1)}, bf16[512,1024]{1,0:T(8,128)(2,1)}, u32[]{:S(2)}, u32[]{:S(2)}) collective-permute-start(bf16[512,1024]{1,0:T(8,128)(2,1)} %get-tuple-element.307), channel_id=1, source_target_pairs={{16,0},{17,1},{18,2},{19,3},{20,4},{21,5},{22,6},{23,7},{24,8},{25... | collective-permute-start | bytes 3145736 | tf_op jit(solution)/shard_map/ppermute | solution.py:1023
  348.6 26.4 %collective-permute-start.41 = (bf16[512,1024]{1,0:T(8,128)(2,1)S(1)}, bf16[512,1024]{1,0:T(8,128)(2,1)S(1)}, u32[]{:S(2)}, u32[]{:S(2)}) collective-permute-start(bf16[512,1024]{1,0:T(8,128)(2,1)S(1)} %copy-done.10), channel_id=1, source_target_pairs={{0,1},{1,0},{2,3},{3,2},{4,5},{5,4},{6,7},{7,6},{8,9},{9,8},{10,11... | collective-permute-start | bytes 3145736 | tf_op jit(solution)/shard_map/ppermute | solution.py:746
  349.1 25.9 %collective-permute-start.42 = (bf16[512,1024]{1,0:T(8,128)(2,1)S(1)}, bf16[512,1024]{1,0:T(8,128)(2,1)S(1)}, u32[]{:S(2)}, u32[]{:S(2)}) collective-permute-start(bf16[512,1024]{1,0:T(8,128)(2,1)S(1)} %copy-done.6), channel_id=1, source_target_pairs={{0,1},{1,0},{2,3},{3,2},{4,5},{5,4},{6,7},{7,6},{8,9},{9,8},{10,11... | collective-permute-start | bytes 3145736 | tf_op jit(solution)/shard_map/ppermute | solution.py:746
  349.2 10.3 %collective-permute-start.43 = (bf16[512,512]{1,0:T(8,128)(2,1)S(1)}, bf16[512,512]{1,0:T(8,128)(2,1)S(1)}, u32[]{:S(2)}, u32[]{:S(2)}) collective-permute-start(bf16[512,512]{1,0:T(8,128)(2,1)S(1)} %slice.269), channel_id=1, source_target_pairs={{0,1},{1,0},{2,3},{3,2},{4,5},{5,4},{6,7},{7,6},{8,9},{9,8},{10,11... | collective-permute-start | bytes 1572872 | tf_op jit(solution)/shard_map/ppermute | solution.py:746
  383.1 33.0 %collective-permute-start.45 = (bf16[4,688,256]{2,1,0:T(8,128)(2,1)S(1)}, bf16[4,688,256]{2,1,0:T(8,128)(2,1)S(1)}, u32[]{:S(2)}, u32[]{:S(2)}) collective-permute-start(bf16[4,688,256]{2,1,0:T(8,128)(2,1)S(1)} %get-tuple-element.318), channel_id=1, source_target_pairs={{0,2},{1,3},{2,0},{3,1},{4,6},{5,7},{6,4},{7,5},{8,10},{9,11},{10,... | collective-permute-start | bytes 4227080 | tf_op jit(solution)/shard_map/ppermute | solution.py:751
  416.7 13.3 %collective-permute-start.46 = (bf16[688,256]{1,0:T(8,128)(2,1)S(1)}, bf16[688,256]{1,0:T(8,128)(2,1)S(1)}, u32[]{:S(2)}, u32[]{:S(2)}) collective-permute-start(bf16[688,256]{1,0:T(8,128)(2,1)S(1)} %fusion.19), channel_id=1, source_target_pairs={{0,4},{4,8},{8,12},{12,0},{1,5},{5,9},{9,13},{13,1},{2,6},{6,10},{... | collective-permute-start | bytes 1056776 | tf_op jit(solution)/shard_map/ppermute | solution.py:756
  430.2 12.3 %collective-permute-start.50 = (bf16[688,256]{1,0:T(8,128)(2,1)S(1)}, bf16[688,256]{1,0:T(8,128)(2,1)S(1)}, u32[]{:S(2)}, u32[]{:S(2)}) collective-permute-start(bf16[688,256]{1,0:T(8,128)(2,1)S(1)} %fusion.10), channel_id=1, source_target_pairs={{0,4},{4,8},{8,12},{12,0},{1,5},{5,9},{9,13},{13,1},{2,6},{6,10},{... | collective-permute-start | bytes 1056776 | tf_op jit(solution)/shard_map/ppermute | solution.py:756
  430.7 45.0 %collective-permute-start.52 = (bf16[4,688,256]{2,1,0:T(8,128)(2,1)}, bf16[4,688,256]{2,1,0:T(8,128)(2,1)}, u32[]{:S(2)}, u32[]{:S(2)}) collective-permute-start(bf16[4,688,256]{2,1,0:T(8,128)(2,1)} %get-tuple-element.353), channel_id=1, source_target_pairs={{0,2},{1,3},{2,0},{3,1},{4,6},{5,7},{6,4},{7,5},{8,10},{9,11},{10,... | collective-permute-start | bytes 4227080 | tf_op jit(solution)/shard_map/ppermute | solution.py:751
  443.6 32.1 %collective-permute-start.53 = (bf16[688,256]{1,0:T(8,128)(2,1)S(1)}, bf16[688,256]{1,0:T(8,128)(2,1)S(1)}, u32[]{:S(2)}, u32[]{:S(2)}) collective-permute-start(bf16[688,256]{1,0:T(8,128)(2,1)S(1)} %fusion.9), channel_id=1, source_target_pairs={{0,4},{4,8},{8,12},{12,0},{1,5},{5,9},{9,13},{13,1},{2,6},{6,10},{... | collective-permute-start | bytes 1056776 | tf_op jit(solution)/shard_map/ppermute | solution.py:756
  443.8 31.2 %collective-permute-start.54 = (bf16[2,256,256]{2,1,0:T(8,128)(2,1)S(1)}, bf16[2,256,256]{2,1,0:T(8,128)(2,1)S(1)}, u32[]{:S(2)}, u32[]{:S(2)}) collective-permute-start(bf16[2,256,256]{2,1,0:T(8,128)(2,1)S(1)} %pad_maximum_fusion.13), channel_id=1, source_target_pairs={{0,12},{4,0},{8,4},{12,8},{1,13},{5,1},{9,5},{13,9},{2,14},{6,2},{... | collective-permute-start | bytes 786440 | tf_op jit(solution)/shard_map/ppermute | solution.py:779
  447.7 28.0 %collective-permute-start.55 = (bf16[2,256,256]{2,1,0:T(8,128)(2,1)S(1)}, bf16[2,256,256]{2,1,0:T(8,128)(2,1)S(1)}, u32[]{:S(2)}, u32[]{:S(2)}) collective-permute-start(bf16[2,256,256]{2,1,0:T(8,128)(2,1)S(1)} %pad_maximum_fusion.14), channel_id=1, source_target_pairs={{0,8},{4,12},{8,0},{12,4},{1,9},{5,13},{9,1},{13,5},{2,10},{6,14},... | collective-permute-start | bytes 786440 | tf_op jit(solution)/shard_map/ppermute | solution.py:779
  447.8 27.9 %collective-permute-start.56 = (bf16[2,256,256]{2,1,0:T(8,128)(2,1)S(1)}, bf16[2,256,256]{2,1,0:T(8,128)(2,1)S(1)}, u32[]{:S(2)}, u32[]{:S(2)}) collective-permute-start(bf16[2,256,256]{2,1,0:T(8,128)(2,1)S(1)} %pad_maximum_fusion.15), channel_id=1, source_target_pairs={{0,4},{4,8},{8,12},{12,0},{1,5},{5,9},{9,13},{13,1},{2,6},{6,10},{... | collective-permute-start | bytes 786440 | tf_op jit(solution)/shard_map/ppermute | solution.py:779
  475.8 33.6 %collective-permute-start.51 = (bf16[4,688,256]{2,1,0:T(8,128)(2,1)}, bf16[4,688,256]{2,1,0:T(8,128)(2,1)}, u32[]{:S(2)}, u32[]{:S(2)}) collective-permute-start(bf16[4,688,256]{2,1,0:T(8,128)(2,1)} %get-tuple-element.351), channel_id=1, source_target_pairs={{0,2},{1,3},{2,0},{3,1},{4,6},{5,7},{6,4},{7,5},{8,10},{9,11},{10,... | collective-permute-start | bytes 4227080 | tf_op jit(solution)/shard_map/ppermute | solution.py:751
  479.3 30.2 %collective-permute-start.57 = (bf16[688,256]{1,0:T(8,128)(2,1)}, bf16[688,256]{1,0:T(8,128)(2,1)}, u32[]{:S(2)}, u32[]{:S(2)}) collective-permute-start(bf16[688,256]{1,0:T(8,128)(2,1)} %get-tuple-element.450), channel_id=1, source_target_pairs={{0,12},{4,0},{8,4},{12,8},{1,13},{5,1},{9,5},{13,9},{2,14},{6,2},{... | collective-permute-start | bytes 1056776 | tf_op jit(solution)/shard_map/ppermute | solution.py:779
  482.6 32.5 %collective-permute-start.58 = (bf16[688,256]{1,0:T(8,128)(2,1)}, bf16[688,256]{1,0:T(8,128)(2,1)}, u32[]{:S(2)}, u32[]{:S(2)}) collective-permute-start(bf16[688,256]{1,0:T(8,128)(2,1)} %get-tuple-element.449), channel_id=1, source_target_pairs={{0,8},{4,12},{8,0},{12,4},{1,9},{5,13},{9,1},{13,5},{2,10},{6,14},... | collective-permute-start | bytes 1056776 | tf_op jit(solution)/shard_map/ppermute | solution.py:779
  483.7 31.4 %collective-permute-start.59 = (bf16[688,256]{1,0:T(8,128)(2,1)}, bf16[688,256]{1,0:T(8,128)(2,1)}, u32[]{:S(2)}, u32[]{:S(2)}) collective-permute-start(bf16[688,256]{1,0:T(8,128)(2,1)} %get-tuple-element.448), channel_id=1, source_target_pairs={{0,4},{4,8},{8,12},{12,0},{1,5},{5,9},{9,13},{13,1},{2,6},{6,10},{... | collective-permute-start | bytes 1056776 | tf_op jit(solution)/shard_map/ppermute | solution.py:779
  515.1 10.2 %collective-permute-start.64 = (bf16[2,512,768]{2,1,0:T(8,128)(2,1)}, bf16[2,512,768]{2,1,0:T(8,128)(2,1)}, u32[]{:S(2)}, u32[]{:S(2)}) collective-permute-start(bf16[2,512,768]{2,1,0:T(8,128)(2,1)} %get-tuple-element.387), channel_id=1, source_target_pairs={{0,1},{1,0},{2,3},{3,2},{4,5},{5,4},{6,7},{7,6},{8,9},{9,8},{10,11... | collective-permute-start | bytes 4718600 | tf_op jit(solution)/shard_map/ppermute | solution.py:746
  516.9 15.4 %collective-permute-start.63 = (bf16[256,256]{1,0:T(8,128)(2,1)}, bf16[256,256]{1,0:T(8,128)(2,1)S(1)}, u32[]{:S(2)}, u32[]{:S(2)}) collective-permute-start(bf16[256,256]{1,0:T(8,128)(2,1)} %fusion.44), channel_id=1, source_target_pairs={{0,2},{1,3},{2,0},{3,1},{4,6},{5,7},{6,4},{7,5},{8,10},{9,11},{10,... | collective-permute-start | bytes 393224 | tf_op jit(solution)/shard_map/ppermute | solution.py:751
  522.5 18.3 %collective-permute-start.62 = (bf16[256,1024]{1,0:T(8,128)(2,1)S(1)}, bf16[256,1024]{1,0:T(8,128)(2,1)S(1)}, u32[]{:S(2)}, u32[]{:S(2)}) collective-permute-start(bf16[256,1024]{1,0:T(8,128)(2,1)S(1)} %slice_select_fusion.1), channel_id=1, source_target_pairs={{0,2},{1,3},{2,0},{3,1},{4,6},{5,7},{6,4},{7,5},{8,10},{9,11},{10,... | collective-permute-start | bytes 1572872 | tf_op jit(solution)/shard_map/ppermute | solution.py:751
  524.1 16.7 %collective-permute-start.67 = (bf16[336,256]{1,0:T(8,128)(2,1)S(1)}, bf16[336,256]{1,0:T(8,128)(2,1)S(1)}, u32[]{:S(2)}, u32[]{:S(2)}) collective-permute-start(bf16[336,256]{1,0:T(8,128)(2,1)S(1)} %get-tuple-element.395), channel_id=1, source_target_pairs={{0,8},{4,12},{8,0},{12,4},{1,9},{5,13},{9,1},{13,5},{2,10},{6,14},... | collective-permute-start | bytes 516104 | tf_op jit(solution)/shard_map/ppermute | solution.py:779
  525.3 15.5 %collective-permute-start.68 = (bf16[336,256]{1,0:T(8,128)(2,1)S(1)}, bf16[336,256]{1,0:T(8,128)(2,1)S(1)}, u32[]{:S(2)}, u32[]{:S(2)}) collective-permute-start(bf16[336,256]{1,0:T(8,128)(2,1)S(1)} %get-tuple-element.396), channel_id=1, source_target_pairs={{0,4},{4,8},{8,12},{12,0},{1,5},{5,9},{9,13},{13,1},{2,6},{6,10},{... | collective-permute-start | bytes 516104 | tf_op jit(solution)/shard_map/ppermute | solution.py:779
  540.9 21.5 %collective-permute-start.69 = (bf16[4,384,256]{2,1,0:T(8,128)(2,1)S(1)}, bf16[4,384,256]{2,1,0:T(8,128)(2,1)S(1)}, u32[]{:S(2)}, u32[]{:S(2)}) collective-permute-start(bf16[4,384,256]{2,1,0:T(8,128)(2,1)S(1)} %get-tuple-element.460), channel_id=1, source_target_pairs={{0,2},{1,3},{2,0},{3,1},{4,6},{5,7},{6,4},{7,5},{8,10},{9,11},{10,... | collective-permute-start | bytes 2359304 | tf_op jit(solution)/shard_map/ppermute | solution.py:751
  542.8 17.4 %collective-permute-start.70 = (f32[3,1024]{1,0:T(4,128)S(1)}, f32[3,1024]{1,0:T(4,128)S(1)}, u32[]{:S(2)}, u32[]{:S(2)}) collective-permute-start(f32[3,1024]{1,0:T(4,128)S(1)} %fusion.61), channel_id=1, source_target_pairs={{0,2},{1,3},{2,0},{3,1},{4,6},{5,7},{6,4},{7,5},{8,10},{9,11},{10,... | collective-permute-start | bytes 36872 | tf_op jit(solution)/shard_map/ppermute | solution.py:751
  544.7 16.2 %collective-permute-start.71 = (bf16[352,256]{1,0:T(8,128)(2,1)S(1)}, bf16[352,256]{1,0:T(8,128)(2,1)S(1)}, u32[]{:S(2)}, u32[]{:S(2)}) collective-permute-start(bf16[352,256]{1,0:T(8,128)(2,1)S(1)} %get-tuple-element.443), channel_id=1, source_target_pairs={{0,12},{4,0},{8,4},{12,8},{1,13},{5,1},{9,5},{13,9},{2,14},{6,2},{... | collective-permute-start | bytes 540680 | tf_op jit(solution)/shard_map/ppermute | solution.py:779
  544.8 17.6 %collective-permute-start.72 = (bf16[352,256]{1,0:T(8,128)(2,1)S(1)}, bf16[352,256]{1,0:T(8,128)(2,1)S(1)}, u32[]{:S(2)}, u32[]{:S(2)}) collective-permute-start(bf16[352,256]{1,0:T(8,128)(2,1)S(1)} %get-tuple-element.442), channel_id=1, source_target_pairs={{0,8},{4,12},{8,0},{12,4},{1,9},{5,13},{9,1},{13,5},{2,10},{6,14},... | collective-permute-start | bytes 540680 | tf_op jit(solution)/shard_map/ppermute | solution.py:779
  546.6 15.9 %collective-permute-start.73 = (bf16[352,256]{1,0:T(8,128)(2,1)S(1)}, bf16[352,256]{1,0:T(8,128)(2,1)S(1)}, u32[]{:S(2)}, u32[]{:S(2)}) collective-permute-start(bf16[352,256]{1,0:T(8,128)(2,1)S(1)} %get-tuple-element.441), channel_id=1, source_target_pairs={{0,4},{4,8},{8,12},{12,0},{1,5},{5,9},{9,13},{13,1},{2,6},{6,10},{... | collective-permute-start | bytes 540680 | tf_op jit(solution)/shard_map/ppermute | solution.py:779
  560.2 17.9 %collective-permute-start.74 = (bf16[4,384,256]{2,1,0:T(8,128)(2,1)S(1)}, bf16[4,384,256]{2,1,0:T(8,128)(2,1)S(1)}, u32[]{:S(2)}, u32[]{:S(2)}) collective-permute-start(bf16[4,384,256]{2,1,0:T(8,128)(2,1)S(1)} %get-tuple-element.461), channel_id=1, source_target_pairs={{0,2},{1,3},{2,0},{3,1},{4,6},{5,7},{6,4},{7,5},{8,10},{9,11},{10,... | collective-permute-start | bytes 2359304 | tf_op jit(solution)/shard_map/ppermute | solution.py:751
  562.6 15.5 %collective-permute-start.76 = (bf16[384,256]{1,0:T(8,128)(2,1)S(1)}, bf16[384,256]{1,0:T(8,128)(2,1)S(1)}, u32[]{:S(2)}, u32[]{:S(2)}) collective-permute-start(bf16[384,256]{1,0:T(8,128)(2,1)S(1)} %get-tuple-element.457), channel_id=1, source_target_pairs={{0,12},{4,0},{8,4},{12,8},{1,13},{5,1},{9,5},{13,9},{2,14},{6,2},{... | collective-permute-start | bytes 589832 | tf_op jit(solution)/shard_map/ppermute | solution.py:779
  562.7 18.3 %collective-permute-start.77 = (bf16[384,256]{1,0:T(8,128)(2,1)S(1)}, bf16[384,256]{1,0:T(8,128)(2,1)S(1)}, u32[]{:S(2)}, u32[]{:S(2)}) collective-permute-start(bf16[384,256]{1,0:T(8,128)(2,1)S(1)} %get-tuple-element.456), channel_id=1, source_target_pairs={{0,8},{4,12},{8,0},{12,4},{1,9},{5,13},{9,1},{13,5},{2,10},{6,14},... | collective-permute-start | bytes 589832 | tf_op jit(solution)/shard_map/ppermute | solution.py:779
  563.6 17.3 %collective-permute-start.78 = (bf16[384,256]{1,0:T(8,128)(2,1)S(1)}, bf16[384,256]{1,0:T(8,128)(2,1)S(1)}, u32[]{:S(2)}, u32[]{:S(2)}) collective-permute-start(bf16[384,256]{1,0:T(8,128)(2,1)S(1)} %get-tuple-element.455), channel_id=1, source_target_pairs={{0,4},{4,8},{8,12},{12,0},{1,5},{5,9},{9,13},{13,1},{2,6},{6,10},{... | collective-permute-start | bytes 589832 | tf_op jit(solution)/shard_map/ppermute | solution.py:779
  590.4 17.1 %collective-permute-start.81 = (bf16[384,256]{1,0:T(8,128)(2,1)}, bf16[384,256]{1,0:T(8,128)(2,1)S(1)}, u32[]{:S(2)}, u32[]{:S(2)}) collective-permute-start(bf16[384,256]{1,0:T(8,128)(2,1)} %get-tuple-element.421), channel_id=1, source_target_pairs={{0,8},{4,12},{8,0},{12,4},{1,9},{5,13},{9,1},{13,5},{2,10},{6,14},... | collective-permute-start | bytes 589832 | tf_op jit(solution)/shard_map/ppermute | solution.py:779
  592.0 15.6 %collective-permute-start.80 = (bf16[384,256]{1,0:T(8,128)(2,1)}, bf16[384,256]{1,0:T(8,128)(2,1)S(1)}, u32[]{:S(2)}, u32[]{:S(2)}) collective-permute-start(bf16[384,256]{1,0:T(8,128)(2,1)} %get-tuple-element.420), channel_id=1, source_target_pairs={{0,12},{4,0},{8,4},{12,8},{1,13},{5,1},{9,5},{13,9},{2,14},{6,2},{... | collective-permute-start | bytes 589832 | tf_op jit(solution)/shard_map/ppermute | solution.py:779
  (111 other events, 1111.7 us)

commit v7 on v6

--- a/solution.py
+++ b/solution.py
@@ -409,16 +409,19 @@
 
 
 def ffn_down_kernel(h_ref, zn_ref, zf_ref, zi_ref, *refs):
-    weight, (y_ref, w_ref, sems) = refs[:8], refs[8:]
+    weight, (y_ref, w_ref, sems, acc) = refs[:8], refs[8:]
     pair_start(weight, 1, w_ref, sems)
     for half, z_ref in enumerate((zn_ref, zf_ref)):
         for copy in pair_copies(weight, 1, w_ref, sems, half):
             copy.wait()
-    for z in range(4):
-        r = lax.rem(zi_ref[0] - z + 4, 4)
-        at = slice(z * ZB, (z + 1) * ZB)
-        y = h_ref[:, at] + dot(zn_ref[...], w_ref[r, 0]) + dot(zf_ref[...], w_ref[r, 1])
-        y_ref[:, at] = y.astype(y_ref.dtype)
+        for z in range(4):
+            r = lax.rem(zi_ref[0] - z + 4, 4)
+            at = slice(z * ZB, (z + 1) * ZB)
+            part = dot(z_ref[...], w_ref[r, half])
+            if half == 0:
+                acc[:, at] = h_ref[:, at] + part
+            else:
+                y_ref[:, at] = (acc[:, at] + part).astype(y_ref.dtype)
 
 
 def ffn_down_call(dtype, h, z_near, z_far, zi, wd):
@@ -430,7 +433,7 @@
         in_specs=[vmem] * 3 + [smem()] + [hbm()] * 8,
         out_specs=vmem,
         out_shape=sds((rows, model), dtype),
-        scratch_shapes=pair_scratch(1, hidden),
+        scratch_shapes=pair_scratch(1, hidden) + [pltpu.VMEM((rows, model), F32)],
         compiler_params=pltpu.CompilerParams(vmem_limit_bytes=VMEM_MB * 1024 * 1024),
         cost_estimate=cost(2 * rows * model * 4 * hidden, 8 * hidden * model + 8 * h.size),
     )(h, z_near, z_far, zi, *wd)
@@ -1055,7 +1058,7 @@
     back = attend_back_call(
         scale, None, q, k, k_oth, v, v_oth, do, o, sums, aug_q, aug_k, head_scale, add_k, var_q
     )
-    half = hidden // 32 * 16
+    half = hidden * 3 // 128 * 16
     cut = width * 3 // 2
     if near:
         down_run = ring(plus(down_run, down[3]))

time: 619 us -> 618 us (level)
    unnamed x187 -> x189, local copies, waits for them, and re-layouts: 13.4 us -> 13 us
  transfers between devices with their start and end apart: 83 -> 83, of which waited for: 35 -> 33; matrix products, arithmetic and copies ran while one was open for 8% -> 8% of each run, Pallas kernels for 22% -> 22%
where the time goes in v7:
time: 618 us; the launch traced here: 609 us
  Pallas kernels  260 us (42%)
  waiting for transfers between devices  207 us (33%)
  starting transfers between devices  68.8 us (11%)
  other arithmetic  46.7 us (8%)
  local copies, waits for them, and re-layouts  24 us (4%)
    ppermute x19, waiting for transfers between devices, y_swap(): return lax.ppermute(value, 'tensor', [(i, i ^ 2) for i in range(n)])  56.4 us
    ppermute x12, waiting for transfers between devices, ring(): return lax.ppermute(value, 'dp', [(i, (i + 1) % n) for i in range(n)])  54.3 us
    pallas_call x2, Pallas kernels, attend_back_call(): pl.pallas_call(functools.partial(attend_back_kernel, scale), grid=(pairs,...  53.3 us
    pallas_call x2, Pallas kernels, ffn_back_call(): pl.pallas_call(functools.partial(ffn_back_kernel, out_low), grid=(2,), in...  50.4 us
    pallas_call x2, Pallas kernels, ffn_up_call(): pl.pallas_call(functools.partial(ffn_up_kernel, save, out_low), grid=(2,)...  34.9 us
    ppermute x18, waiting for transfers between devices, to_owner(): return lax.ppermute(part, 'dp', [(i, (i - r) % n) for i in range(n)])  33.1 us
    pallas_call x2, Pallas kernels, qkv_back_call(): pl.pallas_call(qkv_back_kernel, grid=(4,), in_specs=[col] * 7 + [whole((r...  33 us
    pallas_call x2, Pallas kernels, attend_call(): pl.pallas_call(functools.partial(attend_kernel, scale), grid=(pairs,), in...  30.3 us
  transfers between devices with their start and end apart: 83, of which 33 were waited for; matrix products, arithmetic and copies ran while one was open for 8% of the time, Pallas kernels for 22%

profile of v7, /device:TPU:0, one launch (start us, length us, event | category | flops | bytes accessed | tf_op | source)
XLA Modules:
  0.0 609.1 jit_solution(13795449481466714407)
XLA Ops:
  4.3 3.1 collective-permute-start
  7.4 1.7 fusion.14
  9.1 1.6 collective-permute-start.1
  15.5 7.0 %collective-permute-done.1 = bf16[256,1024]{1,0:T(8,128)(2,1)S(1)} collective-permute-done((bf16[256,1024]{1,0:T(8,128)(2,1)S(1)}, bf16[256,1024]{1,0:T(8,128)(2,1)S(1)}, u32[]{:S(2)}, u32[]{:S(2)}) %collective-permute-start.1) | collective-permute-done | bytes 524320 | tf_op jit(solution)/shard_map/ppermute | solution.py:754
  28.7 8.3 %collective-permute-done.2 = bf16[1040,256]{1,0:T(8,128)(2,1)S(1)} collective-permute-done((bf16[1040,256]{1,0:T(8,128)(2,1)S(1)}, bf16[1040,256]{1,0:T(8,128)(2,1)S(1)}, u32[]{:S(2)}, u32[]{:S(2)}) %collective-permute-start.2) | collective-permute-done | bytes 532512 | tf_op jit(solution)/shard_map/ppermute | solution.py:759
  41.1 9.6 %collective-permute-done.4 = bf16[1040,256]{1,0:T(8,128)(2,1)} collective-permute-done((bf16[1040,256]{1,0:T(8,128)(2,1)S(1)}, bf16[1040,256]{1,0:T(8,128)(2,1)}, u32[]{:S(2)}, u32[]{:S(2)}) %collective-permute-start.4) | collective-permute-done | bytes 532512 | tf_op jit(solution)/shard_map/ppermute | solution.py:759
  52.9 12.3 %collective-permute-done.8 = bf16[336,256]{1,0:T(8,128)(2,1)S(1)} collective-permute-done((bf16[336,256]{1,0:T(8,128)(2,1)S(1)}, bf16[336,256]{1,0:T(8,128)(2,1)S(1)}, u32[]{:S(2)}, u32[]{:S(2)}) %collective-permute-start.8) | collective-permute-done | bytes 172064 | tf_op jit(solution)/shard_map/ppermute | solution.py:754
  65.2 2.0 collective-permute-done.6
  70.8 10.4 %collective-permute-done.11 = bf16[352,256]{1,0:T(8,128)(2,1)S(1)} collective-permute-done((bf16[352,256]{1,0:T(8,128)(2,1)S(1)}, bf16[352,256]{1,0:T(8,128)(2,1)S(1)}, u32[]{:S(2)}, u32[]{:S(2)}) %collective-permute-start.11) | collective-permute-done | bytes 180256 | tf_op jit(solution)/shard_map/ppermute | solution.py:754
  81.3 1.7 collective-permute-done.9
  86.4 2.3 pad_maximum_fusion.7.refs_3_
  88.7 9.0 %collective-permute-done.12 = bf16[1376,256]{1,0:T(8,128)(2,1)S(1)} collective-permute-done((bf16[1376,256]{1,0:T(8,128)(2,1)}, bf16[1376,256]{1,0:T(8,128)(2,1)S(1)}, u32[]{:S(2)}, u32[]{:S(2)}) %collective-permute-start.12) | collective-permute-done | bytes 704544 | tf_op jit(solution)/shard_map/ppermute | solution.py:759
  106.6 10.7 %shard_map.171 = (bf16[512,1024]{1,0:T(8,128)(2,1)}, bf16[512,1024]{1,0:T(8,128)(2,1)}, bf16[512,1024]{1,0:T(8,128)(2,1)}) custom-call(bf16[512,1024]{1,0:T(8,128)(2,1)} %maximum_select_fusion.1.x_ref.dy_ref, f32[1,1024]{1,0:T(1,128)} %bitcast.179, s32[1]{0:T(128)} %bitcast.27.zi_ref, f32[512,128]{1,0:T(8,128)} %pad_maximum_fusion.11.cos_ref, ...), custom_call_target="tpu_custom_call" | custom-call | flops 3221225472 | bytes 14680064 | tf_op jit(solution)/shard_map/pallas_call | solution.py:180
  117.3 5.8 collective-permute-done.14.refs_1_.refs_17_
  128.3 15.2 %shard_map.172 = (bf16[512,1024]{1,0:T(8,128)(2,1)}, f32[512,1024]{1,0:T(8,128)}) custom-call(bf16[512,1024]{1,0:T(8,128)(2,1)} %get-tuple-element.264.q_ref, bf16[512,1024]{1,0:T(8,128)(2,1)} %get-tuple-element.265.ko_ref, bf16[512,1024]{1,0:T(8,128)(2,1)} %copy-done.92, bf16[512,1024]{1,0:T(8,128)(2,1)} %get-tuple-element.266.vo_ref, ...), custom_call_target="tpu_custom_call" | custom-call | flops 4294967296 | bytes 10485760 | tf_op jit(solution)/shard_map/pallas_call | solution.py:243
  148.9 1.7 pad_maximum_fusion.2.refs_10_
  150.7 12.4 %collective-permute-done.24.refs_3_.refs_19_ = bf16[2,688,256]{2,1,0:T(8,128)(2,1)S(1)} collective-permute-done((bf16[2,688,256]{2,1,0:T(8,128)(2,1)S(1)}, bf16[2,688,256]{2,1,0:T(8,128)(2,1)S(1)}, u32[]{:S(2)}, u32[]{:S(2)}) %collective-permute-start.24) | collective-permute-done | bytes 704544 | tf_op jit(solution)/shard_map/ppermute | solution.py:759
  167.6 16.8 %shard_map.173 = (f32[512,1024]{1,0:T(8,128)}, bf16[512,1408]{1,0:T(8,128)(2,1)}, bf16[512,1408]{1,0:T(8,128)(2,1)}) custom-call(bf16[512,1024]{1,0:T(8,128)(2,1)} %maximum_select_fusion.1.x_ref.dy_ref, bf16[512,1024]{1,0:T(8,128)(2,1)} %get-tuple-element.271.o_ref, f32[1,1024]{1,0:T(1,128)} %bitcast.193, s32[1]{0:T(128)} %bitcast.27.zi_ref, ...), custom_call_target="tpu_custom_call" | custom-call | flops 6845104128 | bytes 21757952 | tf_op jit(solution)/shard_map/pallas_call | solution.py:394
  186.0 9.0 %shard_map.174 = bf16[512,1024]{1,0:T(8,128)(2,1)} custom-call(f32[512,1024]{1,0:T(8,128)} %get-tuple-element.279.h_ref, bf16[512,1408]{1,0:T(8,128)(2,1)} %get-tuple-element.280.zn_ref, bf16[512,1408]{1,0:T(8,128)(2,1)} %get-tuple-element.281.zf_ref, s32[1]{0:T(128)} %bitcast.27.zi_ref, bf16[2,688,256]{2,1,0:T(8,128)(2,1)} %copy-done.25, ...), custom_call_target="tpu_custom_call" | custom-call | flops 2885681152 | bytes 9830400 | tf_op jit(solution)/shard_map/pallas_call | solution.py:431
  195.0 3.6 collective-permute-start.34
  198.7 22.8 %collective-permute-done.34 = bf16[512,1024]{1,0:T(8,128)(2,1)S(1)} collective-permute-done((bf16[512,1024]{1,0:T(8,128)(2,1)}, bf16[512,1024]{1,0:T(8,128)(2,1)S(1)}, u32[]{:S(2)}, u32[]{:S(2)}) %collective-permute-start.34) | collective-permute-done | bytes 1048608 | tf_op jit(solution)/shard_map/ppermute | solution.py:1006
  222.6 11.2 %shard_map.175 = (bf16[512,1024]{1,0:T(8,128)(2,1)}, bf16[512,1024]{1,0:T(8,128)(2,1)}, bf16[512,1024]{1,0:T(8,128)(2,1)}, bf16[512,1024]{1,0:T(8,128)(2,1)}, bf...) custom-call(bf16[512,1024]{1,0:T(8,128)(2,1)} %broadcast_select_fusion.2.x_ref, f32[1,1024]{1,0:T(1,128)} %bitcast.180, ...), custom_call_target="tpu_custom_call" | custom-call | flops 3221225472 | bytes 14680064 | tf_op jit(solution)/shard_map/pallas_call | solution.py:180
  234.3 2.4 collective-permute-done.35.kx_ref
  239.2 15.1 %shard_map.176 = (bf16[512,1024]{1,0:T(8,128)(2,1)}, f32[512,1024]{1,0:T(8,128)}) custom-call(bf16[512,1024]{1,0:T(8,128)(2,1)} %get-tuple-element.284.q_ref, bf16[512,1024]{1,0:T(8,128)(2,1)} %get-tuple-element.285.ko_ref, bf16[512,1024]{1,0:T(8,128)(2,1)} %copy-done.90, bf16[512,1024]{1,0:T(8,128)(2,1)} %get-tuple-element.286.vo_ref, ...), custom_call_target="tpu_custom_call" | custom-call | flops 4294967296 | bytes 10485760 | tf_op jit(solution)/shard_map/pallas_call | solution.py:243
  254.4 18.1 %shard_map.177 = (f32[512,1024]{1,0:T(8,128)}, bf16[512,1408]{1,0:T(8,128)(2,1)}, bf16[512,1408]{1,0:T(8,128)(2,1)}, bf16[512,1024]{1,0:T(8,128)(2,1)}, bf16[2,5...) custom-call(bf16[512,1024]{1,0:T(8,128)(2,1)} %broadcast_select_fusion.2.x_ref, ...), custom_call_target="tpu_custom_call" | custom-call | flops 6845104128 | bytes 21757952 | tf_op jit(solution)/shard_map/pallas_call | solution.py:394
  272.5 25.3 %shard_map.178 = (f32[512,1024]{1,0:T(8,128)}, bf16[512,1024]{1,0:T(8,128)(2,1)}, bf16[512,1024]{1,0:T(8,128)(2,1)}, bf16[512,1408]{1,0:T(8,128)(2,1)}, bf16[512...) custom-call(bf16[512,1024]{1,0:T(8,128)(2,1)} %maximum_select_fusion.1.x_ref.dy_re, ...), custom_call_target="tpu_custom_call" | custom-call | flops 9730785280 | bytes 27394048 | tf_op jit(solution)/shard_map/pallas_call | solution.py:515
  297.8 26.7 %shard_map.179 = (bf16[512,1024]{1,0:T(8,128)(2,1)}, bf16[512,1024]{1,0:T(8,128)(2,1)}, bf16[512,1024]{1,0:T(8,128)(2,1)}, bf16[512,1024]{1,0:T(8,128)(2,1)}, bf...) custom-call(bf16[512,1024]{1,0:T(8,128)(2,1)} %get-tuple-element.284.q_ref, bf16[512,1024]{1,0:T(8,128)(2,1)} %get-tuple-element.285.ko_ref, ...), custom_call_target="tpu_custom_call" | custom-call | flops 10737418240 | bytes 20971520 | tf_op jit(solution)/shard_map/pallas_call | solution.py:617
  325.1 2.3 collective-permute-done.37.dkr_ref
  329.9 16.8 %shard_map.180 = (bf16[2,512,768]{2,1,0:T(8,128)(2,1)}, bf16[2,512,768]{2,1,0:T(8,128)(2,1)}, f32[512,1024]{1,0:T(8,128)}, bf16[512,1024]{1,0:T(8,128)(2,1)}, f32[1,1024]{1,0:T(1,128)}) custom-call(bf16[512,1024]{1,0:T(8,128)(2,1)} %get-tuple-element.295.dq_ref, bf16[512,1024]{1,0:T(8,128)(2,1)} %get-tuple-element.296.dk_ref, bf16[512,1024]{1,0:T(8,128)(2,1)} %copy-done.47, ...), custom_call_target="tpu_custom_call" | custom-call | flops 3221225472 | bytes 27262976 | tf_op jit(solution)/shard_map/pallas_call | solution.py:700
  349.1 9.3 %shard_map.181 = f32[512,1024]{1,0:T(8,128)} custom-call(f32[512,1024]{1,0:T(8,128)} %get-tuple-element.288.h_ref, bf16[512,1408]{1,0:T(8,128)(2,1)} %get-tuple-element.308.zn_ref.ao_ref, bf16[512,1408]{1,0:T(8,128)(2,1)} %get-tuple-element.309.zf_ref, s32[1]{0:T(128)} %bitcast.27.zi_ref, bf16[2,688,256]{2,1,0:T(8,128)(2,1)} %copy-done.25, ...), custom_call_target="tpu_custom_call" | custom-call | flops 2885681152 | bytes 9830400 | tf_op jit(solution)/shard_map/pallas_call | solution.py:431
  358.4 16.1 %collective-permute-done.39 = bf16[512,1024]{1,0:T(8,128)(2,1)} collective-permute-done((bf16[512,1024]{1,0:T(8,128)(2,1)}, bf16[512,1024]{1,0:T(8,128)(2,1)}, u32[]{:S(2)}, u32[]{:S(2)}) %collective-permute-start.39) | collective-permute-done | bytes 1048608 | tf_op jit(solution)/shard_map/ppermute | solution.py:1026
  374.5 2.1 broadcast_select_fusion.1.bo_ref.dy_ref
  376.7 2.6 collective-permute-done.44.bx_ref
  379.4 3.2 shard_map.182
  384.2 25.1 %shard_map.183 = (f32[512,1024]{1,0:T(8,128)}, bf16[512,1024]{1,0:T(8,128)(2,1)}, bf16[512,1024]{1,0:T(8,128)(2,1)}, bf16[512,1408]{1,0:T(8,128)(2,1)}, bf16[512...) custom-call(bf16[512,1024]{1,0:T(8,128)(2,1)} %copy-done.2, ...), custom_call_target="tpu_custom_call" | custom-call | flops 9730785280 | bytes 27394048 | tf_op jit(solution)/shard_map/pallas_call | solution.py:515
  409.3 6.3 %collective-permute-done.45 = bf16[4,688,256]{2,1,0:T(8,128)(2,1)S(1)} collective-permute-done((bf16[4,688,256]{2,1,0:T(8,128)(2,1)S(1)}, bf16[4,688,256]{2,1,0:T(8,128)(2,1)S(1)}, u32[]{:S(2)}, u32[]{:S(2)}) %collective-permute-start.45) | collective-permute-done | bytes 1409056 | tf_op jit(solution)/shard_map/ppermute | solution.py:754
  416.6 6.0 collective-permute-done.49.bx_ref
  425.2 4.3 shard_map.184
  433.0 4.3 shard_map.186
  437.2 4.8 collective-permute-done.50
  443.3 3.9 collective-permute-start.54
  447.9 26.6 %shard_map.187 = (bf16[512,1024]{1,0:T(8,128)(2,1)}, bf16[512,1024]{1,0:T(8,128)(2,1)}, bf16[512,1024]{1,0:T(8,128)(2,1)}, bf16[512,1024]{1,0:T(8,128)(2,1)}, bf...) custom-call(bf16[512,1024]{1,0:T(8,128)(2,1)} %get-tuple-element.284.q_ref, bf16[512,1024]{1,0:T(8,128)(2,1)} %get-tuple-element.285.ko_ref, ...), custom_call_target="tpu_custom_call" | custom-call | flops 10737418240 | bytes 20971520 | tf_op jit(solution)/shard_map/pallas_call | solution.py:617
  476.5 2.3 fusion.24
  478.8 3.3 collective-permute-start.57
  484.1 16.3 %shard_map.188 = (bf16[2,512,768]{2,1,0:T(8,128)(2,1)}, bf16[2,512,768]{2,1,0:T(8,128)(2,1)}, f32[512,1024]{1,0:T(8,128)}, bf16[512,1024]{1,0:T(8,128)(2,1)}, f32[1,1024]{1,0:T(1,128)}) custom-call(bf16[512,1024]{1,0:T(8,128)(2,1)} %get-tuple-element.365.dq_ref, bf16[512,1024]{1,0:T(8,128)(2,1)} %get-tuple-element.366.dk_ref, ...), custom_call_target="tpu_custom_call" | custom-call | flops 3221225472 | bytes 27262976 | tf_op jit(solution)/shard_map/pallas_call | solution.py:700
  500.4 8.5 %collective-permute-done.51 = bf16[4,688,256]{2,1,0:T(8,128)(2,1)} collective-permute-done((bf16[4,688,256]{2,1,0:T(8,128)(2,1)}, bf16[4,688,256]{2,1,0:T(8,128)(2,1)}, u32[]{:S(2)}, u32[]{:S(2)}) %collective-permute-start.51) | collective-permute-done | bytes 1409056 | tf_op jit(solution)/shard_map/ppermute | solution.py:754
  508.9 5.7 collective-permute-done.58
  514.7 1.6 fusion.44
  520.1 2.0 convert_select_fusion
  525.0 2.1 collective-permute-start.68
  527.1 5.0 shard_map.189
  532.2 4.9 collective-permute-done.67
  541.3 1.6 collective-permute-start.72
  542.9 1.9 collective-permute-start.73
  544.9 11.7 %collective-permute-done.70 = f32[3,1024]{1,0:T(4,128)S(1)} collective-permute-done((f32[3,1024]{1,0:T(4,128)S(1)}, f32[3,1024]{1,0:T(4,128)S(1)}, u32[]{:S(2)}, u32[]{:S(2)}) %collective-permute-start.70) | collective-permute-done | bytes 12320 | tf_op jit(solution)/shard_map/ppermute | solution.py:754
  557.6 4.7 collective-permute-done.72
  563.6 1.9 collective-permute-start.78
  567.7 7.2 %collective-permute-done.75 = f32[3,1024]{1,0:T(4,128)S(1)} collective-permute-done((f32[3,1024]{1,0:T(4,128)S(1)}, f32[3,1024]{1,0:T(4,128)S(1)}, u32[]{:S(2)}, u32[]{:S(2)}) %collective-permute-start.75) | collective-permute-done | bytes 12320 | tf_op jit(solution)/shard_map/ppermute | solution.py:1105
  575.0 6.2 %collective-permute-done.77 = bf16[384,256]{1,0:T(8,128)(2,1)S(1)} collective-permute-done((bf16[384,256]{1,0:T(8,128)(2,1)S(1)}, bf16[384,256]{1,0:T(8,128)(2,1)S(1)}, u32[]{:S(2)}, u32[]{:S(2)}) %collective-permute-start.77) | collective-permute-done | bytes 196640 | tf_op jit(solution)/shard_map/ppermute | solution.py:782
  583.1 2.1 fusion.5
  590.3 2.0 collective-permute-start.81
  592.3 2.8 collective-permute-start.80
  596.5 3.7 collective-permute-done.82
  600.2 7.2 %collective-permute-done.81 = bf16[384,256]{1,0:T(8,128)(2,1)S(1)} collective-permute-done((bf16[384,256]{1,0:T(8,128)(2,1)}, bf16[384,256]{1,0:T(8,128)(2,1)S(1)}, u32[]{:S(2)}, u32[]{:S(2)}) %collective-permute-start.81) | collective-permute-done | bytes 196640 | tf_op jit(solution)/shard_map/ppermute | solution.py:782
  (430 shorter events, 102.4 us)
Async XLA Ops:
  4.3 18.2 %collective-permute-start = (bf16[1040,256]{1,0:T(8,128)(2,1)S(1)}, bf16[1040,256]{1,0:T(8,128)(2,1)S(1)}, u32[]{:S(2)}, u32[]{:S(2)}) collective-permute-start(bf16[1040,256]{1,0:T(8,128)(2,1)S(1)} %fusion.12), channel_id=1, source_target_pairs={{0,4},{4,8},{8,12},{12,0},{1,5},{5,9},{9,13},{13,1},{2,6},{6,10},{... | collective-permute-start | bytes 1597448 | tf_op jit(solution)/shard_map/ppermute | solution.py:759
  9.1 13.4 %collective-permute-start.1 = (bf16[256,1024]{1,0:T(8,128)(2,1)S(1)}, bf16[256,1024]{1,0:T(8,128)(2,1)S(1)}, u32[]{:S(2)}, u32[]{:S(2)}) collective-permute-start(bf16[256,1024]{1,0:T(8,128)(2,1)S(1)} %get-tuple-element.459), channel_id=1, source_target_pairs={{0,2},{1,3},{2,0},{3,1},{4,6},{5,7},{6,4},{7,5},{8,10},{9,11},{10,... | collective-permute-start | bytes 1572872 | tf_op jit(solution)/shard_map/ppermute | solution.py:754
  22.6 14.4 %collective-permute-start.2 = (bf16[1040,256]{1,0:T(8,128)(2,1)S(1)}, bf16[1040,256]{1,0:T(8,128)(2,1)S(1)}, u32[]{:S(2)}, u32[]{:S(2)}) collective-permute-start(bf16[1040,256]{1,0:T(8,128)(2,1)S(1)} %collective-permute-done), channel_id=1, source_target_pairs={{0,4},{4,8},{8,12},{12,0},{1,5},{5,9},{9,13},{13,1},{2,6},{6,10},{... | collective-permute-start | bytes 1597448 | tf_op jit(solution)/shard_map/ppermute | solution.py:759
  24.1 12.9 %collective-permute-start.3 = (bf16[1040,256]{1,0:T(8,128)(2,1)S(1)}, bf16[1040,256]{1,0:T(8,128)(2,1)S(1)}, u32[]{:S(2)}, u32[]{:S(2)}) collective-permute-start(bf16[1040,256]{1,0:T(8,128)(2,1)S(1)} %fusion.12), channel_id=1, source_target_pairs={{0,2},{1,3},{2,0},{3,1},{4,6},{5,7},{6,4},{7,5},{8,10},{9,11},{10,... | collective-permute-start | bytes 1597448 | tf_op jit(solution)/shard_map/ppermute | solution.py:754
  37.0 13.7 %collective-permute-start.4 = (bf16[1040,256]{1,0:T(8,128)(2,1)S(1)}, bf16[1040,256]{1,0:T(8,128)(2,1)}, u32[]{:S(2)}, u32[]{:S(2)}) collective-permute-start(bf16[1040,256]{1,0:T(8,128)(2,1)S(1)} %collective-permute-done.2), channel_id=1, source_target_pairs={{0,4},{4,8},{8,12},{12,0},{1,5},{5,9},{9,13},{13,1},{2,6},{6,10},{... | collective-permute-start | bytes 1597448 | tf_op jit(solution)/shard_map/ppermute | solution.py:759
  38.1 12.6 %collective-permute-start.5 = (bf16[1040,256]{1,0:T(8,128)(2,1)S(1)}, bf16[1040,256]{1,0:T(8,128)(2,1)}, u32[]{:S(2)}, u32[]{:S(2)}) collective-permute-start(bf16[1040,256]{1,0:T(8,128)(2,1)S(1)} %collective-permute-done), channel_id=1, source_target_pairs={{0,2},{1,3},{2,0},{3,1},{4,6},{5,7},{6,4},{7,5},{8,10},{9,11},{10,... | collective-permute-start | bytes 1597448 | tf_op jit(solution)/shard_map/ppermute | solution.py:754
  50.7 16.5 %collective-permute-start.6 = (bf16[1376,256]{1,0:T(8,128)(2,1)}, bf16[1376,256]{1,0:T(8,128)(2,1)S(1)}, u32[]{:S(2)}, u32[]{:S(2)}) collective-permute-start(bf16[1376,256]{1,0:T(8,128)(2,1)} %bitcast.8), channel_id=1, source_target_pairs={{0,4},{4,8},{8,12},{12,0},{1,5},{5,9},{9,13},{13,1},{2,6},{6,10},{... | collective-permute-start | bytes 2113544 | tf_op jit(solution)/shard_map/ppermute | solution.py:759
  50.8 14.4 %collective-permute-start.7 = (bf16[1040,256]{1,0:T(8,128)(2,1)S(1)}, bf16[1040,256]{1,0:T(8,128)(2,1)S(1)}, u32[]{:S(2)}, u32[]{:S(2)}) collective-permute-start(bf16[1040,256]{1,0:T(8,128)(2,1)S(1)} %collective-permute-done.2), channel_id=1, source_target_pairs={{0,2},{1,3},{2,0},{3,1},{4,6},{5,7},{6,4},{7,5},{8,10},{9,11},{10,... | collective-permute-start | bytes 1597448 | tf_op jit(solution)/shard_map/ppermute | solution.py:754
  52.2 13.0 %collective-permute-start.8 = (bf16[336,256]{1,0:T(8,128)(2,1)S(1)}, bf16[336,256]{1,0:T(8,128)(2,1)S(1)}, u32[]{:S(2)}, u32[]{:S(2)}) collective-permute-start(bf16[336,256]{1,0:T(8,128)(2,1)S(1)} %slice.255), channel_id=1, source_target_pairs={{0,2},{1,3},{2,0},{3,1},{4,6},{5,7},{6,4},{7,5},{8,10},{9,11},{10,... | collective-permute-start | bytes 516104 | tf_op jit(solution)/shard_map/ppermute | solution.py:754
  67.2 15.7 %collective-permute-start.9 = (bf16[1376,256]{1,0:T(8,128)(2,1)S(1)}, bf16[1376,256]{1,0:T(8,128)(2,1)}, u32[]{:S(2)}, u32[]{:S(2)}) collective-permute-start(bf16[1376,256]{1,0:T(8,128)(2,1)S(1)} %collective-permute-done.6), channel_id=1, source_target_pairs={{0,4},{4,8},{8,12},{12,0},{1,5},{5,9},{9,13},{13,1},{2,6},{6,10},{... | collective-permute-start | bytes 2113544 | tf_op jit(solution)/shard_map/ppermute | solution.py:759
  67.2 14.0 %collective-permute-start.10 = (bf16[1040,256]{1,0:T(8,128)(2,1)}, bf16[1040,256]{1,0:T(8,128)(2,1)}, u32[]{:S(2)}, u32[]{:S(2)}) collective-permute-start(bf16[1040,256]{1,0:T(8,128)(2,1)} %collective-permute-done.4), channel_id=1, source_target_pairs={{0,2},{1,3},{2,0},{3,1},{4,6},{5,7},{6,4},{7,5},{8,10},{9,11},{10,... | collective-permute-start | bytes 1597448 | tf_op jit(solution)/shard_map/ppermute | solution.py:754
  70.0 11.2 %collective-permute-start.11 = (bf16[352,256]{1,0:T(8,128)(2,1)S(1)}, bf16[352,256]{1,0:T(8,128)(2,1)S(1)}, u32[]{:S(2)}, u32[]{:S(2)}) collective-permute-start(bf16[352,256]{1,0:T(8,128)(2,1)S(1)} %slice.256), channel_id=1, source_target_pairs={{0,2},{1,3},{2,0},{3,1},{4,6},{5,7},{6,4},{7,5},{8,10},{9,11},{10,... | collective-permute-start | bytes 540680 | tf_op jit(solution)/shard_map/ppermute | solution.py:754
  70.7 33.6 %collective-permute-start.16 = (bf16[2,1040,256]{2,1,0:T(8,128)(2,1)S(1)}, bf16[2,1040,256]{2,1,0:T(8,128)(2,1)}, u32[]{:S(2)}, u32[]{:S(2)}) collective-permute-start(bf16[2,1040,256]{2,1,0:T(8,128)(2,1)S(1)} %pad_maximum_fusion.4.refs_0_), channel_id=1, source_target_pairs={{0,1},{1,0},{2,3},{3,2},{4,5},{5,4},{6,7},{7,6},{8,9},{9,8},{10,11... | collective-permute-start | bytes 3194888 | tf_op jit(solution)/shard_map/ppermute | solution.py:749
  82.9 14.7 %collective-permute-start.12 = (bf16[1376,256]{1,0:T(8,128)(2,1)}, bf16[1376,256]{1,0:T(8,128)(2,1)S(1)}, u32[]{:S(2)}, u32[]{:S(2)}) collective-permute-start(bf16[1376,256]{1,0:T(8,128)(2,1)} %collective-permute-done.9), channel_id=1, source_target_pairs={{0,4},{4,8},{8,12},{12,0},{1,5},{5,9},{9,13},{13,1},{2,6},{6,10},{... | collective-permute-start | bytes 2113544 | tf_op jit(solution)/shard_map/ppermute | solution.py:759
  84.1 22.4 %collective-permute-start.17 = (bf16[2,1040,256]{2,1,0:T(8,128)(2,1)S(1)}, bf16[2,1040,256]{2,1,0:T(8,128)(2,1)}, u32[]{:S(2)}, u32[]{:S(2)}) collective-permute-start(bf16[2,1040,256]{2,1,0:T(8,128)(2,1)S(1)} %pad_maximum_fusion.5.refs_1_), channel_id=1, source_target_pairs={{0,1},{1,0},{2,3},{3,2},{4,5},{5,4},{6,7},{7,6},{8,9},{9,8},{10,11... | collective-permute-start | bytes 3194888 | tf_op jit(solution)/shard_map/ppermute | solution.py:749
  84.3 22.2 %collective-permute-start.18 = (bf16[2,1040,256]{2,1,0:T(8,128)(2,1)S(1)}, bf16[2,1040,256]{2,1,0:T(8,128)(2,1)}, u32[]{:S(2)}, u32[]{:S(2)}) collective-permute-start(bf16[2,1040,256]{2,1,0:T(8,128)(2,1)S(1)} %pad_maximum_fusion.6.refs_2_), channel_id=1, source_target_pairs={{0,1},{1,0},{2,3},{3,2},{4,5},{5,4},{6,7},{7,6},{8,9},{9,8},{10,11... | collective-permute-start | bytes 3194888 | tf_op jit(solution)/shard_map/ppermute | solution.py:749
  84.9 18.1 %collective-permute-start.13 = (bf16[1376,256]{1,0:T(8,128)(2,1)}, bf16[1376,256]{1,0:T(8,128)(2,1)}, u32[]{:S(2)}, u32[]{:S(2)}) collective-permute-start(bf16[1376,256]{1,0:T(8,128)(2,1)} %bitcast.8), channel_id=1, source_target_pairs={{0,2},{1,3},{2,0},{3,1},{4,6},{5,7},{6,4},{7,5},{8,10},{9,11},{10,... | collective-permute-start | bytes 2113544 | tf_op jit(solution)/shard_map/ppermute | solution.py:754
  103.1 20.0 %collective-permute-start.14 = (bf16[2,688,256]{2,1,0:T(8,128)(2,1)S(1)}, bf16[2,688,256]{2,1,0:T(8,128)(2,1)S(1)}, u32[]{:S(2)}, u32[]{:S(2)}) collective-permute-start(bf16[2,688,256]{2,1,0:T(8,128)(2,1)S(1)} %pad_maximum_fusion.9.refs_0_.refs_16_), channel_id=1, source_target_pairs={{0,4},{4,8},{8,12},{12,0},{1,5},{5,9},{9,13},{13,1},{2,6},{6,10},{... | collective-permute-start | bytes 2113544 | tf_op jit(solution)/shard_map/ppermute | solution.py:759
  104.3 18.7 %collective-permute-start.15 = (bf16[1376,256]{1,0:T(8,128)(2,1)S(1)}, bf16[1376,256]{1,0:T(8,128)(2,1)S(1)}, u32[]{:S(2)}, u32[]{:S(2)}) collective-permute-start(bf16[1376,256]{1,0:T(8,128)(2,1)S(1)} %copy-done.50), channel_id=1, source_target_pairs={{0,2},{1,3},{2,0},{3,1},{4,6},{5,7},{6,4},{7,5},{8,10},{9,11},{10,... | collective-permute-start | bytes 2113544 | tf_op jit(solution)/shard_map/ppermute | solution.py:754
  124.7 19.5 %collective-permute-start.20 = (bf16[2,688,256]{2,1,0:T(8,128)(2,1)}, bf16[2,688,256]{2,1,0:T(8,128)(2,1)S(1)}, u32[]{:S(2)}, u32[]{:S(2)}) collective-permute-start(bf16[2,688,256]{2,1,0:T(8,128)(2,1)} %copy-done.29), channel_id=1, source_target_pairs={{0,4},{4,8},{8,12},{12,0},{1,5},{5,9},{9,13},{13,1},{2,6},{6,10},{... | collective-permute-start | bytes 2113544 | tf_op jit(solution)/shard_map/ppermute | solution.py:759
  124.7 19.5 %collective-permute-start.21 = (bf16[1376,256]{1,0:T(8,128)(2,1)}, bf16[1376,256]{1,0:T(8,128)(2,1)S(1)}, u32[]{:S(2)}, u32[]{:S(2)}) collective-permute-start(bf16[1376,256]{1,0:T(8,128)(2,1)} %collective-permute-done.9), channel_id=1, source_target_pairs={{0,2},{1,3},{2,0},{3,1},{4,6},{5,7},{6,4},{7,5},{8,10},{9,11},{10,... | collective-permute-start | bytes 2113544 | tf_op jit(solution)/shard_map/ppermute | solution.py:754
  144.2 18.9 %collective-permute-start.24 = (bf16[2,688,256]{2,1,0:T(8,128)(2,1)S(1)}, bf16[2,688,256]{2,1,0:T(8,128)(2,1)S(1)}, u32[]{:S(2)}, u32[]{:S(2)}) collective-permute-start(bf16[2,688,256]{2,1,0:T(8,128)(2,1)S(1)} %collective-permute-done.20.refs_2_.refs_18_), channel_id=1, source_target_pairs={{0,4},{4,8},{8,12},{12,0},{1,5},{5,9},{9,13},{13,1},{2,6},{6,10},{... | collective-permute-start | bytes 2113544 | tf_op jit(solution)/shard_map/ppermute | solution.py:759
  145.3 17.8 %collective-permute-start.25 = (bf16[1376,256]{1,0:T(8,128)(2,1)S(1)}, bf16[1376,256]{1,0:T(8,128)(2,1)S(1)}, u32[]{:S(2)}, u32[]{:S(2)}) collective-permute-start(bf16[1376,256]{1,0:T(8,128)(2,1)S(1)} %copy-done.53), channel_id=1, source_target_pairs={{0,2},{1,3},{2,0},{3,1},{4,6},{5,7},{6,4},{7,5},{8,10},{9,11},{10,... | collective-permute-start | bytes 2113544 | tf_op jit(solution)/shard_map/ppermute | solution.py:754
  147.8 16.9 %collective-permute-start.26 = (bf16[2,1376,256]{2,1,0:T(8,128)(2,1)S(1)}, bf16[2,1376,256]{2,1,0:T(8,128)(2,1)S(1)}, u32[]{:S(2)}, u32[]{:S(2)}) collective-permute-start(bf16[2,1376,256]{2,1,0:T(8,128)(2,1)S(1)} %pad_maximum_fusion.refs_8_), channel_id=1, source_target_pairs={{0,1},{1,0},{2,3},{3,2},{4,5},{5,4},{6,7},{7,6},{8,9},{9,8},{10,11... | collective-permute-start | bytes 4227080 | tf_op jit(solution)/shard_map/ppermute | solution.py:749
  148.9 16.4 %collective-permute-start.27 = (bf16[2,1376,256]{2,1,0:T(8,128)(2,1)S(1)}, bf16[2,1376,256]{2,1,0:T(8,128)(2,1)S(1)}, u32[]{:S(2)}, u32[]{:S(2)}) collective-permute-start(bf16[2,1376,256]{2,1,0:T(8,128)(2,1)S(1)} %pad_maximum_fusion.1.refs_9_), channel_id=1, source_target_pairs={{0,1},{1,0},{2,3},{3,2},{4,5},{5,4},{6,7},{7,6},{8,9},{9,8},{10,11... | collective-permute-start | bytes 4227080 | tf_op jit(solution)/shard_map/ppermute | solution.py:749
  150.6 14.8 %collective-permute-start.28 = (bf16[2,1376,256]{2,1,0:T(8,128)(2,1)S(1)}, bf16[2,1376,256]{2,1,0:T(8,128)(2,1)S(1)}, u32[]{:S(2)}, u32[]{:S(2)}) collective-permute-start(bf16[2,1376,256]{2,1,0:T(8,128)(2,1)S(1)} %pad_maximum_fusion.2.refs_10_), channel_id=1, source_target_pairs={{0,1},{1,0},{2,3},{3,2},{4,5},{5,4},{6,7},{7,6},{8,9},{9,8},{10,11... | collective-permute-start | bytes 4227080 | tf_op jit(solution)/shard_map/ppermute | solution.py:749
  164.7 19.8 %collective-permute-start.30 = (bf16[2,688,256]{2,1,0:T(8,128)(2,1)S(1)}, bf16[2,688,256]{2,1,0:T(8,128)(2,1)S(1)}, u32[]{:S(2)}, u32[]{:S(2)}) collective-permute-start(bf16[2,688,256]{2,1,0:T(8,128)(2,1)S(1)} %copy-done.26), channel_id=1, source_target_pairs={{0,1},{1,0},{2,3},{3,2},{4,5},{5,4},{6,7},{7,6},{8,9},{9,8},{10,11... | collective-permute-start | bytes 2113544 | tf_op jit(solution)/shard_map/ppermute | solution.py:749
  164.7 19.8 %collective-permute-start.32 = (bf16[2,688,256]{2,1,0:T(8,128)(2,1)S(1)}, bf16[2,688,256]{2,1,0:T(8,128)(2,1)S(1)}, u32[]{:S(2)}, u32[]{:S(2)}) collective-permute-start(bf16[2,688,256]{2,1,0:T(8,128)(2,1)S(1)} %collective-permute-done.20.refs_2_.refs_18_), channel_id=1, source_target_pairs={{0,1},{1,0},{2,3},{3,2},{4,5},{5,4},{6,7},{7,6},{8,9},{9,8},{10,11... | collective-permute-start | bytes 2113544 | tf_op jit(solution)/shard_map/ppermute | solution.py:749
  165.3 19.2 %collective-permute-start.31 = (bf16[2,688,256]{2,1,0:T(8,128)(2,1)S(1)}, bf16[2,688,256]{2,1,0:T(8,128)(2,1)S(1)}, u32[]{:S(2)}, u32[]{:S(2)}) collective-permute-start(bf16[2,688,256]{2,1,0:T(8,128)(2,1)S(1)} %copy-done.30), channel_id=1, source_target_pairs={{0,1},{1,0},{2,3},{3,2},{4,5},{5,4},{6,7},{7,6},{8,9},{9,8},{10,11... | collective-permute-start | bytes 2113544 | tf_op jit(solution)/shard_map/ppermute | solution.py:749
  165.4 19.1 %collective-permute-start.33 = (bf16[2,688,256]{2,1,0:T(8,128)(2,1)S(1)}, bf16[2,688,256]{2,1,0:T(8,128)(2,1)S(1)}, u32[]{:S(2)}, u32[]{:S(2)}) collective-permute-start(bf16[2,688,256]{2,1,0:T(8,128)(2,1)S(1)} %collective-permute-done.24.refs_3_.refs_19_), channel_id=1, source_target_pairs={{0,1},{1,0},{2,3},{3,2},{4,5},{5,4},{6,7},{7,6},{8,9},{9,8},{10,11... | collective-permute-start | bytes 2113544 | tf_op jit(solution)/shard_map/ppermute | solution.py:749
  195.0 26.4 %collective-permute-start.34 = (bf16[512,1024]{1,0:T(8,128)(2,1)}, bf16[512,1024]{1,0:T(8,128)(2,1)S(1)}, u32[]{:S(2)}, u32[]{:S(2)}) collective-permute-start(bf16[512,1024]{1,0:T(8,128)(2,1)} %shard_map.174), channel_id=1, source_target_pairs={{0,16},{1,17},{2,18},{3,19},{4,20},{5,21},{6,22},{7,23},{8,24},{9,... | collective-permute-start | bytes 3145736 | tf_op jit(solution)/shard_map/ppermute | solution.py:1006
  346.6 27.9 %collective-permute-start.40 = (bf16[512,1408]{1,0:T(8,128)(2,1)}, bf16[512,1408]{1,0:T(8,128)(2,1)S(1)}, u32[]{:S(2)}, u32[]{:S(2)}) collective-permute-start(bf16[512,1408]{1,0:T(8,128)(2,1)} %get-tuple-element.309.zf_ref), channel_id=1, source_target_pairs={{0,1},{1,0},{2,3},{3,2},{4,5},{5,4},{6,7},{7,6},{8,9},{9,8},{10,11... | collective-permute-start | bytes 4325384 | tf_op jit(solution)/shard_map/ppermute | solution.py:749
  346.9 27.7 %collective-permute-start.39 = (bf16[512,1024]{1,0:T(8,128)(2,1)}, bf16[512,1024]{1,0:T(8,128)(2,1)}, u32[]{:S(2)}, u32[]{:S(2)}) collective-permute-start(bf16[512,1024]{1,0:T(8,128)(2,1)} %get-tuple-element.307), channel_id=1, source_target_pairs={{16,0},{17,1},{18,2},{19,3},{20,4},{21,5},{22,6},{23,7},{24,8},{25... | collective-permute-start | bytes 3145736 | tf_op jit(solution)/shard_map/ppermute | solution.py:1026
  348.1 26.4 %collective-permute-start.41 = (bf16[512,1024]{1,0:T(8,128)(2,1)S(1)}, bf16[512,1024]{1,0:T(8,128)(2,1)S(1)}, u32[]{:S(2)}, u32[]{:S(2)}) collective-permute-start(bf16[512,1024]{1,0:T(8,128)(2,1)S(1)} %copy-done.10), channel_id=1, source_target_pairs={{0,1},{1,0},{2,3},{3,2},{4,5},{5,4},{6,7},{7,6},{8,9},{9,8},{10,11... | collective-permute-start | bytes 3145736 | tf_op jit(solution)/shard_map/ppermute | solution.py:749
  348.6 25.9 %collective-permute-start.42 = (bf16[512,1024]{1,0:T(8,128)(2,1)S(1)}, bf16[512,1024]{1,0:T(8,128)(2,1)S(1)}, u32[]{:S(2)}, u32[]{:S(2)}) collective-permute-start(bf16[512,1024]{1,0:T(8,128)(2,1)S(1)} %copy-done.6), channel_id=1, source_target_pairs={{0,1},{1,0},{2,3},{3,2},{4,5},{5,4},{6,7},{7,6},{8,9},{9,8},{10,11... | collective-permute-start | bytes 3145736 | tf_op jit(solution)/shard_map/ppermute | solution.py:749
  382.6 33.0 %collective-permute-start.45 = (bf16[4,688,256]{2,1,0:T(8,128)(2,1)S(1)}, bf16[4,688,256]{2,1,0:T(8,128)(2,1)S(1)}, u32[]{:S(2)}, u32[]{:S(2)}) collective-permute-start(bf16[4,688,256]{2,1,0:T(8,128)(2,1)S(1)} %get-tuple-element.318), channel_id=1, source_target_pairs={{0,2},{1,3},{2,0},{3,1},{4,6},{5,7},{6,4},{7,5},{8,10},{9,11},{10,... | collective-permute-start | bytes 4227080 | tf_op jit(solution)/shard_map/ppermute | solution.py:754
  416.2 13.3 %collective-permute-start.46 = (bf16[688,256]{1,0:T(8,128)(2,1)S(1)}, bf16[688,256]{1,0:T(8,128)(2,1)S(1)}, u32[]{:S(2)}, u32[]{:S(2)}) collective-permute-start(bf16[688,256]{1,0:T(8,128)(2,1)S(1)} %fusion.19), channel_id=1, source_target_pairs={{0,4},{4,8},{8,12},{12,0},{1,5},{5,9},{9,13},{13,1},{2,6},{6,10},{... | collective-permute-start | bytes 1056776 | tf_op jit(solution)/shard_map/ppermute | solution.py:759
  429.7 12.3 %collective-permute-start.50 = (bf16[688,256]{1,0:T(8,128)(2,1)S(1)}, bf16[688,256]{1,0:T(8,128)(2,1)S(1)}, u32[]{:S(2)}, u32[]{:S(2)}) collective-permute-start(bf16[688,256]{1,0:T(8,128)(2,1)S(1)} %fusion.10), channel_id=1, source_target_pairs={{0,4},{4,8},{8,12},{12,0},{1,5},{5,9},{9,13},{13,1},{2,6},{6,10},{... | collective-permute-start | bytes 1056776 | tf_op jit(solution)/shard_map/ppermute | solution.py:759
  430.3 45.0 %collective-permute-start.52 = (bf16[4,688,256]{2,1,0:T(8,128)(2,1)}, bf16[4,688,256]{2,1,0:T(8,128)(2,1)}, u32[]{:S(2)}, u32[]{:S(2)}) collective-permute-start(bf16[4,688,256]{2,1,0:T(8,128)(2,1)} %get-tuple-element.353), channel_id=1, source_target_pairs={{0,2},{1,3},{2,0},{3,1},{4,6},{5,7},{6,4},{7,5},{8,10},{9,11},{10,... | collective-permute-start | bytes 4227080 | tf_op jit(solution)/shard_map/ppermute | solution.py:754
  443.1 32.1 %collective-permute-start.53 = (bf16[688,256]{1,0:T(8,128)(2,1)S(1)}, bf16[688,256]{1,0:T(8,128)(2,1)S(1)}, u32[]{:S(2)}, u32[]{:S(2)}) collective-permute-start(bf16[688,256]{1,0:T(8,128)(2,1)S(1)} %fusion.9), channel_id=1, source_target_pairs={{0,4},{4,8},{8,12},{12,0},{1,5},{5,9},{9,13},{13,1},{2,6},{6,10},{... | collective-permute-start | bytes 1056776 | tf_op jit(solution)/shard_map/ppermute | solution.py:759
  443.3 31.2 %collective-permute-start.54 = (bf16[2,256,256]{2,1,0:T(8,128)(2,1)S(1)}, bf16[2,256,256]{2,1,0:T(8,128)(2,1)S(1)}, u32[]{:S(2)}, u32[]{:S(2)}) collective-permute-start(bf16[2,256,256]{2,1,0:T(8,128)(2,1)S(1)} %pad_maximum_fusion.13), channel_id=1, source_target_pairs={{0,12},{4,0},{8,4},{12,8},{1,13},{5,1},{9,5},{13,9},{2,14},{6,2},{... | collective-permute-start | bytes 786440 | tf_op jit(solution)/shard_map/ppermute | solution.py:782
  447.2 28.0 %collective-permute-start.55 = (bf16[2,256,256]{2,1,0:T(8,128)(2,1)S(1)}, bf16[2,256,256]{2,1,0:T(8,128)(2,1)S(1)}, u32[]{:S(2)}, u32[]{:S(2)}) collective-permute-start(bf16[2,256,256]{2,1,0:T(8,128)(2,1)S(1)} %pad_maximum_fusion.14), channel_id=1, source_target_pairs={{0,8},{4,12},{8,0},{12,4},{1,9},{5,13},{9,1},{13,5},{2,10},{6,14},... | collective-permute-start | bytes 786440 | tf_op jit(solution)/shard_map/ppermute | solution.py:782
  447.3 27.9 %collective-permute-start.56 = (bf16[2,256,256]{2,1,0:T(8,128)(2,1)S(1)}, bf16[2,256,256]{2,1,0:T(8,128)(2,1)S(1)}, u32[]{:S(2)}, u32[]{:S(2)}) collective-permute-start(bf16[2,256,256]{2,1,0:T(8,128)(2,1)S(1)} %pad_maximum_fusion.15), channel_id=1, source_target_pairs={{0,4},{4,8},{8,12},{12,0},{1,5},{5,9},{9,13},{13,1},{2,6},{6,10},{... | collective-permute-start | bytes 786440 | tf_op jit(solution)/shard_map/ppermute | solution.py:782
  475.3 33.6 %collective-permute-start.51 = (bf16[4,688,256]{2,1,0:T(8,128)(2,1)}, bf16[4,688,256]{2,1,0:T(8,128)(2,1)}, u32[]{:S(2)}, u32[]{:S(2)}) collective-permute-start(bf16[4,688,256]{2,1,0:T(8,128)(2,1)} %get-tuple-element.351), channel_id=1, source_target_pairs={{0,2},{1,3},{2,0},{3,1},{4,6},{5,7},{6,4},{7,5},{8,10},{9,11},{10,... | collective-permute-start | bytes 4227080 | tf_op jit(solution)/shard_map/ppermute | solution.py:754
  478.8 30.1 %collective-permute-start.57 = (bf16[688,256]{1,0:T(8,128)(2,1)}, bf16[688,256]{1,0:T(8,128)(2,1)}, u32[]{:S(2)}, u32[]{:S(2)}) collective-permute-start(bf16[688,256]{1,0:T(8,128)(2,1)} %get-tuple-element.450), channel_id=1, source_target_pairs={{0,12},{4,0},{8,4},{12,8},{1,13},{5,1},{9,5},{13,9},{2,14},{6,2},{... | collective-permute-start | bytes 1056776 | tf_op jit(solution)/shard_map/ppermute | solution.py:782
  482.1 32.5 %collective-permute-start.58 = (bf16[688,256]{1,0:T(8,128)(2,1)}, bf16[688,256]{1,0:T(8,128)(2,1)}, u32[]{:S(2)}, u32[]{:S(2)}) collective-permute-start(bf16[688,256]{1,0:T(8,128)(2,1)} %get-tuple-element.449), channel_id=1, source_target_pairs={{0,8},{4,12},{8,0},{12,4},{1,9},{5,13},{9,1},{13,5},{2,10},{6,14},... | collective-permute-start | bytes 1056776 | tf_op jit(solution)/shard_map/ppermute | solution.py:782
  483.2 31.4 %collective-permute-start.59 = (bf16[688,256]{1,0:T(8,128)(2,1)}, bf16[688,256]{1,0:T(8,128)(2,1)}, u32[]{:S(2)}, u32[]{:S(2)}) collective-permute-start(bf16[688,256]{1,0:T(8,128)(2,1)} %get-tuple-element.448), channel_id=1, source_target_pairs={{0,4},{4,8},{8,12},{12,0},{1,5},{5,9},{9,13},{13,1},{2,6},{6,10},{... | collective-permute-start | bytes 1056776 | tf_op jit(solution)/shard_map/ppermute | solution.py:782
  514.6 10.4 %collective-permute-start.64 = (bf16[2,512,768]{2,1,0:T(8,128)(2,1)}, bf16[2,512,768]{2,1,0:T(8,128)(2,1)}, u32[]{:S(2)}, u32[]{:S(2)}) collective-permute-start(bf16[2,512,768]{2,1,0:T(8,128)(2,1)} %get-tuple-element.387), channel_id=1, source_target_pairs={{0,1},{1,0},{2,3},{3,2},{4,5},{5,4},{6,7},{7,6},{8,9},{9,8},{10,11... | collective-permute-start | bytes 4718600 | tf_op jit(solution)/shard_map/ppermute | solution.py:749
  516.3 15.8 %collective-permute-start.63 = (bf16[256,256]{1,0:T(8,128)(2,1)}, bf16[256,256]{1,0:T(8,128)(2,1)S(1)}, u32[]{:S(2)}, u32[]{:S(2)}) collective-permute-start(bf16[256,256]{1,0:T(8,128)(2,1)} %fusion.44), channel_id=1, source_target_pairs={{0,2},{1,3},{2,0},{3,1},{4,6},{5,7},{6,4},{7,5},{8,10},{9,11},{10,... | collective-permute-start | bytes 393224 | tf_op jit(solution)/shard_map/ppermute | solution.py:754
  522.2 14.9 %collective-permute-start.62 = (bf16[256,1024]{1,0:T(8,128)(2,1)S(1)}, bf16[256,1024]{1,0:T(8,128)(2,1)S(1)}, u32[]{:S(2)}, u32[]{:S(2)}) collective-permute-start(bf16[256,1024]{1,0:T(8,128)(2,1)S(1)} %slice_select_fusion.1), channel_id=1, source_target_pairs={{0,2},{1,3},{2,0},{3,1},{4,6},{5,7},{6,4},{7,5},{8,10},{9,11},{10,... | collective-permute-start | bytes 1572872 | tf_op jit(solution)/shard_map/ppermute | solution.py:754
  523.8 13.3 %collective-permute-start.67 = (bf16[256,256]{1,0:T(8,128)(2,1)S(1)}, bf16[256,256]{1,0:T(8,128)(2,1)S(1)}, u32[]{:S(2)}, u32[]{:S(2)}) collective-permute-start(bf16[256,256]{1,0:T(8,128)(2,1)S(1)} %get-tuple-element.395), channel_id=1, source_target_pairs={{0,8},{4,12},{8,0},{12,4},{1,9},{5,13},{9,1},{13,5},{2,10},{6,14},... | collective-permute-start | bytes 393224 | tf_op jit(solution)/shard_map/ppermute | solution.py:782
  525.0 12.1 %collective-permute-start.68 = (bf16[256,256]{1,0:T(8,128)(2,1)S(1)}, bf16[256,256]{1,0:T(8,128)(2,1)S(1)}, u32[]{:S(2)}, u32[]{:S(2)}) collective-permute-start(bf16[256,256]{1,0:T(8,128)(2,1)S(1)} %get-tuple-element.396), channel_id=1, source_target_pairs={{0,4},{4,8},{8,12},{12,0},{1,5},{5,9},{9,13},{13,1},{2,6},{6,10},{... | collective-permute-start | bytes 393224 | tf_op jit(solution)/shard_map/ppermute | solution.py:782
  537.2 25.0 %collective-permute-start.69 = (bf16[4,384,256]{2,1,0:T(8,128)(2,1)S(1)}, bf16[4,384,256]{2,1,0:T(8,128)(2,1)S(1)}, u32[]{:S(2)}, u32[]{:S(2)}) collective-permute-start(bf16[4,384,256]{2,1,0:T(8,128)(2,1)S(1)} %get-tuple-element.460), channel_id=1, source_target_pairs={{0,2},{1,3},{2,0},{3,1},{4,6},{5,7},{6,4},{7,5},{8,10},{9,11},{10,... | collective-permute-start | bytes 2359304 | tf_op jit(solution)/shard_map/ppermute | solution.py:754
  539.1 17.5 %collective-permute-start.70 = (f32[3,1024]{1,0:T(4,128)S(1)}, f32[3,1024]{1,0:T(4,128)S(1)}, u32[]{:S(2)}, u32[]{:S(2)}) collective-permute-start(f32[3,1024]{1,0:T(4,128)S(1)} %fusion.61), channel_id=1, source_target_pairs={{0,2},{1,3},{2,0},{3,1},{4,6},{5,7},{6,4},{7,5},{8,10},{9,11},{10,... | collective-permute-start | bytes 36872 | tf_op jit(solution)/shard_map/ppermute | solution.py:754
  541.2 16.3 %collective-permute-start.71 = (bf16[432,256]{1,0:T(8,128)(2,1)S(1)}, bf16[432,256]{1,0:T(8,128)(2,1)S(1)}, u32[]{:S(2)}, u32[]{:S(2)}) collective-permute-start(bf16[432,256]{1,0:T(8,128)(2,1)S(1)} %get-tuple-element.443), channel_id=1, source_target_pairs={{0,12},{4,0},{8,4},{12,8},{1,13},{5,1},{9,5},{13,9},{2,14},{6,2},{... | collective-permute-start | bytes 663560 | tf_op jit(solution)/shard_map/ppermute | solution.py:782
  541.3 20.9 %collective-permute-start.72 = (bf16[432,256]{1,0:T(8,128)(2,1)S(1)}, bf16[432,256]{1,0:T(8,128)(2,1)S(1)}, u32[]{:S(2)}, u32[]{:S(2)}) collective-permute-start(bf16[432,256]{1,0:T(8,128)(2,1)S(1)} %get-tuple-element.442), channel_id=1, source_target_pairs={{0,8},{4,12},{8,0},{12,4},{1,9},{5,13},{9,1},{13,5},{2,10},{6,14},... | collective-permute-start | bytes 663560 | tf_op jit(solution)/shard_map/ppermute | solution.py:782
  542.9 19.4 %collective-permute-start.73 = (bf16[432,256]{1,0:T(8,128)(2,1)S(1)}, bf16[432,256]{1,0:T(8,128)(2,1)S(1)}, u32[]{:S(2)}, u32[]{:S(2)}) collective-permute-start(bf16[432,256]{1,0:T(8,128)(2,1)S(1)} %get-tuple-element.441), channel_id=1, source_target_pairs={{0,4},{4,8},{8,12},{12,0},{1,5},{5,9},{9,13},{13,1},{2,6},{6,10},{... | collective-permute-start | bytes 663560 | tf_op jit(solution)/shard_map/ppermute | solution.py:782
  556.6 18.4 %collective-permute-start.74 = (bf16[4,384,256]{2,1,0:T(8,128)(2,1)S(1)}, bf16[4,384,256]{2,1,0:T(8,128)(2,1)S(1)}, u32[]{:S(2)}, u32[]{:S(2)}) collective-permute-start(bf16[4,384,256]{2,1,0:T(8,128)(2,1)S(1)} %get-tuple-element.461), channel_id=1, source_target_pairs={{0,2},{1,3},{2,0},{3,1},{4,6},{5,7},{6,4},{7,5},{8,10},{9,11},{10,... | collective-permute-start | bytes 2359304 | tf_op jit(solution)/shard_map/ppermute | solution.py:754
  562.4 12.5 %collective-permute-start.76 = (bf16[384,256]{1,0:T(8,128)(2,1)S(1)}, bf16[384,256]{1,0:T(8,128)(2,1)S(1)}, u32[]{:S(2)}, u32[]{:S(2)}) collective-permute-start(bf16[384,256]{1,0:T(8,128)(2,1)S(1)} %get-tuple-element.457), channel_id=1, source_target_pairs={{0,12},{4,0},{8,4},{12,8},{1,13},{5,1},{9,5},{13,9},{2,14},{6,2},{... | collective-permute-start | bytes 589832 | tf_op jit(solution)/shard_map/ppermute | solution.py:782
  562.5 18.7 %collective-permute-start.77 = (bf16[384,256]{1,0:T(8,128)(2,1)S(1)}, bf16[384,256]{1,0:T(8,128)(2,1)S(1)}, u32[]{:S(2)}, u32[]{:S(2)}) collective-permute-start(bf16[384,256]{1,0:T(8,128)(2,1)S(1)} %get-tuple-element.456), channel_id=1, source_target_pairs={{0,8},{4,12},{8,0},{12,4},{1,9},{5,13},{9,1},{13,5},{2,10},{6,14},... | collective-permute-start | bytes 589832 | tf_op jit(solution)/shard_map/ppermute | solution.py:782
  563.6 17.6 %collective-permute-start.78 = (bf16[384,256]{1,0:T(8,128)(2,1)S(1)}, bf16[384,256]{1,0:T(8,128)(2,1)S(1)}, u32[]{:S(2)}, u32[]{:S(2)}) collective-permute-start(bf16[384,256]{1,0:T(8,128)(2,1)S(1)} %get-tuple-element.455), channel_id=1, source_target_pairs={{0,4},{4,8},{8,12},{12,0},{1,5},{5,9},{9,13},{13,1},{2,6},{6,10},{... | collective-permute-start | bytes 589832 | tf_op jit(solution)/shard_map/ppermute | solution.py:782
  590.2 10.0 %collective-permute-start.82 = (bf16[384,256]{1,0:T(8,128)(2,1)}, bf16[384,256]{1,0:T(8,128)(2,1)S(1)}, u32[]{:S(2)}, u32[]{:S(2)}) collective-permute-start(bf16[384,256]{1,0:T(8,128)(2,1)} %get-tuple-element.422), channel_id=1, source_target_pairs={{0,4},{4,8},{8,12},{12,0},{1,5},{5,9},{9,13},{13,1},{2,6},{6,10},{... | collective-permute-start | bytes 589832 | tf_op jit(solution)/shard_map/ppermute | solution.py:782
  590.3 17.1 %collective-permute-start.81 = (bf16[384,256]{1,0:T(8,128)(2,1)}, bf16[384,256]{1,0:T(8,128)(2,1)S(1)}, u32[]{:S(2)}, u32[]{:S(2)}) collective-permute-start(bf16[384,256]{1,0:T(8,128)(2,1)} %get-tuple-element.421), channel_id=1, source_target_pairs={{0,8},{4,12},{8,0},{12,4},{1,9},{5,13},{9,1},{13,5},{2,10},{6,14},... | collective-permute-start | bytes 589832 | tf_op jit(solution)/shard_map/ppermute | solution.py:782
  592.3 15.1 %collective-permute-start.80 = (bf16[384,256]{1,0:T(8,128)(2,1)}, bf16[384,256]{1,0:T(8,128)(2,1)S(1)}, u32[]{:S(2)}, u32[]{:S(2)}) collective-permute-start(bf16[384,256]{1,0:T(8,128)(2,1)} %get-tuple-element.420), channel_id=1, source_target_pairs={{0,12},{4,0},{8,4},{12,8},{1,13},{5,1},{9,5},{13,9},{2,14},{6,2},{... | collective-permute-start | bytes 589832 | tf_op jit(solution)/shard_map/ppermute | solution.py:782
  (112 other events, 1148.2 us)

commit v8 on v6

--- a/solution.py
+++ b/solution.py
@@ -649,7 +649,7 @@
 
     @pl.when(t == 0)
     def _():
-        start_all(weight, 0, w_ref, sems)
+        start_all(weight, 0, w_ref, sems, range(1))
         acc[...] = jnp.zeros_like(acc)
 
     cos, sin = cos_ref[...], sin_ref[...]
@@ -670,6 +670,11 @@
         dp_scr[:, which * width : (which + 1) * width] = out.astype(BF)
     dp_scr[:, 2 * width :] = (dv_ref[...].astype(F32) + dvr_ref[...].astype(F32)).astype(BF)
     wait_for(weight, 0, w_ref, sems, t)
+
+    @pl.when(t == 0)
+    def _():
+        start_all(weight, 0, w_ref, sems, range(1, 4))
+
     dp = dp_scr[...]
     put(t < 2, dpn_ref, dpf_ref, dp, 0)
     for r in range(4):

time: 619 us -> 619 us (level)
  no operation moved by 1% of the time
where the time goes in v8:
time: 619 us; the launch traced here: 609 us
  Pallas kernels  261 us (42%)
  waiting for transfers between devices  207 us (33%)
  starting transfers between devices  68.3 us (11%)
  other arithmetic  46.2 us (7%)
  local copies, waits for them, and re-layouts  24.3 us (4%)
    ppermute x19, waiting for transfers between devices, y_swap(): return lax.ppermute(value, 'tensor', [(i, i ^ 2) for i in range(n)])  59.3 us
    ppermute x12, waiting for transfers between devices, ring(): return lax.ppermute(value, 'dp', [(i, (i + 1) % n) for i in range(n)])  54.2 us
    pallas_call x2, Pallas kernels, attend_back_call(): pl.pallas_call(functools.partial(attend_back_kernel, scale), grid=(pairs,...  53.3 us
    pallas_call x2, Pallas kernels, ffn_back_call(): pl.pallas_call(functools.partial(ffn_back_kernel, out_low), grid=(2,), in...  50.4 us
    pallas_call x2, Pallas kernels, ffn_up_call(): pl.pallas_call(functools.partial(ffn_up_kernel, save, out_low), grid=(2,)...  34.9 us
    pallas_call x2, Pallas kernels, qkv_back_call(): pl.pallas_call(qkv_back_kernel, grid=(4,), in_specs=[col] * 7 + [whole((r...  33.1 us
    ppermute x18, waiting for transfers between devices, to_owner(): return lax.ppermute(part, 'dp', [(i, (i - r) % n) for i in range(n)])  30.6 us
    pallas_call x2, Pallas kernels, attend_call(): pl.pallas_call(functools.partial(attend_kernel, scale), grid=(pairs,), in...  30.3 us
  transfers between devices with their start and end apart: 83, of which 35 were waited for; matrix products, arithmetic and copies ran while one was open for 8% of the time, Pallas kernels for 22%

profile of v8, /device:TPU:0, one launch (start us, length us, event | category | flops | bytes accessed | tf_op | source)
XLA Modules:
  0.0 609.3 jit_solution(2296740147253879095)
XLA Ops:
  4.3 3.1 collective-permute-start
  7.4 1.7 fusion.14
  9.1 1.6 collective-permute-start.1
  15.5 7.0 %collective-permute-done.1 = bf16[256,1024]{1,0:T(8,128)(2,1)S(1)} collective-permute-done((bf16[256,1024]{1,0:T(8,128)(2,1)S(1)}, bf16[256,1024]{1,0:T(8,128)(2,1)S(1)}, u32[]{:S(2)}, u32[]{:S(2)}) %collective-permute-start.1) | collective-permute-done | bytes 524320 | tf_op jit(solution)/shard_map/ppermute | solution.py:756
  28.7 8.3 %collective-permute-done.2 = bf16[1040,256]{1,0:T(8,128)(2,1)S(1)} collective-permute-done((bf16[1040,256]{1,0:T(8,128)(2,1)S(1)}, bf16[1040,256]{1,0:T(8,128)(2,1)S(1)}, u32[]{:S(2)}, u32[]{:S(2)}) %collective-permute-start.2) | collective-permute-done | bytes 532512 | tf_op jit(solution)/shard_map/ppermute | solution.py:761
  41.1 9.6 %collective-permute-done.4 = bf16[1040,256]{1,0:T(8,128)(2,1)} collective-permute-done((bf16[1040,256]{1,0:T(8,128)(2,1)S(1)}, bf16[1040,256]{1,0:T(8,128)(2,1)}, u32[]{:S(2)}, u32[]{:S(2)}) %collective-permute-start.4) | collective-permute-done | bytes 532512 | tf_op jit(solution)/shard_map/ppermute | solution.py:761
  52.9 12.3 %collective-permute-done.8 = bf16[336,256]{1,0:T(8,128)(2,1)S(1)} collective-permute-done((bf16[336,256]{1,0:T(8,128)(2,1)S(1)}, bf16[336,256]{1,0:T(8,128)(2,1)S(1)}, u32[]{:S(2)}, u32[]{:S(2)}) %collective-permute-start.8) | collective-permute-done | bytes 172064 | tf_op jit(solution)/shard_map/ppermute | solution.py:756
  65.2 2.0 collective-permute-done.6
  67.2 1.6 collective-permute-start.10
  70.8 10.4 %collective-permute-done.11 = bf16[352,256]{1,0:T(8,128)(2,1)S(1)} collective-permute-done((bf16[352,256]{1,0:T(8,128)(2,1)S(1)}, bf16[352,256]{1,0:T(8,128)(2,1)S(1)}, u32[]{:S(2)}, u32[]{:S(2)}) %collective-permute-start.11) | collective-permute-done | bytes 180256 | tf_op jit(solution)/shard_map/ppermute | solution.py:756
  81.3 1.7 collective-permute-done.9
  86.4 2.3 pad_maximum_fusion.7.refs_3_
  88.7 9.0 %collective-permute-done.12 = bf16[1376,256]{1,0:T(8,128)(2,1)S(1)} collective-permute-done((bf16[1376,256]{1,0:T(8,128)(2,1)}, bf16[1376,256]{1,0:T(8,128)(2,1)S(1)}, u32[]{:S(2)}, u32[]{:S(2)}) %collective-permute-start.12) | collective-permute-done | bytes 704544 | tf_op jit(solution)/shard_map/ppermute | solution.py:761
  106.6 10.7 %shard_map.171 = (bf16[512,1024]{1,0:T(8,128)(2,1)}, bf16[512,1024]{1,0:T(8,128)(2,1)}, bf16[512,1024]{1,0:T(8,128)(2,1)}) custom-call(bf16[512,1024]{1,0:T(8,128)(2,1)} %maximum_select_fusion.1.x_ref.dy_ref, f32[1,1024]{1,0:T(1,128)} %bitcast.179, s32[1]{0:T(128)} %bitcast.27.zi_ref, f32[512,128]{1,0:T(8,128)} %pad_maximum_fusion.11.cos_ref, ...), custom_call_target="tpu_custom_call" | custom-call | flops 3221225472 | bytes 14680064 | tf_op jit(solution)/shard_map/pallas_call | solution.py:180
  117.3 5.8 collective-permute-done.14.refs_1_.refs_17_
  128.3 15.2 %shard_map.172 = (bf16[512,1024]{1,0:T(8,128)(2,1)}, f32[512,1024]{1,0:T(8,128)}) custom-call(bf16[512,1024]{1,0:T(8,128)(2,1)} %get-tuple-element.264.q_ref, bf16[512,1024]{1,0:T(8,128)(2,1)} %get-tuple-element.265.ko_ref, bf16[512,1024]{1,0:T(8,128)(2,1)} %copy-done.91, bf16[512,1024]{1,0:T(8,128)(2,1)} %get-tuple-element.266.vo_ref, ...), custom_call_target="tpu_custom_call" | custom-call | flops 4294967296 | bytes 10485760 | tf_op jit(solution)/shard_map/pallas_call | solution.py:243
  148.8 1.7 pad_maximum_fusion.2.refs_10_
  150.7 12.4 %collective-permute-done.24.refs_3_.refs_19_ = bf16[2,688,256]{2,1,0:T(8,128)(2,1)S(1)} collective-permute-done((bf16[2,688,256]{2,1,0:T(8,128)(2,1)S(1)}, bf16[2,688,256]{2,1,0:T(8,128)(2,1)S(1)}, u32[]{:S(2)}, u32[]{:S(2)}) %collective-permute-start.24) | collective-permute-done | bytes 704544 | tf_op jit(solution)/shard_map/ppermute | solution.py:761
  167.5 16.8 %shard_map.173 = (f32[512,1024]{1,0:T(8,128)}, bf16[512,1408]{1,0:T(8,128)(2,1)}, bf16[512,1408]{1,0:T(8,128)(2,1)}) custom-call(bf16[512,1024]{1,0:T(8,128)(2,1)} %maximum_select_fusion.1.x_ref.dy_ref, bf16[512,1024]{1,0:T(8,128)(2,1)} %get-tuple-element.271.o_ref, f32[1,1024]{1,0:T(1,128)} %bitcast.193, s32[1]{0:T(128)} %bitcast.27.zi_ref, ...), custom_call_target="tpu_custom_call" | custom-call | flops 6845104128 | bytes 21757952 | tf_op jit(solution)/shard_map/pallas_call | solution.py:394
  185.9 9.6 %shard_map.174 = bf16[512,1024]{1,0:T(8,128)(2,1)} custom-call(f32[512,1024]{1,0:T(8,128)} %get-tuple-element.279.h_ref, bf16[512,1408]{1,0:T(8,128)(2,1)} %get-tuple-element.280.zn_ref, bf16[512,1408]{1,0:T(8,128)(2,1)} %get-tuple-element.281.zf_ref, s32[1]{0:T(128)} %bitcast.27.zi_ref, bf16[2,688,256]{2,1,0:T(8,128)(2,1)} %copy-done.25, ...), custom_call_target="tpu_custom_call" | custom-call | flops 2885681152 | bytes 9830400 | tf_op jit(solution)/shard_map/pallas_call | solution.py:428
  195.6 3.6 collective-permute-start.34
  199.2 22.8 %collective-permute-done.34 = bf16[512,1024]{1,0:T(8,128)(2,1)S(1)} collective-permute-done((bf16[512,1024]{1,0:T(8,128)(2,1)}, bf16[512,1024]{1,0:T(8,128)(2,1)S(1)}, u32[]{:S(2)}, u32[]{:S(2)}) %collective-permute-start.34) | collective-permute-done | bytes 1048608 | tf_op jit(solution)/shard_map/ppermute | solution.py:1008
  223.1 11.2 %shard_map.175 = (bf16[512,1024]{1,0:T(8,128)(2,1)}, bf16[512,1024]{1,0:T(8,128)(2,1)}, bf16[512,1024]{1,0:T(8,128)(2,1)}, bf16[512,1024]{1,0:T(8,128)(2,1)}, bf...) custom-call(bf16[512,1024]{1,0:T(8,128)(2,1)} %broadcast_select_fusion.2.x_ref, f32[1,1024]{1,0:T(1,128)} %bitcast.180, ...), custom_call_target="tpu_custom_call" | custom-call | flops 3221225472 | bytes 14680064 | tf_op jit(solution)/shard_map/pallas_call | solution.py:180
  234.8 2.4 collective-permute-done.35.kx_ref
  239.7 15.1 %shard_map.176 = (bf16[512,1024]{1,0:T(8,128)(2,1)}, f32[512,1024]{1,0:T(8,128)}) custom-call(bf16[512,1024]{1,0:T(8,128)(2,1)} %get-tuple-element.284.q_ref, bf16[512,1024]{1,0:T(8,128)(2,1)} %get-tuple-element.285.ko_ref, bf16[512,1024]{1,0:T(8,128)(2,1)} %copy-done.89, bf16[512,1024]{1,0:T(8,128)(2,1)} %get-tuple-element.286.vo_ref, ...), custom_call_target="tpu_custom_call" | custom-call | flops 4294967296 | bytes 10485760 | tf_op jit(solution)/shard_map/pallas_call | solution.py:243
  254.9 18.1 %shard_map.177 = (f32[512,1024]{1,0:T(8,128)}, bf16[512,1408]{1,0:T(8,128)(2,1)}, bf16[512,1408]{1,0:T(8,128)(2,1)}, bf16[512,1024]{1,0:T(8,128)(2,1)}, bf16[2,5...) custom-call(bf16[512,1024]{1,0:T(8,128)(2,1)} %broadcast_select_fusion.2.x_ref, ...), custom_call_target="tpu_custom_call" | custom-call | flops 6845104128 | bytes 21757952 | tf_op jit(solution)/shard_map/pallas_call | solution.py:394
  272.9 25.3 %shard_map.178 = (f32[512,1024]{1,0:T(8,128)}, bf16[512,1024]{1,0:T(8,128)(2,1)}, bf16[512,1024]{1,0:T(8,128)(2,1)}, bf16[512,1408]{1,0:T(8,128)(2,1)}, bf16[512...) custom-call(bf16[512,1024]{1,0:T(8,128)(2,1)} %maximum_select_fusion.1.x_ref.dy_re, ...), custom_call_target="tpu_custom_call" | custom-call | flops 9730785280 | bytes 27394048 | tf_op jit(solution)/shard_map/pallas_call | solution.py:512
  298.3 26.7 %shard_map.179 = (bf16[512,1024]{1,0:T(8,128)(2,1)}, bf16[512,1024]{1,0:T(8,128)(2,1)}, bf16[512,1024]{1,0:T(8,128)(2,1)}, bf16[512,1024]{1,0:T(8,128)(2,1)}, bf...) custom-call(bf16[512,1024]{1,0:T(8,128)(2,1)} %get-tuple-element.284.q_ref, bf16[512,1024]{1,0:T(8,128)(2,1)} %get-tuple-element.285.ko_ref, ...), custom_call_target="tpu_custom_call" | custom-call | flops 10737418240 | bytes 20971520 | tf_op jit(solution)/shard_map/pallas_call | solution.py:614
  325.6 2.3 collective-permute-done.37.dkr_ref
  330.4 16.8 %shard_map.180 = (bf16[2,512,768]{2,1,0:T(8,128)(2,1)}, bf16[2,512,768]{2,1,0:T(8,128)(2,1)}, f32[512,1024]{1,0:T(8,128)}, bf16[512,1024]{1,0:T(8,128)(2,1)}, f32[1,1024]{1,0:T(1,128)}) custom-call(bf16[512,1024]{1,0:T(8,128)(2,1)} %get-tuple-element.295.dq_ref, bf16[512,1024]{1,0:T(8,128)(2,1)} %get-tuple-element.296.dk_ref, bf16[512,1024]{1,0:T(8,128)(2,1)} %copy-done.46, ...), custom_call_target="tpu_custom_call" | custom-call | flops 3221225472 | bytes 27262976 | tf_op jit(solution)/shard_map/pallas_call | solution.py:702
  349.6 9.9 %shard_map.181 = f32[512,1024]{1,0:T(8,128)} custom-call(f32[512,1024]{1,0:T(8,128)} %get-tuple-element.288.h_ref, bf16[512,1408]{1,0:T(8,128)(2,1)} %get-tuple-element.308.zn_ref.ao_ref, bf16[512,1408]{1,0:T(8,128)(2,1)} %get-tuple-element.309.zf_ref, s32[1]{0:T(128)} %bitcast.27.zi_ref, bf16[2,688,256]{2,1,0:T(8,128)(2,1)} %copy-done.25, ...), custom_call_target="tpu_custom_call" | custom-call | flops 2885681152 | bytes 9830400 | tf_op jit(solution)/shard_map/pallas_call | solution.py:428
  359.6 15.4 %collective-permute-done.39 = bf16[512,1024]{1,0:T(8,128)(2,1)} collective-permute-done((bf16[512,1024]{1,0:T(8,128)(2,1)}, bf16[512,1024]{1,0:T(8,128)(2,1)}, u32[]{:S(2)}, u32[]{:S(2)}) %collective-permute-start.39) | collective-permute-done | bytes 1048608 | tf_op jit(solution)/shard_map/ppermute | solution.py:1028
  375.0 2.1 broadcast_select_fusion.1.bo_ref.dy_ref
  377.2 2.6 collective-permute-done.44.bx_ref
  379.9 3.2 shard_map.182
  384.7 25.1 %shard_map.183 = (f32[512,1024]{1,0:T(8,128)}, bf16[512,1024]{1,0:T(8,128)(2,1)}, bf16[512,1024]{1,0:T(8,128)(2,1)}, bf16[512,1408]{1,0:T(8,128)(2,1)}, bf16[512...) custom-call(bf16[512,1024]{1,0:T(8,128)(2,1)} %copy-done.2, ...), custom_call_target="tpu_custom_call" | custom-call | flops 9730785280 | bytes 27394048 | tf_op jit(solution)/shard_map/pallas_call | solution.py:512
  409.8 6.3 %collective-permute-done.45 = bf16[4,688,256]{2,1,0:T(8,128)(2,1)S(1)} collective-permute-done((bf16[4,688,256]{2,1,0:T(8,128)(2,1)S(1)}, bf16[4,688,256]{2,1,0:T(8,128)(2,1)S(1)}, u32[]{:S(2)}, u32[]{:S(2)}) %collective-permute-start.45) | collective-permute-done | bytes 1409056 | tf_op jit(solution)/shard_map/ppermute | solution.py:756
  417.1 6.0 collective-permute-done.49.bx_ref
  425.7 4.3 shard_map.184
  433.5 4.3 shard_map.186
  437.8 4.8 collective-permute-done.50
  443.8 3.9 collective-permute-start.54
  448.4 26.6 %shard_map.187 = (bf16[512,1024]{1,0:T(8,128)(2,1)}, bf16[512,1024]{1,0:T(8,128)(2,1)}, bf16[512,1024]{1,0:T(8,128)(2,1)}, bf16[512,1024]{1,0:T(8,128)(2,1)}, bf...) custom-call(bf16[512,1024]{1,0:T(8,128)(2,1)} %get-tuple-element.284.q_ref, bf16[512,1024]{1,0:T(8,128)(2,1)} %get-tuple-element.285.ko_ref, ...), custom_call_target="tpu_custom_call" | custom-call | flops 10737418240 | bytes 20971520 | tf_op jit(solution)/shard_map/pallas_call | solution.py:614
  477.0 2.3 fusion.24
  479.3 3.3 collective-permute-start.57
  484.6 16.3 %shard_map.188 = (bf16[2,512,768]{2,1,0:T(8,128)(2,1)}, bf16[2,512,768]{2,1,0:T(8,128)(2,1)}, f32[512,1024]{1,0:T(8,128)}, bf16[512,1024]{1,0:T(8,128)(2,1)}, f32[1,1024]{1,0:T(1,128)}) custom-call(bf16[512,1024]{1,0:T(8,128)(2,1)} %get-tuple-element.365.dq_ref, bf16[512,1024]{1,0:T(8,128)(2,1)} %get-tuple-element.366.dk_ref, ...), custom_call_target="tpu_custom_call" | custom-call | flops 3221225472 | bytes 27262976 | tf_op jit(solution)/shard_map/pallas_call | solution.py:702
  500.9 8.5 %collective-permute-done.51 = bf16[4,688,256]{2,1,0:T(8,128)(2,1)} collective-permute-done((bf16[4,688,256]{2,1,0:T(8,128)(2,1)}, bf16[4,688,256]{2,1,0:T(8,128)(2,1)}, u32[]{:S(2)}, u32[]{:S(2)}) %collective-permute-start.51) | collective-permute-done | bytes 1409056 | tf_op jit(solution)/shard_map/ppermute | solution.py:756
  509.4 5.7 collective-permute-done.58
  515.2 1.6 fusion.44
  525.3 2.1 collective-permute-start.68
  527.4 4.9 shard_map.189
  532.3 8.5 %collective-permute-done.67 = bf16[336,256]{1,0:T(8,128)(2,1)S(1)} collective-permute-done((bf16[336,256]{1,0:T(8,128)(2,1)S(1)}, bf16[336,256]{1,0:T(8,128)(2,1)S(1)}, u32[]{:S(2)}, u32[]{:S(2)}) %collective-permute-start.67) | collective-permute-done | bytes 172064 | tf_op jit(solution)/shard_map/ppermute | solution.py:784
  544.8 1.8 collective-permute-start.72
  546.6 1.9 collective-permute-start.73
  548.5 11.7 %collective-permute-done.70 = f32[3,1024]{1,0:T(4,128)S(1)} collective-permute-done((f32[3,1024]{1,0:T(4,128)S(1)}, f32[3,1024]{1,0:T(4,128)S(1)}, u32[]{:S(2)}, u32[]{:S(2)}) %collective-permute-start.70) | collective-permute-done | bytes 12320 | tf_op jit(solution)/shard_map/ppermute | solution.py:756
  563.6 1.9 collective-permute-start.78
  567.9 7.2 %collective-permute-done.75 = f32[3,1024]{1,0:T(4,128)S(1)} collective-permute-done((f32[3,1024]{1,0:T(4,128)S(1)}, f32[3,1024]{1,0:T(4,128)S(1)}, u32[]{:S(2)}, u32[]{:S(2)}) %collective-permute-start.75) | collective-permute-done | bytes 12320 | tf_op jit(solution)/shard_map/ppermute | solution.py:1107
  575.1 3.0 collective-permute-done.74
  578.1 2.8 collective-permute-done.77
  583.3 2.1 fusion.5
  586.7 1.6 fusion.8
  592.0 2.8 collective-permute-start.80
  596.2 4.1 collective-permute-done.82
  600.3 7.2 %collective-permute-done.81 = bf16[384,256]{1,0:T(8,128)(2,1)S(1)} collective-permute-done((bf16[384,256]{1,0:T(8,128)(2,1)}, bf16[384,256]{1,0:T(8,128)(2,1)S(1)}, u32[]{:S(2)}, u32[]{:S(2)}) %collective-permute-start.81) | collective-permute-done | bytes 196640 | tf_op jit(solution)/shard_map/ppermute | solution.py:784
  (428 shorter events, 103.9 us)
Async XLA Ops:
  4.3 18.2 %collective-permute-start = (bf16[1040,256]{1,0:T(8,128)(2,1)S(1)}, bf16[1040,256]{1,0:T(8,128)(2,1)S(1)}, u32[]{:S(2)}, u32[]{:S(2)}) collective-permute-start(bf16[1040,256]{1,0:T(8,128)(2,1)S(1)} %fusion.12), channel_id=1, source_target_pairs={{0,4},{4,8},{8,12},{12,0},{1,5},{5,9},{9,13},{13,1},{2,6},{6,10},{... | collective-permute-start | bytes 1597448 | tf_op jit(solution)/shard_map/ppermute | solution.py:761
  9.1 13.4 %collective-permute-start.1 = (bf16[256,1024]{1,0:T(8,128)(2,1)S(1)}, bf16[256,1024]{1,0:T(8,128)(2,1)S(1)}, u32[]{:S(2)}, u32[]{:S(2)}) collective-permute-start(bf16[256,1024]{1,0:T(8,128)(2,1)S(1)} %get-tuple-element.459), channel_id=1, source_target_pairs={{0,2},{1,3},{2,0},{3,1},{4,6},{5,7},{6,4},{7,5},{8,10},{9,11},{10,... | collective-permute-start | bytes 1572872 | tf_op jit(solution)/shard_map/ppermute | solution.py:756
  22.6 14.4 %collective-permute-start.2 = (bf16[1040,256]{1,0:T(8,128)(2,1)S(1)}, bf16[1040,256]{1,0:T(8,128)(2,1)S(1)}, u32[]{:S(2)}, u32[]{:S(2)}) collective-permute-start(bf16[1040,256]{1,0:T(8,128)(2,1)S(1)} %collective-permute-done), channel_id=1, source_target_pairs={{0,4},{4,8},{8,12},{12,0},{1,5},{5,9},{9,13},{13,1},{2,6},{6,10},{... | collective-permute-start | bytes 1597448 | tf_op jit(solution)/shard_map/ppermute | solution.py:761
  24.1 12.9 %collective-permute-start.3 = (bf16[1040,256]{1,0:T(8,128)(2,1)S(1)}, bf16[1040,256]{1,0:T(8,128)(2,1)S(1)}, u32[]{:S(2)}, u32[]{:S(2)}) collective-permute-start(bf16[1040,256]{1,0:T(8,128)(2,1)S(1)} %fusion.12), channel_id=1, source_target_pairs={{0,2},{1,3},{2,0},{3,1},{4,6},{5,7},{6,4},{7,5},{8,10},{9,11},{10,... | collective-permute-start | bytes 1597448 | tf_op jit(solution)/shard_map/ppermute | solution.py:756
  37.0 13.7 %collective-permute-start.4 = (bf16[1040,256]{1,0:T(8,128)(2,1)S(1)}, bf16[1040,256]{1,0:T(8,128)(2,1)}, u32[]{:S(2)}, u32[]{:S(2)}) collective-permute-start(bf16[1040,256]{1,0:T(8,128)(2,1)S(1)} %collective-permute-done.2), channel_id=1, source_target_pairs={{0,4},{4,8},{8,12},{12,0},{1,5},{5,9},{9,13},{13,1},{2,6},{6,10},{... | collective-permute-start | bytes 1597448 | tf_op jit(solution)/shard_map/ppermute | solution.py:761
  38.1 12.6 %collective-permute-start.5 = (bf16[1040,256]{1,0:T(8,128)(2,1)S(1)}, bf16[1040,256]{1,0:T(8,128)(2,1)}, u32[]{:S(2)}, u32[]{:S(2)}) collective-permute-start(bf16[1040,256]{1,0:T(8,128)(2,1)S(1)} %collective-permute-done), channel_id=1, source_target_pairs={{0,2},{1,3},{2,0},{3,1},{4,6},{5,7},{6,4},{7,5},{8,10},{9,11},{10,... | collective-permute-start | bytes 1597448 | tf_op jit(solution)/shard_map/ppermute | solution.py:756
  50.7 16.5 %collective-permute-start.6 = (bf16[1376,256]{1,0:T(8,128)(2,1)}, bf16[1376,256]{1,0:T(8,128)(2,1)S(1)}, u32[]{:S(2)}, u32[]{:S(2)}) collective-permute-start(bf16[1376,256]{1,0:T(8,128)(2,1)} %bitcast.8), channel_id=1, source_target_pairs={{0,4},{4,8},{8,12},{12,0},{1,5},{5,9},{9,13},{13,1},{2,6},{6,10},{... | collective-permute-start | bytes 2113544 | tf_op jit(solution)/shard_map/ppermute | solution.py:761
  50.8 14.4 %collective-permute-start.7 = (bf16[1040,256]{1,0:T(8,128)(2,1)S(1)}, bf16[1040,256]{1,0:T(8,128)(2,1)S(1)}, u32[]{:S(2)}, u32[]{:S(2)}) collective-permute-start(bf16[1040,256]{1,0:T(8,128)(2,1)S(1)} %collective-permute-done.2), channel_id=1, source_target_pairs={{0,2},{1,3},{2,0},{3,1},{4,6},{5,7},{6,4},{7,5},{8,10},{9,11},{10,... | collective-permute-start | bytes 1597448 | tf_op jit(solution)/shard_map/ppermute | solution.py:756
  52.2 13.0 %collective-permute-start.8 = (bf16[336,256]{1,0:T(8,128)(2,1)S(1)}, bf16[336,256]{1,0:T(8,128)(2,1)S(1)}, u32[]{:S(2)}, u32[]{:S(2)}) collective-permute-start(bf16[336,256]{1,0:T(8,128)(2,1)S(1)} %slice.255), channel_id=1, source_target_pairs={{0,2},{1,3},{2,0},{3,1},{4,6},{5,7},{6,4},{7,5},{8,10},{9,11},{10,... | collective-permute-start | bytes 516104 | tf_op jit(solution)/shard_map/ppermute | solution.py:756
  67.2 15.7 %collective-permute-start.9 = (bf16[1376,256]{1,0:T(8,128)(2,1)S(1)}, bf16[1376,256]{1,0:T(8,128)(2,1)}, u32[]{:S(2)}, u32[]{:S(2)}) collective-permute-start(bf16[1376,256]{1,0:T(8,128)(2,1)S(1)} %collective-permute-done.6), channel_id=1, source_target_pairs={{0,4},{4,8},{8,12},{12,0},{1,5},{5,9},{9,13},{13,1},{2,6},{6,10},{... | collective-permute-start | bytes 2113544 | tf_op jit(solution)/shard_map/ppermute | solution.py:761
  67.2 14.0 %collective-permute-start.10 = (bf16[1040,256]{1,0:T(8,128)(2,1)}, bf16[1040,256]{1,0:T(8,128)(2,1)}, u32[]{:S(2)}, u32[]{:S(2)}) collective-permute-start(bf16[1040,256]{1,0:T(8,128)(2,1)} %collective-permute-done.4), channel_id=1, source_target_pairs={{0,2},{1,3},{2,0},{3,1},{4,6},{5,7},{6,4},{7,5},{8,10},{9,11},{10,... | collective-permute-start | bytes 1597448 | tf_op jit(solution)/shard_map/ppermute | solution.py:756
  70.0 11.2 %collective-permute-start.11 = (bf16[352,256]{1,0:T(8,128)(2,1)S(1)}, bf16[352,256]{1,0:T(8,128)(2,1)S(1)}, u32[]{:S(2)}, u32[]{:S(2)}) collective-permute-start(bf16[352,256]{1,0:T(8,128)(2,1)S(1)} %slice.256), channel_id=1, source_target_pairs={{0,2},{1,3},{2,0},{3,1},{4,6},{5,7},{6,4},{7,5},{8,10},{9,11},{10,... | collective-permute-start | bytes 540680 | tf_op jit(solution)/shard_map/ppermute | solution.py:756
  70.7 33.6 %collective-permute-start.16 = (bf16[2,1040,256]{2,1,0:T(8,128)(2,1)S(1)}, bf16[2,1040,256]{2,1,0:T(8,128)(2,1)}, u32[]{:S(2)}, u32[]{:S(2)}) collective-permute-start(bf16[2,1040,256]{2,1,0:T(8,128)(2,1)S(1)} %pad_maximum_fusion.4.refs_0_), channel_id=1, source_target_pairs={{0,1},{1,0},{2,3},{3,2},{4,5},{5,4},{6,7},{7,6},{8,9},{9,8},{10,11... | collective-permute-start | bytes 3194888 | tf_op jit(solution)/shard_map/ppermute | solution.py:751
  82.9 14.7 %collective-permute-start.12 = (bf16[1376,256]{1,0:T(8,128)(2,1)}, bf16[1376,256]{1,0:T(8,128)(2,1)S(1)}, u32[]{:S(2)}, u32[]{:S(2)}) collective-permute-start(bf16[1376,256]{1,0:T(8,128)(2,1)} %collective-permute-done.9), channel_id=1, source_target_pairs={{0,4},{4,8},{8,12},{12,0},{1,5},{5,9},{9,13},{13,1},{2,6},{6,10},{... | collective-permute-start | bytes 2113544 | tf_op jit(solution)/shard_map/ppermute | solution.py:761
  84.1 22.4 %collective-permute-start.17 = (bf16[2,1040,256]{2,1,0:T(8,128)(2,1)S(1)}, bf16[2,1040,256]{2,1,0:T(8,128)(2,1)}, u32[]{:S(2)}, u32[]{:S(2)}) collective-permute-start(bf16[2,1040,256]{2,1,0:T(8,128)(2,1)S(1)} %pad_maximum_fusion.5.refs_1_), channel_id=1, source_target_pairs={{0,1},{1,0},{2,3},{3,2},{4,5},{5,4},{6,7},{7,6},{8,9},{9,8},{10,11... | collective-permute-start | bytes 3194888 | tf_op jit(solution)/shard_map/ppermute | solution.py:751
  84.3 22.2 %collective-permute-start.18 = (bf16[2,1040,256]{2,1,0:T(8,128)(2,1)S(1)}, bf16[2,1040,256]{2,1,0:T(8,128)(2,1)}, u32[]{:S(2)}, u32[]{:S(2)}) collective-permute-start(bf16[2,1040,256]{2,1,0:T(8,128)(2,1)S(1)} %pad_maximum_fusion.6.refs_2_), channel_id=1, source_target_pairs={{0,1},{1,0},{2,3},{3,2},{4,5},{5,4},{6,7},{7,6},{8,9},{9,8},{10,11... | collective-permute-start | bytes 3194888 | tf_op jit(solution)/shard_map/ppermute | solution.py:751
  84.9 18.1 %collective-permute-start.13 = (bf16[1376,256]{1,0:T(8,128)(2,1)}, bf16[1376,256]{1,0:T(8,128)(2,1)}, u32[]{:S(2)}, u32[]{:S(2)}) collective-permute-start(bf16[1376,256]{1,0:T(8,128)(2,1)} %bitcast.8), channel_id=1, source_target_pairs={{0,2},{1,3},{2,0},{3,1},{4,6},{5,7},{6,4},{7,5},{8,10},{9,11},{10,... | collective-permute-start | bytes 2113544 | tf_op jit(solution)/shard_map/ppermute | solution.py:756
  103.1 20.0 %collective-permute-start.14 = (bf16[2,688,256]{2,1,0:T(8,128)(2,1)S(1)}, bf16[2,688,256]{2,1,0:T(8,128)(2,1)S(1)}, u32[]{:S(2)}, u32[]{:S(2)}) collective-permute-start(bf16[2,688,256]{2,1,0:T(8,128)(2,1)S(1)} %pad_maximum_fusion.9.refs_0_.refs_16_), channel_id=1, source_target_pairs={{0,4},{4,8},{8,12},{12,0},{1,5},{5,9},{9,13},{13,1},{2,6},{6,10},{... | collective-permute-start | bytes 2113544 | tf_op jit(solution)/shard_map/ppermute | solution.py:761
  104.3 18.7 %collective-permute-start.15 = (bf16[1376,256]{1,0:T(8,128)(2,1)S(1)}, bf16[1376,256]{1,0:T(8,128)(2,1)S(1)}, u32[]{:S(2)}, u32[]{:S(2)}) collective-permute-start(bf16[1376,256]{1,0:T(8,128)(2,1)S(1)} %copy-done.49), channel_id=1, source_target_pairs={{0,2},{1,3},{2,0},{3,1},{4,6},{5,7},{6,4},{7,5},{8,10},{9,11},{10,... | collective-permute-start | bytes 2113544 | tf_op jit(solution)/shard_map/ppermute | solution.py:756
  124.7 19.5 %collective-permute-start.20 = (bf16[2,688,256]{2,1,0:T(8,128)(2,1)}, bf16[2,688,256]{2,1,0:T(8,128)(2,1)S(1)}, u32[]{:S(2)}, u32[]{:S(2)}) collective-permute-start(bf16[2,688,256]{2,1,0:T(8,128)(2,1)} %copy-done.29), channel_id=1, source_target_pairs={{0,4},{4,8},{8,12},{12,0},{1,5},{5,9},{9,13},{13,1},{2,6},{6,10},{... | collective-permute-start | bytes 2113544 | tf_op jit(solution)/shard_map/ppermute | solution.py:761
  124.7 19.5 %collective-permute-start.21 = (bf16[1376,256]{1,0:T(8,128)(2,1)}, bf16[1376,256]{1,0:T(8,128)(2,1)S(1)}, u32[]{:S(2)}, u32[]{:S(2)}) collective-permute-start(bf16[1376,256]{1,0:T(8,128)(2,1)} %collective-permute-done.9), channel_id=1, source_target_pairs={{0,2},{1,3},{2,0},{3,1},{4,6},{5,7},{6,4},{7,5},{8,10},{9,11},{10,... | collective-permute-start | bytes 2113544 | tf_op jit(solution)/shard_map/ppermute | solution.py:756
  144.2 18.9 %collective-permute-start.24 = (bf16[2,688,256]{2,1,0:T(8,128)(2,1)S(1)}, bf16[2,688,256]{2,1,0:T(8,128)(2,1)S(1)}, u32[]{:S(2)}, u32[]{:S(2)}) collective-permute-start(bf16[2,688,256]{2,1,0:T(8,128)(2,1)S(1)} %collective-permute-done.20.refs_2_.refs_18_), channel_id=1, source_target_pairs={{0,4},{4,8},{8,12},{12,0},{1,5},{5,9},{9,13},{13,1},{2,6},{6,10},{... | collective-permute-start | bytes 2113544 | tf_op jit(solution)/shard_map/ppermute | solution.py:761
  145.3 17.7 %collective-permute-start.25 = (bf16[1376,256]{1,0:T(8,128)(2,1)S(1)}, bf16[1376,256]{1,0:T(8,128)(2,1)S(1)}, u32[]{:S(2)}, u32[]{:S(2)}) collective-permute-start(bf16[1376,256]{1,0:T(8,128)(2,1)S(1)} %copy-done.52), channel_id=1, source_target_pairs={{0,2},{1,3},{2,0},{3,1},{4,6},{5,7},{6,4},{7,5},{8,10},{9,11},{10,... | collective-permute-start | bytes 2113544 | tf_op jit(solution)/shard_map/ppermute | solution.py:756
  147.8 16.9 %collective-permute-start.26 = (bf16[2,1376,256]{2,1,0:T(8,128)(2,1)S(1)}, bf16[2,1376,256]{2,1,0:T(8,128)(2,1)S(1)}, u32[]{:S(2)}, u32[]{:S(2)}) collective-permute-start(bf16[2,1376,256]{2,1,0:T(8,128)(2,1)S(1)} %pad_maximum_fusion.refs_8_), channel_id=1, source_target_pairs={{0,1},{1,0},{2,3},{3,2},{4,5},{5,4},{6,7},{7,6},{8,9},{9,8},{10,11... | collective-permute-start | bytes 4227080 | tf_op jit(solution)/shard_map/ppermute | solution.py:751
  148.8 16.4 %collective-permute-start.27 = (bf16[2,1376,256]{2,1,0:T(8,128)(2,1)S(1)}, bf16[2,1376,256]{2,1,0:T(8,128)(2,1)S(1)}, u32[]{:S(2)}, u32[]{:S(2)}) collective-permute-start(bf16[2,1376,256]{2,1,0:T(8,128)(2,1)S(1)} %pad_maximum_fusion.1.refs_9_), channel_id=1, source_target_pairs={{0,1},{1,0},{2,3},{3,2},{4,5},{5,4},{6,7},{7,6},{8,9},{9,8},{10,11... | collective-permute-start | bytes 4227080 | tf_op jit(solution)/shard_map/ppermute | solution.py:751
  150.6 14.7 %collective-permute-start.28 = (bf16[2,1376,256]{2,1,0:T(8,128)(2,1)S(1)}, bf16[2,1376,256]{2,1,0:T(8,128)(2,1)S(1)}, u32[]{:S(2)}, u32[]{:S(2)}) collective-permute-start(bf16[2,1376,256]{2,1,0:T(8,128)(2,1)S(1)} %pad_maximum_fusion.2.refs_10_), channel_id=1, source_target_pairs={{0,1},{1,0},{2,3},{3,2},{4,5},{5,4},{6,7},{7,6},{8,9},{9,8},{10,11... | collective-permute-start | bytes 4227080 | tf_op jit(solution)/shard_map/ppermute | solution.py:751
  164.7 19.7 %collective-permute-start.30 = (bf16[2,688,256]{2,1,0:T(8,128)(2,1)S(1)}, bf16[2,688,256]{2,1,0:T(8,128)(2,1)S(1)}, u32[]{:S(2)}, u32[]{:S(2)}) collective-permute-start(bf16[2,688,256]{2,1,0:T(8,128)(2,1)S(1)} %copy-done.26), channel_id=1, source_target_pairs={{0,1},{1,0},{2,3},{3,2},{4,5},{5,4},{6,7},{7,6},{8,9},{9,8},{10,11... | collective-permute-start | bytes 2113544 | tf_op jit(solution)/shard_map/ppermute | solution.py:751
  164.7 19.7 %collective-permute-start.32 = (bf16[2,688,256]{2,1,0:T(8,128)(2,1)S(1)}, bf16[2,688,256]{2,1,0:T(8,128)(2,1)S(1)}, u32[]{:S(2)}, u32[]{:S(2)}) collective-permute-start(bf16[2,688,256]{2,1,0:T(8,128)(2,1)S(1)} %collective-permute-done.20.refs_2_.refs_18_), channel_id=1, source_target_pairs={{0,1},{1,0},{2,3},{3,2},{4,5},{5,4},{6,7},{7,6},{8,9},{9,8},{10,11... | collective-permute-start | bytes 2113544 | tf_op jit(solution)/shard_map/ppermute | solution.py:751
  165.2 19.2 %collective-permute-start.31 = (bf16[2,688,256]{2,1,0:T(8,128)(2,1)S(1)}, bf16[2,688,256]{2,1,0:T(8,128)(2,1)S(1)}, u32[]{:S(2)}, u32[]{:S(2)}) collective-permute-start(bf16[2,688,256]{2,1,0:T(8,128)(2,1)S(1)} %copy-done.30), channel_id=1, source_target_pairs={{0,1},{1,0},{2,3},{3,2},{4,5},{5,4},{6,7},{7,6},{8,9},{9,8},{10,11... | collective-permute-start | bytes 2113544 | tf_op jit(solution)/shard_map/ppermute | solution.py:751
  165.3 19.1 %collective-permute-start.33 = (bf16[2,688,256]{2,1,0:T(8,128)(2,1)S(1)}, bf16[2,688,256]{2,1,0:T(8,128)(2,1)S(1)}, u32[]{:S(2)}, u32[]{:S(2)}) collective-permute-start(bf16[2,688,256]{2,1,0:T(8,128)(2,1)S(1)} %collective-permute-done.24.refs_3_.refs_19_), channel_id=1, source_target_pairs={{0,1},{1,0},{2,3},{3,2},{4,5},{5,4},{6,7},{7,6},{8,9},{9,8},{10,11... | collective-permute-start | bytes 2113544 | tf_op jit(solution)/shard_map/ppermute | solution.py:751
  195.6 26.4 %collective-permute-start.34 = (bf16[512,1024]{1,0:T(8,128)(2,1)}, bf16[512,1024]{1,0:T(8,128)(2,1)S(1)}, u32[]{:S(2)}, u32[]{:S(2)}) collective-permute-start(bf16[512,1024]{1,0:T(8,128)(2,1)} %shard_map.174), channel_id=1, source_target_pairs={{0,16},{1,17},{2,18},{3,19},{4,20},{5,21},{6,22},{7,23},{8,24},{9,... | collective-permute-start | bytes 3145736 | tf_op jit(solution)/shard_map/ppermute | solution.py:1008
  347.1 27.9 %collective-permute-start.40 = (bf16[512,1408]{1,0:T(8,128)(2,1)}, bf16[512,1408]{1,0:T(8,128)(2,1)S(1)}, u32[]{:S(2)}, u32[]{:S(2)}) collective-permute-start(bf16[512,1408]{1,0:T(8,128)(2,1)} %get-tuple-element.309.zf_ref), channel_id=1, source_target_pairs={{0,1},{1,0},{2,3},{3,2},{4,5},{5,4},{6,7},{7,6},{8,9},{9,8},{10,11... | collective-permute-start | bytes 4325384 | tf_op jit(solution)/shard_map/ppermute | solution.py:751
  347.3 27.7 %collective-permute-start.39 = (bf16[512,1024]{1,0:T(8,128)(2,1)}, bf16[512,1024]{1,0:T(8,128)(2,1)}, u32[]{:S(2)}, u32[]{:S(2)}) collective-permute-start(bf16[512,1024]{1,0:T(8,128)(2,1)} %get-tuple-element.307), channel_id=1, source_target_pairs={{16,0},{17,1},{18,2},{19,3},{20,4},{21,5},{22,6},{23,7},{24,8},{25... | collective-permute-start | bytes 3145736 | tf_op jit(solution)/shard_map/ppermute | solution.py:1028
  348.6 26.4 %collective-permute-start.41 = (bf16[512,1024]{1,0:T(8,128)(2,1)S(1)}, bf16[512,1024]{1,0:T(8,128)(2,1)S(1)}, u32[]{:S(2)}, u32[]{:S(2)}) collective-permute-start(bf16[512,1024]{1,0:T(8,128)(2,1)S(1)} %copy-done.10), channel_id=1, source_target_pairs={{0,1},{1,0},{2,3},{3,2},{4,5},{5,4},{6,7},{7,6},{8,9},{9,8},{10,11... | collective-permute-start | bytes 3145736 | tf_op jit(solution)/shard_map/ppermute | solution.py:751
  349.1 25.9 %collective-permute-start.42 = (bf16[512,1024]{1,0:T(8,128)(2,1)S(1)}, bf16[512,1024]{1,0:T(8,128)(2,1)S(1)}, u32[]{:S(2)}, u32[]{:S(2)}) collective-permute-start(bf16[512,1024]{1,0:T(8,128)(2,1)S(1)} %copy-done.6), channel_id=1, source_target_pairs={{0,1},{1,0},{2,3},{3,2},{4,5},{5,4},{6,7},{7,6},{8,9},{9,8},{10,11... | collective-permute-start | bytes 3145736 | tf_op jit(solution)/shard_map/ppermute | solution.py:751
  349.2 10.3 %collective-permute-start.43 = (bf16[512,512]{1,0:T(8,128)(2,1)S(1)}, bf16[512,512]{1,0:T(8,128)(2,1)S(1)}, u32[]{:S(2)}, u32[]{:S(2)}) collective-permute-start(bf16[512,512]{1,0:T(8,128)(2,1)S(1)} %slice.269), channel_id=1, source_target_pairs={{0,1},{1,0},{2,3},{3,2},{4,5},{5,4},{6,7},{7,6},{8,9},{9,8},{10,11... | collective-permute-start | bytes 1572872 | tf_op jit(solution)/shard_map/ppermute | solution.py:751
  383.1 33.0 %collective-permute-start.45 = (bf16[4,688,256]{2,1,0:T(8,128)(2,1)S(1)}, bf16[4,688,256]{2,1,0:T(8,128)(2,1)S(1)}, u32[]{:S(2)}, u32[]{:S(2)}) collective-permute-start(bf16[4,688,256]{2,1,0:T(8,128)(2,1)S(1)} %get-tuple-element.318), channel_id=1, source_target_pairs={{0,2},{1,3},{2,0},{3,1},{4,6},{5,7},{6,4},{7,5},{8,10},{9,11},{10,... | collective-permute-start | bytes 4227080 | tf_op jit(solution)/shard_map/ppermute | solution.py:756
  416.7 13.3 %collective-permute-start.46 = (bf16[688,256]{1,0:T(8,128)(2,1)S(1)}, bf16[688,256]{1,0:T(8,128)(2,1)S(1)}, u32[]{:S(2)}, u32[]{:S(2)}) collective-permute-start(bf16[688,256]{1,0:T(8,128)(2,1)S(1)} %fusion.19), channel_id=1, source_target_pairs={{0,4},{4,8},{8,12},{12,0},{1,5},{5,9},{9,13},{13,1},{2,6},{6,10},{... | collective-permute-start | bytes 1056776 | tf_op jit(solution)/shard_map/ppermute | solution.py:761
  430.2 12.3 %collective-permute-start.50 = (bf16[688,256]{1,0:T(8,128)(2,1)S(1)}, bf16[688,256]{1,0:T(8,128)(2,1)S(1)}, u32[]{:S(2)}, u32[]{:S(2)}) collective-permute-start(bf16[688,256]{1,0:T(8,128)(2,1)S(1)} %fusion.10), channel_id=1, source_target_pairs={{0,4},{4,8},{8,12},{12,0},{1,5},{5,9},{9,13},{13,1},{2,6},{6,10},{... | collective-permute-start | bytes 1056776 | tf_op jit(solution)/shard_map/ppermute | solution.py:761
  430.8 45.0 %collective-permute-start.52 = (bf16[4,688,256]{2,1,0:T(8,128)(2,1)}, bf16[4,688,256]{2,1,0:T(8,128)(2,1)}, u32[]{:S(2)}, u32[]{:S(2)}) collective-permute-start(bf16[4,688,256]{2,1,0:T(8,128)(2,1)} %get-tuple-element.353), channel_id=1, source_target_pairs={{0,2},{1,3},{2,0},{3,1},{4,6},{5,7},{6,4},{7,5},{8,10},{9,11},{10,... | collective-permute-start | bytes 4227080 | tf_op jit(solution)/shard_map/ppermute | solution.py:756
  443.6 32.1 %collective-permute-start.53 = (bf16[688,256]{1,0:T(8,128)(2,1)S(1)}, bf16[688,256]{1,0:T(8,128)(2,1)S(1)}, u32[]{:S(2)}, u32[]{:S(2)}) collective-permute-start(bf16[688,256]{1,0:T(8,128)(2,1)S(1)} %fusion.9), channel_id=1, source_target_pairs={{0,4},{4,8},{8,12},{12,0},{1,5},{5,9},{9,13},{13,1},{2,6},{6,10},{... | collective-permute-start | bytes 1056776 | tf_op jit(solution)/shard_map/ppermute | solution.py:761
  443.8 31.2 %collective-permute-start.54 = (bf16[2,256,256]{2,1,0:T(8,128)(2,1)S(1)}, bf16[2,256,256]{2,1,0:T(8,128)(2,1)S(1)}, u32[]{:S(2)}, u32[]{:S(2)}) collective-permute-start(bf16[2,256,256]{2,1,0:T(8,128)(2,1)S(1)} %pad_maximum_fusion.13), channel_id=1, source_target_pairs={{0,12},{4,0},{8,4},{12,8},{1,13},{5,1},{9,5},{13,9},{2,14},{6,2},{... | collective-permute-start | bytes 786440 | tf_op jit(solution)/shard_map/ppermute | solution.py:784
  447.7 28.0 %collective-permute-start.55 = (bf16[2,256,256]{2,1,0:T(8,128)(2,1)S(1)}, bf16[2,256,256]{2,1,0:T(8,128)(2,1)S(1)}, u32[]{:S(2)}, u32[]{:S(2)}) collective-permute-start(bf16[2,256,256]{2,1,0:T(8,128)(2,1)S(1)} %pad_maximum_fusion.14), channel_id=1, source_target_pairs={{0,8},{4,12},{8,0},{12,4},{1,9},{5,13},{9,1},{13,5},{2,10},{6,14},... | collective-permute-start | bytes 786440 | tf_op jit(solution)/shard_map/ppermute | solution.py:784
  447.8 27.9 %collective-permute-start.56 = (bf16[2,256,256]{2,1,0:T(8,128)(2,1)S(1)}, bf16[2,256,256]{2,1,0:T(8,128)(2,1)S(1)}, u32[]{:S(2)}, u32[]{:S(2)}) collective-permute-start(bf16[2,256,256]{2,1,0:T(8,128)(2,1)S(1)} %pad_maximum_fusion.15), channel_id=1, source_target_pairs={{0,4},{4,8},{8,12},{12,0},{1,5},{5,9},{9,13},{13,1},{2,6},{6,10},{... | collective-permute-start | bytes 786440 | tf_op jit(solution)/shard_map/ppermute | solution.py:784
  475.8 33.6 %collective-permute-start.51 = (bf16[4,688,256]{2,1,0:T(8,128)(2,1)}, bf16[4,688,256]{2,1,0:T(8,128)(2,1)}, u32[]{:S(2)}, u32[]{:S(2)}) collective-permute-start(bf16[4,688,256]{2,1,0:T(8,128)(2,1)} %get-tuple-element.351), channel_id=1, source_target_pairs={{0,2},{1,3},{2,0},{3,1},{4,6},{5,7},{6,4},{7,5},{8,10},{9,11},{10,... | collective-permute-start | bytes 4227080 | tf_op jit(solution)/shard_map/ppermute | solution.py:756
  479.3 30.2 %collective-permute-start.57 = (bf16[688,256]{1,0:T(8,128)(2,1)}, bf16[688,256]{1,0:T(8,128)(2,1)}, u32[]{:S(2)}, u32[]{:S(2)}) collective-permute-start(bf16[688,256]{1,0:T(8,128)(2,1)} %get-tuple-element.450), channel_id=1, source_target_pairs={{0,12},{4,0},{8,4},{12,8},{1,13},{5,1},{9,5},{13,9},{2,14},{6,2},{... | collective-permute-start | bytes 1056776 | tf_op jit(solution)/shard_map/ppermute | solution.py:784
  482.6 32.5 %collective-permute-start.58 = (bf16[688,256]{1,0:T(8,128)(2,1)}, bf16[688,256]{1,0:T(8,128)(2,1)}, u32[]{:S(2)}, u32[]{:S(2)}) collective-permute-start(bf16[688,256]{1,0:T(8,128)(2,1)} %get-tuple-element.449), channel_id=1, source_target_pairs={{0,8},{4,12},{8,0},{12,4},{1,9},{5,13},{9,1},{13,5},{2,10},{6,14},... | collective-permute-start | bytes 1056776 | tf_op jit(solution)/shard_map/ppermute | solution.py:784
  483.7 31.4 %collective-permute-start.59 = (bf16[688,256]{1,0:T(8,128)(2,1)}, bf16[688,256]{1,0:T(8,128)(2,1)}, u32[]{:S(2)}, u32[]{:S(2)}) collective-permute-start(bf16[688,256]{1,0:T(8,128)(2,1)} %get-tuple-element.448), channel_id=1, source_target_pairs={{0,4},{4,8},{8,12},{12,0},{1,5},{5,9},{9,13},{13,1},{2,6},{6,10},{... | collective-permute-start | bytes 1056776 | tf_op jit(solution)/shard_map/ppermute | solution.py:784
  515.1 10.2 %collective-permute-start.64 = (bf16[2,512,768]{2,1,0:T(8,128)(2,1)}, bf16[2,512,768]{2,1,0:T(8,128)(2,1)}, u32[]{:S(2)}, u32[]{:S(2)}) collective-permute-start(bf16[2,512,768]{2,1,0:T(8,128)(2,1)} %get-tuple-element.387), channel_id=1, source_target_pairs={{0,1},{1,0},{2,3},{3,2},{4,5},{5,4},{6,7},{7,6},{8,9},{9,8},{10,11... | collective-permute-start | bytes 4718600 | tf_op jit(solution)/shard_map/ppermute | solution.py:751
  516.9 15.4 %collective-permute-start.63 = (bf16[256,256]{1,0:T(8,128)(2,1)}, bf16[256,256]{1,0:T(8,128)(2,1)S(1)}, u32[]{:S(2)}, u32[]{:S(2)}) collective-permute-start(bf16[256,256]{1,0:T(8,128)(2,1)} %fusion.44), channel_id=1, source_target_pairs={{0,2},{1,3},{2,0},{3,1},{4,6},{5,7},{6,4},{7,5},{8,10},{9,11},{10,... | collective-permute-start | bytes 393224 | tf_op jit(solution)/shard_map/ppermute | solution.py:756
  522.5 18.3 %collective-permute-start.62 = (bf16[256,1024]{1,0:T(8,128)(2,1)S(1)}, bf16[256,1024]{1,0:T(8,128)(2,1)S(1)}, u32[]{:S(2)}, u32[]{:S(2)}) collective-permute-start(bf16[256,1024]{1,0:T(8,128)(2,1)S(1)} %slice_select_fusion.1), channel_id=1, source_target_pairs={{0,2},{1,3},{2,0},{3,1},{4,6},{5,7},{6,4},{7,5},{8,10},{9,11},{10,... | collective-permute-start | bytes 1572872 | tf_op jit(solution)/shard_map/ppermute | solution.py:756
  524.1 16.7 %collective-permute-start.67 = (bf16[336,256]{1,0:T(8,128)(2,1)S(1)}, bf16[336,256]{1,0:T(8,128)(2,1)S(1)}, u32[]{:S(2)}, u32[]{:S(2)}) collective-permute-start(bf16[336,256]{1,0:T(8,128)(2,1)S(1)} %get-tuple-element.395), channel_id=1, source_target_pairs={{0,8},{4,12},{8,0},{12,4},{1,9},{5,13},{9,1},{13,5},{2,10},{6,14},... | collective-permute-start | bytes 516104 | tf_op jit(solution)/shard_map/ppermute | solution.py:784
  525.3 15.5 %collective-permute-start.68 = (bf16[336,256]{1,0:T(8,128)(2,1)S(1)}, bf16[336,256]{1,0:T(8,128)(2,1)S(1)}, u32[]{:S(2)}, u32[]{:S(2)}) collective-permute-start(bf16[336,256]{1,0:T(8,128)(2,1)S(1)} %get-tuple-element.396), channel_id=1, source_target_pairs={{0,4},{4,8},{8,12},{12,0},{1,5},{5,9},{9,13},{13,1},{2,6},{6,10},{... | collective-permute-start | bytes 516104 | tf_op jit(solution)/shard_map/ppermute | solution.py:784
  541.0 21.5 %collective-permute-start.69 = (bf16[4,384,256]{2,1,0:T(8,128)(2,1)S(1)}, bf16[4,384,256]{2,1,0:T(8,128)(2,1)S(1)}, u32[]{:S(2)}, u32[]{:S(2)}) collective-permute-start(bf16[4,384,256]{2,1,0:T(8,128)(2,1)S(1)} %get-tuple-element.460), channel_id=1, source_target_pairs={{0,2},{1,3},{2,0},{3,1},{4,6},{5,7},{6,4},{7,5},{8,10},{9,11},{10,... | collective-permute-start | bytes 2359304 | tf_op jit(solution)/shard_map/ppermute | solution.py:756
  542.8 17.4 %collective-permute-start.70 = (f32[3,1024]{1,0:T(4,128)S(1)}, f32[3,1024]{1,0:T(4,128)S(1)}, u32[]{:S(2)}, u32[]{:S(2)}) collective-permute-start(f32[3,1024]{1,0:T(4,128)S(1)} %fusion.61), channel_id=1, source_target_pairs={{0,2},{1,3},{2,0},{3,1},{4,6},{5,7},{6,4},{7,5},{8,10},{9,11},{10,... | collective-permute-start | bytes 36872 | tf_op jit(solution)/shard_map/ppermute | solution.py:756
  544.7 16.2 %collective-permute-start.71 = (bf16[352,256]{1,0:T(8,128)(2,1)S(1)}, bf16[352,256]{1,0:T(8,128)(2,1)S(1)}, u32[]{:S(2)}, u32[]{:S(2)}) collective-permute-start(bf16[352,256]{1,0:T(8,128)(2,1)S(1)} %get-tuple-element.443), channel_id=1, source_target_pairs={{0,12},{4,0},{8,4},{12,8},{1,13},{5,1},{9,5},{13,9},{2,14},{6,2},{... | collective-permute-start | bytes 540680 | tf_op jit(solution)/shard_map/ppermute | solution.py:784
  544.8 17.6 %collective-permute-start.72 = (bf16[352,256]{1,0:T(8,128)(2,1)S(1)}, bf16[352,256]{1,0:T(8,128)(2,1)S(1)}, u32[]{:S(2)}, u32[]{:S(2)}) collective-permute-start(bf16[352,256]{1,0:T(8,128)(2,1)S(1)} %get-tuple-element.442), channel_id=1, source_target_pairs={{0,8},{4,12},{8,0},{12,4},{1,9},{5,13},{9,1},{13,5},{2,10},{6,14},... | collective-permute-start | bytes 540680 | tf_op jit(solution)/shard_map/ppermute | solution.py:784
  546.6 15.9 %collective-permute-start.73 = (bf16[352,256]{1,0:T(8,128)(2,1)S(1)}, bf16[352,256]{1,0:T(8,128)(2,1)S(1)}, u32[]{:S(2)}, u32[]{:S(2)}) collective-permute-start(bf16[352,256]{1,0:T(8,128)(2,1)S(1)} %get-tuple-element.441), channel_id=1, source_target_pairs={{0,4},{4,8},{8,12},{12,0},{1,5},{5,9},{9,13},{13,1},{2,6},{6,10},{... | collective-permute-start | bytes 540680 | tf_op jit(solution)/shard_map/ppermute | solution.py:784
  560.2 17.9 %collective-permute-start.74 = (bf16[4,384,256]{2,1,0:T(8,128)(2,1)S(1)}, bf16[4,384,256]{2,1,0:T(8,128)(2,1)S(1)}, u32[]{:S(2)}, u32[]{:S(2)}) collective-permute-start(bf16[4,384,256]{2,1,0:T(8,128)(2,1)S(1)} %get-tuple-element.461), channel_id=1, source_target_pairs={{0,2},{1,3},{2,0},{3,1},{4,6},{5,7},{6,4},{7,5},{8,10},{9,11},{10,... | collective-permute-start | bytes 2359304 | tf_op jit(solution)/shard_map/ppermute | solution.py:756
  562.6 15.5 %collective-permute-start.76 = (bf16[384,256]{1,0:T(8,128)(2,1)S(1)}, bf16[384,256]{1,0:T(8,128)(2,1)S(1)}, u32[]{:S(2)}, u32[]{:S(2)}) collective-permute-start(bf16[384,256]{1,0:T(8,128)(2,1)S(1)} %get-tuple-element.457), channel_id=1, source_target_pairs={{0,12},{4,0},{8,4},{12,8},{1,13},{5,1},{9,5},{13,9},{2,14},{6,2},{... | collective-permute-start | bytes 589832 | tf_op jit(solution)/shard_map/ppermute | solution.py:784
  562.7 18.3 %collective-permute-start.77 = (bf16[384,256]{1,0:T(8,128)(2,1)S(1)}, bf16[384,256]{1,0:T(8,128)(2,1)S(1)}, u32[]{:S(2)}, u32[]{:S(2)}) collective-permute-start(bf16[384,256]{1,0:T(8,128)(2,1)S(1)} %get-tuple-element.456), channel_id=1, source_target_pairs={{0,8},{4,12},{8,0},{12,4},{1,9},{5,13},{9,1},{13,5},{2,10},{6,14},... | collective-permute-start | bytes 589832 | tf_op jit(solution)/shard_map/ppermute | solution.py:784
  563.6 17.3 %collective-permute-start.78 = (bf16[384,256]{1,0:T(8,128)(2,1)S(1)}, bf16[384,256]{1,0:T(8,128)(2,1)S(1)}, u32[]{:S(2)}, u32[]{:S(2)}) collective-permute-start(bf16[384,256]{1,0:T(8,128)(2,1)S(1)} %get-tuple-element.455), channel_id=1, source_target_pairs={{0,4},{4,8},{8,12},{12,0},{1,5},{5,9},{9,13},{13,1},{2,6},{6,10},{... | collective-permute-start | bytes 589832 | tf_op jit(solution)/shard_map/ppermute | solution.py:784
  590.4 17.1 %collective-permute-start.81 = (bf16[384,256]{1,0:T(8,128)(2,1)}, bf16[384,256]{1,0:T(8,128)(2,1)S(1)}, u32[]{:S(2)}, u32[]{:S(2)}) collective-permute-start(bf16[384,256]{1,0:T(8,128)(2,1)} %get-tuple-element.421), channel_id=1, source_target_pairs={{0,8},{4,12},{8,0},{12,4},{1,9},{5,13},{9,1},{13,5},{2,10},{6,14},... | collective-permute-start | bytes 589832 | tf_op jit(solution)/shard_map/ppermute | solution.py:784
  592.0 15.6 %collective-permute-start.80 = (bf16[384,256]{1,0:T(8,128)(2,1)}, bf16[384,256]{1,0:T(8,128)(2,1)S(1)}, u32[]{:S(2)}, u32[]{:S(2)}) collective-permute-start(bf16[384,256]{1,0:T(8,128)(2,1)} %get-tuple-element.420), channel_id=1, source_target_pairs={{0,12},{4,0},{8,4},{12,8},{1,13},{5,1},{9,5},{13,9},{2,14},{6,2},{... | collective-permute-start | bytes 589832 | tf_op jit(solution)/shard_map/ppermute | solution.py:784
  (111 other events, 1111.8 us)
